TPU v7x, 32 devices: a whole 2x2x4 slice. The times are simulated.
32 devices in a mesh: ctx: 8 (over z, core), ch: 4 (over y, x).
Axes of the slice: x: 2, y: 2, z: 4, core: 2. Of those that a mesh axis runs over, the one named last changes fastest.
Arguments:
- features: bfloat16 [4096, 3, 4096], P('ctx', None, 'ch'), may hold values from -6 to 6
- residual_in: bfloat16 [4096, 4096], P('ctx', 'ch'), may hold values from -6 to 6
- short_filter: float32 [3, 7, 256], P(None, None, 'ch'), may hold values from -2 to 2
- medium_filter: float32 [128, 256], P(None, 'ch'), may hold values from -0.5 to 0.5
- skip_gain: float32 [4096], P('ch'), may hold values from -4 to 4
- out_weight: bfloat16 [4096, 4096], P('ch'), may hold values from -0.125 to 0.125
- norm_gain: float32 [4096], replicated, may hold values from 0.1 to 1.9
- attn_weight: bfloat16 [4096, 6144], P(None, 'ch'), may hold values from -2 to 2, as said below
- attn_out: bfloat16 [2048, 4096], P('ch'), may hold values from -0.1875 to 0.1875
Outputs:
- result: bfloat16 [4096, 4096], P('ctx', 'ch')
Inputs may be any that keep to these rules, and one draw needn't show every extreme that they name: `attn_weight`: entries of order 4096 ** -0.5 times a few.
All inputs are finite; a program needn't handle non-finite values.
Results may differ from a plain program's by a relative error of at most 0.03.
Values may be sent and summed in bfloat16 or wider, within the bound.
No kernel may reach another device: no remote copies, remote signals or barrier semaphores. Data moves between devices by JAX's collectives and lax.ppermute only.
A program may use at most 128 MiB of HBM per device.

v0:
```python
import jax
import jax.numpy as jnp
from jax import lax
from jax.sharding import PartitionSpec as P

HEAD = 128
GROUP_SIZE = 16


norm_eps = 1e-05


def shifted(value, axis, steps):
    count = lax.axis_size(axis)
    initial, last = (max(0, -steps), min(count, count - steps))
    return lax.ppermute(value, axis, [(source, source + steps) for source in range(initial, last)])


def rotate_rows(block, positions):
    half_size = block.shape[-1] // 2
    frequency = 10000.0 ** (-jnp.arange(half_size, dtype=jnp.float32) * 2.0 / block.shape[-1])
    angles = positions.astype(jnp.float32)[:, None] * frequency[None, :]
    cosine = jnp.cos(angles)[:, None, :]
    sine_part = jnp.sin(angles)[:, None, :]
    first_half = block[..., :half_size]
    second_half = block[..., half_size:]
    return jnp.concatenate(
        [
            first_half * cosine - second_half * sine_part,
            second_half * cosine + first_half * sine_part,
        ],
        axis=-1,
    )


def featurize(extended, short_taps, row_count):
    lead_rows = short_taps.shape[1] - 1
    widened = extended.astype(jnp.float32)
    featured = jnp.zeros((row_count,) + extended.shape[1:], jnp.float32)
    for tap_index in range(short_taps.shape[1]):
        begin_row = lead_rows - tap_index
        featured = (
            featured
            + short_taps[:, tap_index, :][None] * widened[begin_row : begin_row + row_count]
        )
    return featured


def medium_mix(product_rim, product, filter_taps, skip_part):
    filter_len = filter_taps.shape[0]
    row_count, chan_count = product.shape
    group_count = filter_taps.shape[1]
    padded = jnp.concatenate(
        [jnp.zeros((1, chan_count), product.dtype), product_rim, product], axis=0
    )
    blocked = padded.reshape(
        row_count // filter_len + 1, filter_len, group_count, chan_count // group_count
    )
    windows = jnp.concatenate([blocked[:-1], blocked[1:]], axis=1).astype(jnp.float32)
    offsets = filter_len + jnp.arange(filter_len)[:, None] - jnp.arange(2 * filter_len)[None, :]
    inside = (offsets >= 0) & (offsets < filter_len)
    table = jnp.where(inside[:, :, None], filter_taps[jnp.clip(offsets, 0, filter_len - 1)], 0.0)
    toeplitz = jnp.transpose(table, (2, 0, 1))
    mixed = jnp.einsum("grs,nsgc->nrgc", toeplitz, windows, precision=lax.Precision.HIGHEST)
    return mixed.reshape(row_count, chan_count) + skip_part[None, :] * product.astype(jnp.float32)


def run_attention(queries, query_pos, key_rows, value_rows, position_of):
    head_count = queries.shape[1]
    row_count = queries.shape[0]
    head_size = queries.shape[2]
    scale_factor = 1.0 / head_size**0.5
    last_query = jnp.max(query_pos)
    initial = (
        jnp.zeros((head_count, row_count, head_size), jnp.float32),
        jnp.full((head_count, row_count), -1e30, jnp.float32),
        jnp.zeros((head_count, row_count), jnp.float32),
    )
    piece_keys = lax.all_gather(key_rows, "ctx", axis=0, tiled=True)
    piece_values = lax.all_gather(value_rows, "ctx", axis=0, tiled=True)
    piece_rows = piece_keys.shape[0]
    block_rows = 512

    def one_block(state_in, block_index):
        first_block = block_index * block_rows
        key_block = lax.dynamic_slice_in_dim(piece_keys, first_block, block_rows, 0)
        value_block = lax.dynamic_slice_in_dim(piece_values, first_block, block_rows, 0)
        key_pos = position_of(first_block + jnp.arange(block_rows))

        def update(state_old):
            acc_sum, run_max, run_total = state_old
            scores = (
                jnp.einsum("thd,khd->htk", queries, key_block, preferred_element_type=jnp.float32)
                * scale_factor
            )
            causal = (key_pos[None, :] <= query_pos[:, None])[None]
            block_max = jnp.max(jnp.where(causal, scores, -1e30), axis=-1)
            new_max = jnp.maximum(run_max, block_max)
            weights = jnp.where(causal, jnp.exp(scores - new_max[..., None]), 0.0)
            correction = jnp.exp(run_max - new_max)
            new_total = run_total * correction + jnp.sum(weights, axis=-1)
            update_sum = jnp.einsum(
                "htk,khd->htd",
                weights.astype(jnp.bfloat16),
                value_block,
                preferred_element_type=jnp.float32,
            )
            return (acc_sum * correction[..., None] + update_sum, new_max, new_total)

        def unchanged(state_old):
            return state_old

        state_out = lax.cond(jnp.min(key_pos) > last_query, unchanged, update, state_in)
        return (state_out, None)

    state_end, unused = lax.scan(one_block, initial, jnp.arange(piece_rows // block_rows))
    acc_sum, run_max, run_total = state_end
    output = acc_sum / run_total[..., None]
    return jnp.transpose(output, (1, 0, 2)).astype(jnp.bfloat16)


def shards(
    features,
    residual_in,
    short_filter,
    medium_filter,
    skip_gain,
    out_weight,
    norm_gain,
    attn_weight,
    attn_out,
):
    tok_rows = features.shape[0]
    chan_count = features.shape[2]
    short_taps = jnp.repeat(short_filter, GROUP_SIZE, axis=2)
    filter_len = medium_filter.shape[0]
    lead_rows = short_filter.shape[1] - 1
    rim_rows = shifted(features[tok_rows - lead_rows :], "ctx", 1)
    featured = featurize(jnp.concatenate([rim_rows, features], axis=0), short_taps, tok_rows)
    product = (featured[:, 1, :] * featured[:, 2, :]).astype(jnp.bfloat16)
    product_rim = shifted(product[tok_rows - (filter_len - 1) :], "ctx", 1)
    query_feat = featured[:, 0, :]
    mixed = medium_mix(product_rim, product, medium_filter, skip_gain)
    gated = (query_feat * mixed).astype(jnp.bfloat16)
    hyena_terms = jnp.dot(gated, out_weight, preferred_element_type=jnp.float32)
    hyena_out = lax.psum_scatter(
        hyena_terms.astype(jnp.bfloat16), "ch", scatter_dimension=1, tiled=True
    ).astype(jnp.float32)
    stream = (residual_in.astype(jnp.float32) + hyena_out).astype(jnp.bfloat16)
    stream_wide = stream.astype(jnp.float32)
    full_width = chan_count * lax.axis_size("ch")
    head_cols = attn_weight.shape[1]
    square_total = lax.psum(jnp.sum(stream_wide * stream_wide, axis=1), "ch")
    inverse = lax.rsqrt(square_total / full_width + norm_eps)
    gain_part = lax.dynamic_slice_in_dim(norm_gain, lax.axis_index("ch") * chan_count, chan_count)
    normed = (stream_wide * inverse[:, None] * gain_part[None, :]).astype(jnp.bfloat16)
    projected = jnp.dot(
        lax.all_gather(normed, "ch", axis=1, tiled=True),
        attn_weight,
        preferred_element_type=jnp.float32,
    )
    head_count = head_cols // (3 * HEAD)
    projected = projected.reshape(tok_rows, head_count, 3, HEAD)
    ctx_index = lax.axis_index("ctx")
    positions = ctx_index * tok_rows + jnp.arange(tok_rows, dtype=jnp.int32)
    queries = rotate_rows(projected[:, :, 0, :], positions).astype(jnp.bfloat16)
    key_rows = rotate_rows(projected[:, :, 1, :], positions).astype(jnp.bfloat16)
    value_rows = projected[:, :, 2, :].astype(jnp.bfloat16)

    def position_of(global_row):
        return global_row

    attended = run_attention(queries, positions, key_rows, value_rows, position_of)
    head_terms = jnp.dot(
        attended.reshape(tok_rows, head_count * HEAD), attn_out, preferred_element_type=jnp.float32
    )
    attn_mix = lax.psum_scatter(
        head_terms.astype(jnp.bfloat16), "ch", scatter_dimension=1, tiled=True
    ).astype(jnp.float32)
    return (stream_wide + attn_mix).astype(jnp.bfloat16)


def solution(mesh):
    in_specs = (
        P("ctx", None, "ch"),
        P("ctx", "ch"),
        P(None, None, "ch"),
        P(None, "ch"),
        P("ch"),
        P("ch", None),
        P(),
        P(None, "ch"),
        P("ch", None),
    )
    out_specs = P("ctx", "ch")
    return jax.shard_map(shards, mesh=mesh, in_specs=in_specs, out_specs=out_specs, check_vma=False)
```

profile of v0, /device:TPU:0, one launch (start us, length us, event | category | flops | bytes accessed | tf_op | source)
XLA Modules:
  0.0 568.6 jit_solution(12522805427994757676)
XLA Ops:
  12.1 3.2 copy.33
  16.1 108.2 %gather_fusion = f32[32768,64]{1,0:T(8,128)} fusion(f32[128,64]{1,0:T(8,128)S(1)} %copy.36, s32[32768]{0:T(1024)S(1)} %broadcast_clamp_fusion), kind=kCustom, calls=%fused_computation | custom fusion | bytes 16908288 | tf_op jit(solution)/shard_map/gather | solution.py:62
  124.4 13.6 %copy.37 = f32[128,256,64]{1,0,2:T(8,128)} copy(f32[128,256,64]{2,1,0:T(8,128)} %bitcast.98) | data formatting | bytes 16777216 | tf_op jit(solution)/shard_map/gather | solution.py:62
  139.2 2.8 maximum_convert_fusion
  142.1 14.1 %fusion.27 = f32[512,3,1024]{0,2,1:T(8,128)S(1)} fusion(f32[518,3,1024]{0,2,1:T(8,128)S(1)} %maximum_convert_fusion, f32[3,1024]{1,0:T(4,128)S(1)} %get-tuple-element.262, f32[3,1024]{1,0:T(4,128)S(1)} %get-tuple-element.263, f32[3,1024]{1,0:T(4,128)S(1)} %get-tuple-element.264, f32[3,1024]{1,0:T(4,128)S(1)} %get-tuple-element.265, ...), kind=kLoop, calls=%fused_computation.32 | loop fusion | flops 20447232 | bytes 50417664 | tf_op jit(solution)/shard_map/add | solution.py:43
  156.1 2.7 copy-done
  159.9 4.8 collective-permute-start.1
  170.4 7.7 %fusion.45 = f32[4,128,64,16]{1,3,0,2:T(8,128)S(1)} fusion(f32[128,256,64]{1,0,2:T(8,128)} %copy.37, pred[128,256]{1,0:T(8,128)(4,1)S(1)} %fusion.55, bf16[4,128,64,16]{1,3,0,2:T(8,128)(2,1)S(1)} %copy.35, bf16[4,128,64,16]{1,3,0,2:T(8,128)(2,1)S(1)} %copy.34), kind=kOutput, calls=%fused_computation.66 | convolution fusion | flops 1616904192 | bytes 12615680 | tf_op jit(solution)/shard_map/grs,nsgc->nrgc/dot_general | solution.py:64
  179.1 10.0 %convolution_convert_fusion = bf16[512,4096]{1,0:T(8,128)(2,1)} fusion(bf16[1024,4096]{1,0:T(8,128)(2,1)} %param.18, f32[128,8,4,128]{3,2,1,0:T(4,128)S(1)} %bitcast.101, f32[512,3,1024]{0,2,1:T(8,128)S(1)} %bitcast.100, f32[1024]{0:T(1024)S(1)} %copy-done.4, bf16[512,1,1024]{0,2,1:T(8,128)(2,1)S(1)} %fusion.41), kind=kOutput, calls=%fused_computation.44 | convolution fusion | flops 4299685888 | bytes 17829888 | tf_op jit(solution)/shard_map/dot_general | solution.py:145
  189.9 54.6 %reduce-scatter.3.cloned.1.call-done = bf16[512,1024]{1,0:T(8,128)(2,1)} async-done(((bf16[512,4096]{1,0:T(8,128)(2,1)}), bf16[512,1024]{1,0:T(8,128)(2,1)}) %reduce-scatter.3.cloned.1.call-update) | async-done | bytes 1048592 | tf_op jit(solution)/shard_map/reduce_scatter | solution.py:146
  246.1 8.9 %psum.7 = f32[512]{0:T(512)S(1)} all-reduce(f32[512]{0:T(512)S(1)} %fusion.35), channel_id=1, replica_groups=mesh['ctx'=8,'ch'=4] {'ch'}, use_global_device_ids=true, to_apply=%region_2.3 | all-reduce | flops 512 | bytes 4096 | tf_op jit(solution)/shard_map/psum | solution.py:153
  255.0 2.6 fusion.37
  257.7 52.7 %all-gather.5.cloned.1.call-done = bf16[512,4096]{1,0:T(8,128)(2,1)} async-done(((bf16[512,1024]{1,0:T(8,128)(2,1)}), bf16[512,4096]{1,0:T(8,128)(2,1)}) %all-gather.5.cloned.1.call-update) | async-done | bytes 4194320 | tf_op jit(solution)/shard_map/all_gather | solution.py:158
  310.4 10.6 %fusion.62 = f32[512,1536]{0,1:T(8,128)S(1)} fusion(bf16[512,4096]{1,0:T(8,128)(2,1)} %all-gather.5.cloned.1.call-done, bf16[4096,1536]{1,0:T(8,128)(2,1)} %param.20), kind=kOutput, calls=%fused_computation.107 | convolution fusion | flops 6442450944 | bytes 19922944 | tf_op jit(solution)/shard_map/dot_general | solution.py:157
  328.5 42.4 %all-gather.9.cloned.1.call-done = bf16[4096,4,1,128]{0,3,2,1:T(8,128)(2,1)} async-done(((bf16[512,4,1,128]{0,3,2,1:T(8,128)(2,1)}), bf16[4096,4,1,128]{0,3,2,1:T(8,128)(2,1)}) %all-gather.9.cloned.1.call-update) | async-done | bytes 4194320 | tf_op jit(solution)/shard_map/all_gather | solution.py:80
  370.9 6.3 %copy.43 = bf16[4096,4,128]{2,0,1:T(8,128)(2,1)} copy(bf16[4096,4,128]{0,2,1:T(8,128)(2,1)} %bitcast.102) | data formatting | bytes 8388608
  377.2 41.1 %all-gather.7.cloned.1.call-done = bf16[4096,4,128]{0,2,1:T(8,128)(2,1)} async-done(((bf16[512,4,128]{0,2,1:T(8,128)(2,1)}), bf16[4096,4,128]{0,2,1:T(8,128)(2,1)}) %all-gather.7.cloned.1.call-update) | async-done | bytes 4194320 | tf_op jit(solution)/shard_map/all_gather | solution.py:79
  418.3 6.3 %copy.41 = bf16[4096,4,128]{2,0,1:T(8,128)(2,1)} copy(bf16[4096,4,128]{0,2,1:T(8,128)(2,1)} %all-gather.7.cloned.1.call-done) | data formatting | bytes 8388608
  424.7 31.9 %while.15 = (s32[]{:T(128)}, f32[4,512,128]{2,1,0:T(8,128)S(1)}, f32[4,512]{1,0:T(4,128)S(1)}, f32[4,512]{1,0:T(4,128)S(1)}, s32[8]{0:T(128)S(1)}, /*index=5*/s3...) while((s32[]{:T(128)}, f32[4,512,128]{2,1,0:T(8,128)S(1)}, ...), condition=%wide.region_10.11_spmd.clone, body=%wide.region_4.10_spmd.clone.sunk | while | flops 549197312 | bytes 17445208 | solution.py:116
  427.9 6.0 %conditional.3 = (f32[4,512,128]{2,1,0:T(8,128)S(1)}, f32[4,512]{1,0:T(4,128)S(1)}, f32[4,512]{1,0:T(4,128)S(1)}) conditional(s32[]{:T(128)} %convert_element_type.148, (s32[512]{0:T(512)S(1)}, s32[]{:T(128)}, s32[]{:T(128)}, bf16[4096,4,128]{2,0,1:T(8,128)(2,1)}, bf16[512,4,128]{2,0,1:T(8,128)(2,1)S(1)}, /*index=5*/f32[4,512]{1,0:T(4,128)S(1)}, ...), branch_computations={%region_6.8_spmd, %region_9.9_spmd} | conditional | flops 549196288 | bytes 17424454 | solution.py:113
  431.1 2.8 fusion.13
  459.3 6.5 %convolution_convert_fusion.1 = bf16[512,4096]{1,0:T(8,128)(2,1)} fusion(bf16[512,512]{0,1:T(8,128)(2,1)S(1)} %bitcast.105, bf16[512,4096]{1,0:T(8,128)(2,1)} %param.21), kind=kOutput, calls=%fused_computation.45 | convolution fusion | flops 2149580800 | bytes 8912896 | tf_op jit(solution)/shard_map/dot_general | solution.py:174
  465.8 93.5 %reduce-scatter.5.cloned.1.call-done = bf16[512,1024]{1,0:T(8,128)(2,1)} async-done(((bf16[512,4096]{1,0:T(8,128)(2,1)}), bf16[512,1024]{1,0:T(8,128)(2,1)}) %reduce-scatter.5.cloned.1.call-update) | async-done | bytes 1048592 | tf_op jit(solution)/shard_map/reduce_scatter | solution.py:177
  559.3 2.8 fusion.38
  (127 shorter events, 41.2 us)
Async XLA Ops:
  6.5 237.9 %reduce-scatter.3.cloned.1.call-start = ((), (), s32[]{:S(2)}) async-start(), calls=%async_computation.2 | async-start | bytes 5242880 | tf_op jit(solution)/shard_map/reduce_scatter | solution.py:146
  8.0 130.0 %collective-permute-start = (bf16[6,3,1024]{2,0,1:T(8,128)(2,1)}, bf16[6,3,1024]{2,0,1:T(8,128)(2,1)S(1)}, u32[]{:S(2)}, u32[]{:S(2)}) collective-permute-start(bf16[6,3,1024]{2,0,1:T(8,128)(2,1)} %slice.91), channel_id=1, source_target_pairs={{0,4},{4,8},{8,12},{12,16},{16,20},{20,24},{24,28},{1,5},{5,9},{9,... | collective-permute-start | bytes 110600 | tf_op jit(solution)/shard_map/ppermute | solution.py:16
  138.0 4.1 copy-start.5
  156.1 2.7 copy-start
  159.5 7.8 %slice-start.2 = ((bf16[640]{0:T(1024)(128)(2,1)}), bf16[512]{0:T(512)(128)(2,1)S(1)}, s32[]{:S(2)}) async-start(bf16[640]{0:T(1024)(128)(2,1)} %copy-done.5), calls=%async_computation.9 | async-start | bytes 2048 | tf_op jit(solution)/shard_map/slice | solution.py:59
  159.9 7.4 %collective-permute-start.1 = (bf16[127,1024]{0,1:T(8,128)(2,1)S(1)}, bf16[127,1024]{0,1:T(8,128)(2,1)S(1)}, u32[]{:S(2)}, u32[]{:S(2)}) collective-permute-start(bf16[127,1024]{0,1:T(8,128)(2,1)S(1)} %slice_bitcast_fusion.3), channel_id=1, source_target_pairs={{0,4},{4,8},{8,12},{12,16},{16,20},{20,24},{24,28},{1,5},{5,9},{9,... | collective-permute-start | bytes 780296 | tf_op jit(solution)/shard_map/ppermute | solution.py:16
  168.7 10.3 %slice-start = ((s8[6291456]{0:T(1024)(128)(4,1)}), s8[4194304]{0:T(1024)(128)(4,1)S(1)}, s32[]{:S(2)}) async-start(s8[6291456]{0:T(1024)(128)(4,1)} %bitcast.99), calls=%async_computation.7 | async-start | bytes 8388608
  170.3 8.7 %slice-start.1 = ((s8[6291456]{0:T(1024)(128)(4,1)}), s8[2097152]{0:T(1024)(128)(4,1)S(1)}, s32[]{:S(2)}) async-start(s8[6291456]{0:T(1024)(128)(4,1)} %bitcast.99), calls=%async_computation.8 | async-start | bytes 4194304
  178.0 1.0 copy-start.4
  189.0 55.4 %copy-start.1 = (bf16[512,1024]{1,0:T(8,128)(2,1)S(1)}, bf16[512,1024]{1,0:T(8,128)(2,1)}, u32[]{:S(2)}) copy-start(bf16[512,1024]{1,0:T(8,128)(2,1)} %param.14) | copy-start | bytes 3145732
  189.0 121.3 %all-gather.5.cloned.1.call-start = ((), (), s32[]{:S(2)}) async-start(), calls=%async_computation.3 | async-start | bytes 5242880 | tf_op jit(solution)/shard_map/all_gather | solution.py:158
  257.6 113.2 %all-gather.9.cloned.1.call-start = ((), (), s32[]{:S(2)}) async-start(), calls=%async_computation.6 | async-start | bytes 4718592 | tf_op jit(solution)/shard_map/all_gather | solution.py:80
  321.0 1.6 copy-start.3
  323.5 94.8 %all-gather.7.cloned.1.call-start = ((), (), s32[]{:S(2)}) async-start(), calls=%async_computation.4 | async-start | bytes 4718592 | tf_op jit(solution)/shard_map/all_gather | solution.py:79
  327.2 232.1 %reduce-scatter.5.cloned.1.call-start = ((), (), s32[]{:S(2)}) async-start(), calls=%async_computation.5 | async-start | bytes 5242880 | tf_op jit(solution)/shard_map/reduce_scatter | solution.py:177
  465.8 93.5 %copy-start.2 = (bf16[512,1024]{1,0:T(8,128)(2,1)S(1)}, bf16[512,1024]{1,0:T(8,128)(2,1)}, u32[]{:S(2)}) copy-start(bf16[512,1024]{1,0:T(8,128)(2,1)} %reduce-scatter.3.cloned.1.call-done) | copy-start | bytes 3145732
Sparse Core Ops, SparseCore 0:
  189.2 55.2 reduce-scatter.2
  257.7 52.5 all-gather.4
  323.7 47.1 all-gather.8
  372.4 45.8 all-gather.6
  465.9 93.2 reduce-scatter.4
where the time goes:
time: 571 us; the launch traced here: 569 us
  waiting for transfers between devices  284 us (50%)
  local copies, waits for them, and re-layouts  161 us (28%)
  matrix products  39.6 us (7%)
  other arithmetic  37.6 us (7%)
  loops' own time  15.9 us (3%)
  between operations  13.5 us (2%)
  blocking collectives  8.93 us (2%)
  starting transfers between devices  7.52 us (1%)
    gather x2, local copies, waits for them, and re-layouts, medium_mix(): filter_taps[jnp.clip(offsets, 0, filter_len - 1)]  122 us
    reduce_scatter x1, waiting for transfers between devices, shards(): lax.psum_scatter(head_terms.astype(jnp.bfloat16), 'ch', scatter_dimension...  93.5 us
    reduce_scatter x1, waiting for transfers between devices, shards(): lax.psum_scatter(hyena_terms.astype(jnp.bfloat16), 'ch', scatter_dimensio...  54.6 us
    all_gather x1, waiting for transfers between devices, shards(): lax.all_gather(normed, 'ch', axis=1, tiled=True)  52.7 us
    all_gather x1, waiting for transfers between devices, run_attention(): piece_values = lax.all_gather(value_rows, 'ctx', axis=0, tiled=True)  42.4 us
    all_gather x1, waiting for transfers between devices, run_attention(): piece_keys = lax.all_gather(key_rows, 'ctx', axis=0, tiled=True)  41.1 us
    unnamed x26, local copies, waits for them, and re-layouts  21.4 us
    another operation x1, loops' own time, run_attention(): lax.scan(one_block, initial, jnp.arange(piece_rows // block_rows))  15.6 us
  transfers between devices with their start and end apart: 7, of which 5 were waited for; matrix products, arithmetic and copies ran while one was open for 25% of the time, Pallas kernels for 0%

commit v1 on v0

--- a/solution.py
+++ b/solution.py
@@ -1,19 +1,376 @@
+import functools
+
 import jax
 import jax.numpy as jnp
 from jax import lax
+from jax.experimental import pallas as pl
+from jax.experimental.pallas import tpu as pltpu
 from jax.sharding import PartitionSpec as P
 
 HEAD = 128
 GROUP_SIZE = 16
-
-
+LANES = 128
+LEAD = 16
 norm_eps = 1e-05
-
-
-def shifted(value, axis, steps):
-    count = lax.axis_size(axis)
-    initial, last = (max(0, -steps), min(count, count - steps))
-    return lax.ppermute(value, axis, [(source, source + steps) for source in range(initial, last)])
+MIB = 1024 * 1024
+F32 = jnp.float32
+BF16 = jnp.bfloat16
+
+
+def swap_ch(value, mask):
+    count = lax.axis_size("ch")
+    return lax.ppermute(value, "ch", [(i, i ^ mask) for i in range(count)])
+
+
+def swap_core(value):
+    count = lax.axis_size("ctx")
+    return lax.ppermute(value, "ctx", [(i, i ^ 1) for i in range(count)])
+
+
+def rotate_chips(value, distance):
+    count = lax.axis_size("ctx")
+    return lax.ppermute(value, "ctx", [(i, (i + 2 * distance) % count) for i in range(count)])
+
+
+def conv_kernel(first_row, halo_rows, taps_ref, base_ref, skip_ref, *rest):
+    if first_row == 0:
+        halo_ref, rows_ref, out_ref, wide, product, table = rest
+    else:
+        rows_ref, out_ref, wide, product, table = rest
+    count = out_ref.shape[0]
+    length = base_ref.shape[1] // 2
+    taps = taps_ref.shape[0] // 3
+
+    if first_row == 0:
+        wide[0, halo_rows - LEAD : halo_rows] = halo_ref[2 * halo_rows : 2 * halo_rows + LEAD].astype(F32)
+        wide[1, :halo_rows] = halo_ref[:halo_rows].astype(F32)
+        wide[2, :halo_rows] = halo_ref[halo_rows : 2 * halo_rows].astype(F32)
+        for kind in range(3):
+            wide[kind, halo_rows:] = rows_ref[kind].astype(F32)
+    else:
+        for kind in range(3):
+            wide[kind] = rows_ref[kind, first_row - halo_rows : first_row + count].astype(F32)
+
+    groups = base_ref.shape[0]
+    for group in range(groups):
+        spread = jnp.broadcast_to(base_ref[group : group + 1, :], (length, 2 * length))
+        rolled = pltpu.roll(spread, 0, 1, stride=1, stride_axis=0)
+        table[group * length : (group + 1) * length, :] = rolled.astype(BF16)
+
+    def featured(kind, start):
+        total = taps_ref[kind * taps : kind * taps + 1, :] * wide[kind, start : start + length, :]
+        for tap in range(1, taps):
+            weight = taps_ref[kind * taps + tap : kind * taps + tap + 1, :]
+            total = total + weight * wide[kind, start - tap : start - tap + length, :]
+        return total
+
+    for block in range(count // length + 1):
+        start = LEAD + block * length
+        product[block * length : (block + 1) * length, :] = (
+            featured(1, start) * featured(2, start)
+        ).astype(BF16)
+
+    group_of = lax.broadcasted_iota(jnp.int32, (length, 2 * LANES), 1) % LANES // GROUP_SIZE
+    for pair in range(count // (2 * length)):
+        begin = pair * 2 * length
+        window = jnp.concatenate(
+            [
+                product[begin : begin + 2 * length, :],
+                product[begin + length : begin + 3 * length, :],
+            ],
+            axis=1,
+        )
+        spread = jnp.dot(table[...], window, preferred_element_type=F32)
+        mixed = spread[:length]
+        for group in range(1, groups):
+            mixed = jnp.where(group_of == group, spread[group * length : (group + 1) * length], mixed)
+        for part in range(2):
+            row = begin + part * length
+            direct = skip_ref[...] * product[row + length : row + 2 * length, :].astype(F32)
+            gate = featured(0, halo_rows + row)
+            out_ref[row : row + length, :] = (
+                gate * (mixed[:, part * LANES : (part + 1) * LANES] + direct)
+            ).astype(BF16)
+
+
+def conv_chunk(features, halo, first_row, count, taps, base, skip):
+    kinds, rows, channels = features.shape
+    length = base.shape[1] // 2
+    halo_rows = length + LEAD
+    groups = LANES // GROUP_SIZE
+    specs = [
+        pl.BlockSpec((taps.shape[0], LANES), lambda i: (0, i)),
+        pl.BlockSpec((groups, 2 * length), lambda i: (i, 0)),
+        pl.BlockSpec((1, LANES), lambda i: (0, i)),
+    ]
+    operands = [taps, base, skip]
+    if first_row == 0:
+        specs.append(pl.BlockSpec((halo.shape[0], LANES), lambda i: (0, i)))
+        operands.append(halo)
+        specs.append(pl.BlockSpec((kinds, count, LANES), lambda i: (0, 0, i)))
+    else:
+        specs.append(pl.BlockSpec((kinds, rows, LANES), lambda i: (0, 0, i)))
+    operands.append(features)
+    return pl.pallas_call(
+        functools.partial(conv_kernel, first_row, halo_rows),
+        grid=(channels // LANES,),
+        in_specs=specs,
+        out_specs=pl.BlockSpec((count, LANES), lambda i: (0, i)),
+        out_shape=jax.ShapeDtypeStruct((count, channels), BF16),
+        scratch_shapes=[
+            pltpu.VMEM((kinds, halo_rows + count, LANES), F32),
+            pltpu.VMEM((length + count, LANES), BF16),
+            pltpu.VMEM((groups * length, 2 * length), BF16),
+        ],
+        compiler_params=pltpu.CompilerParams(vmem_limit_bytes=24 * MIB),
+        name="hyena_filters",
+    )(*operands)
+
+
+def columns_kernel(steps_of, order_ref, left_ref, right_ref, *outs):
+    step = pl.program_id(0)
+    value = jnp.dot(left_ref[...], right_ref[...], preferred_element_type=F32).astype(BF16)
+    begin = 0
+    for out, steps in zip(outs, steps_of):
+
+        @pl.when((step >= begin) & (step < begin + steps))
+        def _():
+            out[...] = value
+
+        begin += steps
+
+
+def column_products(left, right, order, steps_of, width):
+    rows, depth = left.shape
+    specs, shapes, begin = [], [], 0
+    for steps in steps_of:
+        specs.append(
+            pl.BlockSpec(
+                (rows, width),
+                functools.partial(lambda b, s, i, order: (0, jnp.clip(i - b, 0, s - 1)), begin, steps),
+            )
+        )
+        shapes.append(jax.ShapeDtypeStruct((rows, steps * width), BF16))
+        begin += steps
+    return pl.pallas_call(
+        functools.partial(columns_kernel, steps_of),
+        grid_spec=pltpu.PrefetchScalarGridSpec(
+            num_scalar_prefetch=1,
+            grid=(sum(steps_of),),
+            in_specs=[
+                pl.BlockSpec((rows, depth), lambda i, order: (0, 0)),
+                pl.BlockSpec((depth, width), lambda i, order: (0, order[i])),
+            ],
+            out_specs=specs,
+        ),
+        out_shape=shapes,
+        compiler_params=pltpu.CompilerParams(vmem_limit_bytes=24 * MIB),
+        name="hyena_projection",
+    )(order, left, right)
+
+
+def qkv_kernel(chips, meta_ref, own, from_x, from_y, diag_a, diag_b, gain, cosine, sine, weight, *rest):
+    outs, (normed, total) = rest[:chips], rest[chips:]
+    step = pl.program_id(0)
+    steps = pl.num_programs(0)
+    depth = weight.shape[0]
+    rows, channels = own.shape
+    per_block = channels // depth
+
+    @pl.when(step == 0)
+    def _():
+        half = rows // 2
+        blocks = [own[...], from_x[...], from_y[...], None]
+        blocks[3] = jnp.concatenate([diag_a[...], diag_b[...]], axis=0)
+        square = jnp.zeros((rows, 1), F32)
+        for block in blocks:
+            wide = block.astype(F32)
+            square = square + jnp.sum(wide * wide, axis=1, keepdims=True)
+        inverse = lax.rsqrt(square / (4 * channels) + norm_eps)
+        for index, block in enumerate(blocks):
+            scaled = block.astype(F32) * inverse * gain[pl.ds(meta_ref[index], 1), :]
+            for part in range(per_block):
+                normed[index * per_block + part] = scaled[:, part * depth : (part + 1) * depth].astype(BF16)
+
+    term = jnp.dot(normed[step], weight[...], preferred_element_type=F32)
+
+    @pl.when(step == 0)
+    def _():
+        total[...] = term
+
+    @pl.when(step > 0)
+    def _():
+        total[...] += term
+
+    @pl.when(step == steps - 1)
+    def _():
+        for distance, out in enumerate(outs):
+            head = lax.rem(meta_ref[4] + distance, chips)
+            for kind in range(3):
+                column = pl.multiple_of((head * 3 + kind) * HEAD, HEAD)
+                part = total[:, pl.ds(column, HEAD)]
+                if kind < 2:
+                    part = part * cosine[...] + pltpu.roll(part, HEAD // 2, 1) * sine[...]
+                out[kind] = part.astype(BF16)
+
+
+def project(meta, own, from_x, from_y, diag_a, diag_b, gain, cosine, sine, weight, chips):
+    rows, channels = own.shape
+    width = weight.shape[1]
+    depth = 512
+    per_block = channels // depth
+    full = lambda shape: pl.BlockSpec(shape, lambda i, meta: (0,) * len(shape))
+    return pl.pallas_call(
+        functools.partial(qkv_kernel, chips),
+        grid_spec=pltpu.PrefetchScalarGridSpec(
+            num_scalar_prefetch=1,
+            grid=(4 * per_block,),
+            in_specs=[
+                full(own.shape),
+                full(from_x.shape),
+                full(from_y.shape),
+                full(diag_a.shape),
+                full(diag_b.shape),
+                full(gain.shape),
+                full(cosine.shape),
+                full(sine.shape),
+                pl.BlockSpec(
+                    (depth, width),
+                    lambda i, meta: (meta[i // per_block] * per_block + i % per_block, 0),
+                ),
+            ],
+            out_specs=[full((3, rows, HEAD))] * chips,
+            scratch_shapes=[
+                pltpu.VMEM((4 * per_block, rows, depth), BF16),
+                pltpu.VMEM((rows, width), F32),
+            ],
+        ),
+        out_shape=[jax.ShapeDtypeStruct((3, rows, HEAD), BF16)] * chips,
+        compiler_params=pltpu.CompilerParams(vmem_limit_bytes=40 * MIB),
+        name="norm_qkv",
+    )(meta, own, from_x, from_y, diag_a, diag_b, gain, cosine, sine, weight)
+
+
+def attention_kernel(chips, chunks, meta_ref, *refs):
+    own, other, outs = refs[:chunks], refs[chunks : 2 * chunks], refs[2 * chunks :]
+    chip, core = meta_ref[4], meta_ref[5]
+    scale = 1.0 / HEAD**0.5 * 1.4426950408889634
+
+    def rows(refs_in, distance, kind):
+        return jnp.concatenate([ref[distance, kind] for ref in refs_in], axis=0)
+
+    def scores_of(queries, keys):
+        return lax.dot_general(queries, keys, (((1,), (1,)), ((), ())), preferred_element_type=F32) * scale
+
+    def update(state, scores, values):
+        top, total, acc = state
+        new_top = jnp.maximum(top, jnp.max(scores, axis=1, keepdims=True))
+        weights = jnp.exp2(scores - new_top)
+        shrink = jnp.exp2(top - new_top)
+        total = total * shrink + jnp.sum(weights, axis=1, keepdims=True)
+        acc = acc * shrink + jnp.dot(weights.astype(BF16), values, preferred_element_type=F32)
+        return new_top, total, acc
+
+    for distance, out in enumerate(outs):
+        place = lax.rem(chip + distance, chips)
+        here = lax.rem(chip - place + chips, chips)
+        queries = rows(own, here, 0)
+        count = queries.shape[0]
+        scores = scores_of(queries, rows(own, here, 1))
+        row = lax.broadcasted_iota(jnp.int32, scores.shape, 0)
+        column = lax.broadcasted_iota(jnp.int32, scores.shape, 1)
+        scores = jnp.where(column <= row, scores, -1e30)
+        state = (
+            jnp.full((count, 1), -1e30, F32),
+            jnp.zeros((count, 1), F32),
+            jnp.zeros((count, HEAD), F32),
+        )
+        state = update(state, scores, rows(own, here, 2))
+
+        def own_block(index, state):
+            there = lax.rem(chip - index + chips, chips)
+            return update(state, scores_of(queries, rows(own, there, 1)), rows(own, there, 2))
+
+        def other_block(index, state):
+            there = lax.rem(chip - index + chips, chips)
+            return update(state, scores_of(queries, rows(other, there, 0)), rows(other, there, 1))
+
+        state = lax.fori_loop(0, place, own_block, state)
+        state = lax.fori_loop(0, place + core, other_block, state)
+        out[...] = (state[2] / state[1]).astype(BF16)
+
+
+def attend(meta, own, other, chips):
+    chunks = len(own)
+    count = sum(piece.shape[2] for piece in own)
+    whole = lambda shape: pl.BlockSpec(shape, lambda i, meta: (0,) * len(shape))
+    return pl.pallas_call(
+        functools.partial(attention_kernel, chips, chunks),
+        grid_spec=pltpu.PrefetchScalarGridSpec(
+            num_scalar_prefetch=1,
+            grid=(1,),
+            in_specs=[whole(piece.shape) for piece in own + other],
+            out_specs=[whole((count, HEAD))] * chips,
+        ),
+        out_shape=[jax.ShapeDtypeStruct((count, HEAD), BF16)] * chips,
+        compiler_params=pltpu.CompilerParams(vmem_limit_bytes=40 * MIB),
+        name="attention",
+    )(meta, *own, *other)
+
+
+def mix_kernel(chips, meta_ref, own, from_x, from_y, diag_a, diag_b, stream, own_w, near_w, far_w, out, ordered):
+    chip, core = meta_ref[4], meta_ref[5]
+    rows = stream.shape[0]
+    half_rows = near_w.shape[1]
+
+    @pl.when(pl.program_id(0) == 0)
+    def _():
+        for distance in range(chips):
+            head = lax.rem(chip - distance + chips, chips)
+            column = pl.ds(pl.multiple_of(head * HEAD, HEAD), HEAD)
+            ordered[0, :, column] = own[distance]
+            ordered[1, :, column] = from_x[distance]
+            ordered[2, :, column] = from_y[distance]
+            ordered[3, : rows // 2, column] = diag_a[distance]
+            ordered[3, rows // 2 :, column] = diag_b[distance]
+
+    total = stream[...].astype(F32)
+    total = total + jnp.dot(ordered[0], own_w[...], preferred_element_type=F32)
+    near = pl.ds(pl.multiple_of(core * half_rows, half_rows), half_rows)
+    far = pl.ds(pl.multiple_of((1 - core) * half_rows, half_rows), half_rows)
+    for index in range(3):
+        total = total + jnp.dot(ordered[index + 1, :, near], near_w[index], preferred_element_type=F32)
+        total = total + jnp.dot(ordered[index + 1, :, far], far_w[index], preferred_element_type=F32)
+    out[...] = total.astype(BF16)
+
+
+def mix(meta, own, from_x, from_y, diag_a, diag_b, stream, own_w, near_w, far_w, chips):
+    rows, channels = stream.shape
+    width = 256
+    full = lambda shape: pl.BlockSpec(shape, lambda i, meta: (0,) * len(shape))
+    return pl.pallas_call(
+        functools.partial(mix_kernel, chips),
+        grid_spec=pltpu.PrefetchScalarGridSpec(
+            num_scalar_prefetch=1,
+            grid=(channels // width,),
+            in_specs=[
+                full(own.shape),
+                full(from_x.shape),
+                full(from_y.shape),
+                full(diag_a.shape),
+                full(diag_b.shape),
+                pl.BlockSpec((rows, width), lambda i, meta: (0, i)),
+                pl.BlockSpec((own_w.shape[0], width), lambda i, meta: (0, i)),
+                pl.BlockSpec((3, near_w.shape[1], width), lambda i, meta: (0, 0, i)),
+                pl.BlockSpec((3, far_w.shape[1], width), lambda i, meta: (0, 0, i)),
+            ],
+            out_specs=pl.BlockSpec((rows, width), lambda i, meta: (0, i)),
+            scratch_shapes=[pltpu.VMEM((4, rows, chips * HEAD), BF16)],
+        ),
+        out_shape=jax.ShapeDtypeStruct((rows, channels), BF16),
+        compiler_params=pltpu.CompilerParams(vmem_limit_bytes=40 * MIB),
+        name="attention_mix",
+    )(meta, own, from_x, from_y, diag_a, diag_b, stream, own_w, near_w, far_w)
 
 
 def rotate_rows(block, positions):
@@ -31,38 +388,6 @@
         ],
         axis=-1,
     )
-
-
-def featurize(extended, short_taps, row_count):
-    lead_rows = short_taps.shape[1] - 1
-    widened = extended.astype(jnp.float32)
-    featured = jnp.zeros((row_count,) + extended.shape[1:], jnp.float32)
-    for tap_index in range(short_taps.shape[1]):
-        begin_row = lead_rows - tap_index
-        featured = (
-            featured
-            + short_taps[:, tap_index, :][None] * widened[begin_row : begin_row + row_count]
-        )
-    return featured
-
-
-def medium_mix(product_rim, product, filter_taps, skip_part):
-    filter_len = filter_taps.shape[0]
-    row_count, chan_count = product.shape
-    group_count = filter_taps.shape[1]
-    padded = jnp.concatenate(
-        [jnp.zeros((1, chan_count), product.dtype), product_rim, product], axis=0
-    )
-    blocked = padded.reshape(
-        row_count // filter_len + 1, filter_len, group_count, chan_count // group_count
-    )
-    windows = jnp.concatenate([blocked[:-1], blocked[1:]], axis=1).astype(jnp.float32)
-    offsets = filter_len + jnp.arange(filter_len)[:, None] - jnp.arange(2 * filter_len)[None, :]
-    inside = (offsets >= 0) & (offsets < filter_len)
-    table = jnp.where(inside[:, :, None], filter_taps[jnp.clip(offsets, 0, filter_len - 1)], 0.0)
-    toeplitz = jnp.transpose(table, (2, 0, 1))
-    mixed = jnp.einsum("grs,nsgc->nrgc", toeplitz, windows, precision=lax.Precision.HIGHEST)
-    return mixed.reshape(row_count, chan_count) + skip_part[None, :] * product.astype(jnp.float32)
 
 
 def run_attention(queries, query_pos, key_rows, value_rows, position_of):
@@ -119,29 +444,8 @@
     return jnp.transpose(output, (1, 0, 2)).astype(jnp.bfloat16)
 
 
-def shards(
-    features,
-    residual_in,
-    short_filter,
-    medium_filter,
-    skip_gain,
-    out_weight,
-    norm_gain,
-    attn_weight,
-    attn_out,
-):
-    tok_rows = features.shape[0]
-    chan_count = features.shape[2]
-    short_taps = jnp.repeat(short_filter, GROUP_SIZE, axis=2)
-    filter_len = medium_filter.shape[0]
-    lead_rows = short_filter.shape[1] - 1
-    rim_rows = shifted(features[tok_rows - lead_rows :], "ctx", 1)
-    featured = featurize(jnp.concatenate([rim_rows, features], axis=0), short_taps, tok_rows)
-    product = (featured[:, 1, :] * featured[:, 2, :]).astype(jnp.bfloat16)
-    product_rim = shifted(product[tok_rows - (filter_len - 1) :], "ctx", 1)
-    query_feat = featured[:, 0, :]
-    mixed = medium_mix(product_rim, product, medium_filter, skip_gain)
-    gated = (query_feat * mixed).astype(jnp.bfloat16)
+def after_gating(gated, residual_in, out_weight, norm_gain, attn_weight, attn_out):
+    tok_rows, chan_count = gated.shape
     hyena_terms = jnp.dot(gated, out_weight, preferred_element_type=jnp.float32)
     hyena_out = lax.psum_scatter(
         hyena_terms.astype(jnp.bfloat16), "ch", scatter_dimension=1, tiled=True
@@ -180,6 +484,119 @@
     return (stream_wide + attn_mix).astype(jnp.bfloat16)
 
 
+def rotation_tables(positions):
+    half_size = HEAD // 2
+    frequency = 10000.0 ** (-jnp.arange(half_size, dtype=F32) * 2.0 / HEAD)
+    angles = positions.astype(F32)[:, None] * frequency[None, :]
+    cosine, sine = jnp.cos(angles), jnp.sin(angles)
+    return jnp.concatenate([cosine, cosine], axis=1), jnp.concatenate([-sine, sine], axis=1)
+
+
+def shards(
+    features,
+    residual_in,
+    short_filter,
+    medium_filter,
+    skip_gain,
+    out_weight,
+    norm_gain,
+    attn_weight,
+    attn_out,
+):
+    rows, _, channels = features.shape
+    chips = lax.axis_size("ctx") // 2
+    length = medium_filter.shape[0]
+    chunk = rows // 2
+    half = channels // 2
+    ctx, ch = lax.axis_index("ctx"), lax.axis_index("ch")
+    meta = jnp.stack([ch, ch ^ 1, ch ^ 2, ch ^ 3, ctx // 2, ctx % 2]).astype(jnp.int32)
+
+    by_kind = jnp.transpose(features, (1, 0, 2))
+    halo_rows = length + LEAD
+    edge = jnp.concatenate(
+        [by_kind[1, rows - halo_rows :], by_kind[2, rows - halo_rows :], by_kind[0, rows - LEAD :]], axis=0
+    )
+    count = lax.axis_size("ctx")
+    halo = lax.ppermute(edge, "ctx", [(i, i + 1) for i in range(count - 1)])
+
+    taps = jnp.repeat(short_filter, GROUP_SIZE, axis=2).reshape(-1, channels)
+    base = jnp.pad(medium_filter.T[:, ::-1], ((0, 0), (1, length - 1)))
+    skip = skip_gain.reshape(1, channels)
+    starts = [rows - chunk, 0]
+    if lax.axis_size("ch") != 4 or attn_weight.shape[1] != 3 * HEAD * chips:
+        gated = [conv_chunk(by_kind, halo, start, chunk, taps, base, skip) for start in starts]
+        return after_gating(
+            jnp.concatenate(gated[::-1], axis=0), residual_in, out_weight, norm_gain, attn_weight, attn_out
+        )
+
+    gain = norm_gain.reshape(4, channels)
+    cosine, sine = rotation_tables(ctx * rows + jnp.arange(rows, dtype=jnp.int32))
+
+    first = jnp.stack([2 * (ch ^ 3), 2 * (ch ^ 1), 2 * (ch ^ 3) + 1, 2 * (ch ^ 2) + 1]).astype(jnp.int32)
+    second = jnp.stack([2 * (ch ^ 1) + 1, 2 * (ch ^ 2), 2 * ch, 2 * ch + 1]).astype(jnp.int32)
+
+    stream = {}
+    for start in starts:
+        gated = conv_chunk(by_kind, halo, start, chunk, taps, base, skip)
+        to_x, to_y = column_products(gated, out_weight, first, (2, 2), half)
+        from_x, from_y = swap_ch(to_x, 1), swap_ch(to_y, 2)
+        along_x, along_y, kept = column_products(gated, out_weight, second, (1, 1, 2), half)
+        along_x = (along_x.astype(F32) + from_y[:, :half].astype(F32)).astype(BF16)
+        along_y = (along_y.astype(F32) + from_x[:, :half].astype(F32)).astype(BF16)
+        late_x, late_y = swap_ch(along_x, 1), swap_ch(along_y, 2)
+        hyena = kept.astype(F32) + jnp.concatenate(
+            [
+                from_x[:, half:].astype(F32) + late_y.astype(F32),
+                from_y[:, half:].astype(F32) + late_x.astype(F32),
+            ],
+            axis=1,
+        )
+        stream[start] = (residual_in[start : start + chunk].astype(F32) + hyena).astype(BF16)
+
+    own, other = {}, {}
+    for start in starts:
+        part = stream[start]
+        near_x, near_y = swap_ch(part, 1), swap_ch(part, 2)
+        diag_a = swap_ch(near_x[: chunk // 2], 2)
+        diag_b = swap_ch(near_y[chunk // 2 :], 1)
+        outs = project(
+            meta,
+            part,
+            near_x,
+            near_y,
+            diag_a,
+            diag_b,
+            gain,
+            cosine[start : start + chunk],
+            sine[start : start + chunk],
+            attn_weight,
+            chips,
+        )
+        pieces = [outs[0]] + [rotate_chips(outs[d], d) for d in range(1, chips)]
+        own[start] = jnp.stack(pieces)
+        other[start] = swap_core(jnp.stack([piece[1:] for piece in pieces]))
+
+    later, _ = lax.optimization_barrier((attn_out, stream[0]))
+    half_rows = later.shape[0] // 2
+    mine = lax.dynamic_slice_in_dim(later, (ctx % 2) * half_rows, half_rows, 0)
+    near_w = jnp.stack(
+        [
+            swap_ch(lax.dynamic_slice_in_dim(mine, (ch ^ mask) * channels, channels, 1), mask)
+            for mask in (1, 2, 3)
+        ]
+    )
+    far_w = swap_core(near_w)
+    own_w = lax.dynamic_slice_in_dim(attn_out, ch * channels, channels, 1)
+
+    outs = attend(meta, [own[0], own[chunk]], [other[0], other[chunk]], chips)
+    heads = jnp.stack([outs[0]] + [rotate_chips(outs[d], d) for d in range(1, chips)])
+    near_x, near_y = swap_ch(heads, 1), swap_ch(heads, 2)
+    diag_a = swap_ch(near_x[:, : rows // 2], 2)
+    diag_b = swap_ch(near_y[:, rows // 2 :], 1)
+    whole_stream = jnp.concatenate([stream[0], stream[chunk]], axis=0)
+    return mix(meta, heads, near_x, near_y, diag_a, diag_b, whole_stream, own_w, near_w, far_w, chips)
+
+
 def solution(mesh):
     in_specs = (
         P("ctx", None, "ch"),

time: 571 us -> 220 us (0.39)
  waiting for transfers between devices: 284 us -> 69.3 us
  local copies, waits for them, and re-layouts: 161 us -> 25.3 us
  Pallas kernels: 0 us -> 66.4 us
  starting transfers between devices: 7.52 us -> 49.2 us
  matrix products: 39.6 us -> 0 us
  other arithmetic: 37.6 us -> 7.82 us
  loops' own time: 15.9 us -> 0 us
  between operations: 13.5 us -> 0.45 us
  blocking collectives: 8.93 us -> 0 us
    reduce_scatter x2 -> x0, waiting for transfers between devices: 148 us -> none  [the longest x1 93.5 us: shards(): lax.psum_scatter(head_terms.astype(jnp.bfloat16), 'ch', scatter_dimension...]
    all_gather x3 -> x0, waiting for transfers between devices: 136 us -> none  [the longest x1 52.7 us: shards(): lax.all_gather(normed, 'ch', axis=1, tiled=True)]
    gather x2 -> x0, local copies, waits for them, and re-layouts: 122 us -> none  [medium_mix(): filter_taps[jnp.clip(offsets, 0, filter_len - 1)]]
    ppermute x2 -> x36, waiting for transfers between devices: 0.01 us -> 69.3 us  [the longest x23 48.2 us: swap_ch(): return lax.ppermute(value, 'ch', [(i, i ^ mask) for i in range(count)])]
    pallas_call x0 -> x10, Pallas kernels: none -> 66.4 us  [the longest x2 23 us: project(): pl.pallas_call(functools.partial(qkv_kernel, chips), grid_spec=pltpu.Pref...]
    ppermute x2 -> x36, starting transfers between devices: 7.14 us -> 49.2 us  [the longest x23 28 us: swap_ch(): return lax.ppermute(value, 'ch', [(i, i ^ mask) for i in range(count)])]
    dot_general x6 -> x0, matrix products: 39.6 us -> none  [the longest x1 10.6 us: shards(): jnp.dot(lax.all_gather(normed, 'ch', axis=1, tiled=True), attn_weight, pr...]
    add x12 -> x4, other arithmetic: 19.3 us -> 2.17 us  [the longest x2 1.08 us: shards(): from_x[:, half:].astype(F32) + late_y.astype(F32)]
  transfers between devices with their start and end apart: 7 -> 36, of which waited for: 5 -> 18; matrix products, arithmetic and copies ran while one was open for 25% -> 7% of each run, Pallas kernels for 0% -> 27%
where the time goes in v1:
time: 220 us; the launch traced here: 218 us
  waiting for transfers between devices  69.3 us (32%)
  Pallas kernels  66.4 us (30%)
  starting transfers between devices  49.2 us (22%)
  local copies, waits for them, and re-layouts  25.3 us (12%)
  other arithmetic  7.82 us (4%)
    ppermute x23, waiting for transfers between devices, swap_ch(): return lax.ppermute(value, 'ch', [(i, i ^ mask) for i in range(count)])  48.2 us
    ppermute x23, starting transfers between devices, swap_ch(): return lax.ppermute(value, 'ch', [(i, i ^ mask) for i in range(count)])  28 us
    pallas_call x2, Pallas kernels, project(): pl.pallas_call(functools.partial(qkv_kernel, chips), grid_spec=pltpu.Pref...  23 us
    ppermute x9, waiting for transfers between devices, rotate_chips(): lax.ppermute(value, 'ctx', [(i, (i + 2 * distance) % count) for i in rang...  20.2 us
    ppermute x9, starting transfers between devices, rotate_chips(): lax.ppermute(value, 'ctx', [(i, (i + 2 * distance) % count) for i in rang...  17.4 us
    unnamed x24, local copies, waits for them, and re-layouts  14.7 us
    pallas_call x4, Pallas kernels, column_products(): pl.pallas_call(functools.partial(columns_kernel, steps_of), grid_spec=plt...  12.6 us
    pallas_call x2, Pallas kernels, conv_chunk(): pl.pallas_call(functools.partial(conv_kernel, first_row, halo_rows), grid...  12.3 us
  transfers between devices with their start and end apart: 36, of which 18 were waited for; matrix products, arithmetic and copies ran while one was open for 7% of the time, Pallas kernels for 27%

profile of v1, /device:TPU:0, one launch (start us, length us, event | category | flops | bytes accessed | tf_op | source)
XLA Modules:
  0.0 218.5 jit_solution(14027532868410320498)
XLA Ops:
  2.9 3.2 %collective-permute-start = (bf16[304,1024]{1,0:T(8,128)(2,1)}, bf16[304,1024]{1,0:T(8,128)(2,1)}, u32[]{:S(2)}, u32[]{:S(2)}) collective-permute-start(bf16[304,1024]{1,0:T(8,128)(2,1)} %pad_maximum_fusion.4), channel_id=1, source_target_pairs={{0,4},{4,8},{8,12},{12,16},{16,20},{20,24},{24,28},{1,5},{5,9},{9,... | collective-permute-start | bytes 1867784 | tf_op jit(solution)/shard_map/ppermute | solution.py:520
  8.8 5.7 %hyena_filters.3.left_ref = bf16[256,1024]{1,0:T(8,128)(2,1)S(1)} custom-call(f32[21,1024]{1,0:T(8,128)S(1)} %reshape_reshape.3.taps_ref, f32[64,256]{1,0:T(8,128)S(1)} %pad.4.base_ref, f32[1,1024]{1,0:T(1,128)S(1)} %bitcast.63, bf16[3,512,1024]{2,1,0:T(8,128)(2,1)S(1)} %bitcast.58), custom_call_target="tpu_custom_call" | custom-call | tf_op jit(solution)/shard_map/hyena_filters/pallas_call | solution.py:114
  14.6 3.5 %copy-done = bf16[1024,4096]{1,0:T(8,128)(2,1)S(1)} copy-done((bf16[1024,4096]{1,0:T(8,128)(2,1)S(1)}, bf16[1024,4096]{1,0:T(8,128)(2,1)}, u32[]{:S(2)}) %copy-start) | copy-done | bytes 8388632
  18.1 3.9 %hyena_projection.7 = (bf16[256,1024]{1,0:T(8,128)(2,1)}, bf16[256,1024]{1,0:T(8,128)(2,1)}) custom-call(s32[4]{0:T(128)S(1)} %pad_add_fusion.1.order_ref, bf16[256,1024]{1,0:T(8,128)(2,1)S(1)} %hyena_filters.3.left_ref, bf16[1024,4096]{1,0:T(8,128)(2,1)S(1)} %copy-done), custom_call_target="tpu_custom_call" | custom-call | tf_op jit(solution)/shard_map/hyena_projection/pallas_call | solution.py:155
  25.9 3.4 %copy-done.1 = bf16[1024,4096]{1,0:T(8,128)(2,1)S(1)} copy-done((bf16[1024,4096]{1,0:T(8,128)(2,1)S(1)}, bf16[1024,4096]{1,0:T(8,128)(2,1)}, u32[]{:S(2)}) %copy-start.1) | copy-done | bytes 8388632
  33.2 6.7 %hyena_filters.2.left_ref = bf16[256,1024]{1,0:T(8,128)(2,1)S(1)} custom-call(f32[21,1024]{1,0:T(8,128)S(1)} %reshape_reshape.3.taps_ref, f32[64,256]{1,0:T(8,128)S(1)} %pad.4.base_ref, f32[1,1024]{1,0:T(1,128)S(1)} %bitcast.64, bf16[304,1024]{1,0:T(8,128)(2,1)} %collective-permute-done.rest_0_, bf16[3,512,1024]{2,1,0:T(8,128)(2,1)S(1)} %bitcast.59), custom_call_target="tpu_custom_call" | custom-call | tf_op jit(solution)/shard_map/hyena_filters/pallas_call | solution.py:114
  39.9 3.4 %copy-done.2 = bf16[1024,4096]{1,0:T(8,128)(2,1)S(1)} copy-done((bf16[1024,4096]{1,0:T(8,128)(2,1)S(1)}, bf16[1024,4096]{1,0:T(8,128)(2,1)}, u32[]{:S(2)}) %copy-start.2) | copy-done | bytes 8388632
  43.3 3.0 %hyena_projection.5 = (bf16[256,1024]{1,0:T(8,128)(2,1)S(1)}, bf16[256,1024]{1,0:T(8,128)(2,1)S(1)}) custom-call(s32[4]{0:T(128)S(1)} %pad_add_fusion.1.order_ref, bf16[256,1024]{1,0:T(8,128)(2,1)S(1)} %hyena_filters.2.left_ref, bf16[1024,4096]{1,0:T(8,128)(2,1)S(1)} %copy-done.2), custom_call_target="tpu_custom_call" | custom-call | tf_op jit(solution)/shard_map/hyena_projection/pallas_call | solution.py:155
  52.6 3.4 %copy-done.3 = bf16[1024,4096]{1,0:T(8,128)(2,1)S(1)} copy-done((bf16[1024,4096]{1,0:T(8,128)(2,1)S(1)}, bf16[1024,4096]{1,0:T(8,128)(2,1)}, u32[]{:S(2)}) %copy-start.3) | copy-done | bytes 8388632
  56.0 2.9 %hyena_projection.4 = (bf16[256,512]{1,0:T(8,128)(2,1)S(1)}, bf16[256,512]{1,0:T(8,128)(2,1)S(1)}, bf16[256,1024]{1,0:T(8,128)(2,1)S(1)}) custom-call(s32[4]{0:T(128)S(1)} %pad_add_fusion.order_ref, bf16[256,1024]{1,0:T(8,128)(2,1)S(1)} %hyena_filters.2.left_ref, bf16[1024,4096]{1,0:T(8,128)(2,1)S(1)} %copy-done.3), custom_call_target="tpu_custom_call" | custom-call | tf_op jit(solution)/shard_map/hyena_projection/pallas_call | solution.py:155
  61.8 6.5 %collective-permute-done.3 = bf16[256,1024]{1,0:T(8,128)(2,1)S(1)} collective-permute-done((bf16[256,1024]{1,0:T(8,128)(2,1)S(1)}, bf16[256,1024]{1,0:T(8,128)(2,1)S(1)}, u32[]{:S(2)}, u32[]{:S(2)}) %collective-permute-start.3) | collective-permute-done | bytes 524320 | tf_op jit(solution)/shard_map/ppermute | solution.py:22
  81.4 9.7 %collective-permute-done.17.from_y = bf16[256,1024]{1,0:T(8,128)(2,1)S(1)} collective-permute-done((bf16[256,1024]{1,0:T(8,128)(2,1)S(1)}, bf16[256,1024]{1,0:T(8,128)(2,1)S(1)}, u32[]{:S(2)}, u32[]{:S(2)}) %collective-permute-start.17) | collective-permute-done | bytes 524320 | tf_op jit(solution)/shard_map/ppermute | solution.py:22
  93.4 8.9 %collective-permute-done.6.from_y = bf16[256,1024]{1,0:T(8,128)(2,1)S(1)} collective-permute-done((bf16[256,1024]{1,0:T(8,128)(2,1)S(1)}, bf16[256,1024]{1,0:T(8,128)(2,1)S(1)}, u32[]{:S(2)}, u32[]{:S(2)}) %collective-permute-start.6) | collective-permute-done | bytes 524320 | tf_op jit(solution)/shard_map/ppermute | solution.py:22
  111.3 11.5 %norm_qkv.3 = (bf16[3,256,128]{2,1,0:T(8,128)(2,1)S(1)}, bf16[3,256,128]{2,1,0:T(8,128)(2,1)S(1)}, bf16[3,256,128]{2,1,0:T(8,128)(2,1)S(1)}, bf16[3,256,128]{2,1,0:T(8,128)(2,1)S(1)}) custom-call(s32[6]{0:T(128)S(1)} %stack.144.meta_ref, bf16[256,1024]{1,0:T(8,128)(2,1)S(1)} %get-tuple-element.56.own, bf16[256,1024]{1,0:T(8,128)(2,1)S(1)} %collective-permute-done.16.from_x, ...), custom_call_target="tpu_custom_call" | custom-call | tf_op jit(solution)/shard_map/norm_qkv/pallas_call | solution.py:223
  125.3 3.1 %collective-permute-start.21 = (bf16[3,256,128]{2,1,0:T(8,128)(2,1)S(1)}, bf16[3,256,128]{2,1,0:T(8,128)(2,1)S(1)}, u32[]{:S(2)}, u32[]{:S(2)}) collective-permute-start(bf16[3,256,128]{2,1,0:T(8,128)(2,1)S(1)} %get-tuple-element.44), channel_id=1, source_target_pairs={{0,16},{4,20},{8,24},{12,28},{16,0},{20,4},{24,8},{28,12},{1,17},{... | collective-permute-start | bytes 589832 | tf_op jit(solution)/shard_map/ppermute | solution.py:32
  128.4 11.5 %norm_qkv.2 = (bf16[3,256,128]{2,1,0:T(8,128)(2,1)S(1)}, bf16[3,256,128]{2,1,0:T(8,128)(2,1)S(1)}, bf16[3,256,128]{2,1,0:T(8,128)(2,1)S(1)}, bf16[3,256,128]{2,1,0:T(8,128)(2,1)S(1)}) custom-call(s32[6]{0:T(128)S(1)} %stack.144.meta_ref, bf16[256,1024]{1,0:T(8,128)(2,1)S(1)} %get-tuple-element.57.own, bf16[256,1024]{1,0:T(8,128)(2,1)S(1)} %collective-permute-done.5.from_x, ...), custom_call_target="tpu_custom_call" | custom-call | tf_op jit(solution)/shard_map/norm_qkv/pallas_call | solution.py:223
  142.1 7.2 %collective-permute-done.22 = bf16[3,256,128]{2,1,0:T(8,128)(2,1)S(1)} collective-permute-done((bf16[3,256,128]{2,1,0:T(8,128)(2,1)S(1)}, bf16[3,256,128]{2,1,0:T(8,128)(2,1)S(1)}, u32[]{:S(2)}, u32[]{:S(2)}) %collective-permute-start.22) | collective-permute-done | bytes 196640 | tf_op jit(solution)/shard_map/ppermute | solution.py:32
  151.3 3.1 %collective-permute-start.11 = (bf16[3,256,128]{2,1,0:T(8,128)(2,1)S(1)}, bf16[3,256,128]{2,1,0:T(8,128)(2,1)S(1)}, u32[]{:S(2)}, u32[]{:S(2)}) collective-permute-start(bf16[3,256,128]{2,1,0:T(8,128)(2,1)S(1)} %get-tuple-element.36), channel_id=1, source_target_pairs={{0,24},{4,28},{8,0},{12,4},{16,8},{20,12},{24,16},{28,20},{1,25},{... | collective-permute-start | bytes 589832 | tf_op jit(solution)/shard_map/ppermute | solution.py:32
  160.0 11.6 %attention.1 = (bf16[512,128]{1,0:T(8,128)(2,1)S(1)}, bf16[512,128]{1,0:T(8,128)(2,1)S(1)}, bf16[512,128]{1,0:T(8,128)(2,1)S(1)}, bf16[512,128]{1,0:T(8,128)(2,1)S(1)}) custom-call(s32[6]{0:T(128)S(1)} %stack.144.meta_ref, bf16[4,3,256,128]{3,2,1,0:T(8,128)(2,1)S(1)} %pad_maximum_fusion.2.refs_0_, bf16[4,3,256,128]{3,2,1,0:T(8,128)(2,1)S(1)} %pad_maximum_fusion.3.refs_1_, ...), custom_call_target="tpu_custom_call" | custom-call | tf_op jit(solution)/shard_map/attention/pallas_call | solution.py:307
  178.6 7.2 %collective-permute-done.26 = bf16[512,128]{1,0:T(8,128)(2,1)S(1)} collective-permute-done((bf16[512,128]{1,0:T(8,128)(2,1)S(1)}, bf16[512,128]{1,0:T(8,128)(2,1)S(1)}, u32[]{:S(2)}, u32[]{:S(2)}) %collective-permute-start.26) | collective-permute-done | bytes 131104 | tf_op jit(solution)/shard_map/ppermute | solution.py:32
  185.9 3.6 %collective-permute-start.29 = (bf16[4,512,128]{2,1,0:T(8,128)(2,1)S(1)}, bf16[4,512,128]{2,1,0:T(8,128)(2,1)}, u32[]{:S(2)}, u32[]{:S(2)}) collective-permute-start(bf16[4,512,128]{2,1,0:T(8,128)(2,1)S(1)} %pad_maximum_fusion.7.own), channel_id=1, source_target_pairs={{0,2},{1,3},{2,0},{3,1},{4,6},{5,7},{6,4},{7,5},{8,10},{9,11},{10,... | collective-permute-start | bytes 1572872 | tf_op jit(solution)/shard_map/ppermute | solution.py:22
  189.6 12.2 %collective-permute-done.29.from_y = bf16[4,512,128]{2,1,0:T(8,128)(2,1)} collective-permute-done((bf16[4,512,128]{2,1,0:T(8,128)(2,1)S(1)}, bf16[4,512,128]{2,1,0:T(8,128)(2,1)}, u32[]{:S(2)}, u32[]{:S(2)}) %collective-permute-start.29) | collective-permute-done | bytes 524320 | tf_op jit(solution)/shard_map/ppermute | solution.py:22
  207.1 3.5 %collective-permute-done.31.diag_b = bf16[4,256,128]{2,1,0:T(8,128)(2,1)S(1)} collective-permute-done((bf16[4,256,128]{2,1,0:T(8,128)(2,1)S(1)}, bf16[4,256,128]{2,1,0:T(8,128)(2,1)S(1)}, u32[]{:S(2)}, u32[]{:S(2)}) %collective-permute-start.31) | collective-permute-done | bytes 262176 | tf_op jit(solution)/shard_map/ppermute | solution.py:22
  211.7 6.8 %attention_mix.1 = bf16[512,1024]{1,0:T(8,128)(2,1)} custom-call(s32[6]{0:T(128)S(1)} %stack.144.meta_ref, bf16[4,512,128]{2,1,0:T(8,128)(2,1)S(1)} %pad_maximum_fusion.7.own, bf16[4,512,128]{2,1,0:T(8,128)(2,1)} %collective-permute-done.28.from_x, bf16[4,512,128]{2,1,0:T(8,128)(2,1)} %collective-permute-done.29.from_y, ...), custom_call_target="tpu_custom_call" | custom-call | tf_op jit(solution)/shard_map/attention_mix/pallas_call | solution.py:351
  (129 shorter events, 72.7 us)
Async XLA Ops:
  2.9 30.3 %collective-permute-start = (bf16[304,1024]{1,0:T(8,128)(2,1)}, bf16[304,1024]{1,0:T(8,128)(2,1)}, u32[]{:S(2)}, u32[]{:S(2)}) collective-permute-start(bf16[304,1024]{1,0:T(8,128)(2,1)} %pad_maximum_fusion.4), channel_id=1, source_target_pairs={{0,4},{4,8},{8,12},{12,16},{16,20},{20,24},{24,28},{1,5},{5,9},{9,... | collective-permute-start | bytes 1867784 | tf_op jit(solution)/shard_map/ppermute | solution.py:520
  22.0 24.9 %collective-permute-start.12 = (bf16[256,1024]{1,0:T(8,128)(2,1)}, bf16[256,1024]{1,0:T(8,128)(2,1)}, u32[]{:S(2)}, u32[]{:S(2)}) collective-permute-start(bf16[256,1024]{1,0:T(8,128)(2,1)} %get-tuple-element.38), channel_id=1, source_target_pairs={{0,1},{1,0},{2,3},{3,2},{4,5},{5,4},{6,7},{7,6},{8,9},{9,8},{10,11... | collective-permute-start | bytes 1572872 | tf_op jit(solution)/shard_map/ppermute | solution.py:22
  24.4 25.6 %collective-permute-start.14 = (bf16[256,1024]{1,0:T(8,128)(2,1)}, bf16[256,1024]{1,0:T(8,128)(2,1)}, u32[]{:S(2)}, u32[]{:S(2)}) collective-permute-start(bf16[256,1024]{1,0:T(8,128)(2,1)} %get-tuple-element.40), channel_id=1, source_target_pairs={{0,2},{1,3},{2,0},{3,1},{4,6},{5,7},{6,4},{7,5},{8,10},{9,11},{10,... | collective-permute-start | bytes 1572872 | tf_op jit(solution)/shard_map/ppermute | solution.py:22
  46.3 14.8 %collective-permute-start.1 = (bf16[256,1024]{1,0:T(8,128)(2,1)S(1)}, bf16[256,1024]{1,0:T(8,128)(2,1)S(1)}, u32[]{:S(2)}, u32[]{:S(2)}) collective-permute-start(bf16[256,1024]{1,0:T(8,128)(2,1)S(1)} %get-tuple-element.29), channel_id=1, source_target_pairs={{0,1},{1,0},{2,3},{3,2},{4,5},{5,4},{6,7},{7,6},{8,9},{9,8},{10,11... | collective-permute-start | bytes 1572872 | tf_op jit(solution)/shard_map/ppermute | solution.py:22
  48.1 20.3 %collective-permute-start.3 = (bf16[256,1024]{1,0:T(8,128)(2,1)S(1)}, bf16[256,1024]{1,0:T(8,128)(2,1)S(1)}, u32[]{:S(2)}, u32[]{:S(2)}) collective-permute-start(bf16[256,1024]{1,0:T(8,128)(2,1)S(1)} %get-tuple-element.31), channel_id=1, source_target_pairs={{0,2},{1,3},{2,0},{3,1},{4,6},{5,7},{6,4},{7,5},{8,10},{9,11},{10,... | collective-permute-start | bytes 1572872 | tf_op jit(solution)/shard_map/ppermute | solution.py:22
  51.0 19.0 %collective-permute-start.15 = (bf16[256,512]{1,0:T(8,128)(2,1)S(1)}, bf16[256,512]{1,0:T(8,128)(2,1)S(1)}, u32[]{:S(2)}, u32[]{:S(2)}) collective-permute-start(bf16[256,512]{1,0:T(8,128)(2,1)S(1)} %add_convert_fusion), channel_id=1, source_target_pairs={{0,1},{1,0},{2,3},{3,2},{4,5},{5,4},{6,7},{7,6},{8,9},{9,8},{10,11... | collective-permute-start | bytes 786440 | tf_op jit(solution)/shard_map/ppermute | solution.py:22
  61.2 12.1 %collective-permute-start.2 = (bf16[256,512]{1,0:T(8,128)(2,1)S(1)}, bf16[256,512]{1,0:T(8,128)(2,1)S(1)}, u32[]{:S(2)}, u32[]{:S(2)}) collective-permute-start(bf16[256,512]{1,0:T(8,128)(2,1)S(1)} %add_convert_fusion.3), channel_id=1, source_target_pairs={{0,2},{1,3},{2,0},{3,1},{4,6},{5,7},{6,4},{7,5},{8,10},{9,11},{10,... | collective-permute-start | bytes 786440 | tf_op jit(solution)/shard_map/ppermute | solution.py:22
  76.1 14.9 %collective-permute-start.17 = (bf16[256,1024]{1,0:T(8,128)(2,1)S(1)}, bf16[256,1024]{1,0:T(8,128)(2,1)S(1)}, u32[]{:S(2)}, u32[]{:S(2)}) collective-permute-start(bf16[256,1024]{1,0:T(8,128)(2,1)S(1)} %get-tuple-element.56.own), channel_id=1, source_target_pairs={{0,2},{1,3},{2,0},{3,1},{4,6},{5,7},{6,4},{7,5},{8,10},{9,11},{10,... | collective-permute-start | bytes 1572872 | tf_op jit(solution)/shard_map/ppermute | solution.py:22
  77.1 15.4 %collective-permute-start.16 = (bf16[256,1024]{1,0:T(8,128)(2,1)S(1)}, bf16[256,1024]{1,0:T(8,128)(2,1)S(1)}, u32[]{:S(2)}, u32[]{:S(2)}) collective-permute-start(bf16[256,1024]{1,0:T(8,128)(2,1)S(1)} %get-tuple-element.56.own), channel_id=1, source_target_pairs={{0,1},{1,0},{2,3},{3,2},{4,5},{5,4},{6,7},{7,6},{8,9},{9,8},{10,11... | collective-permute-start | bytes 1572872 | tf_op jit(solution)/shard_map/ppermute | solution.py:22
  78.1 24.2 %collective-permute-start.6 = (bf16[256,1024]{1,0:T(8,128)(2,1)S(1)}, bf16[256,1024]{1,0:T(8,128)(2,1)S(1)}, u32[]{:S(2)}, u32[]{:S(2)}) collective-permute-start(bf16[256,1024]{1,0:T(8,128)(2,1)S(1)} %get-tuple-element.57.own), channel_id=1, source_target_pairs={{0,2},{1,3},{2,0},{3,1},{4,6},{5,7},{6,4},{7,5},{8,10},{9,11},{10,... | collective-permute-start | bytes 1572872 | tf_op jit(solution)/shard_map/ppermute | solution.py:22
  79.6 24.2 %collective-permute-start.5 = (bf16[256,1024]{1,0:T(8,128)(2,1)S(1)}, bf16[256,1024]{1,0:T(8,128)(2,1)S(1)}, u32[]{:S(2)}, u32[]{:S(2)}) collective-permute-start(bf16[256,1024]{1,0:T(8,128)(2,1)S(1)} %get-tuple-element.57.own), channel_id=1, source_target_pairs={{0,1},{1,0},{2,3},{3,2},{4,5},{5,4},{6,7},{7,6},{8,9},{9,8},{10,11... | collective-permute-start | bytes 1572872 | tf_op jit(solution)/shard_map/ppermute | solution.py:22
  91.1 17.8 %collective-permute-start.19 = (bf16[128,1024]{1,0:T(8,128)(2,1)S(1)}, bf16[128,1024]{1,0:T(8,128)(2,1)S(1)}, u32[]{:S(2)}, u32[]{:S(2)}) collective-permute-start(bf16[128,1024]{1,0:T(8,128)(2,1)S(1)} %slice.142), channel_id=1, source_target_pairs={{0,1},{1,0},{2,3},{3,2},{4,5},{5,4},{6,7},{7,6},{8,9},{9,8},{10,11... | collective-permute-start | bytes 786440 | tf_op jit(solution)/shard_map/ppermute | solution.py:22
  92.6 18.2 %collective-permute-start.18 = (bf16[128,1024]{1,0:T(8,128)(2,1)S(1)}, bf16[128,1024]{1,0:T(8,128)(2,1)S(1)}, u32[]{:S(2)}, u32[]{:S(2)}) collective-permute-start(bf16[128,1024]{1,0:T(8,128)(2,1)S(1)} %slice.141), channel_id=1, source_target_pairs={{0,2},{1,3},{2,0},{3,1},{4,6},{5,7},{6,4},{7,5},{8,10},{9,11},{10,... | collective-permute-start | bytes 786440 | tf_op jit(solution)/shard_map/ppermute | solution.py:22
  102.3 20.5 %collective-permute-start.8 = (bf16[128,1024]{1,0:T(8,128)(2,1)S(1)}, bf16[128,1024]{1,0:T(8,128)(2,1)S(1)}, u32[]{:S(2)}, u32[]{:S(2)}) collective-permute-start(bf16[128,1024]{1,0:T(8,128)(2,1)S(1)} %slice.132), channel_id=1, source_target_pairs={{0,1},{1,0},{2,3},{3,2},{4,5},{5,4},{6,7},{7,6},{8,9},{9,8},{10,11... | collective-permute-start | bytes 786440 | tf_op jit(solution)/shard_map/ppermute | solution.py:22
  103.8 21.5 %collective-permute-start.7 = (bf16[128,1024]{1,0:T(8,128)(2,1)S(1)}, bf16[128,1024]{1,0:T(8,128)(2,1)S(1)}, u32[]{:S(2)}, u32[]{:S(2)}) collective-permute-start(bf16[128,1024]{1,0:T(8,128)(2,1)S(1)} %slice.131), channel_id=1, source_target_pairs={{0,2},{1,3},{2,0},{3,1},{4,6},{5,7},{6,4},{7,5},{8,10},{9,11},{10,... | collective-permute-start | bytes 786440 | tf_op jit(solution)/shard_map/ppermute | solution.py:22
  106.8 51.4 %collective-permute-start.32 = (bf16[256,1024]{1,0:T(8,128)(2,1)S(1)}, bf16[256,1024]{1,0:T(8,128)(2,1)S(1)}, u32[]{:S(2)}, u32[]{:S(2)}) collective-permute-start(bf16[256,1024]{1,0:T(8,128)(2,1)S(1)} %get-tuple-element.51), channel_id=1, source_target_pairs={{0,1},{1,0},{2,3},{3,2},{4,5},{5,4},{6,7},{7,6},{8,9},{9,8},{10,11... | collective-permute-start | bytes 1572872 | tf_op jit(solution)/shard_map/ppermute | solution.py:22
  108.8 49.3 %collective-permute-start.34 = (bf16[256,1024]{1,0:T(8,128)(2,1)S(1)}, bf16[256,1024]{1,0:T(8,128)(2,1)S(1)}, u32[]{:S(2)}, u32[]{:S(2)}) collective-permute-start(bf16[256,1024]{1,0:T(8,128)(2,1)S(1)} %get-tuple-element.52), channel_id=1, source_target_pairs={{0,3},{1,2},{2,1},{3,0},{4,7},{5,6},{6,5},{7,4},{8,11},{9,10},{10,... | collective-permute-start | bytes 1572872 | tf_op jit(solution)/shard_map/ppermute | solution.py:22
  110.8 47.4 %collective-permute-start.33 = (bf16[256,1024]{1,0:T(8,128)(2,1)S(1)}, bf16[256,1024]{1,0:T(8,128)(2,1)S(1)}, u32[]{:S(2)}, u32[]{:S(2)}) collective-permute-start(bf16[256,1024]{1,0:T(8,128)(2,1)S(1)} %get-tuple-element.53), channel_id=1, source_target_pairs={{0,2},{1,3},{2,0},{3,1},{4,6},{5,7},{6,4},{7,5},{8,10},{9,11},{10,... | collective-permute-start | bytes 1572872 | tf_op jit(solution)/shard_map/ppermute | solution.py:22
  122.8 17.1 %collective-permute-start.20 = (bf16[3,256,128]{2,1,0:T(8,128)(2,1)S(1)}, bf16[3,256,128]{2,1,0:T(8,128)(2,1)S(1)}, u32[]{:S(2)}, u32[]{:S(2)}) collective-permute-start(bf16[3,256,128]{2,1,0:T(8,128)(2,1)S(1)} %get-tuple-element.43), channel_id=1, source_target_pairs={{0,8},{4,12},{8,16},{12,20},{16,24},{20,28},{24,0},{28,4},{1,9},{5... | collective-permute-start | bytes 589832 | tf_op jit(solution)/shard_map/ppermute | solution.py:32
  125.3 15.6 %collective-permute-start.21 = (bf16[3,256,128]{2,1,0:T(8,128)(2,1)S(1)}, bf16[3,256,128]{2,1,0:T(8,128)(2,1)S(1)}, u32[]{:S(2)}, u32[]{:S(2)}) collective-permute-start(bf16[3,256,128]{2,1,0:T(8,128)(2,1)S(1)} %get-tuple-element.44), channel_id=1, source_target_pairs={{0,16},{4,20},{8,24},{12,28},{16,0},{20,4},{24,8},{28,12},{1,17},{... | collective-permute-start | bytes 589832 | tf_op jit(solution)/shard_map/ppermute | solution.py:32
  158.4 48.8 %collective-permute-start.35 = (bf16[3,256,1024]{2,1,0:T(8,128)(2,1)S(1)}, bf16[3,256,1024]{2,1,0:T(8,128)(2,1)}, u32[]{:S(2)}, u32[]{:S(2)}) collective-permute-start(bf16[3,256,1024]{2,1,0:T(8,128)(2,1)S(1)} %pad_maximum_fusion.near_w), channel_id=1, source_target_pairs={{0,4},{4,0},{8,12},{12,8},{16,20},{20,16},{24,28},{28,24},{1,5},{5... | collective-permute-start | bytes 4718600 | tf_op jit(solution)/shard_map/ppermute | solution.py:27
  174.4 11.4 %collective-permute-start.26 = (bf16[512,128]{1,0:T(8,128)(2,1)S(1)}, bf16[512,128]{1,0:T(8,128)(2,1)S(1)}, u32[]{:S(2)}, u32[]{:S(2)}) collective-permute-start(bf16[512,128]{1,0:T(8,128)(2,1)S(1)} %get-tuple-element.48), channel_id=1, source_target_pairs={{0,16},{4,20},{8,24},{12,28},{16,0},{20,4},{24,8},{28,12},{1,17},{... | collective-permute-start | bytes 393224 | tf_op jit(solution)/shard_map/ppermute | solution.py:32
  185.9 15.9 %collective-permute-start.29 = (bf16[4,512,128]{2,1,0:T(8,128)(2,1)S(1)}, bf16[4,512,128]{2,1,0:T(8,128)(2,1)}, u32[]{:S(2)}, u32[]{:S(2)}) collective-permute-start(bf16[4,512,128]{2,1,0:T(8,128)(2,1)S(1)} %pad_maximum_fusion.7.own), channel_id=1, source_target_pairs={{0,2},{1,3},{2,0},{3,1},{4,6},{5,7},{6,4},{7,5},{8,10},{9,11},{10,... | collective-permute-start | bytes 1572872 | tf_op jit(solution)/shard_map/ppermute | solution.py:22
  189.5 13.8 %collective-permute-start.28 = (bf16[4,512,128]{2,1,0:T(8,128)(2,1)S(1)}, bf16[4,512,128]{2,1,0:T(8,128)(2,1)}, u32[]{:S(2)}, u32[]{:S(2)}) collective-permute-start(bf16[4,512,128]{2,1,0:T(8,128)(2,1)S(1)} %pad_maximum_fusion.7.own), channel_id=1, source_target_pairs={{0,1},{1,0},{2,3},{3,2},{4,5},{5,4},{6,7},{7,6},{8,9},{9,8},{10,11... | collective-permute-start | bytes 1572872 | tf_op jit(solution)/shard_map/ppermute | solution.py:22
  (24 other events, 149.3 us)

commit v2 on v1

--- a/solution.py
+++ b/solution.py
@@ -32,36 +32,41 @@
     return lax.ppermute(value, "ctx", [(i, (i + 2 * distance) % count) for i in range(count)])
 
 
-def conv_kernel(first_row, halo_rows, taps_ref, base_ref, skip_ref, *rest):
-    if first_row == 0:
-        halo_ref, rows_ref, out_ref, wide, product, table = rest
-    else:
-        rows_ref, out_ref, wide, product, table = rest
-    count = out_ref.shape[0]
-    length = base_ref.shape[1] // 2
-    taps = taps_ref.shape[0] // 3
-
-    if first_row == 0:
-        wide[0, halo_rows - LEAD : halo_rows] = halo_ref[2 * halo_rows : 2 * halo_rows + LEAD].astype(F32)
-        wide[1, :halo_rows] = halo_ref[:halo_rows].astype(F32)
-        wide[2, :halo_rows] = halo_ref[halo_rows : 2 * halo_rows].astype(F32)
-        for kind in range(3):
+def filter_tile(first_row, tile, short_ref, medium_ref, skip_ref, halo_ref, rows_ref, wide, product, table, store):
+    taps, groups_all = short_ref.shape[1:]
+    groups, length = medium_ref.shape
+    span = wide.shape[1]
+    halo_rows = length + LEAD
+    count = span - halo_rows
+
+    for kind in range(3):
+        if first_row == 0:
+            wide[kind, :halo_rows] = halo_ref[kind].astype(F32)
             wide[kind, halo_rows:] = rows_ref[kind].astype(F32)
-    else:
-        for kind in range(3):
+        else:
             wide[kind] = rows_ref[kind, first_row - halo_rows : first_row + count].astype(F32)
 
-    groups = base_ref.shape[0]
+    group_row = lax.broadcasted_iota(jnp.int32, (groups_all, LANES), 0)
+    group_col = lax.broadcasted_iota(jnp.int32, (groups_all, LANES), 1) // GROUP_SIZE + tile * groups
+    chosen = jnp.where(group_row == group_col, 1.0, 0.0).astype(F32)
+    weights = [
+        jnp.dot(short_ref[kind], chosen, precision=lax.Precision.HIGHEST, preferred_element_type=F32)
+        for kind in range(3)
+    ]
+
+    tap_row = lax.broadcasted_iota(jnp.int32, (length, 2 * length), 0)
+    place = lax.broadcasted_iota(jnp.int32, (length, 2 * length), 1)
+    turned = jnp.where(tap_row + place == length, 1.0, 0.0).astype(BF16)
+    base = jnp.dot(medium_ref[...].astype(BF16), turned, preferred_element_type=F32)
     for group in range(groups):
-        spread = jnp.broadcast_to(base_ref[group : group + 1, :], (length, 2 * length))
+        spread = jnp.broadcast_to(base[group : group + 1, :], (length, 2 * length))
         rolled = pltpu.roll(spread, 0, 1, stride=1, stride_axis=0)
         table[group * length : (group + 1) * length, :] = rolled.astype(BF16)
 
     def featured(kind, start):
-        total = taps_ref[kind * taps : kind * taps + 1, :] * wide[kind, start : start + length, :]
+        total = weights[kind][0:1, :] * wide[kind, start : start + length, :]
         for tap in range(1, taps):
-            weight = taps_ref[kind * taps + tap : kind * taps + tap + 1, :]
-            total = total + weight * wide[kind, start - tap : start - tap + length, :]
+            total = total + weights[kind][tap : tap + 1, :] * wide[kind, start - tap : start - tap + length, :]
         return total
 
     for block in range(count // length + 1):
@@ -88,167 +93,276 @@
             row = begin + part * length
             direct = skip_ref[...] * product[row + length : row + 2 * length, :].astype(F32)
             gate = featured(0, halo_rows + row)
-            out_ref[row : row + length, :] = (
-                gate * (mixed[:, part * LANES : (part + 1) * LANES] + direct)
-            ).astype(BF16)
-
-
-def conv_chunk(features, halo, first_row, count, taps, base, skip):
+            store(row, (gate * (mixed[:, part * LANES : (part + 1) * LANES] + direct)).astype(BF16))
+
+
+def filter_call(body, features, halo, first_row, count, short_filter, medium_rows, skip, more, scalars):
     kinds, rows, channels = features.shape
-    length = base.shape[1] // 2
-    halo_rows = length + LEAD
+    length = medium_rows.shape[1]
     groups = LANES // GROUP_SIZE
+    extra, out_specs, out_shape, scratch, limit, name = more
     specs = [
-        pl.BlockSpec((taps.shape[0], LANES), lambda i: (0, i)),
-        pl.BlockSpec((groups, 2 * length), lambda i: (i, 0)),
-        pl.BlockSpec((1, LANES), lambda i: (0, i)),
+        pl.BlockSpec(short_filter.shape, lambda i, *_: (0, 0, 0)),
+        pl.BlockSpec((groups, length), lambda i, *_: (i, 0)),
+        pl.BlockSpec((1, LANES), lambda i, *_: (0, i)),
     ]
-    operands = [taps, base, skip]
+    operands = [short_filter, medium_rows, skip]
     if first_row == 0:
-        specs.append(pl.BlockSpec((halo.shape[0], LANES), lambda i: (0, i)))
+        specs.append(pl.BlockSpec((kinds, length + LEAD, LANES), lambda i, *_: (0, 0, i)))
         operands.append(halo)
-        specs.append(pl.BlockSpec((kinds, count, LANES), lambda i: (0, 0, i)))
+        specs.append(pl.BlockSpec((kinds, count, LANES), lambda i, *_: (0, 0, i)))
     else:
-        specs.append(pl.BlockSpec((kinds, rows, LANES), lambda i: (0, 0, i)))
+        specs.append(pl.BlockSpec((kinds, rows, LANES), lambda i, *_: (0, 0, i)))
     operands.append(features)
     return pl.pallas_call(
-        functools.partial(conv_kernel, first_row, halo_rows),
-        grid=(channels // LANES,),
-        in_specs=specs,
-        out_specs=pl.BlockSpec((count, LANES), lambda i: (0, i)),
-        out_shape=jax.ShapeDtypeStruct((count, channels), BF16),
-        scratch_shapes=[
-            pltpu.VMEM((kinds, halo_rows + count, LANES), F32),
-            pltpu.VMEM((length + count, LANES), BF16),
-            pltpu.VMEM((groups * length, 2 * length), BF16),
-        ],
-        compiler_params=pltpu.CompilerParams(vmem_limit_bytes=24 * MIB),
-        name="hyena_filters",
-    )(*operands)
-
-
-def columns_kernel(steps_of, order_ref, left_ref, right_ref, *outs):
-    step = pl.program_id(0)
-    value = jnp.dot(left_ref[...], right_ref[...], preferred_element_type=F32).astype(BF16)
-    begin = 0
-    for out, steps in zip(outs, steps_of):
-
-        @pl.when((step >= begin) & (step < begin + steps))
-        def _():
-            out[...] = value
-
-        begin += steps
-
-
-def column_products(left, right, order, steps_of, width):
-    rows, depth = left.shape
-    specs, shapes, begin = [], [], 0
-    for steps in steps_of:
-        specs.append(
-            pl.BlockSpec(
-                (rows, width),
-                functools.partial(lambda b, s, i, order: (0, jnp.clip(i - b, 0, s - 1)), begin, steps),
-            )
-        )
-        shapes.append(jax.ShapeDtypeStruct((rows, steps * width), BF16))
-        begin += steps
-    return pl.pallas_call(
-        functools.partial(columns_kernel, steps_of),
+        functools.partial(body, first_row),
         grid_spec=pltpu.PrefetchScalarGridSpec(
             num_scalar_prefetch=1,
-            grid=(sum(steps_of),),
-            in_specs=[
-                pl.BlockSpec((rows, depth), lambda i, order: (0, 0)),
-                pl.BlockSpec((depth, width), lambda i, order: (0, order[i])),
-            ],
-            out_specs=specs,
+            grid=(channels // LANES,),
+            in_specs=specs + [pl.BlockSpec(memory_space=pltpu.HBM)] * len(extra),
+            out_specs=out_specs,
+            scratch_shapes=[
+                pltpu.VMEM((kinds, length + LEAD + count, LANES), F32),
+                pltpu.VMEM((length + count, LANES), BF16),
+                pltpu.VMEM((groups * length, 2 * length), BF16),
+            ]
+            + scratch,
         ),
-        out_shape=shapes,
-        compiler_params=pltpu.CompilerParams(vmem_limit_bytes=24 * MIB),
-        name="hyena_projection",
-    )(order, left, right)
-
-
-def qkv_kernel(chips, meta_ref, own, from_x, from_y, diag_a, diag_b, gain, cosine, sine, weight, *rest):
-    outs, (normed, total) = rest[:chips], rest[chips:]
-    step = pl.program_id(0)
-    steps = pl.num_programs(0)
-    depth = weight.shape[0]
-    rows, channels = own.shape
-    per_block = channels // depth
-
-    @pl.when(step == 0)
+        out_shape=out_shape,
+        compiler_params=pltpu.CompilerParams(vmem_limit_bytes=limit * MIB),
+        name=name,
+    )(scalars, *operands, *extra)
+
+
+def split_refs(first_row, refs):
+    head, rest = refs[:3], refs[3:]
+    halo_ref, rest = (rest[0], rest[1:]) if first_row == 0 else (None, rest)
+    return head, halo_ref, rest[0], rest[1:]
+
+
+def gated_kernel(first_row, scalars, *refs):
+    head, halo_ref, rows_ref, (out_ref, wide, product, table) = split_refs(first_row, refs)
+
+    def store(row, value):
+        out_ref[row : row + value.shape[0], :] = value
+
+    filter_tile(first_row, pl.program_id(0), *head, halo_ref, rows_ref, wide, product, table, store)
+
+
+def gated_chunk(features, halo, first_row, count, short_filter, medium_rows, skip, scalars):
+    channels = features.shape[2]
+    more = (
+        [],
+        pl.BlockSpec((count, LANES), lambda i, *_: (0, i)),
+        jax.ShapeDtypeStruct((count, channels), BF16),
+        [],
+        24,
+        "hyena_filters",
+    )
+    return filter_call(
+        gated_kernel, features, halo, first_row, count, short_filter, medium_rows, skip, more, scalars
+    )
+
+
+def terms_kernel(first_row, order_ref, *refs):
+    head, halo_ref, rows_ref, rest = split_refs(first_row, refs)
+    weight, to_x, to_y, along_x, along_y, kept, wide, product, table, gated, held, sems = rest
+    tile = pl.program_id(0)
+    pieces, _, width = held.shape
+
+    def fetch(piece):
+        columns = pl.ds(pl.multiple_of(order_ref[piece] * width, width), width)
+        return pltpu.make_async_copy(weight.at[:, columns], held.at[piece], sems.at[piece])
+
+    @pl.when(tile == 0)
     def _():
-        half = rows // 2
-        blocks = [own[...], from_x[...], from_y[...], None]
-        blocks[3] = jnp.concatenate([diag_a[...], diag_b[...]], axis=0)
-        square = jnp.zeros((rows, 1), F32)
-        for block in blocks:
-            wide = block.astype(F32)
-            square = square + jnp.sum(wide * wide, axis=1, keepdims=True)
-        inverse = lax.rsqrt(square / (4 * channels) + norm_eps)
-        for index, block in enumerate(blocks):
-            scaled = block.astype(F32) * inverse * gain[pl.ds(meta_ref[index], 1), :]
-            for part in range(per_block):
-                normed[index * per_block + part] = scaled[:, part * depth : (part + 1) * depth].astype(BF16)
-
-    term = jnp.dot(normed[step], weight[...], preferred_element_type=F32)
-
-    @pl.when(step == 0)
+        for piece in range(pieces):
+            fetch(piece).start()
+
+    lanes = pl.ds(pl.multiple_of(tile * LANES, LANES), LANES)
+
+    def store(row, value):
+        gated[row : row + value.shape[0], lanes] = value
+
+    filter_tile(first_row, tile, *head, halo_ref, rows_ref, wide, product, table, store)
+
+    @pl.when(tile == pl.num_programs(0) - 1)
     def _():
-        total[...] = term
-
-    @pl.when(step > 0)
-    def _():
-        total[...] += term
-
-    @pl.when(step == steps - 1)
-    def _():
-        for distance, out in enumerate(outs):
-            head = lax.rem(meta_ref[4] + distance, chips)
-            for kind in range(3):
-                column = pl.multiple_of((head * 3 + kind) * HEAD, HEAD)
-                part = total[:, pl.ds(column, HEAD)]
-                if kind < 2:
-                    part = part * cosine[...] + pltpu.roll(part, HEAD // 2, 1) * sine[...]
-                out[kind] = part.astype(BF16)
-
-
-def project(meta, own, from_x, from_y, diag_a, diag_b, gain, cosine, sine, weight, chips):
+        places = [(to_x, 0), (to_x, 1), (to_y, 0), (to_y, 1), (along_x, 0), (along_y, 0), (kept, 0), (kept, 1)]
+        for piece, (out, part) in enumerate(places):
+            fetch(piece).wait()
+            term = jnp.dot(gated[...], held[piece], preferred_element_type=F32)
+            out[:, part * width : (part + 1) * width] = term.astype(BF16)
+
+
+def terms_chunk(features, halo, first_row, count, short_filter, medium_rows, skip, order, out_weight):
+    depth, columns = out_weight.shape
+    width = columns // 8
+    widths = [2 * width, 2 * width, width, width, 2 * width]
+    more = (
+        [out_weight],
+        [pl.BlockSpec((count, w), lambda i, *_: (0, 0)) for w in widths],
+        [jax.ShapeDtypeStruct((count, w), BF16) for w in widths],
+        [
+            pltpu.VMEM((count, depth), BF16),
+            pltpu.VMEM((8, depth, width), BF16),
+            pltpu.SemaphoreType.DMA((8,)),
+        ],
+        32,
+        "hyena_terms",
+    )
+    return filter_call(
+        terms_kernel, features, halo, first_row, count, short_filter, medium_rows, skip, more, order
+    )
+
+
+def forward_kernel(along_x, along_y, from_x, from_y, out_x, out_y):
+    out_x[...] = (along_x[...].astype(F32) + from_y[...].astype(F32)).astype(BF16)
+    out_y[...] = (along_y[...].astype(F32) + from_x[...].astype(F32)).astype(BF16)
+
+
+def add_forwarded(along_x, along_y, from_x, from_y):
+    shape = along_x.shape
+    spec = pl.BlockSpec(shape, lambda i: (0, 0))
+    return pl.pallas_call(
+        forward_kernel,
+        grid=(1,),
+        in_specs=[spec] * 4,
+        out_specs=[spec] * 2,
+        out_shape=[jax.ShapeDtypeStruct(shape, BF16)] * 2,
+        name="add_forwarded",
+    )(along_x, along_y, from_x, from_y)
+
+
+def stream_kernel(kept, from_x, from_y, late_x, late_y, residual, out):
+    half = late_x.shape[1]
+    wide = lambda ref: ref[...].astype(F32)
+    left = kept[:, :half].astype(F32) + wide(from_x) + wide(late_y)
+    right = kept[:, half:].astype(F32) + wide(from_y) + wide(late_x)
+    out[:, :half] = (residual[:, :half].astype(F32) + left).astype(BF16)
+    out[:, half:] = (residual[:, half:].astype(F32) + right).astype(BF16)
+
+
+def add_stream(kept, from_x, from_y, late_x, late_y, residual, start):
+    rows, channels = kept.shape
+    half = channels // 2
+    full = pl.BlockSpec((rows, channels), lambda i: (0, 0))
+    second = pl.BlockSpec((rows, half), lambda i: (0, 1))
+    late = pl.BlockSpec((rows, half), lambda i: (0, 0))
+    return pl.pallas_call(
+        stream_kernel,
+        grid=(1,),
+        in_specs=[full, second, second, late, late, pl.BlockSpec((rows, channels), lambda i: (start // rows, 0))],
+        out_specs=full,
+        out_shape=jax.ShapeDtypeStruct((rows, channels), BF16),
+        name="add_stream",
+    )(kept, from_x, from_y, late_x, late_y, residual)
+
+
+def fetch_rows(meta_ref, weight, held, sems, first, blocks):
+    depth = held.shape[1]
+    copies = []
+    for index in range(blocks):
+        for part in range(2):
+            row = pl.multiple_of(meta_ref[first + index] * 2 * depth + part * depth, depth)
+            slot = 2 * index + part
+            copies.append(pltpu.make_async_copy(weight.at[pl.ds(row, depth), :], held.at[slot], sems.at[slot]))
+    return copies
+
+
+def near_kernel(meta_ref, own, from_x, from_y, gain, weight, total, square, held, sems):
+    depth = held.shape[1]
+    copies = fetch_rows(meta_ref, weight, held, sems, 0, 3)
+    for copy in copies:
+        copy.start()
+    squares = jnp.zeros(square.shape, F32)
+    for index, block in enumerate([own, from_x, from_y]):
+        for part in range(2):
+            wide = block[:, part * depth : (part + 1) * depth].astype(F32)
+            squares = squares + jnp.sum(wide * wide, axis=1, keepdims=True)
+            factor = gain[pl.ds(meta_ref[index], 1), part * depth : (part + 1) * depth]
+            copies[2 * index + part].wait()
+            term = jnp.dot((wide * factor).astype(BF16), held[2 * index + part], preferred_element_type=F32)
+            if index + part == 0:
+                total[...] = term
+            else:
+                total[...] += term
+    square[...] = squares
+
+
+def project_near(meta, own, from_x, from_y, gain, weight):
     rows, channels = own.shape
     width = weight.shape[1]
-    depth = 512
-    per_block = channels // depth
     full = lambda shape: pl.BlockSpec(shape, lambda i, meta: (0,) * len(shape))
     return pl.pallas_call(
-        functools.partial(qkv_kernel, chips),
+        near_kernel,
         grid_spec=pltpu.PrefetchScalarGridSpec(
             num_scalar_prefetch=1,
-            grid=(4 * per_block,),
-            in_specs=[
-                full(own.shape),
-                full(from_x.shape),
-                full(from_y.shape),
-                full(diag_a.shape),
-                full(diag_b.shape),
-                full(gain.shape),
-                full(cosine.shape),
-                full(sine.shape),
-                pl.BlockSpec(
-                    (depth, width),
-                    lambda i, meta: (meta[i // per_block] * per_block + i % per_block, 0),
-                ),
+            grid=(1,),
+            in_specs=[full(own.shape)] * 3 + [full(gain.shape), pl.BlockSpec(memory_space=pltpu.HBM)],
+            out_specs=[full((rows, width)), full((rows, LANES))],
+            scratch_shapes=[
+                pltpu.VMEM((6, channels // 2, width), BF16),
+                pltpu.SemaphoreType.DMA((6,)),
             ],
+        ),
+        out_shape=[jax.ShapeDtypeStruct((rows, width), F32), jax.ShapeDtypeStruct((rows, LANES), F32)],
+        compiler_params=pltpu.CompilerParams(vmem_limit_bytes=32 * MIB),
+        name="qkv_near",
+    )(meta, own, from_x, from_y, gain, weight)
+
+
+def far_kernel(chips, channels, meta_ref, diag_a, diag_b, near, square, gain, cosine, sine, weight, *rest):
+    outs, (total, held, sems) = rest[:chips], rest[chips:]
+    depth = held.shape[1]
+    copies = fetch_rows(meta_ref, weight, held, sems, 3, 1)
+    for copy in copies:
+        copy.start()
+    squares = square[...]
+    for part in range(2):
+        columns = slice(part * depth, (part + 1) * depth)
+        wide = jnp.concatenate([diag_a[:, columns], diag_b[:, columns]], axis=0).astype(F32)
+        squares = squares + jnp.sum(wide * wide, axis=1, keepdims=True)
+        factor = gain[pl.ds(meta_ref[3], 1), columns]
+        copies[part].wait()
+        term = jnp.dot((wide * factor).astype(BF16), held[part], preferred_element_type=F32)
+        if part == 0:
+            total[...] = near[...] + term
+        else:
+            total[...] += term
+    inverse = lax.rsqrt(squares / (4 * channels) + norm_eps)
+    for distance, out in enumerate(outs):
+        head = lax.rem(meta_ref[4] + distance, chips)
+        for kind in range(3):
+            column = pl.multiple_of((head * 3 + kind) * HEAD, HEAD)
+            part = total[:, pl.ds(column, HEAD)] * inverse
+            if kind < 2:
+                part = part * cosine[...] + pltpu.roll(part, HEAD // 2, 1) * sine[...]
+            out[kind] = part.astype(BF16)
+
+
+def project_far(meta, diag_a, diag_b, near, square, gain, cosine, sine, weight, chips):
+    rows, width = near.shape
+    channels = diag_a.shape[1]
+    full = lambda shape: pl.BlockSpec(shape, lambda i, meta: (0,) * len(shape))
+    return pl.pallas_call(
+        functools.partial(far_kernel, chips, channels),
+        grid_spec=pltpu.PrefetchScalarGridSpec(
+            num_scalar_prefetch=1,
+            grid=(1,),
+            in_specs=[full(x.shape) for x in (diag_a, diag_b, near, square, gain, cosine, sine)]
+            + [pl.BlockSpec(memory_space=pltpu.HBM)],
             out_specs=[full((3, rows, HEAD))] * chips,
             scratch_shapes=[
-                pltpu.VMEM((4 * per_block, rows, depth), BF16),
                 pltpu.VMEM((rows, width), F32),
+                pltpu.VMEM((2, channels // 2, width), BF16),
+                pltpu.SemaphoreType.DMA((2,)),
             ],
         ),
         out_shape=[jax.ShapeDtypeStruct((3, rows, HEAD), BF16)] * chips,
-        compiler_params=pltpu.CompilerParams(vmem_limit_bytes=40 * MIB),
-        name="norm_qkv",
-    )(meta, own, from_x, from_y, diag_a, diag_b, gain, cosine, sine, weight)
+        compiler_params=pltpu.CompilerParams(vmem_limit_bytes=32 * MIB),
+        name="qkv_far",
+    )(meta, diag_a, diag_b, near, square, gain, cosine, sine, weight)
 
 
 def attention_kernel(chips, chunks, meta_ref, *refs):
@@ -507,51 +621,39 @@
     chips = lax.axis_size("ctx") // 2
     length = medium_filter.shape[0]
     chunk = rows // 2
-    half = channels // 2
     ctx, ch = lax.axis_index("ctx"), lax.axis_index("ch")
     meta = jnp.stack([ch, ch ^ 1, ch ^ 2, ch ^ 3, ctx // 2, ctx % 2]).astype(jnp.int32)
 
     by_kind = jnp.transpose(features, (1, 0, 2))
-    halo_rows = length + LEAD
-    edge = jnp.concatenate(
-        [by_kind[1, rows - halo_rows :], by_kind[2, rows - halo_rows :], by_kind[0, rows - LEAD :]], axis=0
-    )
     count = lax.axis_size("ctx")
-    halo = lax.ppermute(edge, "ctx", [(i, i + 1) for i in range(count - 1)])
-
-    taps = jnp.repeat(short_filter, GROUP_SIZE, axis=2).reshape(-1, channels)
-    base = jnp.pad(medium_filter.T[:, ::-1], ((0, 0), (1, length - 1)))
+    halo = lax.ppermute(by_kind[:, rows - length - LEAD :], "ctx", [(i, i + 1) for i in range(count - 1)])
+    medium_rows = medium_filter.T
     skip = skip_gain.reshape(1, channels)
+
     starts = [rows - chunk, 0]
     if lax.axis_size("ch") != 4 or attn_weight.shape[1] != 3 * HEAD * chips:
-        gated = [conv_chunk(by_kind, halo, start, chunk, taps, base, skip) for start in starts]
+        gated = [
+            gated_chunk(by_kind, halo, start, chunk, short_filter, medium_rows, skip, meta) for start in starts
+        ]
         return after_gating(
             jnp.concatenate(gated[::-1], axis=0), residual_in, out_weight, norm_gain, attn_weight, attn_out
         )
 
     gain = norm_gain.reshape(4, channels)
     cosine, sine = rotation_tables(ctx * rows + jnp.arange(rows, dtype=jnp.int32))
-
-    first = jnp.stack([2 * (ch ^ 3), 2 * (ch ^ 1), 2 * (ch ^ 3) + 1, 2 * (ch ^ 2) + 1]).astype(jnp.int32)
-    second = jnp.stack([2 * (ch ^ 1) + 1, 2 * (ch ^ 2), 2 * ch, 2 * ch + 1]).astype(jnp.int32)
+    near_x, near_y, across = ch ^ 1, ch ^ 2, ch ^ 3
+    order = [2 * across, 2 * near_x, 2 * across + 1, 2 * near_y + 1, 2 * near_x + 1, 2 * near_y, 2 * ch, 2 * ch + 1]
+    order = jnp.stack(order).astype(jnp.int32)
 
     stream = {}
     for start in starts:
-        gated = conv_chunk(by_kind, halo, start, chunk, taps, base, skip)
-        to_x, to_y = column_products(gated, out_weight, first, (2, 2), half)
+        to_x, to_y, along_x, along_y, kept = terms_chunk(
+            by_kind, halo, start, chunk, short_filter, medium_rows, skip, order, out_weight
+        )
         from_x, from_y = swap_ch(to_x, 1), swap_ch(to_y, 2)
-        along_x, along_y, kept = column_products(gated, out_weight, second, (1, 1, 2), half)
-        along_x = (along_x.astype(F32) + from_y[:, :half].astype(F32)).astype(BF16)
-        along_y = (along_y.astype(F32) + from_x[:, :half].astype(F32)).astype(BF16)
+        along_x, along_y = add_forwarded(along_x, along_y, from_x, from_y)
         late_x, late_y = swap_ch(along_x, 1), swap_ch(along_y, 2)
-        hyena = kept.astype(F32) + jnp.concatenate(
-            [
-                from_x[:, half:].astype(F32) + late_y.astype(F32),
-                from_y[:, half:].astype(F32) + late_x.astype(F32),
-            ],
-            axis=1,
-        )
-        stream[start] = (residual_in[start : start + chunk].astype(F32) + hyena).astype(BF16)
+        stream[start] = add_stream(kept, from_x, from_y, late_x, late_y, residual_in, start)
 
     own, other = {}, {}
     for start in starts:
@@ -559,19 +661,9 @@
         near_x, near_y = swap_ch(part, 1), swap_ch(part, 2)
         diag_a = swap_ch(near_x[: chunk // 2], 2)
         diag_b = swap_ch(near_y[chunk // 2 :], 1)
-        outs = project(
-            meta,
-            part,
-            near_x,
-            near_y,
-            diag_a,
-            diag_b,
-            gain,
-            cosine[start : start + chunk],
-            sine[start : start + chunk],
-            attn_weight,
-            chips,
-        )
+        near, square = project_near(meta, part, near_x, near_y, gain, attn_weight)
+        turn = slice(start, start + chunk)
+        outs = project_far(meta, diag_a, diag_b, near, square, gain, cosine[turn], sine[turn], attn_weight, chips)
         pieces = [outs[0]] + [rotate_chips(outs[d], d) for d in range(1, chips)]
         own[start] = jnp.stack(pieces)
         other[start] = swap_core(jnp.stack([piece[1:] for piece in pieces]))

time: 220 us -> 243 us (1.10)
  waiting for transfers between devices: 69.3 us -> 83.5 us
  local copies, waits for them, and re-layouts: 25.3 us -> 39.4 us
  other arithmetic: 7.82 us -> 3.72 us
  starting transfers between devices: 49.2 us -> 45.3 us
    unnamed x24 -> x60, local copies, waits for them, and re-layouts: 14.7 us -> 29.2 us
    ppermute x9, waiting for transfers between devices: 20.2 us -> 30.7 us  [rotate_chips(): lax.ppermute(value, 'ctx', [(i, (i + 2 * distance) % count) for i in rang...]
    ppermute x9, starting transfers between devices: 17.4 us -> 13.1 us  [rotate_chips(): lax.ppermute(value, 'ctx', [(i, (i + 2 * distance) % count) for i in rang...]
    ppermute x23, waiting for transfers between devices: 48.2 us -> 51.9 us  [swap_ch(): return lax.ppermute(value, 'ch', [(i, i ^ mask) for i in range(count)])]
    convert_element_type x5 -> x0, other arithmetic: 2.74 us -> none  [the longest x2 1.09 us: shards(): along_x = (along_x.astype(F32) + from_y[:, :half].astype(F32)).astype(BF16)]
    pallas_call x8 -> x10, Pallas kernels: 48 us -> 50 us  [the longest x2 26.1 us: filter_call(): pl.pallas_call(functools.partial(body, first_row), grid_spec=pltpu.Prefet...]
  transfers between devices with their start and end apart: 36 -> 36, of which waited for: 18 -> 20; matrix products, arithmetic and copies ran while one was open for 7% -> 6% of each run, Pallas kernels for 27% -> 21%
where the time goes in v2:
time: 243 us; the launch traced here: 241 us
  waiting for transfers between devices  83.5 us (34%)
  Pallas kernels  68.6 us (28%)
  starting transfers between devices  45.3 us (19%)
  local copies, waits for them, and re-layouts  39.4 us (16%)
  other arithmetic  3.72 us (2%)
    ppermute x23, waiting for transfers between devices, swap_ch(): return lax.ppermute(value, 'ch', [(i, i ^ mask) for i in range(count)])  51.9 us
    ppermute x9, waiting for transfers between devices, rotate_chips(): lax.ppermute(value, 'ctx', [(i, (i + 2 * distance) % count) for i in rang...  30.7 us
    ppermute x23, starting transfers between devices, swap_ch(): return lax.ppermute(value, 'ch', [(i, i ^ mask) for i in range(count)])  29.4 us
    unnamed x60, local copies, waits for them, and re-layouts  29.2 us
    pallas_call x2, Pallas kernels, filter_call(): pl.pallas_call(functools.partial(body, first_row), grid_spec=pltpu.Prefet...  26.1 us
    ppermute x9, starting transfers between devices, rotate_chips(): lax.ppermute(value, 'ctx', [(i, (i + 2 * distance) % count) for i in rang...  13.1 us
    pallas_call x1, Pallas kernels, attend(): pl.pallas_call(functools.partial(attention_kernel, chips, chunks), grid_s...  11.8 us
    pallas_call x2, Pallas kernels, project_near(): pl.pallas_call(near_kernel, grid_spec=pltpu.PrefetchScalarGridSpec(num_sc...  9.67 us
  transfers between devices with their start and end apart: 36, of which 20 were waited for; matrix products, arithmetic and copies ran while one was open for 6% of the time, Pallas kernels for 21%

profile of v2, /device:TPU:0, one launch (start us, length us, event | category | flops | bytes accessed | tf_op | source)
XLA Modules:
  0.0 241.1 jit_solution(13844376799105309072)
XLA Ops:
  0.1 3.4 %copy-done.3 = bf16[1024,4096]{1,0:T(8,128)(2,1)S(1)} copy-done((bf16[1024,4096]{1,0:T(8,128)(2,1)S(1)}, bf16[1024,4096]{1,0:T(8,128)(2,1)}, u32[]{:S(2)}) %copy-start.3) | copy-done | bytes 8388632
  7.5 12.2 %hyena_terms.3 = (bf16[256,1024]{1,0:T(8,128)(2,1)S(1)}, bf16[256,1024]{1,0:T(8,128)(2,1)S(1)}, bf16[256,512]{1,0:T(8,128)(2,1)S(1)}, bf16[256,512]{1,0:T(8,128)(2,1)S(1)}, bf16[256,1024]{1,0:T(8,128)(2,1)S(1)}) custom-call(s32[8]{0:T(128)S(1)} %stack.150.order_ref, f32[3,7,64]{2,1,0:T(8,128)S(1)} %copy-done.17, f32[64,128]{1,0:T(8,128)S(1)} %bitcast.53, ...), custom_call_target="tpu_custom_call" | custom-call | tf_op jit(solution)/shard_map/hyena_terms/pallas_call | solution.py:117
  27.5 7.2 %collective-permute-done.12.from_x = bf16[256,1024]{1,0:T(8,128)(2,1)S(1)} collective-permute-done((bf16[256,1024]{1,0:T(8,128)(2,1)S(1)}, bf16[256,1024]{1,0:T(8,128)(2,1)S(1)}, u32[]{:S(2)}, u32[]{:S(2)}) %collective-permute-start.12) | collective-permute-done | bytes 524320 | tf_op jit(solution)/shard_map/ppermute | solution.py:22
  41.2 5.0 %collective-permute-done.14.late_x = bf16[256,512]{1,0:T(8,128)(2,1)S(1)} collective-permute-done((bf16[256,512]{1,0:T(8,128)(2,1)}, bf16[256,512]{1,0:T(8,128)(2,1)S(1)}, u32[]{:S(2)}, u32[]{:S(2)}) %collective-permute-start.14) | collective-permute-done | bytes 262176 | tf_op jit(solution)/shard_map/ppermute | solution.py:22
  52.2 3.4 %copy-done.4 = bf16[1024,4096]{1,0:T(8,128)(2,1)S(1)} copy-done((bf16[1024,4096]{1,0:T(8,128)(2,1)S(1)}, bf16[1024,4096]{1,0:T(8,128)(2,1)}, u32[]{:S(2)}) %copy-start.4) | copy-done | bytes 8388632
  55.6 13.8 %hyena_terms.2 = (bf16[256,1024]{1,0:T(8,128)(2,1)}, bf16[256,1024]{1,0:T(8,128)(2,1)}, bf16[256,512]{1,0:T(8,128)(2,1)S(1)}, bf16[256,512]{1,0:T(8,128)(2,1)S(1)}, bf16[256,1024]{1,0:T(8,128)(2,1)S(1)}) custom-call(s32[8]{0:T(128)S(1)} %stack.150.order_ref, f32[3,7,64]{2,1,0:T(8,128)S(1)} %copy-done.18, f32[64,128]{1,0:T(8,128)S(1)} %bitcast.54, ...), custom_call_target="tpu_custom_call" | custom-call | tf_op jit(solution)/shard_map/hyena_terms/pallas_call | solution.py:117
  80.8 4.8 %collective-permute-done.1.from_x = bf16[256,1024]{1,0:T(8,128)(2,1)S(1)} collective-permute-done((bf16[256,1024]{1,0:T(8,128)(2,1)}, bf16[256,1024]{1,0:T(8,128)(2,1)S(1)}, u32[]{:S(2)}, u32[]{:S(2)}) %collective-permute-start.1) | collective-permute-done | bytes 524320 | tf_op jit(solution)/shard_map/ppermute | solution.py:22
  92.4 4.6 %copy-done = bf16[4096,1536]{1,0:T(8,128)(2,1)S(1)} copy-done((bf16[4096,1536]{1,0:T(8,128)(2,1)S(1)}, bf16[4096,1536]{1,0:T(8,128)(2,1)}, u32[]{:S(2)}) %copy-start) | copy-done | bytes 12582936
  97.0 5.4 %qkv_near.3 = (f32[256,1536]{1,0:T(8,128)S(1)}, f32[256,128]{1,0:T(8,128)S(1)}) custom-call(s32[6]{0:T(128)S(1)} %stack.141.meta_ref, bf16[256,1024]{1,0:T(8,128)(2,1)S(1)} %copy-done.7, bf16[256,1024]{1,0:T(8,128)(2,1)} %collective-permute-done.16.from_x, bf16[256,1024]{1,0:T(8,128)(2,1)} %collective-permute-done.18.from_y, f32[4,1024]{1,0:T(4,128)S(1)} %reshape.18.gain, ...), custom_call_target="tpu_custom_call" | custom-call | tf_op jit(solution)/shard_map/qkv_near/pallas_call | solution.py:297
  105.0 3.6 %collective-permute-start.22 = (bf16[3,256,128]{2,1,0:T(8,128)(2,1)S(1)}, bf16[3,256,128]{2,1,0:T(8,128)(2,1)S(1)}, u32[]{:S(2)}, u32[]{:S(2)}) collective-permute-start(bf16[3,256,128]{2,1,0:T(8,128)(2,1)S(1)} %get-tuple-element.61), channel_id=1, source_target_pairs={{0,24},{4,28},{8,0},{12,4},{16,8},{20,12},{24,16},{28,20},{1,25},{... | collective-permute-start | bytes 589832 | tf_op jit(solution)/shard_map/ppermute | solution.py:32
  120.5 7.4 %collective-permute-done.5.from_x = bf16[256,1024]{1,0:T(8,128)(2,1)S(1)} collective-permute-done((bf16[256,1024]{1,0:T(8,128)(2,1)}, bf16[256,1024]{1,0:T(8,128)(2,1)S(1)}, u32[]{:S(2)}, u32[]{:S(2)}) %collective-permute-start.5) | collective-permute-done | bytes 524320 | tf_op jit(solution)/shard_map/ppermute | solution.py:22
  130.5 3.2 %collective-permute-done.7.from_y = bf16[256,1024]{1,0:T(8,128)(2,1)S(1)} collective-permute-done((bf16[256,1024]{1,0:T(8,128)(2,1)}, bf16[256,1024]{1,0:T(8,128)(2,1)S(1)}, u32[]{:S(2)}, u32[]{:S(2)}) %collective-permute-start.7) | collective-permute-done | bytes 524320 | tf_op jit(solution)/shard_map/ppermute | solution.py:22
  136.4 4.6 %copy-done.1 = bf16[4096,1536]{1,0:T(8,128)(2,1)S(1)} copy-done((bf16[4096,1536]{1,0:T(8,128)(2,1)S(1)}, bf16[4096,1536]{1,0:T(8,128)(2,1)}, u32[]{:S(2)}) %copy-start.1) | copy-done | bytes 12582936
  141.0 4.2 %qkv_near.2 = (f32[256,1536]{1,0:T(8,128)S(1)}, f32[256,128]{1,0:T(8,128)S(1)}) custom-call(s32[6]{0:T(128)S(1)} %stack.141.meta_ref, bf16[256,1024]{1,0:T(8,128)(2,1)S(1)} %copy-done.8, bf16[256,1024]{1,0:T(8,128)(2,1)S(1)} %collective-permute-done.5.from_x, bf16[256,1024]{1,0:T(8,128)(2,1)S(1)} %collective-permute-done.7.from_y, ...), custom_call_target="tpu_custom_call" | custom-call | tf_op jit(solution)/shard_map/qkv_near/pallas_call | solution.py:297
  147.8 4.6 %copy-done.2 = bf16[4096,1536]{1,0:T(8,128)(2,1)S(1)} copy-done((bf16[4096,1536]{1,0:T(8,128)(2,1)S(1)}, bf16[4096,1536]{1,0:T(8,128)(2,1)}, u32[]{:S(2)}) %copy-start.2) | copy-done | bytes 12582936
  154.9 3.2 %collective-permute-start.11 = (bf16[3,256,128]{2,1,0:T(8,128)(2,1)S(1)}, bf16[3,256,128]{2,1,0:T(8,128)(2,1)S(1)}, u32[]{:S(2)}, u32[]{:S(2)}) collective-permute-start(bf16[3,256,128]{2,1,0:T(8,128)(2,1)S(1)} %get-tuple-element.48), channel_id=1, source_target_pairs={{0,24},{4,28},{8,0},{12,4},{16,8},{20,12},{24,16},{28,20},{1,25},{... | collective-permute-start | bytes 589832 | tf_op jit(solution)/shard_map/ppermute | solution.py:32
  158.0 4.9 %collective-permute-done.11 = bf16[3,256,128]{2,1,0:T(8,128)(2,1)S(1)} collective-permute-done((bf16[3,256,128]{2,1,0:T(8,128)(2,1)S(1)}, bf16[3,256,128]{2,1,0:T(8,128)(2,1)S(1)}, u32[]{:S(2)}, u32[]{:S(2)}) %collective-permute-start.11) | collective-permute-done | bytes 196640 | tf_op jit(solution)/shard_map/ppermute | solution.py:32
  164.5 10.4 %collective-permute-done.10 = bf16[3,256,128]{2,1,0:T(8,128)(2,1)S(1)} collective-permute-done((bf16[3,256,128]{2,1,0:T(8,128)(2,1)S(1)}, bf16[3,256,128]{2,1,0:T(8,128)(2,1)S(1)}, u32[]{:S(2)}, u32[]{:S(2)}) %collective-permute-start.10) | collective-permute-done | bytes 196640 | tf_op jit(solution)/shard_map/ppermute | solution.py:32
  174.8 7.7 %collective-permute-done.9 = bf16[3,256,128]{2,1,0:T(8,128)(2,1)S(1)} collective-permute-done((bf16[3,256,128]{2,1,0:T(8,128)(2,1)S(1)}, bf16[3,256,128]{2,1,0:T(8,128)(2,1)S(1)}, u32[]{:S(2)}, u32[]{:S(2)}) %collective-permute-start.9) | collective-permute-done | bytes 196640 | tf_op jit(solution)/shard_map/ppermute | solution.py:32
  184.6 11.8 %attention.1 = (bf16[512,128]{1,0:T(8,128)(2,1)S(1)}, bf16[512,128]{1,0:T(8,128)(2,1)S(1)}, bf16[512,128]{1,0:T(8,128)(2,1)S(1)}, bf16[512,128]{1,0:T(8,128)(2,1)S(1)}) custom-call(s32[6]{0:T(128)S(1)} %stack.141.meta_ref, bf16[4,3,256,128]{3,2,1,0:T(8,128)(2,1)S(1)} %pad_maximum_fusion.2.refs_0_, bf16[4,3,256,128]{3,2,1,0:T(8,128)(2,1)S(1)} %pad_maximum_fusion.3.refs_1_, ...), custom_call_target="tpu_custom_call" | custom-call | tf_op jit(solution)/shard_map/attention/pallas_call | solution.py:421
  203.5 4.1 %collective-permute-done.26 = bf16[512,128]{1,0:T(8,128)(2,1)S(1)} collective-permute-done((bf16[512,128]{1,0:T(8,128)(2,1)S(1)}, bf16[512,128]{1,0:T(8,128)(2,1)S(1)}, u32[]{:S(2)}, u32[]{:S(2)}) %collective-permute-start.26) | collective-permute-done | bytes 131104 | tf_op jit(solution)/shard_map/ppermute | solution.py:32
  210.4 11.3 %collective-permute-done.28.from_x = bf16[4,512,128]{2,1,0:T(8,128)(2,1)} collective-permute-done((bf16[4,512,128]{2,1,0:T(8,128)(2,1)S(1)}, bf16[4,512,128]{2,1,0:T(8,128)(2,1)}, u32[]{:S(2)}, u32[]{:S(2)}) %collective-permute-start.28) | collective-permute-done | bytes 524320 | tf_op jit(solution)/shard_map/ppermute | solution.py:22
  227.3 4.3 %collective-permute-done.30.diag_a = bf16[4,256,128]{2,1,0:T(8,128)(2,1)S(1)} collective-permute-done((bf16[4,256,128]{2,1,0:T(8,128)(2,1)S(1)}, bf16[4,256,128]{2,1,0:T(8,128)(2,1)S(1)}, u32[]{:S(2)}, u32[]{:S(2)}) %collective-permute-start.30) | collective-permute-done | bytes 262176 | tf_op jit(solution)/shard_map/ppermute | solution.py:22
  234.4 6.8 %attention_mix.1 = bf16[512,1024]{1,0:T(8,128)(2,1)} custom-call(s32[6]{0:T(128)S(1)} %stack.141.meta_ref, bf16[4,512,128]{2,1,0:T(8,128)(2,1)S(1)} %pad_maximum_fusion.6.own, bf16[4,512,128]{2,1,0:T(8,128)(2,1)} %collective-permute-done.28.from_x, bf16[4,512,128]{2,1,0:T(8,128)(2,1)} %collective-permute-done.29.from_y, ...), custom_call_target="tpu_custom_call" | custom-call | tf_op jit(solution)/shard_map/attention_mix/pallas_call | solution.py:465
  (151 shorter events, 88.8 us)
Async XLA Ops:
  19.8 14.9 %collective-permute-start.12 = (bf16[256,1024]{1,0:T(8,128)(2,1)S(1)}, bf16[256,1024]{1,0:T(8,128)(2,1)S(1)}, u32[]{:S(2)}, u32[]{:S(2)}) collective-permute-start(bf16[256,1024]{1,0:T(8,128)(2,1)S(1)} %get-tuple-element.50), channel_id=1, source_target_pairs={{0,1},{1,0},{2,3},{3,2},{4,5},{5,4},{6,7},{7,6},{8,9},{9,8},{10,11... | collective-permute-start | bytes 1572872 | tf_op jit(solution)/shard_map/ppermute | solution.py:22
  22.8 13.4 %collective-permute-start.13 = (bf16[256,1024]{1,0:T(8,128)(2,1)S(1)}, bf16[256,1024]{1,0:T(8,128)(2,1)S(1)}, u32[]{:S(2)}, u32[]{:S(2)}) collective-permute-start(bf16[256,1024]{1,0:T(8,128)(2,1)S(1)} %get-tuple-element.51), channel_id=1, source_target_pairs={{0,2},{1,3},{2,0},{3,1},{4,6},{5,7},{6,4},{7,5},{8,10},{9,11},{10,... | collective-permute-start | bytes 1572872 | tf_op jit(solution)/shard_map/ppermute | solution.py:22
  25.3 26.9 %collective-permute-start = (bf16[3,144,1024]{2,1,0:T(8,128)(2,1)}, bf16[3,144,1024]{2,1,0:T(8,128)(2,1)}, u32[]{:S(2)}, u32[]{:S(2)}) collective-permute-start(bf16[3,144,1024]{2,1,0:T(8,128)(2,1)} %slice.76), channel_id=1, source_target_pairs={{0,4},{4,8},{8,12},{12,16},{16,20},{20,24},{24,28},{1,5},{5,9},{9,... | collective-permute-start | bytes 2654216 | tf_op jit(solution)/shard_map/ppermute | solution.py:629
  49.5 23.5 %collective-permute-start.16 = (bf16[256,1024]{1,0:T(8,128)(2,1)}, bf16[256,1024]{1,0:T(8,128)(2,1)}, u32[]{:S(2)}, u32[]{:S(2)}) collective-permute-start(bf16[256,1024]{1,0:T(8,128)(2,1)} %add_stream.3.own), channel_id=1, source_target_pairs={{0,1},{1,0},{2,3},{3,2},{4,5},{5,4},{6,7},{7,6},{8,9},{9,8},{10,11... | collective-permute-start | bytes 1572872 | tf_op jit(solution)/shard_map/ppermute | solution.py:22
  50.6 25.6 %collective-permute-start.18 = (bf16[256,1024]{1,0:T(8,128)(2,1)}, bf16[256,1024]{1,0:T(8,128)(2,1)}, u32[]{:S(2)}, u32[]{:S(2)}) collective-permute-start(bf16[256,1024]{1,0:T(8,128)(2,1)} %add_stream.3.own), channel_id=1, source_target_pairs={{0,2},{1,3},{2,0},{3,1},{4,6},{5,7},{6,4},{7,5},{8,10},{9,11},{10,... | collective-permute-start | bytes 1572872 | tf_op jit(solution)/shard_map/ppermute | solution.py:22
  71.6 14.0 %collective-permute-start.1 = (bf16[256,1024]{1,0:T(8,128)(2,1)}, bf16[256,1024]{1,0:T(8,128)(2,1)S(1)}, u32[]{:S(2)}, u32[]{:S(2)}) collective-permute-start(bf16[256,1024]{1,0:T(8,128)(2,1)} %get-tuple-element.37), channel_id=1, source_target_pairs={{0,1},{1,0},{2,3},{3,2},{4,5},{5,4},{6,7},{7,6},{8,9},{9,8},{10,11... | collective-permute-start | bytes 1572872 | tf_op jit(solution)/shard_map/ppermute | solution.py:22
  72.5 14.4 %collective-permute-start.2 = (bf16[256,1024]{1,0:T(8,128)(2,1)}, bf16[256,1024]{1,0:T(8,128)(2,1)S(1)}, u32[]{:S(2)}, u32[]{:S(2)}) collective-permute-start(bf16[256,1024]{1,0:T(8,128)(2,1)} %get-tuple-element.38), channel_id=1, source_target_pairs={{0,2},{1,3},{2,0},{3,1},{4,6},{5,7},{6,4},{7,5},{8,10},{9,11},{10,... | collective-permute-start | bytes 1572872 | tf_op jit(solution)/shard_map/ppermute | solution.py:22
  74.7 27.7 %collective-permute-start.17 = (bf16[128,1024]{1,0:T(8,128)(2,1)}, bf16[128,1024]{1,0:T(8,128)(2,1)S(1)}, u32[]{:S(2)}, u32[]{:S(2)}) collective-permute-start(bf16[128,1024]{1,0:T(8,128)(2,1)} %slice.83), channel_id=1, source_target_pairs={{0,2},{1,3},{2,0},{3,1},{4,6},{5,7},{6,4},{7,5},{8,10},{9,11},{10,... | collective-permute-start | bytes 786440 | tf_op jit(solution)/shard_map/ppermute | solution.py:22
  77.9 24.6 %collective-permute-start.19 = (bf16[128,1024]{1,0:T(8,128)(2,1)}, bf16[128,1024]{1,0:T(8,128)(2,1)S(1)}, u32[]{:S(2)}, u32[]{:S(2)}) collective-permute-start(bf16[128,1024]{1,0:T(8,128)(2,1)} %slice.84), channel_id=1, source_target_pairs={{0,1},{1,0},{2,3},{3,2},{4,5},{5,4},{6,7},{7,6},{8,9},{9,8},{10,11... | collective-permute-start | bytes 786440 | tf_op jit(solution)/shard_map/ppermute | solution.py:22
  89.8 19.8 %collective-permute-start.3 = (bf16[256,512]{1,0:T(8,128)(2,1)}, bf16[256,512]{1,0:T(8,128)(2,1)S(1)}, u32[]{:S(2)}, u32[]{:S(2)}) collective-permute-start(bf16[256,512]{1,0:T(8,128)(2,1)} %get-tuple-element.41), channel_id=1, source_target_pairs={{0,1},{1,0},{2,3},{3,2},{4,5},{5,4},{6,7},{7,6},{8,9},{9,8},{10,11... | collective-permute-start | bytes 786440 | tf_op jit(solution)/shard_map/ppermute | solution.py:22
  90.2 19.4 %collective-permute-start.4 = (bf16[256,512]{1,0:T(8,128)(2,1)}, bf16[256,512]{1,0:T(8,128)(2,1)}, u32[]{:S(2)}, u32[]{:S(2)}) collective-permute-start(bf16[256,512]{1,0:T(8,128)(2,1)} %get-tuple-element.42), channel_id=1, source_target_pairs={{0,2},{1,3},{2,0},{3,1},{4,6},{5,7},{6,4},{7,5},{8,10},{9,11},{10,... | collective-permute-start | bytes 786440 | tf_op jit(solution)/shard_map/ppermute | solution.py:22
  105.0 13.4 %collective-permute-start.22 = (bf16[3,256,128]{2,1,0:T(8,128)(2,1)S(1)}, bf16[3,256,128]{2,1,0:T(8,128)(2,1)S(1)}, u32[]{:S(2)}, u32[]{:S(2)}) collective-permute-start(bf16[3,256,128]{2,1,0:T(8,128)(2,1)S(1)} %get-tuple-element.61), channel_id=1, source_target_pairs={{0,24},{4,28},{8,0},{12,4},{16,8},{20,12},{24,16},{28,20},{1,25},{... | collective-permute-start | bytes 589832 | tf_op jit(solution)/shard_map/ppermute | solution.py:32
  108.5 26.8 %collective-permute-start.20 = (bf16[3,256,128]{2,1,0:T(8,128)(2,1)S(1)}, bf16[3,256,128]{2,1,0:T(8,128)(2,1)S(1)}, u32[]{:S(2)}, u32[]{:S(2)}) collective-permute-start(bf16[3,256,128]{2,1,0:T(8,128)(2,1)S(1)} %get-tuple-element.59), channel_id=1, source_target_pairs={{0,8},{4,12},{8,16},{12,20},{16,24},{20,28},{24,0},{28,4},{1,9},{5... | collective-permute-start | bytes 589832 | tf_op jit(solution)/shard_map/ppermute | solution.py:32
  112.9 15.1 %collective-permute-start.5 = (bf16[256,1024]{1,0:T(8,128)(2,1)}, bf16[256,1024]{1,0:T(8,128)(2,1)S(1)}, u32[]{:S(2)}, u32[]{:S(2)}) collective-permute-start(bf16[256,1024]{1,0:T(8,128)(2,1)} %add_stream.2.own), channel_id=1, source_target_pairs={{0,1},{1,0},{2,3},{3,2},{4,5},{5,4},{6,7},{7,6},{8,9},{9,8},{10,11... | collective-permute-start | bytes 1572872 | tf_op jit(solution)/shard_map/ppermute | solution.py:22
  114.5 19.3 %collective-permute-start.7 = (bf16[256,1024]{1,0:T(8,128)(2,1)}, bf16[256,1024]{1,0:T(8,128)(2,1)S(1)}, u32[]{:S(2)}, u32[]{:S(2)}) collective-permute-start(bf16[256,1024]{1,0:T(8,128)(2,1)} %add_stream.2.own), channel_id=1, source_target_pairs={{0,2},{1,3},{2,0},{3,1},{4,6},{5,7},{6,4},{7,5},{8,10},{9,11},{10,... | collective-permute-start | bytes 1572872 | tf_op jit(solution)/shard_map/ppermute | solution.py:22
  118.4 64.3 %collective-permute-start.32 = (bf16[256,1024]{1,0:T(8,128)(2,1)S(1)}, bf16[256,1024]{1,0:T(8,128)(2,1)S(1)}, u32[]{:S(2)}, u32[]{:S(2)}) collective-permute-start(bf16[256,1024]{1,0:T(8,128)(2,1)S(1)} %get-tuple-element.67), channel_id=1, source_target_pairs={{0,1},{1,0},{2,3},{3,2},{4,5},{5,4},{6,7},{7,6},{8,9},{9,8},{10,11... | collective-permute-start | bytes 1572872 | tf_op jit(solution)/shard_map/ppermute | solution.py:22
  119.0 63.7 %collective-permute-start.33 = (bf16[256,1024]{1,0:T(8,128)(2,1)S(1)}, bf16[256,1024]{1,0:T(8,128)(2,1)S(1)}, u32[]{:S(2)}, u32[]{:S(2)}) collective-permute-start(bf16[256,1024]{1,0:T(8,128)(2,1)S(1)} %get-tuple-element.69), channel_id=1, source_target_pairs={{0,2},{1,3},{2,0},{3,1},{4,6},{5,7},{6,4},{7,5},{8,10},{9,11},{10,... | collective-permute-start | bytes 1572872 | tf_op jit(solution)/shard_map/ppermute | solution.py:22
  128.0 54.7 %collective-permute-start.34 = (bf16[256,1024]{1,0:T(8,128)(2,1)S(1)}, bf16[256,1024]{1,0:T(8,128)(2,1)S(1)}, u32[]{:S(2)}, u32[]{:S(2)}) collective-permute-start(bf16[256,1024]{1,0:T(8,128)(2,1)S(1)} %get-tuple-element.68), channel_id=1, source_target_pairs={{0,3},{1,2},{2,1},{3,0},{4,7},{5,6},{6,5},{7,4},{8,11},{9,10},{10,... | collective-permute-start | bytes 1572872 | tf_op jit(solution)/shard_map/ppermute | solution.py:22
  133.7 14.0 %collective-permute-start.6 = (bf16[128,1024]{1,0:T(8,128)(2,1)S(1)}, bf16[128,1024]{1,0:T(8,128)(2,1)S(1)}, u32[]{:S(2)}, u32[]{:S(2)}) collective-permute-start(bf16[128,1024]{1,0:T(8,128)(2,1)S(1)} %slice.77), channel_id=1, source_target_pairs={{0,2},{1,3},{2,0},{3,1},{4,6},{5,7},{6,4},{7,5},{8,10},{9,11},{10,... | collective-permute-start | bytes 786440 | tf_op jit(solution)/shard_map/ppermute | solution.py:22
  135.3 12.5 %collective-permute-start.8 = (bf16[128,1024]{1,0:T(8,128)(2,1)S(1)}, bf16[128,1024]{1,0:T(8,128)(2,1)S(1)}, u32[]{:S(2)}, u32[]{:S(2)}) collective-permute-start(bf16[128,1024]{1,0:T(8,128)(2,1)S(1)} %slice.78), channel_id=1, source_target_pairs={{0,1},{1,0},{2,3},{3,2},{4,5},{5,4},{6,7},{7,6},{8,9},{9,8},{10,11... | collective-permute-start | bytes 786440 | tf_op jit(solution)/shard_map/ppermute | solution.py:22
  147.8 35.9 %collective-permute-start.24 = (bf16[4,2,256,128]{3,2,1,0:T(8,128)(2,1)S(1)}, bf16[4,2,256,128]{3,2,1,0:T(8,128)(2,1)S(1)}, u32[]{:S(2)}, u32[]{:S(2)}) collective-permute-start(bf16[4,2,256,128]{3,2,1,0:T(8,128)(2,1)S(1)} %pad_maximum_fusion.5), channel_id=1, source_target_pairs={{0,4},{4,0},{8,12},{12,8},{16,20},{20,16},{24,28},{28,24},{1,5},{5... | collective-permute-start | bytes 1572872 | tf_op jit(solution)/shard_map/ppermute | solution.py:27
  182.9 44.4 %collective-permute-start.35 = (bf16[3,256,1024]{2,1,0:T(8,128)(2,1)S(1)}, bf16[3,256,1024]{2,1,0:T(8,128)(2,1)}, u32[]{:S(2)}, u32[]{:S(2)}) collective-permute-start(bf16[3,256,1024]{2,1,0:T(8,128)(2,1)S(1)} %pad_maximum_fusion.near_w), channel_id=1, source_target_pairs={{0,4},{4,0},{8,12},{12,8},{16,20},{20,16},{24,28},{28,24},{1,5},{5... | collective-permute-start | bytes 4718600 | tf_op jit(solution)/shard_map/ppermute | solution.py:27
  208.0 13.6 %collective-permute-start.28 = (bf16[4,512,128]{2,1,0:T(8,128)(2,1)S(1)}, bf16[4,512,128]{2,1,0:T(8,128)(2,1)}, u32[]{:S(2)}, u32[]{:S(2)}) collective-permute-start(bf16[4,512,128]{2,1,0:T(8,128)(2,1)S(1)} %pad_maximum_fusion.6.own), channel_id=1, source_target_pairs={{0,1},{1,0},{2,3},{3,2},{4,5},{5,4},{6,7},{7,6},{8,9},{9,8},{10,11... | collective-permute-start | bytes 1572872 | tf_op jit(solution)/shard_map/ppermute | solution.py:22
  208.8 15.4 %collective-permute-start.29 = (bf16[4,512,128]{2,1,0:T(8,128)(2,1)S(1)}, bf16[4,512,128]{2,1,0:T(8,128)(2,1)}, u32[]{:S(2)}, u32[]{:S(2)}) collective-permute-start(bf16[4,512,128]{2,1,0:T(8,128)(2,1)S(1)} %pad_maximum_fusion.6.own), channel_id=1, source_target_pairs={{0,2},{1,3},{2,0},{3,1},{4,6},{5,7},{6,4},{7,5},{8,10},{9,11},{10,... | collective-permute-start | bytes 1572872 | tf_op jit(solution)/shard_map/ppermute | solution.py:22
  (42 other events, 277.8 us)

commit v3 on v0

--- a/solution.py
+++ b/solution.py
@@ -1,19 +1,358 @@
+import functools
+
 import jax
 import jax.numpy as jnp
 from jax import lax
+from jax.experimental import pallas as pl
+from jax.experimental.pallas import tpu as pltpu
 from jax.sharding import PartitionSpec as P
 
 HEAD = 128
 GROUP_SIZE = 16
-
-
+LANES = 128
+LEAD = 16
 norm_eps = 1e-05
-
-
-def shifted(value, axis, steps):
-    count = lax.axis_size(axis)
-    initial, last = (max(0, -steps), min(count, count - steps))
-    return lax.ppermute(value, axis, [(source, source + steps) for source in range(initial, last)])
+SCORE_SCALE = 1.4426950408889634 / HEAD**0.5
+MIB = 1024 * 1024
+F32 = jnp.float32
+BF16 = jnp.bfloat16
+
+
+def swap_ch(value, mask):
+    count = lax.axis_size("ch")
+    return lax.ppermute(value, "ch", [(i, i ^ mask) for i in range(count)])
+
+
+def swap_core(value):
+    count = lax.axis_size("ctx")
+    return lax.ppermute(value, "ctx", [(i, i ^ 1) for i in range(count)])
+
+
+def rotate_chips(value, distance):
+    count = lax.axis_size("ctx")
+    return lax.ppermute(value, "ctx", [(i, (i + 2 * distance) % count) for i in range(count)])
+
+
+def filter_tile(first_row, tile, short_ref, medium_ref, skip_ref, halo_ref, rows_ref, wide, product, table, store):
+    taps, groups_all = short_ref.shape[1:]
+    groups, length = medium_ref.shape
+    span = wide.shape[1]
+    halo_rows = length + LEAD
+    count = span - halo_rows
+
+    for kind in range(3):
+        if first_row == 0:
+            wide[kind, :halo_rows] = halo_ref[kind].astype(F32)
+            wide[kind, halo_rows:] = rows_ref[kind].astype(F32)
+        else:
+            wide[kind] = rows_ref[kind, first_row - halo_rows : first_row + count].astype(F32)
+
+    group_row = lax.broadcasted_iota(jnp.int32, (groups_all, LANES), 0)
+    group_col = lax.broadcasted_iota(jnp.int32, (groups_all, LANES), 1) // GROUP_SIZE + tile * groups
+    chosen = jnp.where(group_row == group_col, 1.0, 0.0).astype(F32)
+    weights = [
+        jnp.dot(short_ref[kind], chosen, precision=lax.Precision.HIGHEST, preferred_element_type=F32)
+        for kind in range(3)
+    ]
+
+    tap_row = lax.broadcasted_iota(jnp.int32, (length, 2 * length), 0)
+    place = lax.broadcasted_iota(jnp.int32, (length, 2 * length), 1)
+    turned = jnp.where(tap_row + place == length, 1.0, 0.0).astype(BF16)
+    base = jnp.dot(medium_ref[...].astype(BF16), turned, preferred_element_type=F32)
+    for group in range(groups):
+        spread = jnp.broadcast_to(base[group : group + 1, :], (length, 2 * length))
+        rolled = pltpu.roll(spread, 0, 1, stride=1, stride_axis=0)
+        table[group * length : (group + 1) * length, :] = rolled.astype(BF16)
+
+    def featured(kind, start):
+        total = weights[kind][0:1, :] * wide[kind, start : start + length, :]
+        for tap in range(1, taps):
+            total = total + weights[kind][tap : tap + 1, :] * wide[kind, start - tap : start - tap + length, :]
+        return total
+
+    for block in range(count // length + 1):
+        start = LEAD + block * length
+        product[block * length : (block + 1) * length, :] = (
+            featured(1, start) * featured(2, start)
+        ).astype(BF16)
+
+    group_of = lax.broadcasted_iota(jnp.int32, (length, 2 * LANES), 1) % LANES // GROUP_SIZE
+    for pair in range(count // (2 * length)):
+        begin = pair * 2 * length
+        window = jnp.concatenate(
+            [
+                product[begin : begin + 2 * length, :],
+                product[begin + length : begin + 3 * length, :],
+            ],
+            axis=1,
+        )
+        spread = jnp.dot(table[...], window, preferred_element_type=F32)
+        mixed = spread[:length]
+        for group in range(1, groups):
+            mixed = jnp.where(group_of == group, spread[group * length : (group + 1) * length], mixed)
+        for part in range(2):
+            row = begin + part * length
+            direct = skip_ref[...] * product[row + length : row + 2 * length, :].astype(F32)
+            gate = featured(0, halo_rows + row)
+            store(row, (gate * (mixed[:, part * LANES : (part + 1) * LANES] + direct)).astype(BF16))
+
+
+def gated_kernel(first_row, loads, *refs):
+    head, rest = refs[:3], refs[3:]
+    halo_ref, rest = (rest[0], rest[1:]) if first_row == 0 else (None, rest)
+    rows_ref, rest = rest[0], rest[1:]
+    if loads:
+        weight, out_ref, held, wide, product, table, sem = rest
+        copy = pltpu.make_async_copy(weight, held, sem)
+        pl.when(pl.program_id(0) == 0)(copy.start)
+    else:
+        out_ref, wide, product, table = rest
+
+    def store(row, value):
+        out_ref[row : row + value.shape[0], :] = value
+
+    filter_tile(first_row, pl.program_id(0), *head, halo_ref, rows_ref, wide, product, table, store)
+    if loads:
+        pl.when(pl.program_id(0) == pl.num_programs(0) - 1)(copy.wait)
+
+
+def gated_chunk(features, halo, first_row, count, short_filter, medium_rows, skip, weight=None):
+    kinds, rows, channels = features.shape
+    length = medium_rows.shape[1]
+    groups = LANES // GROUP_SIZE
+    loads = weight is not None
+    in_specs = [
+        pl.BlockSpec(short_filter.shape, lambda i: (0, 0, 0)),
+        pl.BlockSpec((groups, length), lambda i: (i, 0)),
+        pl.BlockSpec((1, LANES), lambda i: (0, i)),
+    ]
+    operands = [short_filter, medium_rows, skip]
+    if first_row == 0:
+        in_specs.append(pl.BlockSpec((kinds, length + LEAD, LANES), lambda i: (0, 0, i)))
+        operands.append(halo)
+        in_specs.append(pl.BlockSpec((kinds, count, LANES), lambda i: (0, 0, i)))
+    else:
+        in_specs.append(pl.BlockSpec((kinds, rows, LANES), lambda i: (0, 0, i)))
+    operands.append(features)
+    out_specs = [pl.BlockSpec((count, LANES), lambda i: (0, i))]
+    out_shape = [jax.ShapeDtypeStruct((count, channels), BF16)]
+    scratch = [
+        pltpu.VMEM((kinds, length + LEAD + count, LANES), F32),
+        pltpu.VMEM((length + count, LANES), BF16),
+        pltpu.VMEM((groups * length, 2 * length), BF16),
+    ]
+    if loads:
+        in_specs.append(pl.BlockSpec(memory_space=pltpu.HBM))
+        operands.append(pltpu.with_memory_space_constraint(weight, pltpu.HBM))
+        out_specs.append(pl.BlockSpec(memory_space=pltpu.VMEM))
+        out_shape.append(pltpu.VMEM(weight.shape, weight.dtype))
+        scratch.append(pltpu.SemaphoreType.DMA)
+    outs = pl.pallas_call(
+        functools.partial(gated_kernel, first_row, loads),
+        grid=(channels // LANES,),
+        in_specs=in_specs,
+        out_specs=out_specs,
+        out_shape=out_shape,
+        scratch_shapes=scratch,
+        compiler_params=pltpu.CompilerParams(vmem_limit_bytes=16 * MIB),
+        name="hyena_filters",
+    )(*operands)
+    return outs if loads else outs[0]
+
+
+def vmem_call(body, name, scalars, operands, outs, scratch=()):
+    return pl.pallas_call(
+        body,
+        in_specs=[pl.BlockSpec(memory_space=pltpu.SMEM)] + [pl.BlockSpec(memory_space=pltpu.VMEM)] * len(operands),
+        out_specs=[pl.BlockSpec(memory_space=pltpu.VMEM)] * len(outs),
+        out_shape=[jax.ShapeDtypeStruct(shape, kind) for shape, kind in outs],
+        scratch_shapes=list(scratch),
+        compiler_params=pltpu.CompilerParams(vmem_limit_bytes=20 * MIB),
+        name=name,
+    )(scalars, *operands)
+
+
+def columns_kernel(first, places, order_ref, upper, lower, weight, *outs):
+    gated = jnp.concatenate([upper[...], lower[...]], axis=0)
+    width = weight.shape[1] // 8
+    for piece, (out, part) in enumerate(places):
+        columns = pl.ds(pl.multiple_of(order_ref[first + piece] * width, width), width)
+        term = jnp.dot(gated, weight[:, columns], preferred_element_type=F32)
+        outs[out][:, part * width : (part + 1) * width] = term.astype(BF16)
+
+
+def column_terms(order, upper, lower, weight, first, places):
+    rows, width = 2 * upper.shape[0], weight.shape[1] // 8
+    outs = [((rows, width * sum(p[0] == out for p in places)), BF16) for out in range(places[-1][0] + 1)]
+    body = functools.partial(columns_kernel, first, places)
+    return vmem_call(body, "hyena_terms", order, [upper, lower, weight], outs)
+
+
+def stream_kernel(_, kept, direct_x, direct_y, late_x, late_y, residual, *parts):
+    half = late_x.shape[1]
+    rows = parts[0].shape[0]
+    for index, out in enumerate(parts):
+        span = slice(index * rows, (index + 1) * rows)
+        wide = lambda ref: ref[span].astype(F32)
+        left = wide(residual)[:, :half] + (wide(kept)[:, :half] + wide(direct_x) + wide(late_y))
+        right = wide(residual)[:, half:] + (wide(kept)[:, half:] + wide(direct_y) + wide(late_x))
+        out[...] = jnp.concatenate([left, right], axis=1).astype(BF16)
+
+
+def near_kernel(meta_ref, *refs):
+    halves, (gain, weight, total, square) = refs[:6], refs[6:]
+    channels = halves[0].shape[1]
+    squares = jnp.zeros(square.shape, F32)
+    result = None
+    for index in range(3):
+        wide = jnp.concatenate([half[...] for half in halves[2 * index : 2 * index + 2]], axis=0).astype(F32)
+        squares = squares + jnp.sum(wide * wide, axis=1, keepdims=True)
+        factor = gain[pl.ds(meta_ref[index], 1), :]
+        block = weight[pl.ds(pl.multiple_of(meta_ref[index] * channels, channels), channels), :]
+        term = jnp.dot((wide * factor).astype(BF16), block, preferred_element_type=F32)
+        result = term if result is None else result + term
+    total[...] = result
+    square[...] = squares
+
+
+def far_kernel(chips, meta_ref, diag_a, diag_b, near, square, gain, cosine, sine, weight, *rest):
+    outs, total = rest[:chips], rest[chips]
+    channels = diag_a.shape[1]
+    wide = jnp.concatenate([diag_a[...], diag_b[...]], axis=0).astype(F32)
+    squares = square[...] + jnp.sum(wide * wide, axis=1, keepdims=True)
+    factor = gain[pl.ds(meta_ref[3], 1), :]
+    block = weight[pl.ds(pl.multiple_of(meta_ref[3] * channels, channels), channels), :]
+    total[...] = near[...] + jnp.dot((wide * factor).astype(BF16), block, preferred_element_type=F32)
+    inverse = lax.rsqrt(squares / (4 * channels) + norm_eps)
+    for distance, out in enumerate(outs):
+        head = lax.rem(meta_ref[4] + distance, chips)
+        for kind in range(3):
+            column = pl.multiple_of((head * 3 + kind) * HEAD, HEAD)
+            part = total[:, pl.ds(column, HEAD)] * inverse
+            if kind < 2:
+                part = part * cosine[...] + pltpu.roll(part, HEAD // 2, 1) * sine[...]
+            if kind == 0:
+                part = part * SCORE_SCALE
+            if kind == 2:
+                tiles = [part[row : row + HEAD].T for row in range(0, part.shape[0], HEAD)]
+                part = jnp.concatenate(tiles, axis=0)
+            out[kind] = part.astype(BF16)
+
+
+def gather_keys(chips, chunks, meta_ref, refs, keys, values):
+    pieces = chunks * chips
+    rows = refs[0].shape[1]
+    for side in range(2):
+        for distance in range(chips):
+            place = lax.rem(meta_ref[4] - distance + chips, chips)
+            for chunk in range(chunks):
+                piece = refs[side * pieces + chunk * chips + distance]
+                keys[side, place, chunk * rows : (chunk + 1) * rows, :] = piece[1]
+                for tile in range(rows // HEAD):
+                    first = chunk * rows + tile * HEAD
+                    values[side, place, :, first : first + HEAD] = piece[2, tile * HEAD : (tile + 1) * HEAD, :]
+
+
+def attention_kernel(chips, chunks, distances, leading, meta_ref, *refs):
+    if leading:
+        pieces, rest = refs[: 2 * chunks * chips], refs[2 * chunks * chips :]
+        outs, (keys, values) = rest[: len(distances)], rest[len(distances) :]
+        gather_keys(chips, chunks, meta_ref, pieces, keys, values)
+        backs = [(chips - distance) % chips for distance in distances]
+        sources = [[pieces[chunk * chips + back] for chunk in range(chunks)] for back in backs]
+    else:
+        taken = chunks * len(distances)
+        pieces, (keys, values), outs = refs[:taken], refs[taken : taken + 2], refs[taken + 2 :]
+        sources = [pieces[index * chunks : (index + 1) * chunks] for index in range(len(distances))]
+    chip, core = meta_ref[4], meta_ref[5]
+    count = keys.shape[2]
+
+    def scores_of(side, place, queries):
+        return lax.dot_general(
+            keys[side, place], queries, (((1,), (1,)), ((), ())), preferred_element_type=F32
+        )
+
+    def update(state, mine, others, place):
+        top, total, acc = state
+        new_top = jnp.maximum(jnp.max(mine, axis=0, keepdims=True), jnp.max(others, axis=0, keepdims=True))
+        if top is not None:
+            new_top = jnp.maximum(new_top, top)
+        mine = jnp.exp2(mine - new_top)
+        others = jnp.exp2(others - new_top)
+        gained = jnp.sum(mine, axis=0, keepdims=True) + jnp.sum(others, axis=0, keepdims=True)
+        added = jnp.dot(values[0, place], mine.astype(BF16), preferred_element_type=F32)
+        added = added + jnp.dot(values[1, place], others.astype(BF16), preferred_element_type=F32)
+        if top is None:
+            return new_top, gained, added
+        shrink = jnp.exp2(top - new_top)
+        return new_top, total * shrink + gained, acc * shrink + added
+
+    key_row = lax.broadcasted_iota(jnp.int32, (count, count), 0)
+    query_column = lax.broadcasted_iota(jnp.int32, (count, count), 1)
+    for distance, source, out in zip(distances, sources, outs):
+        place = lax.rem(chip + distance, chips)
+        queries = jnp.concatenate([piece[0] for piece in source], axis=0)
+        mine = jnp.where(key_row <= query_column, scores_of(0, place, queries), -1e30)
+        others = jnp.where(core == 1, scores_of(1, place, queries), -1e30)
+        state = update((None, None, None), mine, others, place)
+
+        def earlier(index, state):
+            return update(state, scores_of(0, index, queries), scores_of(1, index, queries), index)
+
+        state = lax.fori_loop(0, place, earlier, state)
+        out[...] = (state[2] / state[1]).T.astype(BF16)
+
+
+def attend(meta, own, other, groups, chips, chunks):
+    count = own[0].shape[1] * chunks
+    laid = [((2, chips, count, HEAD), BF16), ((2, chips, HEAD, count), BF16)]
+    given = [((count, HEAD), BF16)]
+    first, second = groups
+    body = functools.partial(attention_kernel, chips, chunks, first, True)
+    *early, keys, values = vmem_call(body, "attention", meta, own + other, given * len(first) + laid)
+    pieces = [own[chunk * chips + (chips - distance) % chips] for distance in second for chunk in range(chunks)]
+    body = functools.partial(attention_kernel, chips, chunks, second, False)
+    late = vmem_call(body, "attention", meta, pieces + [keys, values], given * len(second))
+    return early, late
+
+
+def mix_kernel(chips, distances, streams, meta_ref, *refs):
+    heads, refs = refs[:4], refs[4:]
+    before, (own_w, *others_w), (out, ordered) = refs[:streams], refs[streams:-2], refs[-2:]
+    near_w, far_w = others_w[:3], others_w[3:]
+    chip, core = meta_ref[4], meta_ref[5]
+    parity = lax.rem(chip + distances[0], 2)
+    for index, distance in enumerate(distances):
+        head = lax.rem(chip - distance + chips, chips)
+        column = pl.ds(pl.multiple_of(head // 2 * HEAD, HEAD), HEAD)
+        for source in range(4):
+            ordered[source, :, column] = heads[source][index]
+    mine = jnp.concatenate(
+        [own_w[pl.ds(pl.multiple_of((2 * j + parity) * HEAD, HEAD), HEAD), :] for j in range(chips // 2)], axis=0
+    )
+
+    def finish(weights):
+        total = jnp.dot(ordered[0], mine, preferred_element_type=F32)
+        for source in range(3):
+            total = total + jnp.dot(ordered[source + 1], weights[source][...], preferred_element_type=F32)
+        total = total + jnp.concatenate([part[...].astype(F32) for part in before], axis=0)
+        out[...] = total.astype(out.dtype)
+
+    @pl.when(core == parity)
+    def _():
+        finish(near_w)
+
+    @pl.when(core != parity)
+    def _():
+        finish(far_w)
+
+
+def mix(meta, heads, distances, before, own_w, near_w, far_w, kind, chips):
+    rows, channels = heads[0].shape[1], own_w.shape[1]
+    body = functools.partial(mix_kernel, chips, distances, len(before))
+    operands = [*heads, *before, own_w, *near_w, *far_w]
+    scratch = [pltpu.VMEM((4, rows, chips // 2 * HEAD), BF16)]
+    return vmem_call(body, "attention_mix", meta, operands, [((rows, channels), kind)], scratch)[0]
 
 
 def rotate_rows(block, positions):
@@ -31,38 +370,6 @@
         ],
         axis=-1,
     )
-
-
-def featurize(extended, short_taps, row_count):
-    lead_rows = short_taps.shape[1] - 1
-    widened = extended.astype(jnp.float32)
-    featured = jnp.zeros((row_count,) + extended.shape[1:], jnp.float32)
-    for tap_index in range(short_taps.shape[1]):
-        begin_row = lead_rows - tap_index
-        featured = (
-            featured
-            + short_taps[:, tap_index, :][None] * widened[begin_row : begin_row + row_count]
-        )
-    return featured
-
-
-def medium_mix(product_rim, product, filter_taps, skip_part):
-    filter_len = filter_taps.shape[0]
-    row_count, chan_count = product.shape
-    group_count = filter_taps.shape[1]
-    padded = jnp.concatenate(
-        [jnp.zeros((1, chan_count), product.dtype), product_rim, product], axis=0
-    )
-    blocked = padded.reshape(
-        row_count // filter_len + 1, filter_len, group_count, chan_count // group_count
-    )
-    windows = jnp.concatenate([blocked[:-1], blocked[1:]], axis=1).astype(jnp.float32)
-    offsets = filter_len + jnp.arange(filter_len)[:, None] - jnp.arange(2 * filter_len)[None, :]
-    inside = (offsets >= 0) & (offsets < filter_len)
-    table = jnp.where(inside[:, :, None], filter_taps[jnp.clip(offsets, 0, filter_len - 1)], 0.0)
-    toeplitz = jnp.transpose(table, (2, 0, 1))
-    mixed = jnp.einsum("grs,nsgc->nrgc", toeplitz, windows, precision=lax.Precision.HIGHEST)
-    return mixed.reshape(row_count, chan_count) + skip_part[None, :] * product.astype(jnp.float32)
 
 
 def run_attention(queries, query_pos, key_rows, value_rows, position_of):
@@ -119,29 +426,8 @@
     return jnp.transpose(output, (1, 0, 2)).astype(jnp.bfloat16)
 
 
-def shards(
-    features,
-    residual_in,
-    short_filter,
-    medium_filter,
-    skip_gain,
-    out_weight,
-    norm_gain,
-    attn_weight,
-    attn_out,
-):
-    tok_rows = features.shape[0]
-    chan_count = features.shape[2]
-    short_taps = jnp.repeat(short_filter, GROUP_SIZE, axis=2)
-    filter_len = medium_filter.shape[0]
-    lead_rows = short_filter.shape[1] - 1
-    rim_rows = shifted(features[tok_rows - lead_rows :], "ctx", 1)
-    featured = featurize(jnp.concatenate([rim_rows, features], axis=0), short_taps, tok_rows)
-    product = (featured[:, 1, :] * featured[:, 2, :]).astype(jnp.bfloat16)
-    product_rim = shifted(product[tok_rows - (filter_len - 1) :], "ctx", 1)
-    query_feat = featured[:, 0, :]
-    mixed = medium_mix(product_rim, product, medium_filter, skip_gain)
-    gated = (query_feat * mixed).astype(jnp.bfloat16)
+def after_gating(gated, residual_in, out_weight, norm_gain, attn_weight, attn_out):
+    tok_rows, chan_count = gated.shape
     hyena_terms = jnp.dot(gated, out_weight, preferred_element_type=jnp.float32)
     hyena_out = lax.psum_scatter(
         hyena_terms.astype(jnp.bfloat16), "ch", scatter_dimension=1, tiled=True
@@ -180,6 +466,118 @@
     return (stream_wide + attn_mix).astype(jnp.bfloat16)
 
 
+def rotation_tables(positions):
+    half_size = HEAD // 2
+    frequency = 10000.0 ** (-jnp.arange(half_size, dtype=F32) * 2.0 / HEAD)
+    angles = positions.astype(F32)[:, None] * frequency[None, :]
+    cosine, sine = jnp.cos(angles), jnp.sin(angles)
+    return jnp.concatenate([cosine, cosine], axis=1), jnp.concatenate([-sine, sine], axis=1)
+
+
+def shards(
+    features,
+    residual_in,
+    short_filter,
+    medium_filter,
+    skip_gain,
+    out_weight,
+    norm_gain,
+    attn_weight,
+    attn_out,
+):
+    rows, _, channels = features.shape
+    chips = lax.axis_size("ctx") // 2
+    length = medium_filter.shape[0]
+    chunk = rows // 2
+    ctx, ch = lax.axis_index("ctx"), lax.axis_index("ch")
+    meta = jnp.stack([ch, ch ^ 1, ch ^ 2, ch ^ 3, ctx // 2, ctx % 2]).astype(jnp.int32)
+
+    by_kind = jnp.transpose(features, (1, 0, 2))
+    count = lax.axis_size("ctx")
+    halo = lax.ppermute(by_kind[:, rows - length - LEAD :], "ctx", [(i, i + 1) for i in range(count - 1)])
+    medium_rows = medium_filter.T
+    skip = skip_gain.reshape(1, channels)
+
+    starts = [rows - chunk, 0]
+    if lax.axis_size("ch") != 4 or attn_weight.shape[1] != 3 * HEAD * chips or chips % 2:
+        gated = [gated_chunk(by_kind, halo, start, chunk, short_filter, medium_rows, skip) for start in starts]
+        return after_gating(
+            jnp.concatenate(gated[::-1], axis=0), residual_in, out_weight, norm_gain, attn_weight, attn_out
+        )
+
+    gain = norm_gain.reshape(4, channels)
+    cosine, sine = rotation_tables(ctx * rows + jnp.arange(rows, dtype=jnp.int32))
+    near_x, near_y, across = ch ^ 1, ch ^ 2, ch ^ 3
+    order = [2 * across, 2 * across + 1, 2 * near_x, 2 * near_y + 1, 2 * near_x + 1, 2 * near_y, 2 * ch, 2 * ch + 1]
+    order = jnp.stack(order).astype(jnp.int32)
+
+    lower, out_held = gated_chunk(by_kind, halo, chunk, chunk, short_filter, medium_rows, skip, out_weight)
+    upper, qkv_held = gated_chunk(by_kind, halo, 0, chunk, short_filter, medium_rows, skip, attn_weight)
+    across_x, across_y = column_terms(order, upper, lower, out_held, 0, ((0, 0), (1, 0)))
+    across_x, across_y = swap_ch(across_x, 1), swap_ch(across_y, 2)
+    direct_x, direct_y, along_x, along_y, kept = column_terms(
+        order, upper, lower, out_held, 2, ((0, 0), (1, 0), (2, 0), (3, 0), (4, 0), (4, 1))
+    )
+    direct_x, direct_y = swap_ch(direct_x, 1), swap_ch(direct_y, 2)
+    late_x = swap_ch((along_x.astype(F32) + across_y.astype(F32)).astype(BF16), 1)
+    late_y = swap_ch((along_y.astype(F32) + across_x.astype(F32)).astype(BF16), 2)
+    quarters = vmem_call(
+        stream_kernel,
+        "add_stream",
+        order,
+        [kept, direct_x, direct_y, late_x, late_y, residual_in],
+        [((rows // 4, channels), BF16)] * 4,
+    )
+
+    own, other = [], []
+    for start in starts:
+        top, bottom = quarters[start // (rows // 4) : start // (rows // 4) + 2]
+        x_top, y_bottom, x_bottom, y_top = swap_ch(top, 1), swap_ch(bottom, 2), swap_ch(bottom, 1), swap_ch(top, 2)
+        diag_a, diag_b = swap_ch(x_top, 2), swap_ch(y_bottom, 1)
+        width = attn_weight.shape[1]
+        near, square = vmem_call(
+            near_kernel,
+            "qkv_near",
+            meta,
+            [top, bottom, x_top, x_bottom, y_top, y_bottom, gain, qkv_held],
+            [((chunk, width), F32), ((chunk, LANES), F32)],
+        )
+        turn = slice(start, start + chunk)
+        outs = vmem_call(
+            functools.partial(far_kernel, chips),
+            "qkv_far",
+            meta,
+            [diag_a, diag_b, near, square, gain, cosine[turn], sine[turn], qkv_held],
+            [((3, chunk, HEAD), BF16)] * chips,
+            [pltpu.VMEM((chunk, width), F32)],
+        )
+        pieces = [outs[0]] + [rotate_chips(outs[d], d) for d in range(1, chips)]
+        own = pieces + own
+        other = [swap_core(piece) for piece in pieces] + other
+
+    later, _ = lax.optimization_barrier((attn_out, own[0]))
+    by_parity = later.reshape(chips // 2, 2, HEAD, later.shape[1])
+    mine = lax.dynamic_slice_in_dim(by_parity, ctx % 2, 1, 1).reshape(chips // 2 * HEAD, later.shape[1])
+    near_w = [
+        swap_ch(lax.dynamic_slice_in_dim(mine, (ch ^ mask) * channels, channels, 1), mask) for mask in (1, 2, 3)
+    ]
+    own_w = lax.dynamic_slice_in_dim(later, ch * channels, channels, 1)
+
+    groups = [tuple(range(0, chips, 2)), tuple(range(1, chips, 2))]
+    attended = attend(meta, own, other, groups, chips, 2)
+    near_w, _ = lax.optimization_barrier((near_w, attended[1]))
+    far_w = [swap_core(weight) for weight in near_w]
+    before = quarters
+    for group, (distances, kind) in enumerate(zip(groups, [F32, BF16])):
+        backs = [rotate_chips(piece, d) if d else piece for d, piece in zip(distances, attended[group])]
+        backs = jnp.stack(backs)
+        by_x, by_y = swap_ch(backs, 1), swap_ch(backs, 2)
+        by_both = swap_ch(by_x, 2) if group == 0 else swap_ch(by_y, 1)
+        heads = [backs, by_x, by_y, by_both]
+        before = [mix(meta, heads, distances, before, own_w, near_w, far_w, kind, chips)]
+    return before[0]
+
+
 def solution(mesh):
     in_specs = (
         P("ctx", None, "ch"),

time: 571 us -> 225 us (0.39)
  waiting for transfers between devices: 284 us -> 75.6 us
  local copies, waits for them, and re-layouts: 161 us -> 35.4 us
  Pallas kernels: 0 us -> 52.8 us
  starting transfers between devices: 7.52 us -> 57 us
  matrix products: 39.6 us -> 0 us
  other arithmetic: 37.6 us -> 2.23 us
  loops' own time: 15.9 us -> 0 us
  between operations: 13.5 us -> 0.5 us
  blocking collectives: 8.93 us -> 0 us
    reduce_scatter x2 -> x0, waiting for transfers between devices: 148 us -> none  [the longest x1 93.5 us: shards(): lax.psum_scatter(head_terms.astype(jnp.bfloat16), 'ch', scatter_dimension...]
    all_gather x3 -> x0, waiting for transfers between devices: 136 us -> none  [the longest x1 52.7 us: shards(): lax.all_gather(normed, 'ch', axis=1, tiled=True)]
    gather x2 -> x0, local copies, waits for them, and re-layouts: 122 us -> none  [medium_mix(): filter_taps[jnp.clip(offsets, 0, filter_len - 1)]]
    ppermute x2 -> x48, waiting for transfers between devices: 0.01 us -> 75.6 us  [the longest x27 55.1 us: swap_ch(): return lax.ppermute(value, 'ch', [(i, i ^ mask) for i in range(count)])]
    pallas_call x0 -> x13, Pallas kernels: none -> 52.8 us  [the longest x11 35.1 us: vmem_call(): pl.pallas_call(body, in_specs=[pl.BlockSpec(memory_space=pltpu.SMEM)] + [...]
    ppermute x2 -> x48, starting transfers between devices: 7.14 us -> 57 us  [the longest x27 29.4 us: swap_ch(): return lax.ppermute(value, 'ch', [(i, i ^ mask) for i in range(count)])]
    dot_general x6 -> x0, matrix products: 39.6 us -> none  [the longest x1 10.6 us: shards(): jnp.dot(lax.all_gather(normed, 'ch', axis=1, tiled=True), attn_weight, pr...]
    add x12 -> x0, other arithmetic: 19.3 us -> none  [the longest x1 14.1 us: featurize(): featured + short_taps[:, tap_index, :][None] * widened[begin_row:begin_ro...]
  transfers between devices with their start and end apart: 7 -> 48, of which waited for: 5 -> 22; matrix products, arithmetic and copies ran while one was open for 25% -> 3% of each run, Pallas kernels for 0% -> 16%
where the time goes in v3:
time: 225 us; the launch traced here: 224 us
  waiting for transfers between devices  75.6 us (34%)
  starting transfers between devices  57 us (25%)
  Pallas kernels  52.8 us (23%)
  local copies, waits for them, and re-layouts  35.4 us (16%)
    ppermute x27, waiting for transfers between devices, swap_ch(): return lax.ppermute(value, 'ch', [(i, i ^ mask) for i in range(count)])  55.1 us
    pallas_call x11, Pallas kernels, vmem_call(): pl.pallas_call(body, in_specs=[pl.BlockSpec(memory_space=pltpu.SMEM)] + [...  35.1 us
    unnamed x72, local copies, waits for them, and re-layouts  29.9 us
    ppermute x27, starting transfers between devices, swap_ch(): return lax.ppermute(value, 'ch', [(i, i ^ mask) for i in range(count)])  29.4 us
    ppermute x9, starting transfers between devices, rotate_chips(): lax.ppermute(value, 'ctx', [(i, (i + 2 * distance) % count) for i in rang...  23 us
    ppermute x9, waiting for transfers between devices, rotate_chips(): lax.ppermute(value, 'ctx', [(i, (i + 2 * distance) % count) for i in rang...  18.2 us
    pallas_call x2, Pallas kernels, gated_chunk(): pl.pallas_call(functools.partial(gated_kernel, first_row, loads), grid=(c...  17.7 us
  transfers between devices with their start and end apart: 48, of which 22 were waited for; matrix products, arithmetic and copies ran while one was open for 3% of the time, Pallas kernels for 16%

profile of v3, /device:TPU:0, one launch (start us, length us, event | category | flops | bytes accessed | tf_op | source)
XLA Modules:
  0.0 223.6 jit_solution(1476547060777756770)
XLA Ops:
  2.1 3.3 %collective-permute-start = (bf16[3,144,1024]{2,1,0:T(8,128)(2,1)}, bf16[3,144,1024]{2,1,0:T(8,128)(2,1)}, u32[]{:S(2)}, u32[]{:S(2)}) collective-permute-start(bf16[3,144,1024]{2,1,0:T(8,128)(2,1)} %slice.20), channel_id=1, source_target_pairs={{0,4},{4,8},{8,12},{12,16},{16,20},{20,24},{24,28},{1,5},{5,9},{9,... | collective-permute-start | bytes 2654216 | tf_op jit(solution)/shard_map/ppermute | solution.py:497
  9.5 6.9 %hyena_filters.3 = (bf16[256,1024]{1,0:T(8,128)(2,1)S(1)}, bf16[1024,4096]{1,0:T(8,128)(2,1)S(1)}) custom-call(f32[3,7,64]{2,1,0:T(8,128)S(1)} %copy-done.31, f32[64,128]{1,0:T(8,128)S(1)} %bitcast.28, f32[1,1024]{1,0:T(1,128)S(1)} %bitcast.31, bf16[3,512,1024]{2,1,0:T(8,128)(2,1)S(1)} %bitcast.26, bf16[1024,4096]{1,0:T(8,128)(2,1)} %refs_4_.1), custom_call_target="tpu_custom_call" | custom-call | tf_op jit(solution)/shard_map/hyena_filters/pallas_call | solution.py:150
  16.4 3.3 %copy-done.2 = bf16[1024,4096]{1,0:T(8,128)(2,1)} copy-done((bf16[1024,4096]{1,0:T(8,128)(2,1)}, bf16[1024,4096]{1,0:T(8,128)(2,1)S(1)}, u32[]{:S(2)}) %copy-start.2) | copy-done | bytes 8388632
  20.6 10.8 %hyena_filters.2 = (bf16[256,1024]{1,0:T(8,128)(2,1)S(1)}, bf16[4096,1536]{1,0:T(8,128)(2,1)S(1)}) custom-call(f32[3,7,64]{2,1,0:T(8,128)S(1)} %copy-done.32, f32[64,128]{1,0:T(8,128)S(1)} %bitcast.29, f32[1,1024]{1,0:T(1,128)S(1)} %bitcast.32, bf16[3,144,1024]{2,1,0:T(8,128)(2,1)} %collective-permute-done.refs_3_, bf16[3,512,1024]{2,1,0:T(8,128)(2,1)S(1)} %bitcast.27, ...), custom_call_target="tpu_custom_call" | custom-call | tf_op jit(solution)/shard_map/hyena_filters/pallas_call | solution.py:150
  31.4 4.6 %copy-done = bf16[4096,1536]{1,0:T(8,128)(2,1)} copy-done((bf16[4096,1536]{1,0:T(8,128)(2,1)}, bf16[4096,1536]{1,0:T(8,128)(2,1)S(1)}, u32[]{:S(2)}) %copy-start) | copy-done | bytes 12582936
  36.0 3.4 %copy-done.3 = bf16[1024,4096]{1,0:T(8,128)(2,1)S(1)} copy-done((bf16[1024,4096]{1,0:T(8,128)(2,1)S(1)}, bf16[1024,4096]{1,0:T(8,128)(2,1)}, u32[]{:S(2)}) %copy-start.3) | copy-done | bytes 8388632
  45.1 4.0 %hyena_terms.2 = (bf16[512,512]{1,0:T(8,128)(2,1)S(1)}, bf16[512,512]{1,0:T(8,128)(2,1)S(1)}, bf16[512,512]{1,0:T(8,128)(2,1)S(1)}, bf16[512,512]{1,0:T(8,128)(2,1)S(1)}, bf16[512,1024]{1,0:T(8,128)(2,1)S(1)}) custom-call(s32[8]{0:T(128)S(1)} %stack.81.order_ref._, bf16[256,1024]{1,0:T(8,128)(2,1)S(1)} %get-tuple-element.42.upper, ...), custom_call_target="tpu_custom_call" | custom-call | tf_op jit(solution)/shard_map/hyena_terms/pallas_call | solution.py:164
  49.8 6.2 %collective-permute-done.5 = bf16[512,512]{1,0:T(8,128)(2,1)S(1)} collective-permute-done((bf16[512,512]{1,0:T(8,128)(2,1)S(1)}, bf16[512,512]{1,0:T(8,128)(2,1)S(1)}, u32[]{:S(2)}, u32[]{:S(2)}) %collective-permute-start.5) | collective-permute-done | bytes 524320 | tf_op jit(solution)/shard_map/ppermute | solution.py:23
  60.3 6.8 %collective-permute-done.1.direct_x = bf16[512,512]{1,0:T(8,128)(2,1)S(1)} collective-permute-done((bf16[512,512]{1,0:T(8,128)(2,1)S(1)}, bf16[512,512]{1,0:T(8,128)(2,1)S(1)}, u32[]{:S(2)}, u32[]{:S(2)}) %collective-permute-start.1) | collective-permute-done | bytes 524320 | tf_op jit(solution)/shard_map/ppermute | solution.py:23
  69.6 10.9 %collective-permute-done.6.late_y = bf16[512,512]{1,0:T(8,128)(2,1)S(1)} collective-permute-done((bf16[512,512]{1,0:T(8,128)(2,1)S(1)}, bf16[512,512]{1,0:T(8,128)(2,1)S(1)}, u32[]{:S(2)}, u32[]{:S(2)}) %collective-permute-start.6) | collective-permute-done | bytes 524320 | tf_op jit(solution)/shard_map/ppermute | solution.py:23
  86.1 4.9 %collective-permute-done.14.refs_2_ = bf16[128,1024]{1,0:T(8,128)(2,1)S(1)} collective-permute-done((bf16[128,1024]{1,0:T(8,128)(2,1)S(1)}, bf16[128,1024]{1,0:T(8,128)(2,1)S(1)}, u32[]{:S(2)}, u32[]{:S(2)}) %collective-permute-start.14) | collective-permute-done | bytes 262176 | tf_op jit(solution)/shard_map/ppermute | solution.py:23
  93.2 3.4 %collective-permute-done.18.refs_3_ = bf16[128,1024]{1,0:T(8,128)(2,1)S(1)} collective-permute-done((bf16[128,1024]{1,0:T(8,128)(2,1)S(1)}, bf16[128,1024]{1,0:T(8,128)(2,1)S(1)}, u32[]{:S(2)}, u32[]{:S(2)}) %collective-permute-start.18) | collective-permute-done | bytes 262176 | tf_op jit(solution)/shard_map/ppermute | solution.py:23
  98.7 3.5 %collective-permute-done.11.refs_3_ = bf16[128,1024]{1,0:T(8,128)(2,1)S(1)} collective-permute-done((bf16[128,1024]{1,0:T(8,128)(2,1)S(1)}, bf16[128,1024]{1,0:T(8,128)(2,1)S(1)}, u32[]{:S(2)}, u32[]{:S(2)}) %collective-permute-start.11) | collective-permute-done | bytes 262176 | tf_op jit(solution)/shard_map/ppermute | solution.py:23
  104.3 3.6 %collective-permute-done.7.refs_2_ = bf16[128,1024]{1,0:T(8,128)(2,1)S(1)} collective-permute-done((bf16[128,1024]{1,0:T(8,128)(2,1)S(1)}, bf16[128,1024]{1,0:T(8,128)(2,1)S(1)}, u32[]{:S(2)}, u32[]{:S(2)}) %collective-permute-start.7) | collective-permute-done | bytes 262176 | tf_op jit(solution)/shard_map/ppermute | solution.py:23
  110.5 4.6 %copy-done.1 = bf16[4096,1536]{1,0:T(8,128)(2,1)S(1)} copy-done((bf16[4096,1536]{1,0:T(8,128)(2,1)S(1)}, bf16[4096,1536]{1,0:T(8,128)(2,1)}, u32[]{:S(2)}) %copy-start.1) | copy-done | bytes 12582936
  118.3 3.1 %qkv_near.2 = (f32[256,1536]{1,0:T(8,128)S(1)}, f32[256,128]{1,0:T(8,128)S(1)}) custom-call(s32[6]{0:T(128)S(1)} %stack.72.meta_ref, bf16[128,1024]{1,0:T(8,128)(2,1)S(1)} %get-tuple-element.52.refs_0_.refs_4_, bf16[128,1024]{1,0:T(8,128)(2,1)S(1)} %get-tuple-element.53.refs_1_.refs_5_, bf16[128,1024]{1,0:T(8,128)(2,1)S(1)} %collective-permute-done.7.refs_2_, ...), custom_call_target="tpu_custom_call" | custom-call | tf_op jit(solution)/shard_map/qkv_near/pallas_call | solution.py:164
  133.3 7.1 %collective-permute-done.24.refs_6_ = bf16[3,256,128]{2,1,0:T(8,128)(2,1)S(1)} collective-permute-done((bf16[3,256,128]{2,1,0:T(8,128)(2,1)S(1)}, bf16[3,256,128]{2,1,0:T(8,128)(2,1)S(1)}, u32[]{:S(2)}, u32[]{:S(2)}) %collective-permute-start.24) | collective-permute-done | bytes 196640 | tf_op jit(solution)/shard_map/ppermute | solution.py:33
  141.1 11.4 %collective-permute-start.13 = (bf16[3,256,128]{2,1,0:T(8,128)(2,1)S(1)}, bf16[3,256,128]{2,1,0:T(8,128)(2,1)S(1)}, u32[]{:S(2)}, u32[]{:S(2)}) collective-permute-start(bf16[3,256,128]{2,1,0:T(8,128)(2,1)S(1)} %get-tuple-element.57), channel_id=1, source_target_pairs={{0,24},{4,28},{8,0},{12,4},{16,8},{20,12},{24,16},{28,20},{1,25},{... | collective-permute-start | bytes 589832 | tf_op jit(solution)/shard_map/ppermute | solution.py:33
  166.1 4.9 %attention.2 = (bf16[512,128]{1,0:T(8,128)(2,1)S(1)}, bf16[512,128]{1,0:T(8,128)(2,1)S(1)}, bf16[2,4,512,128]{3,2,1,0:T(8,128)(2,1)S(1)}, bf16[2,4,128,512]{3,2,1,0:T(8,128)(2,1)S(1)}) custom-call(s32[6]{0:T(128)S(1)} %stack.72.meta_ref, bf16[3,256,128]{2,1,0:T(8,128)(2,1)S(1)} %copy-done.28, bf16[3,256,128]{2,1,0:T(8,128)(2,1)S(1)} %copy-done.18, ...), custom_call_target="tpu_custom_call" | custom-call | tf_op jit(solution)/shard_map/attention/pallas_call | solution.py:164
  173.2 6.7 %attention.3 = (bf16[512,128]{1,0:T(8,128)(2,1)S(1)}, bf16[512,128]{1,0:T(8,128)(2,1)S(1)}) custom-call(s32[6]{0:T(128)S(1)} %stack.72.meta_ref, bf16[3,256,128]{2,1,0:T(8,128)(2,1)S(1)} %collective-permute-done.13.refs_3_.refs_0_, bf16[3,256,128]{2,1,0:T(8,128)(2,1)S(1)} %collective-permute-done.20.refs_7_.refs_1_, bf16[3,256,128]{2,1,0:T(8,128)(2,1)S(1)} %copy-done.18, ...), custom_call_target="tpu_custom_call" | custom-call | tf_op jit(solution)/shard_map/attention/pallas_call | solution.py:164
  185.9 4.3 %collective-permute-done.33 = bf16[512,128]{1,0:T(8,128)(2,1)S(1)} collective-permute-done((bf16[512,128]{1,0:T(8,128)(2,1)S(1)}, bf16[512,128]{1,0:T(8,128)(2,1)S(1)}, u32[]{:S(2)}, u32[]{:S(2)}) %collective-permute-start.33) | collective-permute-done | bytes 131104 | tf_op jit(solution)/shard_map/ppermute | solution.py:33
  195.4 6.4 %collective-permute-done.40.refs_2_ = bf16[2,512,128]{2,1,0:T(8,128)(2,1)S(1)} collective-permute-done((bf16[2,512,128]{2,1,0:T(8,128)(2,1)S(1)}, bf16[2,512,128]{2,1,0:T(8,128)(2,1)S(1)}, u32[]{:S(2)}, u32[]{:S(2)}) %collective-permute-start.40) | collective-permute-done | bytes 262176 | tf_op jit(solution)/shard_map/ppermute | solution.py:23
  203.0 4.5 %collective-permute-done.36.refs_2_ = bf16[2,512,128]{2,1,0:T(8,128)(2,1)} collective-permute-done((bf16[2,512,128]{2,1,0:T(8,128)(2,1)}, bf16[2,512,128]{2,1,0:T(8,128)(2,1)}, u32[]{:S(2)}, u32[]{:S(2)}) %collective-permute-start.36) | collective-permute-done | bytes 262176 | tf_op jit(solution)/shard_map/ppermute | solution.py:23
  220.0 3.6 %attention_mix.3 = bf16[512,1024]{1,0:T(8,128)(2,1)} custom-call(s32[6]{0:T(128)S(1)} %stack.72.meta_ref, bf16[2,512,128]{2,1,0:T(8,128)(2,1)} %pad_maximum_fusion.refs_0_, bf16[2,512,128]{2,1,0:T(8,128)(2,1)} %collective-permute-done.35.refs_1_, bf16[2,512,128]{2,1,0:T(8,128)(2,1)} %collective-permute-done.36.refs_2_, ...), custom_call_target="tpu_custom_call" | custom-call | tf_op jit(solution)/shard_map/attention_mix/pallas_call | solution.py:164
  (172 shorter events, 91.0 us)
Async XLA Ops:
  2.1 18.4 %collective-permute-start = (bf16[3,144,1024]{2,1,0:T(8,128)(2,1)}, bf16[3,144,1024]{2,1,0:T(8,128)(2,1)}, u32[]{:S(2)}, u32[]{:S(2)}) collective-permute-start(bf16[3,144,1024]{2,1,0:T(8,128)(2,1)} %slice.20), channel_id=1, source_target_pairs={{0,4},{4,8},{8,12},{12,16},{16,20},{20,24},{24,28},{1,5},{5,9},{9,... | collective-permute-start | bytes 2654216 | tf_op jit(solution)/shard_map/ppermute | solution.py:497
  49.1 18.1 %collective-permute-start.1 = (bf16[512,512]{1,0:T(8,128)(2,1)S(1)}, bf16[512,512]{1,0:T(8,128)(2,1)S(1)}, u32[]{:S(2)}, u32[]{:S(2)}) collective-permute-start(bf16[512,512]{1,0:T(8,128)(2,1)S(1)} %get-tuple-element.46), channel_id=1, source_target_pairs={{0,1},{1,0},{2,3},{3,2},{4,5},{5,4},{6,7},{7,6},{8,9},{9,8},{10,11... | collective-permute-start | bytes 1572872 | tf_op jit(solution)/shard_map/ppermute | solution.py:23
  49.7 19.9 %collective-permute-start.2 = (bf16[512,512]{1,0:T(8,128)(2,1)S(1)}, bf16[512,512]{1,0:T(8,128)(2,1)S(1)}, u32[]{:S(2)}, u32[]{:S(2)}) collective-permute-start(bf16[512,512]{1,0:T(8,128)(2,1)S(1)} %get-tuple-element.47), channel_id=1, source_target_pairs={{0,2},{1,3},{2,0},{3,1},{4,6},{5,7},{6,4},{7,5},{8,10},{9,11},{10,... | collective-permute-start | bytes 1572872 | tf_op jit(solution)/shard_map/ppermute | solution.py:23
  56.1 24.5 %collective-permute-start.6 = (bf16[512,512]{1,0:T(8,128)(2,1)S(1)}, bf16[512,512]{1,0:T(8,128)(2,1)S(1)}, u32[]{:S(2)}, u32[]{:S(2)}) collective-permute-start(bf16[512,512]{1,0:T(8,128)(2,1)S(1)} %add_convert_fusion), channel_id=1, source_target_pairs={{0,2},{1,3},{2,0},{3,1},{4,6},{5,7},{6,4},{7,5},{8,10},{9,11},{10,... | collective-permute-start | bytes 1572872 | tf_op jit(solution)/shard_map/ppermute | solution.py:23
  58.8 21.8 %collective-permute-start.4 = (bf16[512,512]{1,0:T(8,128)(2,1)S(1)}, bf16[512,512]{1,0:T(8,128)(2,1)S(1)}, u32[]{:S(2)}, u32[]{:S(2)}) collective-permute-start(bf16[512,512]{1,0:T(8,128)(2,1)S(1)} %add_convert_fusion.1), channel_id=1, source_target_pairs={{0,1},{1,0},{2,3},{3,2},{4,5},{5,4},{6,7},{7,6},{8,9},{9,8},{10,11... | collective-permute-start | bytes 1572872 | tf_op jit(solution)/shard_map/ppermute | solution.py:23
  85.8 16.4 %collective-permute-start.11 = (bf16[128,1024]{1,0:T(8,128)(2,1)S(1)}, bf16[128,1024]{1,0:T(8,128)(2,1)S(1)}, u32[]{:S(2)}, u32[]{:S(2)}) collective-permute-start(bf16[128,1024]{1,0:T(8,128)(2,1)S(1)} %get-tuple-element.53.refs_1_.refs_5_), channel_id=1, source_target_pairs={{0,1},{1,0},{2,3},{3,2},{4,5},{5,4},{6,7},{7,6},{8,9},{9,8},{10,11... | collective-permute-start | bytes 786440 | tf_op jit(solution)/shard_map/ppermute | solution.py:23
  92.5 15.3 %collective-permute-start.7 = (bf16[128,1024]{1,0:T(8,128)(2,1)S(1)}, bf16[128,1024]{1,0:T(8,128)(2,1)S(1)}, u32[]{:S(2)}, u32[]{:S(2)}) collective-permute-start(bf16[128,1024]{1,0:T(8,128)(2,1)S(1)} %get-tuple-element.52.refs_0_.refs_4_), channel_id=1, source_target_pairs={{0,1},{1,0},{2,3},{3,2},{4,5},{5,4},{6,7},{7,6},{8,9},{9,8},{10,11... | collective-permute-start | bytes 786440 | tf_op jit(solution)/shard_map/ppermute | solution.py:23
  96.6 21.7 %collective-permute-start.12 = (bf16[128,1024]{1,0:T(8,128)(2,1)S(1)}, bf16[128,1024]{1,0:T(8,128)(2,1)S(1)}, u32[]{:S(2)}, u32[]{:S(2)}) collective-permute-start(bf16[128,1024]{1,0:T(8,128)(2,1)S(1)} %get-tuple-element.52.refs_0_.refs_4_), channel_id=1, source_target_pairs={{0,2},{1,3},{2,0},{3,1},{4,6},{5,7},{6,4},{7,5},{8,10},{9,11},{10,... | collective-permute-start | bytes 786440 | tf_op jit(solution)/shard_map/ppermute | solution.py:23
  98.1 23.4 %collective-permute-start.15 = (bf16[128,1024]{1,0:T(8,128)(2,1)S(1)}, bf16[128,1024]{1,0:T(8,128)(2,1)S(1)}, u32[]{:S(2)}, u32[]{:S(2)}) collective-permute-start(bf16[128,1024]{1,0:T(8,128)(2,1)S(1)} %collective-permute-done.14.refs_2_), channel_id=1, source_target_pairs={{0,2},{1,3},{2,0},{3,1},{4,6},{5,7},{6,4},{7,5},{8,10},{9,11},{10,... | collective-permute-start | bytes 786440 | tf_op jit(solution)/shard_map/ppermute | solution.py:23
  102.2 19.3 %collective-permute-start.17 = (bf16[128,1024]{1,0:T(8,128)(2,1)S(1)}, bf16[128,1024]{1,0:T(8,128)(2,1)S(1)}, u32[]{:S(2)}, u32[]{:S(2)}) collective-permute-start(bf16[128,1024]{1,0:T(8,128)(2,1)S(1)} %collective-permute-done.16.refs_5_), channel_id=1, source_target_pairs={{0,1},{1,0},{2,3},{3,2},{4,5},{5,4},{6,7},{7,6},{8,9},{9,8},{10,11... | collective-permute-start | bytes 786440 | tf_op jit(solution)/shard_map/ppermute | solution.py:23
  102.5 25.8 %collective-permute-start.10 = (bf16[128,1024]{1,0:T(8,128)(2,1)S(1)}, bf16[128,1024]{1,0:T(8,128)(2,1)S(1)}, u32[]{:S(2)}, u32[]{:S(2)}) collective-permute-start(bf16[128,1024]{1,0:T(8,128)(2,1)S(1)} %collective-permute-done.9.refs_5_), channel_id=1, source_target_pairs={{0,1},{1,0},{2,3},{3,2},{4,5},{5,4},{6,7},{7,6},{8,9},{9,8},{10,11... | collective-permute-start | bytes 786440 | tf_op jit(solution)/shard_map/ppermute | solution.py:23
  107.8 20.4 %collective-permute-start.8 = (bf16[128,1024]{1,0:T(8,128)(2,1)S(1)}, bf16[128,1024]{1,0:T(8,128)(2,1)S(1)}, u32[]{:S(2)}, u32[]{:S(2)}) collective-permute-start(bf16[128,1024]{1,0:T(8,128)(2,1)S(1)} %collective-permute-done.7.refs_2_), channel_id=1, source_target_pairs={{0,2},{1,3},{2,0},{3,1},{4,6},{5,7},{6,4},{7,5},{8,10},{9,11},{10,... | collective-permute-start | bytes 786440 | tf_op jit(solution)/shard_map/ppermute | solution.py:23
  124.3 16.1 %collective-permute-start.24 = (bf16[3,256,128]{2,1,0:T(8,128)(2,1)S(1)}, bf16[3,256,128]{2,1,0:T(8,128)(2,1)S(1)}, u32[]{:S(2)}, u32[]{:S(2)}) collective-permute-start(bf16[3,256,128]{2,1,0:T(8,128)(2,1)S(1)} %get-tuple-element.68), channel_id=1, source_target_pairs={{0,16},{4,20},{8,24},{12,28},{16,0},{20,4},{24,8},{28,12},{1,17},{... | collective-permute-start | bytes 589832 | tf_op jit(solution)/shard_map/ppermute | solution.py:33
  125.4 15.7 %collective-permute-start.20 = (bf16[3,256,128]{2,1,0:T(8,128)(2,1)S(1)}, bf16[3,256,128]{2,1,0:T(8,128)(2,1)S(1)}, u32[]{:S(2)}, u32[]{:S(2)}) collective-permute-start(bf16[3,256,128]{2,1,0:T(8,128)(2,1)S(1)} %get-tuple-element.62), channel_id=1, source_target_pairs={{0,24},{4,28},{8,0},{12,4},{16,8},{20,12},{24,16},{28,20},{1,25},{... | collective-permute-start | bytes 589832 | tf_op jit(solution)/shard_map/ppermute | solution.py:33
  128.2 24.3 %collective-permute-start.29 = (bf16[3,256,128]{2,1,0:T(8,128)(2,1)S(1)}, bf16[3,256,128]{2,1,0:T(8,128)(2,1)S(1)}, u32[]{:S(2)}, u32[]{:S(2)}) collective-permute-start(bf16[3,256,128]{2,1,0:T(8,128)(2,1)S(1)} %get-tuple-element.67.refs_4_), channel_id=1, source_target_pairs={{0,4},{4,0},{8,12},{12,8},{16,20},{20,16},{24,28},{28,24},{1,5},{5... | collective-permute-start | bytes 589832 | tf_op jit(solution)/shard_map/ppermute | solution.py:28
  130.3 22.2 %collective-permute-start.21 = (bf16[3,256,128]{2,1,0:T(8,128)(2,1)S(1)}, bf16[3,256,128]{2,1,0:T(8,128)(2,1)S(1)}, u32[]{:S(2)}, u32[]{:S(2)}) collective-permute-start(bf16[3,256,128]{2,1,0:T(8,128)(2,1)S(1)} %get-tuple-element.63), channel_id=1, source_target_pairs={{0,8},{4,12},{8,16},{12,20},{16,24},{20,28},{24,0},{28,4},{1,9},{5... | collective-permute-start | bytes 589832 | tf_op jit(solution)/shard_map/ppermute | solution.py:33
  133.3 24.4 %collective-permute-start.25 = (bf16[3,256,128]{2,1,0:T(8,128)(2,1)S(1)}, bf16[3,256,128]{2,1,0:T(8,128)(2,1)S(1)}, u32[]{:S(2)}, u32[]{:S(2)}) collective-permute-start(bf16[3,256,128]{2,1,0:T(8,128)(2,1)S(1)} %get-tuple-element.65.refs_0_), channel_id=1, source_target_pairs={{0,4},{4,0},{8,12},{12,8},{16,20},{20,16},{24,28},{28,24},{1,5},{5... | collective-permute-start | bytes 589832 | tf_op jit(solution)/shard_map/ppermute | solution.py:28
  141.1 16.1 %collective-permute-start.13 = (bf16[3,256,128]{2,1,0:T(8,128)(2,1)S(1)}, bf16[3,256,128]{2,1,0:T(8,128)(2,1)S(1)}, u32[]{:S(2)}, u32[]{:S(2)}) collective-permute-start(bf16[3,256,128]{2,1,0:T(8,128)(2,1)S(1)} %get-tuple-element.57), channel_id=1, source_target_pairs={{0,24},{4,28},{8,0},{12,4},{16,8},{20,12},{24,16},{28,20},{1,25},{... | collective-permute-start | bytes 589832 | tf_op jit(solution)/shard_map/ppermute | solution.py:33
  155.0 24.9 %collective-permute-start.42 = (bf16[256,1024]{1,0:T(8,128)(2,1)S(1)}, bf16[256,1024]{1,0:T(8,128)(2,1)S(1)}, u32[]{:S(2)}, u32[]{:S(2)}) collective-permute-start(bf16[256,1024]{1,0:T(8,128)(2,1)S(1)} %get-tuple-element.81), channel_id=1, source_target_pairs={{0,1},{1,0},{2,3},{3,2},{4,5},{5,4},{6,7},{7,6},{8,9},{9,8},{10,11... | collective-permute-start | bytes 1572872 | tf_op jit(solution)/shard_map/ppermute | solution.py:23
  157.1 23.5 %collective-permute-start.43 = (bf16[256,1024]{1,0:T(8,128)(2,1)S(1)}, bf16[256,1024]{1,0:T(8,128)(2,1)S(1)}, u32[]{:S(2)}, u32[]{:S(2)}) collective-permute-start(bf16[256,1024]{1,0:T(8,128)(2,1)S(1)} %get-tuple-element.80), channel_id=1, source_target_pairs={{0,2},{1,3},{2,0},{3,1},{4,6},{5,7},{6,4},{7,5},{8,10},{9,11},{10,... | collective-permute-start | bytes 1572872 | tf_op jit(solution)/shard_map/ppermute | solution.py:23
  157.6 23.0 %collective-permute-start.44 = (bf16[256,1024]{1,0:T(8,128)(2,1)S(1)}, bf16[256,1024]{1,0:T(8,128)(2,1)S(1)}, u32[]{:S(2)}, u32[]{:S(2)}) collective-permute-start(bf16[256,1024]{1,0:T(8,128)(2,1)S(1)} %get-tuple-element.79), channel_id=1, source_target_pairs={{0,3},{1,2},{2,1},{3,0},{4,7},{5,6},{6,5},{7,4},{8,11},{9,10},{10,... | collective-permute-start | bytes 1572872 | tf_op jit(solution)/shard_map/ppermute | solution.py:23
  182.1 26.9 %collective-permute-start.45 = (bf16[256,1024]{1,0:T(8,128)(2,1)S(1)}, bf16[256,1024]{1,0:T(8,128)(2,1)S(1)}, u32[]{:S(2)}, u32[]{:S(2)}) collective-permute-start(bf16[256,1024]{1,0:T(8,128)(2,1)S(1)} %collective-permute-done.42.refs_9_.refs_6_), channel_id=1, source_target_pairs={{0,4},{4,0},{8,12},{12,8},{16,20},{20,16},{24,28},{28,24},{1,5},{5... | collective-permute-start | bytes 1572872 | tf_op jit(solution)/shard_map/ppermute | solution.py:28
  185.9 25.0 %collective-permute-start.46 = (bf16[256,1024]{1,0:T(8,128)(2,1)S(1)}, bf16[256,1024]{1,0:T(8,128)(2,1)S(1)}, u32[]{:S(2)}, u32[]{:S(2)}) collective-permute-start(bf16[256,1024]{1,0:T(8,128)(2,1)S(1)} %collective-permute-done.43.refs_10_.refs_7_), channel_id=1, source_target_pairs={{0,4},{4,0},{8,12},{12,8},{16,20},{20,16},{24,28},{28,24},{1,5},{5... | collective-permute-start | bytes 1572872 | tf_op jit(solution)/shard_map/ppermute | solution.py:28
  190.2 20.7 %collective-permute-start.47 = (bf16[256,1024]{1,0:T(8,128)(2,1)S(1)}, bf16[256,1024]{1,0:T(8,128)(2,1)S(1)}, u32[]{:S(2)}, u32[]{:S(2)}) collective-permute-start(bf16[256,1024]{1,0:T(8,128)(2,1)S(1)} %collective-permute-done.44.refs_11_.refs_8_), channel_id=1, source_target_pairs={{0,4},{4,0},{8,12},{12,8},{16,20},{20,16},{24,28},{28,24},{1,5},{5... | collective-permute-start | bytes 1572872 | tf_op jit(solution)/shard_map/ppermute | solution.py:28
  (60 other events, 640.7 us)

commit v4 on v3

--- a/solution.py
+++ b/solution.py
@@ -98,7 +98,7 @@
 
 
 def gated_kernel(first_row, loads, *refs):
-    head, rest = refs[:3], refs[3:]
+    head, rest = refs[1:4], refs[4:]
     halo_ref, rest = (rest[0], rest[1:]) if first_row == 0 else (None, rest)
     rows_ref, rest = rest[0], rest[1:]
     if loads:
@@ -116,24 +116,26 @@
         pl.when(pl.program_id(0) == pl.num_programs(0) - 1)(copy.wait)
 
 
-def gated_chunk(features, halo, first_row, count, short_filter, medium_rows, skip, weight=None):
+def gated_chunk(meta, features, halo, first_row, count, short_filter, medium_rows, skip, weight=None):
     kinds, rows, channels = features.shape
     length = medium_rows.shape[1]
     groups = LANES // GROUP_SIZE
     loads = weight is not None
+    in_hbm = lambda x: pltpu.with_memory_space_constraint(x, pltpu.HBM)
     in_specs = [
+        pl.BlockSpec(memory_space=pltpu.SMEM),
         pl.BlockSpec(short_filter.shape, lambda i: (0, 0, 0)),
         pl.BlockSpec((groups, length), lambda i: (i, 0)),
         pl.BlockSpec((1, LANES), lambda i: (0, i)),
     ]
-    operands = [short_filter, medium_rows, skip]
+    operands = [meta, in_hbm(short_filter), in_hbm(medium_rows), in_hbm(skip)]
     if first_row == 0:
         in_specs.append(pl.BlockSpec((kinds, length + LEAD, LANES), lambda i: (0, 0, i)))
         operands.append(halo)
         in_specs.append(pl.BlockSpec((kinds, count, LANES), lambda i: (0, 0, i)))
     else:
         in_specs.append(pl.BlockSpec((kinds, rows, LANES), lambda i: (0, 0, i)))
-    operands.append(features)
+    operands.append(in_hbm(features))
     out_specs = [pl.BlockSpec((count, LANES), lambda i: (0, i))]
     out_shape = [jax.ShapeDtypeStruct((count, channels), BF16)]
     scratch = [
@@ -143,7 +145,7 @@
     ]
     if loads:
         in_specs.append(pl.BlockSpec(memory_space=pltpu.HBM))
-        operands.append(pltpu.with_memory_space_constraint(weight, pltpu.HBM))
+        operands.append(in_hbm(weight))
         out_specs.append(pl.BlockSpec(memory_space=pltpu.VMEM))
         out_shape.append(pltpu.VMEM(weight.shape, weight.dtype))
         scratch.append(pltpu.SemaphoreType.DMA)
@@ -172,23 +174,40 @@
     )(scalars, *operands)
 
 
-def columns_kernel(first, places, order_ref, upper, lower, weight, *outs):
+def columns_kernel(pieces, meta_ref, upper, lower, weight, *outs):
     gated = jnp.concatenate([upper[...], lower[...]], axis=0)
     width = weight.shape[1] // 8
-    for piece, (out, part) in enumerate(places):
-        columns = pl.ds(pl.multiple_of(order_ref[first + piece] * width, width), width)
+    for owner, half, out, part in pieces:
+        columns = pl.ds(pl.multiple_of((2 * meta_ref[owner] + half) * width, width), width)
         term = jnp.dot(gated, weight[:, columns], preferred_element_type=F32)
         outs[out][:, part * width : (part + 1) * width] = term.astype(BF16)
 
 
-def column_terms(order, upper, lower, weight, first, places):
+def column_terms(meta, upper, lower, weight, pieces):
     rows, width = 2 * upper.shape[0], weight.shape[1] // 8
-    outs = [((rows, width * sum(p[0] == out for p in places)), BF16) for out in range(places[-1][0] + 1)]
-    body = functools.partial(columns_kernel, first, places)
-    return vmem_call(body, "hyena_terms", order, [upper, lower, weight], outs)
-
-
-def stream_kernel(_, kept, direct_x, direct_y, late_x, late_y, residual, *parts):
+    outs = [((rows, width * sum(p[2] == out for p in pieces)), BF16) for out in range(pieces[-1][2] + 1)]
+    return vmem_call(functools.partial(columns_kernel, pieces), "hyena_terms", meta, [upper, lower, weight], outs)
+
+
+def load_kernel(source, _, held, sem):
+    copy = pltpu.make_async_copy(source, held, sem)
+    copy.start()
+    copy.wait()
+
+
+def load(weight, after):
+    return pl.pallas_call(
+        load_kernel,
+        in_specs=[pl.BlockSpec(memory_space=pltpu.HBM), pl.BlockSpec(memory_space=pltpu.VMEM)],
+        out_specs=pl.BlockSpec(memory_space=pltpu.VMEM),
+        out_shape=pltpu.VMEM(weight.shape, weight.dtype),
+        scratch_shapes=[pltpu.SemaphoreType.DMA],
+        compiler_params=pltpu.CompilerParams(vmem_limit_bytes=4 * MIB),
+        name="load_weight",
+    )(pltpu.with_memory_space_constraint(weight, pltpu.HBM), after)
+
+
+def stream_kernel(_, kept, direct_x, direct_y, late_x, late_y, residual, after, *parts):
     half = late_x.shape[1]
     rows = parts[0].shape[0]
     for index, out in enumerate(parts):
@@ -207,8 +226,8 @@
     for index in range(3):
         wide = jnp.concatenate([half[...] for half in halves[2 * index : 2 * index + 2]], axis=0).astype(F32)
         squares = squares + jnp.sum(wide * wide, axis=1, keepdims=True)
-        factor = gain[pl.ds(meta_ref[index], 1), :]
-        block = weight[pl.ds(pl.multiple_of(meta_ref[index] * channels, channels), channels), :]
+        span = pl.ds(pl.multiple_of(meta_ref[index] * channels, channels), channels)
+        factor, block = gain[:, span], weight[span, :]
         term = jnp.dot((wide * factor).astype(BF16), block, preferred_element_type=F32)
         result = term if result is None else result + term
     total[...] = result
@@ -220,8 +239,8 @@
     channels = diag_a.shape[1]
     wide = jnp.concatenate([diag_a[...], diag_b[...]], axis=0).astype(F32)
     squares = square[...] + jnp.sum(wide * wide, axis=1, keepdims=True)
-    factor = gain[pl.ds(meta_ref[3], 1), :]
-    block = weight[pl.ds(pl.multiple_of(meta_ref[3] * channels, channels), channels), :]
+    span = pl.ds(pl.multiple_of(meta_ref[3] * channels, channels), channels)
+    factor, block = gain[:, span], weight[span, :]
     total[...] = near[...] + jnp.dot((wide * factor).astype(BF16), block, preferred_element_type=F32)
     inverse = lax.rsqrt(squares / (4 * channels) + norm_eps)
     for distance, out in enumerate(outs):
@@ -239,25 +258,27 @@
             out[kind] = part.astype(BF16)
 
 
-def gather_keys(chips, chunks, meta_ref, refs, keys, values):
-    pieces = chunks * chips
-    rows = refs[0].shape[1]
-    for side in range(2):
-        for distance in range(chips):
-            place = lax.rem(meta_ref[4] - distance + chips, chips)
-            for chunk in range(chunks):
-                piece = refs[side * pieces + chunk * chips + distance]
-                keys[side, place, chunk * rows : (chunk + 1) * rows, :] = piece[1]
-                for tile in range(rows // HEAD):
-                    first = chunk * rows + tile * HEAD
-                    values[side, place, :, first : first + HEAD] = piece[2, tile * HEAD : (tile + 1) * HEAD, :]
+def gather_keys(chips, meta_ref, own, other, keys, values):
+    rows = own[0].shape[1]
+    for distance in range(chips):
+        place = lax.rem(meta_ref[4] - distance + chips, chips)
+        for chunk, stacked in enumerate(other):
+            mine = own[chunk * chips + distance]
+            span = slice(chunk * rows, (chunk + 1) * rows)
+            keys[0, place, span, :] = mine[1]
+            keys[1, place, span, :] = stacked[distance, 0]
+            for tile in range(rows // HEAD):
+                first = chunk * rows + tile * HEAD
+                taken = slice(tile * HEAD, (tile + 1) * HEAD)
+                values[0, place, :, first : first + HEAD] = mine[2, taken, :]
+                values[1, place, :, first : first + HEAD] = stacked[distance, 1, taken, :]
 
 
 def attention_kernel(chips, chunks, distances, leading, meta_ref, *refs):
     if leading:
-        pieces, rest = refs[: 2 * chunks * chips], refs[2 * chunks * chips :]
-        outs, (keys, values) = rest[: len(distances)], rest[len(distances) :]
-        gather_keys(chips, chunks, meta_ref, pieces, keys, values)
+        pieces, rest = refs[: chunks * chips], refs[chunks * chips :]
+        other, outs, (keys, values) = rest[:chunks], rest[chunks:-2], rest[-2:]
+        gather_keys(chips, meta_ref, pieces, other, keys, values)
         backs = [(chips - distance) % chips for distance in distances]
         sources = [[pieces[chunk * chips + back] for chunk in range(chunks)] for back in backs]
     else:
@@ -314,6 +335,41 @@
     body = functools.partial(attention_kernel, chips, chunks, second, False)
     late = vmem_call(body, "attention", meta, pieces + [keys, values], given * len(second))
     return early, late
+
+
+def pick_kernel(chips, meta_ref, weight, _, *refs):
+    *near, own, sems = refs
+    channels = own.shape[1]
+    columns = [pl.ds(pl.multiple_of(meta_ref[index] * channels, channels), channels) for index in range(4)]
+    copies = [pltpu.make_async_copy(weight.at[:, columns[0]], own, sems.at[0])]
+    for index, out in enumerate(near):
+        for head in range(chips // 2):
+            rows = pl.ds(pl.multiple_of((2 * head + meta_ref[5]) * HEAD, HEAD), HEAD)
+            target = out.at[head * HEAD : (head + 1) * HEAD]
+            sem = sems.at[1 + index * (chips // 2) + head]
+            copies.append(pltpu.make_async_copy(weight.at[rows, columns[index + 1]], target, sem))
+    for copy in copies:
+        copy.start()
+    for copy in copies:
+        copy.wait()
+
+
+def pick_weights(meta, weight, after, chips, channels):
+    rows = weight.shape[0]
+    near = jax.ShapeDtypeStruct((rows // 2, channels), BF16)
+    return pl.pallas_call(
+        functools.partial(pick_kernel, chips),
+        in_specs=[
+            pl.BlockSpec(memory_space=pltpu.SMEM),
+            pl.BlockSpec(memory_space=pltpu.HBM),
+            pl.BlockSpec(memory_space=pltpu.VMEM),
+        ],
+        out_specs=[pl.BlockSpec(memory_space=pltpu.VMEM)] * 4,
+        out_shape=[near, near, near, jax.ShapeDtypeStruct((rows, channels), BF16)],
+        scratch_shapes=[pltpu.SemaphoreType.DMA((1 + 3 * (chips // 2),))],
+        compiler_params=pltpu.CompilerParams(vmem_limit_bytes=4 * MIB),
+        name="pick_weights",
+    )(meta, pltpu.with_memory_space_constraint(weight, pltpu.HBM), after)
 
 
 def mix_kernel(chips, distances, streams, meta_ref, *refs):
@@ -490,7 +546,8 @@
     length = medium_filter.shape[0]
     chunk = rows // 2
     ctx, ch = lax.axis_index("ctx"), lax.axis_index("ch")
-    meta = jnp.stack([ch, ch ^ 1, ch ^ 2, ch ^ 3, ctx // 2, ctx % 2]).astype(jnp.int32)
+    scalars = [ch, ch ^ 1, ch ^ 2, ch ^ 3, ctx // 2, ctx % 2, ctx * rows, ctx]
+    meta = jnp.stack(scalars).astype(jnp.int32)
 
     by_kind = jnp.transpose(features, (1, 0, 2))
     count = lax.axis_size("ctx")
@@ -500,41 +557,42 @@
 
     starts = [rows - chunk, 0]
     if lax.axis_size("ch") != 4 or attn_weight.shape[1] != 3 * HEAD * chips or chips % 2:
-        gated = [gated_chunk(by_kind, halo, start, chunk, short_filter, medium_rows, skip) for start in starts]
+        gated = [gated_chunk(meta, by_kind, halo, start, chunk, short_filter, medium_rows, skip) for start in starts]
         return after_gating(
             jnp.concatenate(gated[::-1], axis=0), residual_in, out_weight, norm_gain, attn_weight, attn_out
         )
 
-    gain = norm_gain.reshape(4, channels)
-    cosine, sine = rotation_tables(ctx * rows + jnp.arange(rows, dtype=jnp.int32))
-    near_x, near_y, across = ch ^ 1, ch ^ 2, ch ^ 3
-    order = [2 * across, 2 * across + 1, 2 * near_x, 2 * near_y + 1, 2 * near_x + 1, 2 * near_y, 2 * ch, 2 * ch + 1]
-    order = jnp.stack(order).astype(jnp.int32)
-
-    lower, out_held = gated_chunk(by_kind, halo, chunk, chunk, short_filter, medium_rows, skip, out_weight)
-    upper, qkv_held = gated_chunk(by_kind, halo, 0, chunk, short_filter, medium_rows, skip, attn_weight)
-    across_x, across_y = column_terms(order, upper, lower, out_held, 0, ((0, 0), (1, 0)))
+    gain = norm_gain.reshape(1, -1)
+    cosine, sine = rotation_tables(meta[6:7] + jnp.arange(rows, dtype=jnp.int32))
+
+    lower, out_held = gated_chunk(meta, by_kind, halo, chunk, chunk, short_filter, medium_rows, skip, out_weight)
+    upper = gated_chunk(meta, by_kind, halo, 0, chunk, short_filter, medium_rows, skip)
+    across_x, across_y = column_terms(meta, upper, lower, out_held, ((3, 0, 0, 0), (3, 1, 1, 0)))
     across_x, across_y = swap_ch(across_x, 1), swap_ch(across_y, 2)
-    direct_x, direct_y, along_x, along_y, kept = column_terms(
-        order, upper, lower, out_held, 2, ((0, 0), (1, 0), (2, 0), (3, 0), (4, 0), (4, 1))
-    )
+    pieces = ((1, 0, 0, 0), (2, 1, 1, 0), (1, 1, 2, 0), (2, 0, 3, 0), (0, 0, 4, 0), (0, 1, 4, 1))
+    direct_x, direct_y, along_x, along_y, kept = column_terms(meta, upper, lower, out_held, pieces)
     direct_x, direct_y = swap_ch(direct_x, 1), swap_ch(direct_y, 2)
-    late_x = swap_ch((along_x.astype(F32) + across_y.astype(F32)).astype(BF16), 1)
-    late_y = swap_ch((along_y.astype(F32) + across_x.astype(F32)).astype(BF16), 2)
+    along_x = (along_x.astype(F32) + across_y.astype(F32)).astype(BF16)
+    along_y = (along_y.astype(F32) + across_x.astype(F32)).astype(BF16)
+    late_x, late_y = swap_ch(along_x, 1), swap_ch(along_y, 2)
+    qkv_held = load(attn_weight, along_y)
     quarters = vmem_call(
         stream_kernel,
         "add_stream",
-        order,
-        [kept, direct_x, direct_y, late_x, late_y, residual_in],
+        meta,
+        [kept, direct_x, direct_y, late_x, late_y, residual_in, qkv_held],
         [((rows // 4, channels), BF16)] * 4,
     )
 
-    own, other = [], []
+    own, other, after = [], [], None
+    width = attn_weight.shape[1]
     for start in starts:
         top, bottom = quarters[start // (rows // 4) : start // (rows // 4) + 2]
+        if after is not None:
+            (top, bottom), _ = lax.optimization_barrier(((top, bottom), after))
         x_top, y_bottom, x_bottom, y_top = swap_ch(top, 1), swap_ch(bottom, 2), swap_ch(bottom, 1), swap_ch(top, 2)
         diag_a, diag_b = swap_ch(x_top, 2), swap_ch(y_bottom, 1)
-        width = attn_weight.shape[1]
+        after = x_top, y_bottom
         near, square = vmem_call(
             near_kernel,
             "qkv_near",
@@ -551,17 +609,12 @@
             [((3, chunk, HEAD), BF16)] * chips,
             [pltpu.VMEM((chunk, width), F32)],
         )
-        pieces = [outs[0]] + [rotate_chips(outs[d], d) for d in range(1, chips)]
-        own = pieces + own
-        other = [swap_core(piece) for piece in pieces] + other
-
-    later, _ = lax.optimization_barrier((attn_out, own[0]))
-    by_parity = later.reshape(chips // 2, 2, HEAD, later.shape[1])
-    mine = lax.dynamic_slice_in_dim(by_parity, ctx % 2, 1, 1).reshape(chips // 2 * HEAD, later.shape[1])
-    near_w = [
-        swap_ch(lax.dynamic_slice_in_dim(mine, (ch ^ mask) * channels, channels, 1), mask) for mask in (1, 2, 3)
-    ]
-    own_w = lax.dynamic_slice_in_dim(later, ch * channels, channels, 1)
+        arrived = [outs[0]] + [rotate_chips(outs[d], d) for d in range(1, chips)]
+        own = arrived + own
+        other = [swap_core(jnp.stack([piece[1:] for piece in arrived]))] + other
+
+    *near_w, own_w = pick_weights(meta, attn_out, square, chips, channels)
+    near_w = [swap_ch(weight, mask) for mask, weight in zip((1, 2, 3), near_w)]
 
     groups = [tuple(range(0, chips, 2)), tuple(range(1, chips, 2))]
     attended = attend(meta, own, other, groups, chips, 2)

time: 225 us -> 202 us (0.90)
  local copies, waits for them, and re-layouts: 35.4 us -> 1.4 us
  waiting for transfers between devices: 75.6 us -> 96.4 us
  starting transfers between devices: 57 us -> 42.7 us
  Pallas kernels: 52.8 us -> 58.8 us
    unnamed x72 -> x4, local copies, waits for them, and re-layouts: 29.9 us -> 0.01 us
    ppermute x9, waiting for transfers between devices: 18.2 us -> 34.3 us  [rotate_chips(): lax.ppermute(value, 'ctx', [(i, (i + 2 * distance) % count) for i in rang...]
    ppermute x9, starting transfers between devices: 23 us -> 10.5 us  [rotate_chips(): lax.ppermute(value, 'ctx', [(i, (i + 2 * distance) % count) for i in rang...]
    ppermute x27, waiting for transfers between devices: 55.1 us -> 62.1 us  [swap_ch(): return lax.ppermute(value, 'ch', [(i, i ^ mask) for i in range(count)])]
    pallas_call x0 -> x2, Pallas kernels: none -> 6.86 us  [the longest x1 4.58 us: load(): pl.pallas_call(load_kernel, in_specs=[pl.BlockSpec(memory_space=pltpu.HBM...]
    dynamic_slice x3 -> x0, local copies, waits for them, and re-layouts: 3.26 us -> none  [the longest x1 1.8 us: shards(): lax.dynamic_slice_in_dim(by_parity, ctx % 2, 1, 1)]
    ppermute x11 -> x5, waiting for transfers between devices: 2.28 us -> 0.01 us  [swap_core(): return lax.ppermute(value, 'ctx', [(i, i ^ 1) for i in range(count)])]
  transfers between devices with their start and end apart: 48 -> 42, of which waited for: 22 -> 19; matrix products, arithmetic and copies ran while one was open for 3% -> 1% of each run, Pallas kernels for 16% -> 22%
where the time goes in v4:
time: 202 us; the launch traced here: 201 us
  waiting for transfers between devices  96.4 us (48%)
  Pallas kernels  58.8 us (29%)
  starting transfers between devices  42.7 us (21%)
    ppermute x27, waiting for transfers between devices, swap_ch(): return lax.ppermute(value, 'ch', [(i, i ^ mask) for i in range(count)])  62.1 us
    ppermute x9, waiting for transfers between devices, rotate_chips(): lax.ppermute(value, 'ctx', [(i, (i + 2 * distance) % count) for i in rang...  34.3 us
    pallas_call x11, Pallas kernels, vmem_call(): pl.pallas_call(body, in_specs=[pl.BlockSpec(memory_space=pltpu.SMEM)] + [...  33.9 us
    ppermute x27, starting transfers between devices, swap_ch(): return lax.ppermute(value, 'ch', [(i, i ^ mask) for i in range(count)])  29.1 us
    pallas_call x2, Pallas kernels, gated_chunk(): pl.pallas_call(functools.partial(gated_kernel, first_row, loads), grid=(c...  18.1 us
    ppermute x9, starting transfers between devices, rotate_chips(): lax.ppermute(value, 'ctx', [(i, (i + 2 * distance) % count) for i in rang...  10.5 us
    pallas_call x1, Pallas kernels, load(): pl.pallas_call(load_kernel, in_specs=[pl.BlockSpec(memory_space=pltpu.HBM...  4.58 us
  transfers between devices with their start and end apart: 42, of which 19 were waited for; matrix products, arithmetic and copies ran while one was open for 1% of the time, Pallas kernels for 22%

profile of v4, /device:TPU:0, one launch (start us, length us, event | category | flops | bytes accessed | tf_op | source)
XLA Modules:
  0.0 201.4 jit_solution(9515721709159832010)
XLA Ops:
  3.8 10.2 %hyena_filters.3 = (bf16[256,1024]{1,0:T(8,128)(2,1)S(1)}, bf16[1024,4096]{1,0:T(8,128)(2,1)S(1)}) custom-call(s32[8]{0:T(128)S(1)} %stack.83.refs_0_.meta_ref._, f32[3,7,64]{2,1,0:T(8,128)} %refs_1_.3, f32[64,128]{1,0:T(8,128)} %bitcast.40, f32[1,1024]{1,0:T(1,128)} %bitcast.45, bf16[3,512,1024]{2,1,0:T(8,128)(2,1)} %bitcast.38, bf16[1024,4096]{1,0:T(8,128)(2,1)} %refs_5_.1), custom_call_target="tpu_custom_call" | custom-call | tf_op jit(solution)/shard_map/hyena_filters/pallas_call | solution.py:152
  14.0 7.8 %hyena_filters.2.upper = bf16[256,1024]{1,0:T(8,128)(2,1)S(1)} custom-call(s32[8]{0:T(128)S(1)} %stack.83.refs_0_.meta_ref._, f32[3,7,64]{2,1,0:T(8,128)} %refs_1_.3, f32[64,128]{1,0:T(8,128)} %bitcast.41, f32[1,1024]{1,0:T(1,128)} %bitcast.46, bf16[3,144,1024]{2,1,0:T(8,128)(2,1)S(1)} %collective-permute-done.refs_4_, bf16[3,512,1024]{2,1,0:T(8,128)(2,1)} %bitcast.39), custom_call_target="tpu_custom_call" | custom-call | tf_op jit(solution)/shard_map/hyena_filters/pallas_call | solution.py:152
  27.6 4.0 %hyena_terms.2 = (bf16[512,512]{1,0:T(8,128)(2,1)S(1)}, bf16[512,512]{1,0:T(8,128)(2,1)S(1)}, bf16[512,512]{1,0:T(8,128)(2,1)S(1)}, bf16[512,512]{1,0:T(8,128)(2,1)S(1)}, bf16[512,1024]{1,0:T(8,128)(2,1)S(1)}) custom-call(s32[8]{0:T(128)S(1)} %stack.83.refs_0_.meta_ref._, bf16[256,1024]{1,0:T(8,128)(2,1)S(1)} %hyena_filters.2.upper, ...), custom_call_target="tpu_custom_call" | custom-call | tf_op jit(solution)/shard_map/hyena_terms/pallas_call | solution.py:166
  32.2 5.3 %collective-permute-done.3 = bf16[512,512]{1,0:T(8,128)(2,1)S(1)} collective-permute-done((bf16[512,512]{1,0:T(8,128)(2,1)S(1)}, bf16[512,512]{1,0:T(8,128)(2,1)S(1)}, u32[]{:S(2)}, u32[]{:S(2)}) %collective-permute-start.3) | collective-permute-done | bytes 524320 | tf_op jit(solution)/shard_map/ppermute | solution.py:23
  42.0 4.6 %load_weight.1.after.refs_7_.weight = bf16[4096,1536]{1,0:T(8,128)(2,1)S(1)} custom-call(bf16[4096,1536]{1,0:T(8,128)(2,1)} %source.1, bf16[512,512]{1,0:T(8,128)(2,1)S(1)} %add_convert_fusion._), custom_call_target="tpu_custom_call" | custom-call | tf_op jit(solution)/shard_map/load_weight/pallas_call | solution.py:199
  46.6 5.0 %collective-permute-done.1.direct_x = bf16[512,512]{1,0:T(8,128)(2,1)S(1)} collective-permute-done((bf16[512,512]{1,0:T(8,128)(2,1)S(1)}, bf16[512,512]{1,0:T(8,128)(2,1)S(1)}, u32[]{:S(2)}, u32[]{:S(2)}) %collective-permute-start.1) | collective-permute-done | bytes 524320 | tf_op jit(solution)/shard_map/ppermute | solution.py:23
  51.6 11.2 %collective-permute-done.4.late_x = bf16[512,512]{1,0:T(8,128)(2,1)S(1)} collective-permute-done((bf16[512,512]{1,0:T(8,128)(2,1)S(1)}, bf16[512,512]{1,0:T(8,128)(2,1)S(1)}, u32[]{:S(2)}, u32[]{:S(2)}) %collective-permute-start.4) | collective-permute-done | bytes 524320 | tf_op jit(solution)/shard_map/ppermute | solution.py:23
  68.1 5.1 %collective-permute-done.7.refs_2_ = bf16[128,1024]{1,0:T(8,128)(2,1)S(1)} collective-permute-done((bf16[128,1024]{1,0:T(8,128)(2,1)S(1)}, bf16[128,1024]{1,0:T(8,128)(2,1)S(1)}, u32[]{:S(2)}, u32[]{:S(2)}) %collective-permute-start.7) | collective-permute-done | bytes 262176 | tf_op jit(solution)/shard_map/ppermute | solution.py:23
  80.8 5.1 %collective-permute-done.16.diag_a = bf16[128,1024]{1,0:T(8,128)(2,1)S(1)} collective-permute-done((bf16[128,1024]{1,0:T(8,128)(2,1)S(1)}, bf16[128,1024]{1,0:T(8,128)(2,1)S(1)}, u32[]{:S(2)}, u32[]{:S(2)}) %collective-permute-start.16) | collective-permute-done | bytes 262176 | tf_op jit(solution)/shard_map/ppermute | solution.py:23
  87.6 3.2 %qkv_near.3 = (f32[256,1536]{1,0:T(8,128)S(1)}, f32[256,128]{1,0:T(8,128)S(1)}) custom-call(s32[8]{0:T(128)S(1)} %stack.83.refs_0_.meta_ref._, bf16[128,1024]{1,0:T(8,128)(2,1)S(1)} %get-tuple-element.56.refs_0_.refs_6_, bf16[128,1024]{1,0:T(8,128)(2,1)S(1)} %get-tuple-element.57.refs_1_.refs_7_, bf16[128,1024]{1,0:T(8,128)(2,1)S(1)} %collective-permute-done.7.refs_2_, ...), custom_call_target="tpu_custom_call" | custom-call | tf_op jit(solution)/shard_map/qkv_near/pallas_call | solution.py:166
  90.8 4.2 %collective-permute-done.17.diag_b = bf16[128,1024]{1,0:T(8,128)(2,1)S(1)} collective-permute-done((bf16[128,1024]{1,0:T(8,128)(2,1)S(1)}, bf16[128,1024]{1,0:T(8,128)(2,1)S(1)}, u32[]{:S(2)}, u32[]{:S(2)}) %collective-permute-start.17) | collective-permute-done | bytes 262176 | tf_op jit(solution)/shard_map/ppermute | solution.py:23
  102.9 3.2 %qkv_near.2 = (f32[256,1536]{1,0:T(8,128)S(1)}, f32[256,128]{1,0:T(8,128)S(1)}) custom-call(s32[8]{0:T(128)S(1)} %stack.83.refs_0_.meta_ref._, bf16[128,1024]{1,0:T(8,128)(2,1)S(1)} %get-tuple-element.58.refs_0_.refs_4_, bf16[128,1024]{1,0:T(8,128)(2,1)S(1)} %get-tuple-element.59.refs_1_.refs_5_, bf16[128,1024]{1,0:T(8,128)(2,1)S(1)} %collective-permute-done.9.refs_2_, ...), custom_call_target="tpu_custom_call" | custom-call | tf_op jit(solution)/shard_map/qkv_near/pallas_call | solution.py:166
  106.8 8.8 %collective-permute-done.24.refs_6_ = bf16[3,256,128]{2,1,0:T(8,128)(2,1)S(1)} collective-permute-done((bf16[3,256,128]{2,1,0:T(8,128)(2,1)S(1)}, bf16[3,256,128]{2,1,0:T(8,128)(2,1)S(1)}, u32[]{:S(2)}, u32[]{:S(2)}) %collective-permute-start.24) | collective-permute-done | bytes 196640 | tf_op jit(solution)/shard_map/ppermute | solution.py:33
  120.9 10.1 %collective-permute-done.15.refs_3_.refs_0_ = bf16[3,256,128]{2,1,0:T(8,128)(2,1)S(1)} collective-permute-done((bf16[3,256,128]{2,1,0:T(8,128)(2,1)S(1)}, bf16[3,256,128]{2,1,0:T(8,128)(2,1)S(1)}, u32[]{:S(2)}, u32[]{:S(2)}) %collective-permute-start.15) | collective-permute-done | bytes 196640 | tf_op jit(solution)/shard_map/ppermute | solution.py:33
  131.1 5.8 %collective-permute-done.23.refs_2_ = bf16[3,256,128]{2,1,0:T(8,128)(2,1)S(1)} collective-permute-done((bf16[3,256,128]{2,1,0:T(8,128)(2,1)S(1)}, bf16[3,256,128]{2,1,0:T(8,128)(2,1)S(1)}, u32[]{:S(2)}, u32[]{:S(2)}) %collective-permute-start.23) | collective-permute-done | bytes 196640 | tf_op jit(solution)/shard_map/ppermute | solution.py:33
  142.9 4.9 %attention.2 = (bf16[512,128]{1,0:T(8,128)(2,1)S(1)}, bf16[512,128]{1,0:T(8,128)(2,1)S(1)}, bf16[2,4,512,128]{3,2,1,0:T(8,128)(2,1)S(1)}, bf16[2,4,128,512]{3,2,1,0:T(8,128)(2,1)S(1)}) custom-call(s32[8]{0:T(128)S(1)} %stack.83.refs_0_.meta_ref._, bf16[3,256,128]{2,1,0:T(8,128)(2,1)S(1)} %get-tuple-element.68.refs_0_, ...), custom_call_target="tpu_custom_call" | custom-call | tf_op jit(solution)/shard_map/attention/pallas_call | solution.py:166
  147.8 6.7 %attention.3 = (bf16[512,128]{1,0:T(8,128)(2,1)S(1)}, bf16[512,128]{1,0:T(8,128)(2,1)S(1)}) custom-call(s32[8]{0:T(128)S(1)} %stack.83.refs_0_.meta_ref._, bf16[3,256,128]{2,1,0:T(8,128)(2,1)S(1)} %collective-permute-done.15.refs_3_.refs_0_, bf16[3,256,128]{2,1,0:T(8,128)(2,1)S(1)} %collective-permute-done.20.refs_7_.refs_1_, ...), custom_call_target="tpu_custom_call" | custom-call | tf_op jit(solution)/shard_map/attention/pallas_call | solution.py:166
  154.6 3.4 %collective-permute-start.28 = (bf16[512,128]{1,0:T(8,128)(2,1)S(1)}, bf16[512,128]{1,0:T(8,128)(2,1)S(1)}, u32[]{:S(2)}, u32[]{:S(2)}) collective-permute-start(bf16[512,128]{1,0:T(8,128)(2,1)S(1)} %get-tuple-element.75), channel_id=1, source_target_pairs={{0,24},{4,28},{8,0},{12,4},{16,8},{20,12},{24,16},{28,20},{1,25},{... | collective-permute-start | bytes 393224 | tf_op jit(solution)/shard_map/ppermute | solution.py:33
  157.9 8.2 %collective-permute-done.37.refs_10_.refs_7_ = bf16[256,1024]{1,0:T(8,128)(2,1)S(1)} collective-permute-done((bf16[256,1024]{1,0:T(8,128)(2,1)S(1)}, bf16[256,1024]{1,0:T(8,128)(2,1)S(1)}, u32[]{:S(2)}, u32[]{:S(2)}) %collective-permute-start.37) | collective-permute-done | bytes 524320 | tf_op jit(solution)/shard_map/ppermute | solution.py:23
  167.5 8.9 %collective-permute-done.32 = bf16[512,128]{1,0:T(8,128)(2,1)S(1)} collective-permute-done((bf16[512,128]{1,0:T(8,128)(2,1)S(1)}, bf16[512,128]{1,0:T(8,128)(2,1)S(1)}, u32[]{:S(2)}, u32[]{:S(2)}) %collective-permute-start.32) | collective-permute-done | bytes 131104 | tf_op jit(solution)/shard_map/ppermute | solution.py:33
  178.6 5.9 %collective-permute-done.33.refs_1_ = bf16[2,512,128]{2,1,0:T(8,128)(2,1)S(1)} collective-permute-done((bf16[2,512,128]{2,1,0:T(8,128)(2,1)S(1)}, bf16[2,512,128]{2,1,0:T(8,128)(2,1)S(1)}, u32[]{:S(2)}, u32[]{:S(2)}) %collective-permute-start.33) | collective-permute-done | bytes 262176 | tf_op jit(solution)/shard_map/ppermute | solution.py:23
  188.0 3.5 %collective-permute-done.35.refs_3_ = bf16[2,512,128]{2,1,0:T(8,128)(2,1)S(1)} collective-permute-done((bf16[2,512,128]{2,1,0:T(8,128)(2,1)S(1)}, bf16[2,512,128]{2,1,0:T(8,128)(2,1)S(1)}, u32[]{:S(2)}, u32[]{:S(2)}) %collective-permute-start.35) | collective-permute-done | bytes 262176 | tf_op jit(solution)/shard_map/ppermute | solution.py:23
  195.2 3.1 %collective-permute-done.31.refs_3_ = bf16[2,512,128]{2,1,0:T(8,128)(2,1)S(1)} collective-permute-done((bf16[2,512,128]{2,1,0:T(8,128)(2,1)S(1)}, bf16[2,512,128]{2,1,0:T(8,128)(2,1)S(1)}, u32[]{:S(2)}, u32[]{:S(2)}) %collective-permute-start.31) | collective-permute-done | bytes 262176 | tf_op jit(solution)/shard_map/ppermute | solution.py:23
  198.4 3.0 %attention_mix.3 = bf16[512,1024]{1,0:T(8,128)(2,1)} custom-call(s32[8]{0:T(128)S(1)} %stack.83.refs_0_.meta_ref._, bf16[2,512,128]{2,1,0:T(8,128)(2,1)S(1)} %pad_maximum_fusion.2.refs_0_, bf16[2,512,128]{2,1,0:T(8,128)(2,1)S(1)} %collective-permute-done.29.refs_1_, bf16[2,512,128]{2,1,0:T(8,128)(2,1)S(1)} %collective-permute-done.30.refs_2_, ...), custom_call_target="tpu_custom_call" | custom-call | tf_op jit(solution)/shard_map/attention_mix/pallas_call | solution.py:166
  (99 shorter events, 59.7 us)
Async XLA Ops:
  23.7 13.9 %collective-permute-start.3 = (bf16[512,512]{1,0:T(8,128)(2,1)S(1)}, bf16[512,512]{1,0:T(8,128)(2,1)S(1)}, u32[]{:S(2)}, u32[]{:S(2)}) collective-permute-start(bf16[512,512]{1,0:T(8,128)(2,1)S(1)} %get-tuple-element.51), channel_id=1, source_target_pairs={{0,2},{1,3},{2,0},{3,1},{4,6},{5,7},{6,4},{7,5},{8,10},{9,11},{10,... | collective-permute-start | bytes 1572872 | tf_op jit(solution)/shard_map/ppermute | solution.py:23
  26.1 14.3 %collective-permute-start.5 = (bf16[512,512]{1,0:T(8,128)(2,1)S(1)}, bf16[512,512]{1,0:T(8,128)(2,1)S(1)}, u32[]{:S(2)}, u32[]{:S(2)}) collective-permute-start(bf16[512,512]{1,0:T(8,128)(2,1)S(1)} %get-tuple-element.53), channel_id=1, source_target_pairs={{0,1},{1,0},{2,3},{3,2},{4,5},{5,4},{6,7},{7,6},{8,9},{9,8},{10,11... | collective-permute-start | bytes 1572872 | tf_op jit(solution)/shard_map/ppermute | solution.py:23
  31.6 20.1 %collective-permute-start.1 = (bf16[512,512]{1,0:T(8,128)(2,1)S(1)}, bf16[512,512]{1,0:T(8,128)(2,1)S(1)}, u32[]{:S(2)}, u32[]{:S(2)}) collective-permute-start(bf16[512,512]{1,0:T(8,128)(2,1)S(1)} %get-tuple-element.48), channel_id=1, source_target_pairs={{0,1},{1,0},{2,3},{3,2},{4,5},{5,4},{6,7},{7,6},{8,9},{9,8},{10,11... | collective-permute-start | bytes 1572872 | tf_op jit(solution)/shard_map/ppermute | solution.py:23
  32.2 19.5 %collective-permute-start.2 = (bf16[512,512]{1,0:T(8,128)(2,1)S(1)}, bf16[512,512]{1,0:T(8,128)(2,1)S(1)}, u32[]{:S(2)}, u32[]{:S(2)}) collective-permute-start(bf16[512,512]{1,0:T(8,128)(2,1)S(1)} %get-tuple-element.49), channel_id=1, source_target_pairs={{0,2},{1,3},{2,0},{3,1},{4,6},{5,7},{6,4},{7,5},{8,10},{9,11},{10,... | collective-permute-start | bytes 1572872 | tf_op jit(solution)/shard_map/ppermute | solution.py:23
  37.7 25.1 %collective-permute-start.4 = (bf16[512,512]{1,0:T(8,128)(2,1)S(1)}, bf16[512,512]{1,0:T(8,128)(2,1)S(1)}, u32[]{:S(2)}, u32[]{:S(2)}) collective-permute-start(bf16[512,512]{1,0:T(8,128)(2,1)S(1)} %add_convert_fusion.1), channel_id=1, source_target_pairs={{0,1},{1,0},{2,3},{3,2},{4,5},{5,4},{6,7},{7,6},{8,9},{9,8},{10,11... | collective-permute-start | bytes 1572872 | tf_op jit(solution)/shard_map/ppermute | solution.py:23
  40.5 22.3 %collective-permute-start.6 = (bf16[512,512]{1,0:T(8,128)(2,1)S(1)}, bf16[512,512]{1,0:T(8,128)(2,1)S(1)}, u32[]{:S(2)}, u32[]{:S(2)}) collective-permute-start(bf16[512,512]{1,0:T(8,128)(2,1)S(1)} %add_convert_fusion._), channel_id=1, source_target_pairs={{0,2},{1,3},{2,0},{3,1},{4,6},{5,7},{6,4},{7,5},{8,10},{9,11},{10,... | collective-permute-start | bytes 1572872 | tf_op jit(solution)/shard_map/ppermute | solution.py:23
  66.1 14.2 %collective-permute-start.19 = (bf16[128,1024]{1,0:T(8,128)(2,1)S(1)}, bf16[128,1024]{1,0:T(8,128)(2,1)S(1)}, u32[]{:S(2)}, u32[]{:S(2)}) collective-permute-start(bf16[128,1024]{1,0:T(8,128)(2,1)S(1)} %get-tuple-element.56.refs_0_.refs_6_), channel_id=1, source_target_pairs={{0,2},{1,3},{2,0},{3,1},{4,6},{5,7},{6,4},{7,5},{8,10},{9,11},{10,... | collective-permute-start | bytes 786440 | tf_op jit(solution)/shard_map/ppermute | solution.py:23
  74.7 24.5 %collective-permute-start.11 = (bf16[128,1024]{1,0:T(8,128)(2,1)S(1)}, bf16[128,1024]{1,0:T(8,128)(2,1)S(1)}, u32[]{:S(2)}, u32[]{:S(2)}) collective-permute-start(bf16[128,1024]{1,0:T(8,128)(2,1)S(1)} %get-tuple-element.59.refs_1_.refs_5_), channel_id=1, source_target_pairs={{0,2},{1,3},{2,0},{3,1},{4,6},{5,7},{6,4},{7,5},{8,10},{9,11},{10,... | collective-permute-start | bytes 786440 | tf_op jit(solution)/shard_map/ppermute | solution.py:23
  75.2 25.6 %collective-permute-start.13 = (bf16[128,1024]{1,0:T(8,128)(2,1)S(1)}, bf16[128,1024]{1,0:T(8,128)(2,1)S(1)}, u32[]{:S(2)}, u32[]{:S(2)}) collective-permute-start(bf16[128,1024]{1,0:T(8,128)(2,1)S(1)} %get-tuple-element.59.refs_1_.refs_5_), channel_id=1, source_target_pairs={{0,1},{1,0},{2,3},{3,2},{4,5},{5,4},{6,7},{7,6},{8,9},{9,8},{10,11... | collective-permute-start | bytes 786440 | tf_op jit(solution)/shard_map/ppermute | solution.py:23
  78.7 18.3 %collective-permute-start.9 = (bf16[128,1024]{1,0:T(8,128)(2,1)S(1)}, bf16[128,1024]{1,0:T(8,128)(2,1)S(1)}, u32[]{:S(2)}, u32[]{:S(2)}) collective-permute-start(bf16[128,1024]{1,0:T(8,128)(2,1)S(1)} %get-tuple-element.58.refs_0_.refs_4_), channel_id=1, source_target_pairs={{0,1},{1,0},{2,3},{3,2},{4,5},{5,4},{6,7},{7,6},{8,9},{9,8},{10,11... | collective-permute-start | bytes 786440 | tf_op jit(solution)/shard_map/ppermute | solution.py:23
  80.3 21.2 %collective-permute-start.14 = (bf16[128,1024]{1,0:T(8,128)(2,1)S(1)}, bf16[128,1024]{1,0:T(8,128)(2,1)S(1)}, u32[]{:S(2)}, u32[]{:S(2)}) collective-permute-start(bf16[128,1024]{1,0:T(8,128)(2,1)S(1)} %get-tuple-element.58.refs_0_.refs_4_), channel_id=1, source_target_pairs={{0,2},{1,3},{2,0},{3,1},{4,6},{5,7},{6,4},{7,5},{8,10},{9,11},{10,... | collective-permute-start | bytes 786440 | tf_op jit(solution)/shard_map/ppermute | solution.py:23
  97.1 18.5 %collective-permute-start.22 = (bf16[3,256,128]{2,1,0:T(8,128)(2,1)S(1)}, bf16[3,256,128]{2,1,0:T(8,128)(2,1)S(1)}, u32[]{:S(2)}, u32[]{:S(2)}) collective-permute-start(bf16[3,256,128]{2,1,0:T(8,128)(2,1)S(1)} %get-tuple-element.67), channel_id=1, source_target_pairs={{0,8},{4,12},{8,16},{12,20},{16,24},{20,28},{24,0},{28,4},{1,9},{5... | collective-permute-start | bytes 589832 | tf_op jit(solution)/shard_map/ppermute | solution.py:33
  99.1 16.5 %collective-permute-start.24 = (bf16[3,256,128]{2,1,0:T(8,128)(2,1)S(1)}, bf16[3,256,128]{2,1,0:T(8,128)(2,1)S(1)}, u32[]{:S(2)}, u32[]{:S(2)}) collective-permute-start(bf16[3,256,128]{2,1,0:T(8,128)(2,1)S(1)} %get-tuple-element.71), channel_id=1, source_target_pairs={{0,16},{4,20},{8,24},{12,28},{16,0},{20,4},{24,8},{28,12},{1,17},{... | collective-permute-start | bytes 589832 | tf_op jit(solution)/shard_map/ppermute | solution.py:33
  100.9 14.9 %collective-permute-start.10 = (bf16[128,1024]{1,0:T(8,128)(2,1)S(1)}, bf16[128,1024]{1,0:T(8,128)(2,1)S(1)}, u32[]{:S(2)}, u32[]{:S(2)}) collective-permute-start(bf16[128,1024]{1,0:T(8,128)(2,1)S(1)} %collective-permute-done.9.refs_2_), channel_id=1, source_target_pairs={{0,2},{1,3},{2,0},{3,1},{4,6},{5,7},{6,4},{7,5},{8,10},{9,11},{10,... | collective-permute-start | bytes 786440 | tf_op jit(solution)/shard_map/ppermute | solution.py:23
  101.4 14.3 %collective-permute-start.12 = (bf16[128,1024]{1,0:T(8,128)(2,1)S(1)}, bf16[128,1024]{1,0:T(8,128)(2,1)S(1)}, u32[]{:S(2)}, u32[]{:S(2)}) collective-permute-start(bf16[128,1024]{1,0:T(8,128)(2,1)S(1)} %collective-permute-done.11.refs_5_), channel_id=1, source_target_pairs={{0,1},{1,0},{2,3},{3,2},{4,5},{5,4},{6,7},{7,6},{8,9},{9,8},{10,11... | collective-permute-start | bytes 786440 | tf_op jit(solution)/shard_map/ppermute | solution.py:23
  115.7 27.2 %collective-permute-start.26 = (bf16[4,2,256,128]{3,2,1,0:T(8,128)(2,1)S(1)}, bf16[4,2,256,128]{3,2,1,0:T(8,128)(2,1)S(1)}, u32[]{:S(2)}, u32[]{:S(2)}) collective-permute-start(bf16[4,2,256,128]{3,2,1,0:T(8,128)(2,1)S(1)} %pad_maximum_fusion.1), channel_id=1, source_target_pairs={{0,4},{4,0},{8,12},{12,8},{16,20},{20,16},{24,28},{28,24},{1,5},{5... | collective-permute-start | bytes 1572872 | tf_op jit(solution)/shard_map/ppermute | solution.py:28
  120.3 16.6 %collective-permute-start.21 = (bf16[3,256,128]{2,1,0:T(8,128)(2,1)S(1)}, bf16[3,256,128]{2,1,0:T(8,128)(2,1)S(1)}, u32[]{:S(2)}, u32[]{:S(2)}) collective-permute-start(bf16[3,256,128]{2,1,0:T(8,128)(2,1)S(1)} %get-tuple-element.66), channel_id=1, source_target_pairs={{0,8},{4,12},{8,16},{12,20},{16,24},{20,28},{24,0},{28,4},{1,9},{5... | collective-permute-start | bytes 589832 | tf_op jit(solution)/shard_map/ppermute | solution.py:33
  120.3 16.6 %collective-permute-start.23 = (bf16[3,256,128]{2,1,0:T(8,128)(2,1)S(1)}, bf16[3,256,128]{2,1,0:T(8,128)(2,1)S(1)}, u32[]{:S(2)}, u32[]{:S(2)}) collective-permute-start(bf16[3,256,128]{2,1,0:T(8,128)(2,1)S(1)} %get-tuple-element.69), channel_id=1, source_target_pairs={{0,16},{4,20},{8,24},{12,28},{16,0},{20,4},{24,8},{28,12},{1,17},{... | collective-permute-start | bytes 589832 | tf_op jit(solution)/shard_map/ppermute | solution.py:33
  139.4 18.6 %collective-permute-start.36 = (bf16[256,1024]{1,0:T(8,128)(2,1)S(1)}, bf16[256,1024]{1,0:T(8,128)(2,1)S(1)}, u32[]{:S(2)}, u32[]{:S(2)}) collective-permute-start(bf16[256,1024]{1,0:T(8,128)(2,1)S(1)} %get-tuple-element.79), channel_id=1, source_target_pairs={{0,1},{1,0},{2,3},{3,2},{4,5},{5,4},{6,7},{7,6},{8,9},{9,8},{10,11... | collective-permute-start | bytes 1572872 | tf_op jit(solution)/shard_map/ppermute | solution.py:23
  140.9 25.3 %collective-permute-start.37 = (bf16[256,1024]{1,0:T(8,128)(2,1)S(1)}, bf16[256,1024]{1,0:T(8,128)(2,1)S(1)}, u32[]{:S(2)}, u32[]{:S(2)}) collective-permute-start(bf16[256,1024]{1,0:T(8,128)(2,1)S(1)} %get-tuple-element.80), channel_id=1, source_target_pairs={{0,2},{1,3},{2,0},{3,1},{4,6},{5,7},{6,4},{7,5},{8,10},{9,11},{10,... | collective-permute-start | bytes 1572872 | tf_op jit(solution)/shard_map/ppermute | solution.py:23
  141.4 24.8 %collective-permute-start.38 = (bf16[256,1024]{1,0:T(8,128)(2,1)S(1)}, bf16[256,1024]{1,0:T(8,128)(2,1)S(1)}, u32[]{:S(2)}, u32[]{:S(2)}) collective-permute-start(bf16[256,1024]{1,0:T(8,128)(2,1)S(1)} %get-tuple-element.81), channel_id=1, source_target_pairs={{0,3},{1,2},{2,1},{3,0},{4,7},{5,6},{6,5},{7,4},{8,11},{9,10},{10,... | collective-permute-start | bytes 1572872 | tf_op jit(solution)/shard_map/ppermute | solution.py:23
  166.8 19.7 %collective-permute-start.39 = (bf16[256,1024]{1,0:T(8,128)(2,1)S(1)}, bf16[256,1024]{1,0:T(8,128)(2,1)S(1)}, u32[]{:S(2)}, u32[]{:S(2)}) collective-permute-start(bf16[256,1024]{1,0:T(8,128)(2,1)S(1)} %collective-permute-done.36.refs_9_.refs_6_), channel_id=1, source_target_pairs={{0,4},{4,0},{8,12},{12,8},{16,20},{20,16},{24,28},{28,24},{1,5},{5... | collective-permute-start | bytes 1572872 | tf_op jit(solution)/shard_map/ppermute | solution.py:28
  167.0 21.0 %collective-permute-start.40 = (bf16[256,1024]{1,0:T(8,128)(2,1)S(1)}, bf16[256,1024]{1,0:T(8,128)(2,1)S(1)}, u32[]{:S(2)}, u32[]{:S(2)}) collective-permute-start(bf16[256,1024]{1,0:T(8,128)(2,1)S(1)} %collective-permute-done.37.refs_10_.refs_7_), channel_id=1, source_target_pairs={{0,4},{4,0},{8,12},{12,8},{16,20},{20,16},{24,28},{28,24},{1,5},{5... | collective-permute-start | bytes 1572872 | tf_op jit(solution)/shard_map/ppermute | solution.py:28
  167.3 20.7 %collective-permute-start.41 = (bf16[256,1024]{1,0:T(8,128)(2,1)S(1)}, bf16[256,1024]{1,0:T(8,128)(2,1)S(1)}, u32[]{:S(2)}, u32[]{:S(2)}) collective-permute-start(bf16[256,1024]{1,0:T(8,128)(2,1)S(1)} %collective-permute-done.38.refs_11_.refs_8_), channel_id=1, source_target_pairs={{0,4},{4,0},{8,12},{12,8},{16,20},{20,16},{24,28},{28,24},{1,5},{5... | collective-permute-start | bytes 1572872 | tf_op jit(solution)/shard_map/ppermute | solution.py:28
  (20 other events, 227.2 us)

commit v5 on v4

--- a/solution.py
+++ b/solution.py
@@ -18,6 +18,12 @@
 BF16 = jnp.bfloat16
 
 
+def lasting(micros):
+    return pl.CostEstimate(
+        flops=int(micros * 1.1e9), transcendentals=0, bytes_accessed=int(micros * 3.6e6)
+    )
+
+
 def swap_ch(value, mask):
     count = lax.axis_size("ch")
     return lax.ppermute(value, "ch", [(i, i ^ mask) for i in range(count)])
@@ -33,7 +39,7 @@
     return lax.ppermute(value, "ctx", [(i, (i + 2 * distance) % count) for i in range(count)])
 
 
-def filter_tile(first_row, tile, short_ref, medium_ref, skip_ref, halo_ref, rows_ref, wide, product, table, store):
+def filter_tile(first_row, tile, short_ref, medium_ref, skip_ref, halo_ref, rows_ref, wide, product, table, make_table, store):
     taps, groups_all = short_ref.shape[1:]
     groups, length = medium_ref.shape
     span = wide.shape[1]
@@ -55,14 +61,15 @@
         for kind in range(3)
     ]
 
-    tap_row = lax.broadcasted_iota(jnp.int32, (length, 2 * length), 0)
-    place = lax.broadcasted_iota(jnp.int32, (length, 2 * length), 1)
-    turned = jnp.where(tap_row + place == length, 1.0, 0.0).astype(BF16)
-    base = jnp.dot(medium_ref[...].astype(BF16), turned, preferred_element_type=F32)
-    for group in range(groups):
-        spread = jnp.broadcast_to(base[group : group + 1, :], (length, 2 * length))
-        rolled = pltpu.roll(spread, 0, 1, stride=1, stride_axis=0)
-        table[group * length : (group + 1) * length, :] = rolled.astype(BF16)
+    if make_table:
+        tap_row = lax.broadcasted_iota(jnp.int32, (length, 2 * length), 0)
+        place = lax.broadcasted_iota(jnp.int32, (length, 2 * length), 1)
+        turned = jnp.where(tap_row + place == length, 1.0, 0.0).astype(BF16)
+        base = jnp.dot(medium_ref[...].astype(BF16), turned, preferred_element_type=F32)
+        for group in range(groups):
+            spread = jnp.broadcast_to(base[group : group + 1, :], (length, 2 * length))
+            rolled = pltpu.roll(spread, 0, 1, stride=1, stride_axis=0)
+            table[group * length : (group + 1) * length, :] = rolled.astype(BF16)
 
     def featured(kind, start):
         total = weights[kind][0:1, :] * wide[kind, start : start + length, :]
@@ -102,26 +109,54 @@
     halo_ref, rest = (rest[0], rest[1:]) if first_row == 0 else (None, rest)
     rows_ref, rest = rest[0], rest[1:]
     if loads:
-        weight, out_ref, held, wide, product, table, sem = rest
-        copy = pltpu.make_async_copy(weight, held, sem)
-        pl.when(pl.program_id(0) == 0)(copy.start)
+        weight, outer, out_ref, held, picked, table, wide, product, sems, pick_sems = rest
+        parts = sems.shape[0]
+        height = weight.shape[0] // parts
+
+        def copy_of(part):
+            span = pl.ds(pl.multiple_of(part * height, height), height)
+            return pltpu.make_async_copy(weight.at[span, :], held.at[span, :], sems.at[part])
+
+        def pick_of(index):
+            _, taken, width = picked.shape
+            rows = pl.ds(pl.multiple_of(refs[0][7] * taken, taken), taken)
+            columns = pl.ds(pl.multiple_of(refs[0][index + 1] * width, width), width)
+            return pltpu.make_async_copy(outer.at[rows, columns], picked.at[index], pick_sems.at[index])
+
+        copy_of(pl.program_id(0)).start()
+
+        @pl.when(pl.program_id(0) == 0)
+        def _():
+            for index in range(3):
+                pick_of(index).start()
+
+    elif first_row == 0:
+        table, out_ref, wide, product = rest
     else:
-        out_ref, wide, product, table = rest
+        out_ref, table, wide, product = rest
 
     def store(row, value):
         out_ref[row : row + value.shape[0], :] = value
 
-    filter_tile(first_row, pl.program_id(0), *head, halo_ref, rows_ref, wide, product, table, store)
+    make_table = first_row > 0
+    filter_tile(first_row, pl.program_id(0), *head, halo_ref, rows_ref, wide, product, table, make_table, store)
     if loads:
-        pl.when(pl.program_id(0) == pl.num_programs(0) - 1)(copy.wait)
-
-
-def gated_chunk(meta, features, halo, first_row, count, short_filter, medium_rows, skip, weight=None):
+
+        @pl.when(pl.program_id(0) == pl.num_programs(0) - 1)
+        def _():
+            for part in range(parts):
+                copy_of(part).wait()
+            for index in range(3):
+                pick_of(index).wait()
+
+
+def gated_chunk(meta, features, halo, first_row, count, short_filter, medium_rows, skip, weights, tables):
     kinds, rows, channels = features.shape
     length = medium_rows.shape[1]
     groups = LANES // GROUP_SIZE
-    loads = weight is not None
+    loads = weights is not None
     in_hbm = lambda x: pltpu.with_memory_space_constraint(x, pltpu.HBM)
+    table_spec = pl.BlockSpec((groups * length, 2 * length), lambda i: (i, 0))
     in_specs = [
         pl.BlockSpec(memory_space=pltpu.SMEM),
         pl.BlockSpec(short_filter.shape, lambda i: (0, 0, 0)),
@@ -129,27 +164,31 @@
         pl.BlockSpec((1, LANES), lambda i: (0, i)),
     ]
     operands = [meta, in_hbm(short_filter), in_hbm(medium_rows), in_hbm(skip)]
-    if first_row == 0:
-        in_specs.append(pl.BlockSpec((kinds, length + LEAD, LANES), lambda i: (0, 0, i)))
-        operands.append(halo)
-        in_specs.append(pl.BlockSpec((kinds, count, LANES), lambda i: (0, 0, i)))
-    else:
-        in_specs.append(pl.BlockSpec((kinds, rows, LANES), lambda i: (0, 0, i)))
-    operands.append(in_hbm(features))
     out_specs = [pl.BlockSpec((count, LANES), lambda i: (0, i))]
     out_shape = [jax.ShapeDtypeStruct((count, channels), BF16)]
     scratch = [
         pltpu.VMEM((kinds, length + LEAD + count, LANES), F32),
         pltpu.VMEM((length + count, LANES), BF16),
-        pltpu.VMEM((groups * length, 2 * length), BF16),
     ]
-    if loads:
-        in_specs.append(pl.BlockSpec(memory_space=pltpu.HBM))
-        operands.append(in_hbm(weight))
-        out_specs.append(pl.BlockSpec(memory_space=pltpu.VMEM))
-        out_shape.append(pltpu.VMEM(weight.shape, weight.dtype))
-        scratch.append(pltpu.SemaphoreType.DMA)
-    outs = pl.pallas_call(
+    if first_row == 0:
+        in_specs.append(pl.BlockSpec((kinds, length + LEAD, LANES), lambda i: (0, 0, i)))
+        in_specs.append(pl.BlockSpec((kinds, count, LANES), lambda i: (0, 0, i)))
+        in_specs.append(table_spec)
+        operands += [halo, in_hbm(features), tables]
+    else:
+        in_specs.append(pl.BlockSpec((kinds, rows, LANES), lambda i: (0, 0, i)))
+        operands.append(in_hbm(features))
+        if loads:
+            weight, outer = weights
+            in_specs += [pl.BlockSpec(memory_space=pltpu.HBM)] * 2
+            operands += [in_hbm(weight), in_hbm(outer)]
+            out_specs += [pl.BlockSpec(memory_space=pltpu.VMEM)] * 2
+            out_shape.append(pltpu.VMEM(weight.shape, weight.dtype))
+            out_shape.append(pltpu.VMEM((3, HEAD // 2, channels), outer.dtype))
+            scratch += [pltpu.SemaphoreType.DMA((channels // LANES,)), pltpu.SemaphoreType.DMA((3,))]
+        out_specs.append(table_spec)
+        out_shape.append(jax.ShapeDtypeStruct((channels // GROUP_SIZE * length, 2 * length), BF16))
+    return pl.pallas_call(
         functools.partial(gated_kernel, first_row, loads),
         grid=(channels // LANES,),
         in_specs=in_specs,
@@ -157,21 +196,25 @@
         out_shape=out_shape,
         scratch_shapes=scratch,
         compiler_params=pltpu.CompilerParams(vmem_limit_bytes=16 * MIB),
+        cost_estimate=lasting(7),
         name="hyena_filters",
     )(*operands)
-    return outs if loads else outs[0]
-
-
-def vmem_call(body, name, scalars, operands, outs, scratch=()):
+
+
+def vmem_call(body, name, micros, scalars, operands, outs, scratch=(), waits=()):
+    run = lambda *refs: body(*refs[: 1 + len(operands)], *refs[1 + len(operands) + len(waits) :])
     return pl.pallas_call(
-        body,
-        in_specs=[pl.BlockSpec(memory_space=pltpu.SMEM)] + [pl.BlockSpec(memory_space=pltpu.VMEM)] * len(operands),
+        run,
+        in_specs=[pl.BlockSpec(memory_space=pltpu.SMEM)]
+        + [pl.BlockSpec(memory_space=pltpu.VMEM)] * len(operands)
+        + [pl.BlockSpec(memory_space=pltpu.HBM)] * len(waits),
         out_specs=[pl.BlockSpec(memory_space=pltpu.VMEM)] * len(outs),
         out_shape=[jax.ShapeDtypeStruct(shape, kind) for shape, kind in outs],
         scratch_shapes=list(scratch),
         compiler_params=pltpu.CompilerParams(vmem_limit_bytes=20 * MIB),
+        cost_estimate=lasting(micros),
         name=name,
-    )(scalars, *operands)
+    )(scalars, *operands, *[pltpu.with_memory_space_constraint(x, pltpu.HBM) for x in waits])
 
 
 def columns_kernel(pieces, meta_ref, upper, lower, weight, *outs):
@@ -186,28 +229,38 @@
 def column_terms(meta, upper, lower, weight, pieces):
     rows, width = 2 * upper.shape[0], weight.shape[1] // 8
     outs = [((rows, width * sum(p[2] == out for p in pieces)), BF16) for out in range(pieces[-1][2] + 1)]
-    return vmem_call(functools.partial(columns_kernel, pieces), "hyena_terms", meta, [upper, lower, weight], outs)
-
-
-def load_kernel(source, _, held, sem):
-    copy = pltpu.make_async_copy(source, held, sem)
-    copy.start()
-    copy.wait()
-
-
-def load(weight, after):
+    return vmem_call(functools.partial(columns_kernel, pieces), "hyena_terms", 0.7 * len(pieces), meta, [upper, lower, weight], outs)
+
+
+def load_kernel(meta_ref, source, outer, _, held, own, sems):
+    channels = own.shape[1]
+    columns = pl.ds(pl.multiple_of(meta_ref[0] * channels, channels), channels)
+    copies = [
+        pltpu.make_async_copy(source, held, sems.at[0]),
+        pltpu.make_async_copy(outer.at[:, columns], own, sems.at[1]),
+    ]
+    for copy in copies:
+        copy.start()
+    for copy in copies:
+        copy.wait()
+
+
+def load(meta, weight, outer, after, channels):
+    in_hbm = lambda x: pltpu.with_memory_space_constraint(x, pltpu.HBM)
+    hbm, vmem = pl.BlockSpec(memory_space=pltpu.HBM), pl.BlockSpec(memory_space=pltpu.VMEM)
     return pl.pallas_call(
         load_kernel,
-        in_specs=[pl.BlockSpec(memory_space=pltpu.HBM), pl.BlockSpec(memory_space=pltpu.VMEM)],
-        out_specs=pl.BlockSpec(memory_space=pltpu.VMEM),
-        out_shape=pltpu.VMEM(weight.shape, weight.dtype),
-        scratch_shapes=[pltpu.SemaphoreType.DMA],
+        in_specs=[pl.BlockSpec(memory_space=pltpu.SMEM), hbm, hbm, vmem],
+        out_specs=[vmem, vmem],
+        out_shape=[pltpu.VMEM(weight.shape, weight.dtype), pltpu.VMEM((outer.shape[0], channels), outer.dtype)],
+        scratch_shapes=[pltpu.SemaphoreType.DMA((2,))],
         compiler_params=pltpu.CompilerParams(vmem_limit_bytes=4 * MIB),
-        name="load_weight",
-    )(pltpu.with_memory_space_constraint(weight, pltpu.HBM), after)
-
-
-def stream_kernel(_, kept, direct_x, direct_y, late_x, late_y, residual, after, *parts):
+        cost_estimate=lasting(5),
+        name="load_weights",
+    )(meta, in_hbm(weight), in_hbm(outer), after)
+
+
+def stream_kernel(_, kept, direct_x, direct_y, late_x, late_y, residual, after, shares, *parts):
     half = late_x.shape[1]
     rows = parts[0].shape[0]
     for index, out in enumerate(parts):
@@ -274,17 +327,14 @@
                 values[1, place, :, first : first + HEAD] = stacked[distance, 1, taken, :]
 
 
-def attention_kernel(chips, chunks, distances, leading, meta_ref, *refs):
+def attention_kernel(chips, chunks, distance, leading, meta_ref, *refs):
     if leading:
-        pieces, rest = refs[: chunks * chips], refs[chunks * chips :]
-        other, outs, (keys, values) = rest[:chunks], rest[chunks:-2], rest[-2:]
+        pieces, other = refs[: chunks * chips], refs[chunks * chips : chunks * (chips + 1)]
+        out, keys, values = refs[chunks * (chips + 1) :]
         gather_keys(chips, meta_ref, pieces, other, keys, values)
-        backs = [(chips - distance) % chips for distance in distances]
-        sources = [[pieces[chunk * chips + back] for chunk in range(chunks)] for back in backs]
+        source = pieces[(chips - distance) % chips :: chips]
     else:
-        taken = chunks * len(distances)
-        pieces, (keys, values), outs = refs[:taken], refs[taken : taken + 2], refs[taken + 2 :]
-        sources = [pieces[index * chunks : (index + 1) * chunks] for index in range(len(distances))]
+        source, (keys, values), out = refs[:chunks], refs[chunks : chunks + 2], refs[-1]
     chip, core = meta_ref[4], meta_ref[5]
     count = keys.shape[2]
 
@@ -310,105 +360,59 @@
 
     key_row = lax.broadcasted_iota(jnp.int32, (count, count), 0)
     query_column = lax.broadcasted_iota(jnp.int32, (count, count), 1)
-    for distance, source, out in zip(distances, sources, outs):
-        place = lax.rem(chip + distance, chips)
-        queries = jnp.concatenate([piece[0] for piece in source], axis=0)
-        mine = jnp.where(key_row <= query_column, scores_of(0, place, queries), -1e30)
-        others = jnp.where(core == 1, scores_of(1, place, queries), -1e30)
-        state = update((None, None, None), mine, others, place)
-
-        def earlier(index, state):
-            return update(state, scores_of(0, index, queries), scores_of(1, index, queries), index)
-
-        state = lax.fori_loop(0, place, earlier, state)
-        out[...] = (state[2] / state[1]).T.astype(BF16)
-
-
-def attend(meta, own, other, groups, chips, chunks):
+    place = lax.rem(chip + distance, chips)
+    queries = jnp.concatenate([piece[0] for piece in source], axis=0)
+    mine = jnp.where(key_row <= query_column, scores_of(0, place, queries), -1e30)
+    others = jnp.where(core == 1, scores_of(1, place, queries), -1e30)
+    state = update((None, None, None), mine, others, place)
+
+    def earlier(index, state):
+        return update(state, scores_of(0, index, queries), scores_of(1, index, queries), index)
+
+    state = lax.fori_loop(0, place, earlier, state)
+    out[...] = (state[2] / state[1]).T.astype(BF16)
+
+
+def attend(meta, own, other, laid, distance, after, chips):
+    chunks, leading = len(other), laid is None
     count = own[0].shape[1] * chunks
-    laid = [((2, chips, count, HEAD), BF16), ((2, chips, HEAD, count), BF16)]
-    given = [((count, HEAD), BF16)]
-    first, second = groups
-    body = functools.partial(attention_kernel, chips, chunks, first, True)
-    *early, keys, values = vmem_call(body, "attention", meta, own + other, given * len(first) + laid)
-    pieces = [own[chunk * chips + (chips - distance) % chips] for distance in second for chunk in range(chunks)]
-    body = functools.partial(attention_kernel, chips, chunks, second, False)
-    late = vmem_call(body, "attention", meta, pieces + [keys, values], given * len(second))
-    return early, late
-
-
-def pick_kernel(chips, meta_ref, weight, _, *refs):
-    *near, own, sems = refs
-    channels = own.shape[1]
-    columns = [pl.ds(pl.multiple_of(meta_ref[index] * channels, channels), channels) for index in range(4)]
-    copies = [pltpu.make_async_copy(weight.at[:, columns[0]], own, sems.at[0])]
-    for index, out in enumerate(near):
-        for head in range(chips // 2):
-            rows = pl.ds(pl.multiple_of((2 * head + meta_ref[5]) * HEAD, HEAD), HEAD)
-            target = out.at[head * HEAD : (head + 1) * HEAD]
-            sem = sems.at[1 + index * (chips // 2) + head]
-            copies.append(pltpu.make_async_copy(weight.at[rows, columns[index + 1]], target, sem))
-    for copy in copies:
-        copy.start()
-    for copy in copies:
-        copy.wait()
-
-
-def pick_weights(meta, weight, after, chips, channels):
-    rows = weight.shape[0]
-    near = jax.ShapeDtypeStruct((rows // 2, channels), BF16)
-    return pl.pallas_call(
-        functools.partial(pick_kernel, chips),
-        in_specs=[
-            pl.BlockSpec(memory_space=pltpu.SMEM),
-            pl.BlockSpec(memory_space=pltpu.HBM),
-            pl.BlockSpec(memory_space=pltpu.VMEM),
-        ],
-        out_specs=[pl.BlockSpec(memory_space=pltpu.VMEM)] * 4,
-        out_shape=[near, near, near, jax.ShapeDtypeStruct((rows, channels), BF16)],
-        scratch_shapes=[pltpu.SemaphoreType.DMA((1 + 3 * (chips // 2),))],
-        compiler_params=pltpu.CompilerParams(vmem_limit_bytes=4 * MIB),
-        name="pick_weights",
-    )(meta, pltpu.with_memory_space_constraint(weight, pltpu.HBM), after)
+    outs = [((count, HEAD), BF16)]
+    if leading:
+        operands = own + other
+        outs += [((2, chips, count, HEAD), BF16), ((2, chips, HEAD, count), BF16)]
+    else:
+        operands = [*own[(chips - distance) % chips :: chips], *laid, *after]
+    body = functools.partial(attention_kernel, chips, chunks, distance, leading)
+    out, *made = vmem_call(body, "attention", 3, meta, operands, outs)
+    return out, laid or made
 
 
 def mix_kernel(chips, distances, streams, meta_ref, *refs):
     heads, refs = refs[:4], refs[4:]
-    before, (own_w, *others_w), (out, ordered) = refs[:streams], refs[streams:-2], refs[-2:]
-    near_w, far_w = others_w[:3], others_w[3:]
-    chip, core = meta_ref[4], meta_ref[5]
+    before, (own_w, others_w, out, ordered) = refs[:streams], refs[streams:]
+    chip = meta_ref[4]
     parity = lax.rem(chip + distances[0], 2)
     for index, distance in enumerate(distances):
         head = lax.rem(chip - distance + chips, chips)
         column = pl.ds(pl.multiple_of(head // 2 * HEAD, HEAD), HEAD)
         for source in range(4):
             ordered[source, :, column] = heads[source][index]
-    mine = jnp.concatenate(
-        [own_w[pl.ds(pl.multiple_of((2 * j + parity) * HEAD, HEAD), HEAD), :] for j in range(chips // 2)], axis=0
-    )
-
-    def finish(weights):
-        total = jnp.dot(ordered[0], mine, preferred_element_type=F32)
-        for source in range(3):
-            total = total + jnp.dot(ordered[source + 1], weights[source][...], preferred_element_type=F32)
-        total = total + jnp.concatenate([part[...].astype(F32) for part in before], axis=0)
-        out[...] = total.astype(out.dtype)
-
-    @pl.when(core == parity)
-    def _():
-        finish(near_w)
-
-    @pl.when(core != parity)
-    def _():
-        finish(far_w)
-
-
-def mix(meta, heads, distances, before, own_w, near_w, far_w, kind, chips):
+    numbers = [2 * j + parity for j in range(chips // 2)]
+    weights = jnp.concatenate([own_w[pl.ds(pl.multiple_of(n * HEAD, HEAD), HEAD), :] for n in numbers], axis=0)
+    total = jnp.dot(ordered[0], weights, preferred_element_type=F32)
+    for source in range(3):
+        weights = jnp.concatenate([others_w[2 * n + part, source] for n in numbers for part in range(2)], axis=0)
+        total = total + jnp.dot(ordered[source + 1], weights, preferred_element_type=F32)
+    total = total + jnp.concatenate([part[...].astype(F32) for part in before], axis=0)
+    out[...] = total.astype(out.dtype)
+
+
+def mix(meta, heads, distances, before, own_w, others_w, kind, chips):
     rows, channels = heads[0].shape[1], own_w.shape[1]
     body = functools.partial(mix_kernel, chips, distances, len(before))
-    operands = [*heads, *before, own_w, *near_w, *far_w]
+    operands = [*heads, *before, own_w, others_w]
     scratch = [pltpu.VMEM((4, rows, chips // 2 * HEAD), BF16)]
-    return vmem_call(body, "attention_mix", meta, operands, [((rows, channels), kind)], scratch)[0]
+    return vmem_call(body, "attention_mix", 2.5, meta, operands, [((rows, channels), kind)], scratch)[0]
 
 
 def rotate_rows(block, positions):
@@ -557,16 +561,19 @@
 
     starts = [rows - chunk, 0]
     if lax.axis_size("ch") != 4 or attn_weight.shape[1] != 3 * HEAD * chips or chips % 2:
-        gated = [gated_chunk(meta, by_kind, halo, start, chunk, short_filter, medium_rows, skip) for start in starts]
+        lower, tables = gated_chunk(meta, by_kind, halo, chunk, chunk, short_filter, medium_rows, skip, None, None)
+        (upper,) = gated_chunk(meta, by_kind, halo, 0, chunk, short_filter, medium_rows, skip, None, tables)
         return after_gating(
-            jnp.concatenate(gated[::-1], axis=0), residual_in, out_weight, norm_gain, attn_weight, attn_out
+            jnp.concatenate([upper, lower], axis=0), residual_in, out_weight, norm_gain, attn_weight, attn_out
         )
 
     gain = norm_gain.reshape(1, -1)
     cosine, sine = rotation_tables(meta[6:7] + jnp.arange(rows, dtype=jnp.int32))
 
-    lower, out_held = gated_chunk(meta, by_kind, halo, chunk, chunk, short_filter, medium_rows, skip, out_weight)
-    upper = gated_chunk(meta, by_kind, halo, 0, chunk, short_filter, medium_rows, skip)
+    lower, out_held, picked, tables = gated_chunk(
+        meta, by_kind, halo, chunk, chunk, short_filter, medium_rows, skip, (out_weight, attn_out), None
+    )
+    (upper,) = gated_chunk(meta, by_kind, halo, 0, chunk, short_filter, medium_rows, skip, None, tables)
     across_x, across_y = column_terms(meta, upper, lower, out_held, ((3, 0, 0, 0), (3, 1, 1, 0)))
     across_x, across_y = swap_ch(across_x, 1), swap_ch(across_y, 2)
     pieces = ((1, 0, 0, 0), (2, 1, 1, 0), (1, 1, 2, 0), (2, 0, 3, 0), (0, 0, 4, 0), (0, 1, 4, 1))
@@ -575,12 +582,16 @@
     along_x = (along_x.astype(F32) + across_y.astype(F32)).astype(BF16)
     along_y = (along_y.astype(F32) + across_x.astype(F32)).astype(BF16)
     late_x, late_y = swap_ch(along_x, 1), swap_ch(along_y, 2)
-    qkv_held = load(attn_weight, along_y)
+    qkv_held, own_w = load(meta, attn_weight, attn_out, along_y, channels)
+
+    shares = jnp.stack([swap_ch(picked[index], index + 1) for index in range(3)])
+    others_w = lax.all_gather(shares, "ctx", axis=0)
     quarters = vmem_call(
         stream_kernel,
         "add_stream",
+        1,
         meta,
-        [kept, direct_x, direct_y, late_x, late_y, residual_in, qkv_held],
+        [kept, direct_x, direct_y, late_x, late_y, residual_in, qkv_held, shares],
         [((rows // 4, channels), BF16)] * 4,
     )
 
@@ -592,10 +603,11 @@
             (top, bottom), _ = lax.optimization_barrier(((top, bottom), after))
         x_top, y_bottom, x_bottom, y_top = swap_ch(top, 1), swap_ch(bottom, 2), swap_ch(bottom, 1), swap_ch(top, 2)
         diag_a, diag_b = swap_ch(x_top, 2), swap_ch(y_bottom, 1)
-        after = x_top, y_bottom
+        after = diag_a, diag_b
         near, square = vmem_call(
             near_kernel,
             "qkv_near",
+            3,
             meta,
             [top, bottom, x_top, x_bottom, y_top, y_bottom, gain, qkv_held],
             [((chunk, width), F32), ((chunk, LANES), F32)],
@@ -604,30 +616,34 @@
         outs = vmem_call(
             functools.partial(far_kernel, chips),
             "qkv_far",
+            2,
             meta,
             [diag_a, diag_b, near, square, gain, cosine[turn], sine[turn], qkv_held],
             [((3, chunk, HEAD), BF16)] * chips,
             [pltpu.VMEM((chunk, width), F32)],
+            waits=[others_w] if start == starts[-1] else [],
         )
         arrived = [outs[0]] + [rotate_chips(outs[d], d) for d in range(1, chips)]
-        own = arrived + own
-        other = [swap_core(jnp.stack([piece[1:] for piece in arrived]))] + other
-
-    *near_w, own_w = pick_weights(meta, attn_out, square, chips, channels)
-    near_w = [swap_ch(weight, mask) for mask, weight in zip((1, 2, 3), near_w)]
-
-    groups = [tuple(range(0, chips, 2)), tuple(range(1, chips, 2))]
-    attended = attend(meta, own, other, groups, chips, 2)
-    near_w, _ = lax.optimization_barrier((near_w, attended[1]))
-    far_w = [swap_core(weight) for weight in near_w]
-    before = quarters
+        own.append(arrived)
+
+    own, _ = lax.optimization_barrier((own, outs))
+    other = [swap_core(jnp.stack([piece[1:] for piece in arrived])) for arrived in own]
+    own, other = own[1] + own[0], other[::-1]
+
+    laid, after, before, backs = None, [], quarters, []
+    groups = [(*range(2, chips, 2), 0), tuple(range(1, chips, 2))]
+    for distances in groups:
+        back = []
+        for distance in distances:
+            piece, laid = attend(meta, own, other, laid, distance, after, chips)
+            back.append(rotate_chips(piece, distance) if distance else piece)
+        after = [back[0]]
+        backs.append(jnp.stack(back))
     for group, (distances, kind) in enumerate(zip(groups, [F32, BF16])):
-        backs = [rotate_chips(piece, d) if d else piece for d, piece in zip(distances, attended[group])]
-        backs = jnp.stack(backs)
-        by_x, by_y = swap_ch(backs, 1), swap_ch(backs, 2)
+        by_x, by_y = swap_ch(backs[group], 1), swap_ch(backs[group], 2)
         by_both = swap_ch(by_x, 2) if group == 0 else swap_ch(by_y, 1)
-        heads = [backs, by_x, by_y, by_both]
-        before = [mix(meta, heads, distances, before, own_w, near_w, far_w, kind, chips)]
+        heads = [backs[group], by_x, by_y, by_both]
+        before = [mix(meta, heads, distances, before, own_w, others_w, kind, chips)]
     return before[0]
 
 

time: 202 us -> 251 us (1.24)
  starting transfers between devices: 42.7 us -> 90.1 us
  waiting for transfers between devices: 96.4 us -> 65.3 us
  local copies, waits for them, and re-layouts: 1.4 us -> 17.8 us
  between operations: 0.36 us -> 13.8 us
    ppermute x9, starting transfers between devices: 10.5 us -> 58.3 us  [rotate_chips(): lax.ppermute(value, 'ctx', [(i, (i + 2 * distance) % count) for i in rang...]
    ppermute x27, waiting for transfers between devices: 62.1 us -> 40.9 us  [swap_ch(): return lax.ppermute(value, 'ch', [(i, i ^ mask) for i in range(count)])]
    unnamed x4 -> x36, local copies, waits for them, and re-layouts: 0.01 us -> 13.5 us
    ppermute x9, waiting for transfers between devices: 34.3 us -> 20.9 us  [rotate_chips(): lax.ppermute(value, 'ctx', [(i, (i + 2 * distance) % count) for i in rang...]
    another operation x8, local copies, waits for them, and re-layouts: 0.08 us -> 2.8 us  [shards(): jnp.stack([piece[1:] for piece in arrived])]
    pallas_call x13 -> x14, Pallas kernels: 40.7 us -> 42.7 us  [the longest x13 37.3 us: vmem_call(): pl.pallas_call(run, in_specs=[pl.BlockSpec(memory_space=pltpu.SMEM)] + [p...]
  transfers between devices with their start and end apart: 42 -> 40, of which waited for: 19 -> 19; matrix products, arithmetic and copies ran while one was open for 1% -> 2% of each run, Pallas kernels for 22% -> 15%
where the time goes in v5:
time: 251 us; the launch traced here: 250 us
  starting transfers between devices  90.1 us (36%)
  waiting for transfers between devices  65.3 us (26%)
  Pallas kernels  60.9 us (24%)
  local copies, waits for them, and re-layouts  17.8 us (7%)
  between operations  13.8 us (5%)
    ppermute x9, starting transfers between devices, rotate_chips(): lax.ppermute(value, 'ctx', [(i, (i + 2 * distance) % count) for i in rang...  58.3 us
    ppermute x27, waiting for transfers between devices, swap_ch(): return lax.ppermute(value, 'ch', [(i, i ^ mask) for i in range(count)])  40.9 us
    pallas_call x13, Pallas kernels, vmem_call(): pl.pallas_call(run, in_specs=[pl.BlockSpec(memory_space=pltpu.SMEM)] + [p...  37.3 us
    ppermute x27, starting transfers between devices, swap_ch(): return lax.ppermute(value, 'ch', [(i, i ^ mask) for i in range(count)])  29.4 us
    ppermute x9, waiting for transfers between devices, rotate_chips(): lax.ppermute(value, 'ctx', [(i, (i + 2 * distance) % count) for i in rang...  20.9 us
    pallas_call x2, Pallas kernels, gated_chunk(): pl.pallas_call(functools.partial(gated_kernel, first_row, loads), grid=(c...  18.2 us
    unnamed x36, local copies, waits for them, and re-layouts  13.5 us
    pallas_call x1, Pallas kernels, load(): pl.pallas_call(load_kernel, in_specs=[pl.BlockSpec(memory_space=pltpu.SME...  5.44 us
  transfers between devices with their start and end apart: 40, of which 19 were waited for; matrix products, arithmetic and copies ran while one was open for 2% of the time, Pallas kernels for 15%

profile of v5, /device:TPU:0, one launch (start us, length us, event | category | flops | bytes accessed | tf_op | source)
XLA Modules:
  0.0 250.5 jit_solution(1444674836589037953)
XLA Ops:
  6.6 10.3 %hyena_filters.2 = (bf16[256,1024]{1,0:T(8,128)(2,1)S(1)}, bf16[1024,4096]{1,0:T(8,128)(2,1)S(1)}, bf16[3,64,1024]{2,1,0:T(8,128)(2,1)S(1)}, bf16[8192,256]{1,0:T(8,128)(2,1)S(1)}) custom-call(s32[8]{0:T(128)S(1)} %stack.95.refs_0_.meta_ref, f32[3,7,64]{2,1,0:T(8,128)} %refs_1_.3, f32[64,128]{1,0:T(8,128)} %bitcast.61, f32[1,1024]{1,0:T(1,128)} %bitcast.63, ...), custom_call_target="tpu_custom_call" | custom-call | flops 7699999744 | bytes 25200000 | tf_op jit(solution)/shard_map/hyena_filters/pallas_call | solution.py:191
  16.9 3.3 %copy-done.2 = bf16[1024,4096]{1,0:T(8,128)(2,1)} copy-done((bf16[1024,4096]{1,0:T(8,128)(2,1)}, bf16[1024,4096]{1,0:T(8,128)(2,1)S(1)}, u32[]{:S(2)}) %copy-start.2) | copy-done | bytes 8388632
  22.3 4.0 %collective-permute-start.9 = (bf16[64,1024]{1,0:T(8,128)(2,1)S(1)}, bf16[64,1024]{1,0:T(8,128)(2,1)S(1)}, u32[]{:S(2)}, u32[]{:S(2)}) collective-permute-start(bf16[64,1024]{1,0:T(8,128)(2,1)S(1)} %get-tuple-element.92), channel_id=1, source_target_pairs={{0,3},{1,2},{2,1},{3,0},{4,7},{5,6},{6,5},{7,4},{8,11},{9,10},{10,... | collective-permute-start | bytes 393224 | tf_op jit(solution)/shard_map/ppermute | solution.py:29
  26.9 3.3 %collective-permute-done.9 = bf16[64,1024]{1,0:T(8,128)(2,1)S(1)} collective-permute-done((bf16[64,1024]{1,0:T(8,128)(2,1)S(1)}, bf16[64,1024]{1,0:T(8,128)(2,1)S(1)}, u32[]{:S(2)}, u32[]{:S(2)}) %collective-permute-start.9) | collective-permute-done | bytes 131104 | tf_op jit(solution)/shard_map/ppermute | solution.py:29
  41.2 7.9 %hyena_filters.3.refs_1_ = bf16[256,1024]{1,0:T(8,128)(2,1)S(1)} custom-call(s32[8]{0:T(128)S(1)} %stack.95.refs_0_.meta_ref, f32[3,7,64]{2,1,0:T(8,128)} %refs_1_.3, f32[64,128]{1,0:T(8,128)} %bitcast.62, f32[1,1024]{1,0:T(1,128)} %bitcast.64, bf16[3,144,1024]{2,1,0:T(8,128)(2,1)S(1)} %collective-permute-done.refs_4_, bf16[3,512,1024]{2,1,0:T(8,128)(2,1)} %bitcast.55, ...), custom_call_target="tpu_custom_call" | custom-call | flops 7699999744 | bytes 25200000 | tf_op jit(solution)/shard_map/hyena_filters/pallas_call | solution.py:191
  52.7 4.0 %hyena_terms.2 = (bf16[512,512]{1,0:T(8,128)(2,1)S(1)}, bf16[512,512]{1,0:T(8,128)(2,1)S(1)}, bf16[512,512]{1,0:T(8,128)(2,1)S(1)}, bf16[512,512]{1,0:T(8,128)(2,1)S(1)}, bf16[512,1024]{1,0:T(8,128)(2,1)S(1)}) custom-call(s32[8]{0:T(128)S(1)} %stack.95.refs_0_.meta_ref, bf16[256,1024]{1,0:T(8,128)(2,1)S(1)} %hyena_filters.3.refs_1_, ...), custom_call_target="tpu_custom_call" | custom-call | flops 4619999744 | bytes 15119999 | tf_op jit(solution)/shard_map/hyena_terms/pallas_call | solution.py:206
  62.5 5.4 %load_weights.1 = (bf16[4096,1536]{1,0:T(8,128)(2,1)S(1)}, bf16[512,1024]{1,0:T(8,128)(2,1)S(1)}) custom-call(s32[8]{0:T(128)S(1)} %stack.95.refs_0_.meta_ref, bf16[4096,1536]{1,0:T(8,128)(2,1)} %source.1, bf16[512,4096]{1,0:T(8,128)(2,1)} %outer.1, bf16[512,512]{1,0:T(8,128)(2,1)S(1)} %add_convert_fusion._), custom_call_target="tpu_custom_call" | custom-call | flops 5500000256 | bytes 18000000 | tf_op jit(solution)/shard_map/load_weights/pallas_call | solution.py:251
  68.0 5.2 %collective-permute-done.4.refs_4_ = bf16[512,512]{1,0:T(8,128)(2,1)S(1)} collective-permute-done((bf16[512,512]{1,0:T(8,128)(2,1)S(1)}, bf16[512,512]{1,0:T(8,128)(2,1)S(1)}, u32[]{:S(2)}, u32[]{:S(2)}) %collective-permute-start.4) | collective-permute-done | bytes 524320 | tf_op jit(solution)/shard_map/ppermute | solution.py:29
  78.9 5.1 %collective-permute-done.10.refs_3_ = bf16[128,1024]{1,0:T(8,128)(2,1)S(1)} collective-permute-done((bf16[128,1024]{1,0:T(8,128)(2,1)S(1)}, bf16[128,1024]{1,0:T(8,128)(2,1)S(1)}, u32[]{:S(2)}, u32[]{:S(2)}) %collective-permute-start.10) | collective-permute-done | bytes 262176 | tf_op jit(solution)/shard_map/ppermute | solution.py:29
  87.2 8.1 %collective-permute-done.11.refs_1_ = bf16[128,1024]{1,0:T(8,128)(2,1)S(1)} collective-permute-done((bf16[128,1024]{1,0:T(8,128)(2,1)S(1)}, bf16[128,1024]{1,0:T(8,128)(2,1)S(1)}, u32[]{:S(2)}, u32[]{:S(2)}) %collective-permute-start.11) | collective-permute-done | bytes 262176 | tf_op jit(solution)/shard_map/ppermute | solution.py:29
  99.4 3.2 %qkv_near.2 = (f32[256,1536]{1,0:T(8,128)S(1)}, f32[256,128]{1,0:T(8,128)S(1)}) custom-call(s32[8]{0:T(128)S(1)} %stack.95.refs_0_.meta_ref, bf16[128,1024]{1,0:T(8,128)(2,1)S(1)} %get-tuple-element.59.refs_1_.refs_7_, bf16[128,1024]{1,0:T(8,128)(2,1)S(1)} %get-tuple-element.60.refs_2_.refs_8_, bf16[128,1024]{1,0:T(8,128)(2,1)S(1)} %collective-permute-done.10.refs_3_, ...), custom_call_target="tpu_custom_call" | custom-call | flops 3300000000 | bytes 10800000 | tf_op jit(solution)/shard_map/qkv_near/pallas_call | solution.py:206
  105.4 31.3 %collective-permute-start.16 = (bf16[3,256,128]{2,1,0:T(8,128)(2,1)}, bf16[3,256,128]{2,1,0:T(8,128)(2,1)}, u32[]{:S(2)}, u32[]{:S(2)}) collective-permute-start(bf16[3,256,128]{2,1,0:T(8,128)(2,1)} %get-tuple-element.64), channel_id=1, source_target_pairs={{0,8},{4,12},{8,16},{12,20},{16,24},{20,28},{24,0},{28,4},{1,9},{5... | collective-permute-start | bytes 589832 | tf_op jit(solution)/shard_map/ppermute | solution.py:39
  136.6 18.2 %collective-permute-start.17 = (bf16[3,256,128]{2,1,0:T(8,128)(2,1)}, bf16[3,256,128]{2,1,0:T(8,128)(2,1)}, u32[]{:S(2)}, u32[]{:S(2)}) collective-permute-start(bf16[3,256,128]{2,1,0:T(8,128)(2,1)} %get-tuple-element.65), channel_id=1, source_target_pairs={{0,16},{4,20},{8,24},{12,28},{16,0},{20,4},{24,8},{28,12},{1,17},{... | collective-permute-start | bytes 589832 | tf_op jit(solution)/shard_map/ppermute | solution.py:39
  159.6 3.2 %qkv_near.3 = (f32[256,1536]{1,0:T(8,128)S(1)}, f32[256,128]{1,0:T(8,128)S(1)}) custom-call(s32[8]{0:T(128)S(1)} %copy-done.10, bf16[128,1024]{1,0:T(8,128)(2,1)S(1)} %get-tuple-element.69.refs_1_.refs_5_, bf16[128,1024]{1,0:T(8,128)(2,1)S(1)} %get-tuple-element.70.refs_2_.refs_6_, bf16[128,1024]{1,0:T(8,128)(2,1)S(1)} %collective-permute-done.19.refs_3_, ...), custom_call_target="tpu_custom_call" | custom-call | flops 3300000000 | bytes 10800000 | tf_op jit(solution)/shard_map/qkv_near/pallas_call | solution.py:206
  164.1 4.6 %copy-done.1 = bf16[4096,1536]{1,0:T(8,128)(2,1)S(1)} copy-done((bf16[4096,1536]{1,0:T(8,128)(2,1)S(1)}, bf16[4096,1536]{1,0:T(8,128)(2,1)}, u32[]{:S(2)}) %copy-start.1) | copy-done | bytes 12582936
  175.2 3.8 %collective-permute-done.25.refs_2_.refs_1_ = bf16[3,256,128]{2,1,0:T(8,128)(2,1)S(1)} collective-permute-done((bf16[3,256,128]{2,1,0:T(8,128)(2,1)S(1)}, bf16[3,256,128]{2,1,0:T(8,128)(2,1)S(1)}, u32[]{:S(2)}, u32[]{:S(2)}) %collective-permute-start.25) | collective-permute-done | bytes 196640 | tf_op jit(solution)/shard_map/ppermute | solution.py:39
  179.1 5.0 %collective-permute-done.26.refs_3_ = bf16[3,256,128]{2,1,0:T(8,128)(2,1)S(1)} collective-permute-done((bf16[3,256,128]{2,1,0:T(8,128)(2,1)S(1)}, bf16[3,256,128]{2,1,0:T(8,128)(2,1)S(1)}, u32[]{:S(2)}, u32[]{:S(2)}) %collective-permute-start.26) | collective-permute-done | bytes 196640 | tf_op jit(solution)/shard_map/ppermute | solution.py:39
  189.3 4.5 %attention.4 = (bf16[512,128]{1,0:T(8,128)(2,1)S(1)}, bf16[2,4,512,128]{3,2,1,0:T(8,128)(2,1)S(1)}, bf16[2,4,128,512]{3,2,1,0:T(8,128)(2,1)S(1)}) custom-call(s32[8]{0:T(128)S(1)} %copy-done.11, bf16[3,256,128]{2,1,0:T(8,128)(2,1)S(1)} %get-tuple-element.79.refs_1_, bf16[3,256,128]{2,1,0:T(8,128)(2,1)S(1)} %collective-permute-done.25.refs_2_.refs_1_, ...), custom_call_target="tpu_custom_call" | custom-call | flops 3300000000 | bytes 10800000 | tf_op jit(solution)/shard_map/attention/pallas_call | solution.py:206
  195.4 5.0 %collective-permute-done.30.refs_5_ = bf16[512,128]{1,0:T(8,128)(2,1)S(1)} collective-permute-done((bf16[512,128]{1,0:T(8,128)(2,1)S(1)}, bf16[512,128]{1,0:T(8,128)(2,1)S(1)}, u32[]{:S(2)}, u32[]{:S(2)}) %collective-permute-start.30) | collective-permute-done | bytes 131104 | tf_op jit(solution)/shard_map/ppermute | solution.py:39
  200.5 5.1 %attention.6 = bf16[512,128]{1,0:T(8,128)(2,1)S(1)} custom-call(s32[8]{0:T(128)S(1)} %copy-done.11, bf16[3,256,128]{2,1,0:T(8,128)(2,1)S(1)} %collective-permute-done.25.refs_2_.refs_1_, bf16[3,256,128]{2,1,0:T(8,128)(2,1)} %collective-permute-done.16.refs_6_.refs_2_, bf16[2,4,512,128]{3,2,1,0:T(8,128)(2,1)S(1)} %get-tuple-element.85.refs_3_, ...), custom_call_target="tpu_custom_call" | custom-call | flops 3300000000 | bytes 10800000 | tf_op jit(solution)/shard_map/attention/pallas_call | solution.py:206
  213.2 7.0 %collective-permute-done.31 = bf16[512,128]{1,0:T(8,128)(2,1)S(1)} collective-permute-done((bf16[512,128]{1,0:T(8,128)(2,1)S(1)}, bf16[512,128]{1,0:T(8,128)(2,1)S(1)}, u32[]{:S(2)}, u32[]{:S(2)}) %collective-permute-start.31) | collective-permute-done | bytes 131104 | tf_op jit(solution)/shard_map/ppermute | solution.py:39
  224.0 5.5 %collective-permute-done.34.refs_3_ = bf16[2,512,128]{2,1,0:T(8,128)(2,1)S(1)} collective-permute-done((bf16[2,512,128]{2,1,0:T(8,128)(2,1)S(1)}, bf16[2,512,128]{2,1,0:T(8,128)(2,1)S(1)}, u32[]{:S(2)}, u32[]{:S(2)}) %collective-permute-start.34) | collective-permute-done | bytes 262176 | tf_op jit(solution)/shard_map/ppermute | solution.py:29
  230.5 4.7 %collective-permute-done.37.refs_3_ = bf16[2,512,128]{2,1,0:T(8,128)(2,1)S(1)} collective-permute-done((bf16[2,512,128]{2,1,0:T(8,128)(2,1)S(1)}, bf16[2,512,128]{2,1,0:T(8,128)(2,1)S(1)}, u32[]{:S(2)}, u32[]{:S(2)}) %collective-permute-start.37) | collective-permute-done | bytes 262176 | tf_op jit(solution)/shard_map/ppermute | solution.py:29
  235.2 3.5 %collective-permute-done.38.refs_4_ = bf16[2,512,128]{2,1,0:T(8,128)(2,1)S(1)} collective-permute-done((bf16[2,512,128]{2,1,0:T(8,128)(2,1)S(1)}, bf16[2,512,128]{2,1,0:T(8,128)(2,1)S(1)}, u32[]{:S(2)}, u32[]{:S(2)}) %collective-permute-start.38) | collective-permute-done | bytes 262176 | tf_op jit(solution)/shard_map/ppermute | solution.py:29
  (132 shorter events, 75.5 us)
Async XLA Ops:
  6.5 157.6 %all-gather.3.cloned.1.call-start = ((), (), s32[]{:S(2)}) async-start(), calls=%async_computation | async-start | bytes 3538944 | tf_op jit(solution)/shard_map/all_gather | solution.py:588
  52.7 9.3 %collective-permute-start.5 = (bf16[512,512]{1,0:T(8,128)(2,1)S(1)}, bf16[512,512]{1,0:T(8,128)(2,1)S(1)}, u32[]{:S(2)}, u32[]{:S(2)}) collective-permute-start(bf16[512,512]{1,0:T(8,128)(2,1)S(1)} %get-tuple-element.56), channel_id=1, source_target_pairs={{0,1},{1,0},{2,3},{3,2},{4,5},{5,4},{6,7},{7,6},{8,9},{9,8},{10,11... | collective-permute-start | bytes 1572872 | tf_op jit(solution)/shard_map/ppermute | solution.py:29
  56.7 11.2 %collective-permute-start.1 = (bf16[512,512]{1,0:T(8,128)(2,1)S(1)}, bf16[512,512]{1,0:T(8,128)(2,1)S(1)}, u32[]{:S(2)}, u32[]{:S(2)}) collective-permute-start(bf16[512,512]{1,0:T(8,128)(2,1)S(1)} %get-tuple-element.51), channel_id=1, source_target_pairs={{0,1},{1,0},{2,3},{3,2},{4,5},{5,4},{6,7},{7,6},{8,9},{9,8},{10,11... | collective-permute-start | bytes 1572872 | tf_op jit(solution)/shard_map/ppermute | solution.py:29
  60.3 12.8 %collective-permute-start.4 = (bf16[512,512]{1,0:T(8,128)(2,1)S(1)}, bf16[512,512]{1,0:T(8,128)(2,1)S(1)}, u32[]{:S(2)}, u32[]{:S(2)}) collective-permute-start(bf16[512,512]{1,0:T(8,128)(2,1)S(1)} %add_convert_fusion.1), channel_id=1, source_target_pairs={{0,1},{1,0},{2,3},{3,2},{4,5},{5,4},{6,7},{7,6},{8,9},{9,8},{10,11... | collective-permute-start | bytes 1572872 | tf_op jit(solution)/shard_map/ppermute | solution.py:29
  62.2 11.4 %collective-permute-start.6 = (bf16[512,512]{1,0:T(8,128)(2,1)S(1)}, bf16[512,512]{1,0:T(8,128)(2,1)S(1)}, u32[]{:S(2)}, u32[]{:S(2)}) collective-permute-start(bf16[512,512]{1,0:T(8,128)(2,1)S(1)} %add_convert_fusion._), channel_id=1, source_target_pairs={{0,2},{1,3},{2,0},{3,1},{4,6},{5,7},{6,4},{7,5},{8,10},{9,11},{10,... | collective-permute-start | bytes 1572872 | tf_op jit(solution)/shard_map/ppermute | solution.py:29
  74.8 9.5 %collective-permute-start.12 = (bf16[128,1024]{1,0:T(8,128)(2,1)S(1)}, bf16[128,1024]{1,0:T(8,128)(2,1)S(1)}, u32[]{:S(2)}, u32[]{:S(2)}) collective-permute-start(bf16[128,1024]{1,0:T(8,128)(2,1)S(1)} %get-tuple-element.60.refs_2_.refs_8_), channel_id=1, source_target_pairs={{0,2},{1,3},{2,0},{3,1},{4,6},{5,7},{6,4},{7,5},{8,10},{9,11},{10,... | collective-permute-start | bytes 786440 | tf_op jit(solution)/shard_map/ppermute | solution.py:29
  76.7 22.5 %collective-permute-start.14 = (bf16[128,1024]{1,0:T(8,128)(2,1)S(1)}, bf16[128,1024]{1,0:T(8,128)(2,1)S(1)}, u32[]{:S(2)}, u32[]{:S(2)}) collective-permute-start(bf16[128,1024]{1,0:T(8,128)(2,1)S(1)} %get-tuple-element.60.refs_2_.refs_8_), channel_id=1, source_target_pairs={{0,1},{1,0},{2,3},{3,2},{4,5},{5,4},{6,7},{7,6},{8,9},{9,8},{10,11... | collective-permute-start | bytes 786440 | tf_op jit(solution)/shard_map/ppermute | solution.py:29
  77.2 22.2 %collective-permute-start.15 = (bf16[128,1024]{1,0:T(8,128)(2,1)S(1)}, bf16[128,1024]{1,0:T(8,128)(2,1)S(1)}, u32[]{:S(2)}, u32[]{:S(2)}) collective-permute-start(bf16[128,1024]{1,0:T(8,128)(2,1)S(1)} %get-tuple-element.59.refs_1_.refs_7_), channel_id=1, source_target_pairs={{0,2},{1,3},{2,0},{3,1},{4,6},{5,7},{6,4},{7,5},{8,10},{9,11},{10,... | collective-permute-start | bytes 786440 | tf_op jit(solution)/shard_map/ppermute | solution.py:29
  84.0 11.3 %collective-permute-start.11 = (bf16[128,1024]{1,0:T(8,128)(2,1)S(1)}, bf16[128,1024]{1,0:T(8,128)(2,1)S(1)}, u32[]{:S(2)}, u32[]{:S(2)}) collective-permute-start(bf16[128,1024]{1,0:T(8,128)(2,1)S(1)} %collective-permute-done.10.refs_3_), channel_id=1, source_target_pairs={{0,2},{1,3},{2,0},{3,1},{4,6},{5,7},{6,4},{7,5},{8,10},{9,11},{10,... | collective-permute-start | bytes 786440 | tf_op jit(solution)/shard_map/ppermute | solution.py:29
  84.3 11.0 %collective-permute-start.13 = (bf16[128,1024]{1,0:T(8,128)(2,1)S(1)}, bf16[128,1024]{1,0:T(8,128)(2,1)S(1)}, u32[]{:S(2)}, u32[]{:S(2)}) collective-permute-start(bf16[128,1024]{1,0:T(8,128)(2,1)S(1)} %collective-permute-done.12.refs_6_), channel_id=1, source_target_pairs={{0,1},{1,0},{2,3},{3,2},{4,5},{5,4},{6,7},{7,6},{8,9},{9,8},{10,11... | collective-permute-start | bytes 786440 | tf_op jit(solution)/shard_map/ppermute | solution.py:29
  95.3 59.5 %collective-permute-start.21 = (bf16[128,1024]{1,0:T(8,128)(2,1)S(1)}, bf16[128,1024]{1,0:T(8,128)(2,1)S(1)}, u32[]{:S(2)}, u32[]{:S(2)}) collective-permute-start(bf16[128,1024]{1,0:T(8,128)(2,1)S(1)} %get-tuple-element.70.refs_2_.refs_6_), channel_id=1, source_target_pairs={{0,2},{1,3},{2,0},{3,1},{4,6},{5,7},{6,4},{7,5},{8,10},{9,11},{10,... | collective-permute-start | bytes 786440 | tf_op jit(solution)/shard_map/ppermute | solution.py:29
  97.2 59.3 %collective-permute-start.23 = (bf16[128,1024]{1,0:T(8,128)(2,1)S(1)}, bf16[128,1024]{1,0:T(8,128)(2,1)S(1)}, u32[]{:S(2)}, u32[]{:S(2)}) collective-permute-start(bf16[128,1024]{1,0:T(8,128)(2,1)S(1)} %get-tuple-element.70.refs_2_.refs_6_), channel_id=1, source_target_pairs={{0,1},{1,0},{2,3},{3,2},{4,5},{5,4},{6,7},{7,6},{8,9},{9,8},{10,11... | collective-permute-start | bytes 786440 | tf_op jit(solution)/shard_map/ppermute | solution.py:29
  97.6 39.1 %collective-permute-start.19 = (bf16[128,1024]{1,0:T(8,128)(2,1)S(1)}, bf16[128,1024]{1,0:T(8,128)(2,1)S(1)}, u32[]{:S(2)}, u32[]{:S(2)}) collective-permute-start(bf16[128,1024]{1,0:T(8,128)(2,1)S(1)} %get-tuple-element.69.refs_1_.refs_5_), channel_id=1, source_target_pairs={{0,1},{1,0},{2,3},{3,2},{4,5},{5,4},{6,7},{7,6},{8,9},{9,8},{10,11... | collective-permute-start | bytes 786440 | tf_op jit(solution)/shard_map/ppermute | solution.py:29
  99.2 58.5 %collective-permute-start.24 = (bf16[128,1024]{1,0:T(8,128)(2,1)S(1)}, bf16[128,1024]{1,0:T(8,128)(2,1)S(1)}, u32[]{:S(2)}, u32[]{:S(2)}) collective-permute-start(bf16[128,1024]{1,0:T(8,128)(2,1)S(1)} %get-tuple-element.69.refs_1_.refs_5_), channel_id=1, source_target_pairs={{0,2},{1,3},{2,0},{3,1},{4,6},{5,7},{6,4},{7,5},{8,10},{9,11},{10,... | collective-permute-start | bytes 786440 | tf_op jit(solution)/shard_map/ppermute | solution.py:29
  105.4 67.2 %collective-permute-start.16 = (bf16[3,256,128]{2,1,0:T(8,128)(2,1)}, bf16[3,256,128]{2,1,0:T(8,128)(2,1)}, u32[]{:S(2)}, u32[]{:S(2)}) collective-permute-start(bf16[3,256,128]{2,1,0:T(8,128)(2,1)} %get-tuple-element.64), channel_id=1, source_target_pairs={{0,8},{4,12},{8,16},{12,20},{16,24},{20,28},{24,0},{28,4},{1,9},{5... | collective-permute-start | bytes 589832 | tf_op jit(solution)/shard_map/ppermute | solution.py:39
  136.6 38.6 %collective-permute-start.17 = (bf16[3,256,128]{2,1,0:T(8,128)(2,1)}, bf16[3,256,128]{2,1,0:T(8,128)(2,1)}, u32[]{:S(2)}, u32[]{:S(2)}) collective-permute-start(bf16[3,256,128]{2,1,0:T(8,128)(2,1)} %get-tuple-element.65), channel_id=1, source_target_pairs={{0,16},{4,20},{8,24},{12,28},{16,0},{20,4},{24,8},{28,12},{1,17},{... | collective-permute-start | bytes 589832 | tf_op jit(solution)/shard_map/ppermute | solution.py:39
  154.8 20.4 %collective-permute-start.18 = (bf16[3,256,128]{2,1,0:T(8,128)(2,1)}, bf16[3,256,128]{2,1,0:T(8,128)(2,1)}, u32[]{:S(2)}, u32[]{:S(2)}) collective-permute-start(bf16[3,256,128]{2,1,0:T(8,128)(2,1)} %get-tuple-element.66), channel_id=1, source_target_pairs={{0,24},{4,28},{8,0},{12,4},{16,8},{20,12},{24,16},{28,20},{1,25},{... | collective-permute-start | bytes 589832 | tf_op jit(solution)/shard_map/ppermute | solution.py:39
  172.6 11.5 %collective-permute-start.26 = (bf16[3,256,128]{2,1,0:T(8,128)(2,1)S(1)}, bf16[3,256,128]{2,1,0:T(8,128)(2,1)S(1)}, u32[]{:S(2)}, u32[]{:S(2)}) collective-permute-start(bf16[3,256,128]{2,1,0:T(8,128)(2,1)S(1)} %get-tuple-element.75), channel_id=1, source_target_pairs={{0,16},{4,20},{8,24},{12,28},{16,0},{20,4},{24,8},{28,12},{1,17},{... | collective-permute-start | bytes 589832 | tf_op jit(solution)/shard_map/ppermute | solution.py:39
  172.6 11.5 %collective-permute-start.27 = (bf16[3,256,128]{2,1,0:T(8,128)(2,1)S(1)}, bf16[3,256,128]{2,1,0:T(8,128)(2,1)S(1)}, u32[]{:S(2)}, u32[]{:S(2)}) collective-permute-start(bf16[3,256,128]{2,1,0:T(8,128)(2,1)S(1)} %get-tuple-element.76), channel_id=1, source_target_pairs={{0,24},{4,28},{8,0},{12,4},{16,8},{20,12},{24,16},{28,20},{1,25},{... | collective-permute-start | bytes 589832 | tf_op jit(solution)/shard_map/ppermute | solution.py:39
  208.8 13.5 %collective-permute-start.36 = (bf16[2,512,128]{2,1,0:T(8,128)(2,1)S(1)}, bf16[2,512,128]{2,1,0:T(8,128)(2,1)S(1)}, u32[]{:S(2)}, u32[]{:S(2)}) collective-permute-start(bf16[2,512,128]{2,1,0:T(8,128)(2,1)S(1)} %pad_maximum_fusion.4.refs_1_), channel_id=1, source_target_pairs={{0,1},{1,0},{2,3},{3,2},{4,5},{5,4},{6,7},{7,6},{8,9},{9,8},{10,11... | collective-permute-start | bytes 786440 | tf_op jit(solution)/shard_map/ppermute | solution.py:29
  221.1 14.1 %collective-permute-start.37 = (bf16[2,512,128]{2,1,0:T(8,128)(2,1)S(1)}, bf16[2,512,128]{2,1,0:T(8,128)(2,1)S(1)}, u32[]{:S(2)}, u32[]{:S(2)}) collective-permute-start(bf16[2,512,128]{2,1,0:T(8,128)(2,1)S(1)} %pad_maximum_fusion.4.refs_1_), channel_id=1, source_target_pairs={{0,2},{1,3},{2,0},{3,1},{4,6},{5,7},{6,4},{7,5},{8,10},{9,11},{10,... | collective-permute-start | bytes 786440 | tf_op jit(solution)/shard_map/ppermute | solution.py:29
  222.3 16.3 %collective-permute-start.38 = (bf16[2,512,128]{2,1,0:T(8,128)(2,1)S(1)}, bf16[2,512,128]{2,1,0:T(8,128)(2,1)S(1)}, u32[]{:S(2)}, u32[]{:S(2)}) collective-permute-start(bf16[2,512,128]{2,1,0:T(8,128)(2,1)S(1)} %collective-permute-done.36.refs_2_), channel_id=1, source_target_pairs={{0,2},{1,3},{2,0},{3,1},{4,6},{5,7},{6,4},{7,5},{8,10},{9,11},{10,... | collective-permute-start | bytes 786440 | tf_op jit(solution)/shard_map/ppermute | solution.py:29
  223.1 17.5 %collective-permute-start.33 = (bf16[2,512,128]{2,1,0:T(8,128)(2,1)S(1)}, bf16[2,512,128]{2,1,0:T(8,128)(2,1)S(1)}, u32[]{:S(2)}, u32[]{:S(2)}) collective-permute-start(bf16[2,512,128]{2,1,0:T(8,128)(2,1)S(1)} %pad_maximum_fusion.3.refs_1_), channel_id=1, source_target_pairs={{0,1},{1,0},{2,3},{3,2},{4,5},{5,4},{6,7},{7,6},{8,9},{9,8},{10,11... | collective-permute-start | bytes 786440 | tf_op jit(solution)/shard_map/ppermute | solution.py:29
  229.6 11.1 %collective-permute-start.35 = (bf16[2,512,128]{2,1,0:T(8,128)(2,1)S(1)}, bf16[2,512,128]{2,1,0:T(8,128)(2,1)S(1)}, u32[]{:S(2)}, u32[]{:S(2)}) collective-permute-start(bf16[2,512,128]{2,1,0:T(8,128)(2,1)S(1)} %collective-permute-done.34.refs_3_), channel_id=1, source_target_pairs={{0,1},{1,0},{2,3},{3,2},{4,5},{5,4},{6,7},{7,6},{8,9},{9,8},{10,11... | collective-permute-start | bytes 786440 | tf_op jit(solution)/shard_map/ppermute | solution.py:29
  (34 other events, 522.8 us)
Sparse Core Ops, SparseCore 0:
  33.8 40.4 all-gather.2

commit v6 on v5

--- a/solution.py
+++ b/solution.py
@@ -109,7 +109,7 @@
     halo_ref, rest = (rest[0], rest[1:]) if first_row == 0 else (None, rest)
     rows_ref, rest = rest[0], rest[1:]
     if loads:
-        weight, outer, out_ref, held, picked, table, wide, product, sems, pick_sems = rest
+        weight, out_ref, held, table, wide, product, sems = rest
         parts = sems.shape[0]
         height = weight.shape[0] // parts
 
@@ -117,19 +117,7 @@
             span = pl.ds(pl.multiple_of(part * height, height), height)
             return pltpu.make_async_copy(weight.at[span, :], held.at[span, :], sems.at[part])
 
-        def pick_of(index):
-            _, taken, width = picked.shape
-            rows = pl.ds(pl.multiple_of(refs[0][7] * taken, taken), taken)
-            columns = pl.ds(pl.multiple_of(refs[0][index + 1] * width, width), width)
-            return pltpu.make_async_copy(outer.at[rows, columns], picked.at[index], pick_sems.at[index])
-
         copy_of(pl.program_id(0)).start()
-
-        @pl.when(pl.program_id(0) == 0)
-        def _():
-            for index in range(3):
-                pick_of(index).start()
-
     elif first_row == 0:
         table, out_ref, wide, product = rest
     else:
@@ -146,15 +134,13 @@
         def _():
             for part in range(parts):
                 copy_of(part).wait()
-            for index in range(3):
-                pick_of(index).wait()
-
-
-def gated_chunk(meta, features, halo, first_row, count, short_filter, medium_rows, skip, weights, tables):
+
+
+def gated_chunk(meta, features, halo, first_row, count, short_filter, medium_rows, skip, weight, tables):
     kinds, rows, channels = features.shape
     length = medium_rows.shape[1]
     groups = LANES // GROUP_SIZE
-    loads = weights is not None
+    loads = weight is not None
     in_hbm = lambda x: pltpu.with_memory_space_constraint(x, pltpu.HBM)
     table_spec = pl.BlockSpec((groups * length, 2 * length), lambda i: (i, 0))
     in_specs = [
@@ -174,18 +160,16 @@
         in_specs.append(pl.BlockSpec((kinds, length + LEAD, LANES), lambda i: (0, 0, i)))
         in_specs.append(pl.BlockSpec((kinds, count, LANES), lambda i: (0, 0, i)))
         in_specs.append(table_spec)
-        operands += [halo, in_hbm(features), tables]
+        operands += [halo, features, tables]
     else:
         in_specs.append(pl.BlockSpec((kinds, rows, LANES), lambda i: (0, 0, i)))
-        operands.append(in_hbm(features))
+        operands.append(features)
         if loads:
-            weight, outer = weights
-            in_specs += [pl.BlockSpec(memory_space=pltpu.HBM)] * 2
-            operands += [in_hbm(weight), in_hbm(outer)]
-            out_specs += [pl.BlockSpec(memory_space=pltpu.VMEM)] * 2
+            in_specs.append(pl.BlockSpec(memory_space=pltpu.HBM))
+            operands.append(in_hbm(weight))
+            out_specs.append(pl.BlockSpec(memory_space=pltpu.VMEM))
             out_shape.append(pltpu.VMEM(weight.shape, weight.dtype))
-            out_shape.append(pltpu.VMEM((3, HEAD // 2, channels), outer.dtype))
-            scratch += [pltpu.SemaphoreType.DMA((channels // LANES,)), pltpu.SemaphoreType.DMA((3,))]
+            scratch.append(pltpu.SemaphoreType.DMA((channels // LANES,)))
         out_specs.append(table_spec)
         out_shape.append(jax.ShapeDtypeStruct((channels // GROUP_SIZE * length, 2 * length), BF16))
     return pl.pallas_call(
@@ -196,25 +180,24 @@
         out_shape=out_shape,
         scratch_shapes=scratch,
         compiler_params=pltpu.CompilerParams(vmem_limit_bytes=16 * MIB),
-        cost_estimate=lasting(7),
         name="hyena_filters",
     )(*operands)
 
 
 def vmem_call(body, name, micros, scalars, operands, outs, scratch=(), waits=()):
-    run = lambda *refs: body(*refs[: 1 + len(operands)], *refs[1 + len(operands) + len(waits) :])
+    given = 1 + len(operands)
+    run = lambda *refs: body(*refs[:given], *refs[given + len(waits) :])
     return pl.pallas_call(
         run,
         in_specs=[pl.BlockSpec(memory_space=pltpu.SMEM)]
-        + [pl.BlockSpec(memory_space=pltpu.VMEM)] * len(operands)
-        + [pl.BlockSpec(memory_space=pltpu.HBM)] * len(waits),
+        + [pl.BlockSpec(memory_space=pltpu.VMEM)] * (len(operands) + len(waits)),
         out_specs=[pl.BlockSpec(memory_space=pltpu.VMEM)] * len(outs),
         out_shape=[jax.ShapeDtypeStruct(shape, kind) for shape, kind in outs],
         scratch_shapes=list(scratch),
         compiler_params=pltpu.CompilerParams(vmem_limit_bytes=20 * MIB),
-        cost_estimate=lasting(micros),
+        cost_estimate=lasting(micros) if micros else None,
         name=name,
-    )(scalars, *operands, *[pltpu.with_memory_space_constraint(x, pltpu.HBM) for x in waits])
+    )(scalars, *operands, *waits)
 
 
 def columns_kernel(pieces, meta_ref, upper, lower, weight, *outs):
@@ -226,41 +209,32 @@
         outs[out][:, part * width : (part + 1) * width] = term.astype(BF16)
 
 
-def column_terms(meta, upper, lower, weight, pieces):
+def column_terms(meta, upper, lower, weight, pieces, waits=()):
     rows, width = 2 * upper.shape[0], weight.shape[1] // 8
     outs = [((rows, width * sum(p[2] == out for p in pieces)), BF16) for out in range(pieces[-1][2] + 1)]
-    return vmem_call(functools.partial(columns_kernel, pieces), "hyena_terms", 0.7 * len(pieces), meta, [upper, lower, weight], outs)
-
-
-def load_kernel(meta_ref, source, outer, _, held, own, sems):
-    channels = own.shape[1]
-    columns = pl.ds(pl.multiple_of(meta_ref[0] * channels, channels), channels)
-    copies = [
-        pltpu.make_async_copy(source, held, sems.at[0]),
-        pltpu.make_async_copy(outer.at[:, columns], own, sems.at[1]),
-    ]
-    for copy in copies:
-        copy.start()
-    for copy in copies:
-        copy.wait()
-
-
-def load(meta, weight, outer, after, channels):
-    in_hbm = lambda x: pltpu.with_memory_space_constraint(x, pltpu.HBM)
-    hbm, vmem = pl.BlockSpec(memory_space=pltpu.HBM), pl.BlockSpec(memory_space=pltpu.VMEM)
+    body = functools.partial(columns_kernel, pieces)
+    return vmem_call(body, "hyena_terms", None, meta, [upper, lower, weight], outs, waits=waits)
+
+
+def load_kernel(source, _, held, sem):
+    copy = pltpu.make_async_copy(source, held, sem)
+    copy.start()
+    copy.wait()
+
+
+def load(weight, after):
     return pl.pallas_call(
         load_kernel,
-        in_specs=[pl.BlockSpec(memory_space=pltpu.SMEM), hbm, hbm, vmem],
-        out_specs=[vmem, vmem],
-        out_shape=[pltpu.VMEM(weight.shape, weight.dtype), pltpu.VMEM((outer.shape[0], channels), outer.dtype)],
-        scratch_shapes=[pltpu.SemaphoreType.DMA((2,))],
+        in_specs=[pl.BlockSpec(memory_space=pltpu.HBM), pl.BlockSpec(memory_space=pltpu.VMEM)],
+        out_specs=pl.BlockSpec(memory_space=pltpu.VMEM),
+        out_shape=pltpu.VMEM(weight.shape, weight.dtype),
+        scratch_shapes=[pltpu.SemaphoreType.DMA],
         compiler_params=pltpu.CompilerParams(vmem_limit_bytes=4 * MIB),
-        cost_estimate=lasting(5),
-        name="load_weights",
-    )(meta, in_hbm(weight), in_hbm(outer), after)
-
-
-def stream_kernel(_, kept, direct_x, direct_y, late_x, late_y, residual, after, shares, *parts):
+        name="load_weight",
+    )(pltpu.with_memory_space_constraint(weight, pltpu.HBM), after)
+
+
+def stream_kernel(_, kept, direct_x, direct_y, late_x, late_y, residual, *parts):
     half = late_x.shape[1]
     rows = parts[0].shape[0]
     for index, out in enumerate(parts):
@@ -272,12 +246,12 @@
 
 
 def near_kernel(meta_ref, *refs):
-    halves, (gain, weight, total, square) = refs[:6], refs[6:]
-    channels = halves[0].shape[1]
+    blocks, (gain, weight, total, square) = refs[:3], refs[3:]
+    channels = blocks[0].shape[1]
     squares = jnp.zeros(square.shape, F32)
     result = None
     for index in range(3):
-        wide = jnp.concatenate([half[...] for half in halves[2 * index : 2 * index + 2]], axis=0).astype(F32)
+        wide = blocks[index][...].astype(F32)
         squares = squares + jnp.sum(wide * wide, axis=1, keepdims=True)
         span = pl.ds(pl.multiple_of(meta_ref[index] * channels, channels), channels)
         factor, block = gain[:, span], weight[span, :]
@@ -387,30 +361,75 @@
     return out, laid or made
 
 
+def pick_kernel(chips, meta_ref, weight, *refs):
+    *near, own, sems = refs
+    channels = own.shape[1]
+    columns = [pl.ds(pl.multiple_of(meta_ref[index] * channels, channels), channels) for index in range(4)]
+    copies = [pltpu.make_async_copy(weight.at[:, columns[0]], own, sems.at[0])]
+    for index, out in enumerate(near):
+        for head in range(chips // 2):
+            rows = pl.ds(pl.multiple_of((2 * head + meta_ref[5]) * HEAD, HEAD), HEAD)
+            target = out.at[head * HEAD : (head + 1) * HEAD]
+            sem = sems.at[1 + index * (chips // 2) + head]
+            copies.append(pltpu.make_async_copy(weight.at[rows, columns[index + 1]], target, sem))
+    for copy in copies:
+        copy.start()
+    for copy in copies:
+        copy.wait()
+
+
+def pick_weights(meta, weight, chips, channels):
+    rows = weight.shape[0]
+    near = jax.ShapeDtypeStruct((rows // 2, channels), BF16)
+    return pl.pallas_call(
+        functools.partial(pick_kernel, chips),
+        in_specs=[
+            pl.BlockSpec(memory_space=pltpu.SMEM),
+            pl.BlockSpec(memory_space=pltpu.HBM),
+        ],
+        out_specs=[pl.BlockSpec(memory_space=pltpu.VMEM)] * 4,
+        out_shape=[near, near, near, jax.ShapeDtypeStruct((rows, channels), BF16)],
+        scratch_shapes=[pltpu.SemaphoreType.DMA((1 + 3 * (chips // 2),))],
+        compiler_params=pltpu.CompilerParams(vmem_limit_bytes=4 * MIB),
+        name="pick_weights",
+    )(meta, pltpu.with_memory_space_constraint(weight, pltpu.HBM))
+
+
 def mix_kernel(chips, distances, streams, meta_ref, *refs):
     heads, refs = refs[:4], refs[4:]
-    before, (own_w, others_w, out, ordered) = refs[:streams], refs[streams:]
-    chip = meta_ref[4]
+    before, (own_w, *others_w), (out, ordered) = refs[:streams], refs[streams:-2], refs[-2:]
+    near_w, far_w = others_w[:3], others_w[3:]
+    chip, core = meta_ref[4], meta_ref[5]
     parity = lax.rem(chip + distances[0], 2)
     for index, distance in enumerate(distances):
         head = lax.rem(chip - distance + chips, chips)
         column = pl.ds(pl.multiple_of(head // 2 * HEAD, HEAD), HEAD)
         for source in range(4):
             ordered[source, :, column] = heads[source][index]
-    numbers = [2 * j + parity for j in range(chips // 2)]
-    weights = jnp.concatenate([own_w[pl.ds(pl.multiple_of(n * HEAD, HEAD), HEAD), :] for n in numbers], axis=0)
-    total = jnp.dot(ordered[0], weights, preferred_element_type=F32)
-    for source in range(3):
-        weights = jnp.concatenate([others_w[2 * n + part, source] for n in numbers for part in range(2)], axis=0)
-        total = total + jnp.dot(ordered[source + 1], weights, preferred_element_type=F32)
-    total = total + jnp.concatenate([part[...].astype(F32) for part in before], axis=0)
-    out[...] = total.astype(out.dtype)
-
-
-def mix(meta, heads, distances, before, own_w, others_w, kind, chips):
+    mine = jnp.concatenate(
+        [own_w[pl.ds(pl.multiple_of((2 * j + parity) * HEAD, HEAD), HEAD), :] for j in range(chips // 2)], axis=0
+    )
+
+    def finish(weights):
+        total = jnp.dot(ordered[0], mine, preferred_element_type=F32)
+        for source in range(3):
+            total = total + jnp.dot(ordered[source + 1], weights[source][...], preferred_element_type=F32)
+        total = total + jnp.concatenate([part[...].astype(F32) for part in before], axis=0)
+        out[...] = total.astype(out.dtype)
+
+    @pl.when(core == parity)
+    def _():
+        finish(near_w)
+
+    @pl.when(core != parity)
+    def _():
+        finish(far_w)
+
+
+def mix(meta, heads, distances, before, own_w, near_w, far_w, kind, chips):
     rows, channels = heads[0].shape[1], own_w.shape[1]
     body = functools.partial(mix_kernel, chips, distances, len(before))
-    operands = [*heads, *before, own_w, others_w]
+    operands = [*heads, *before, own_w, *near_w, *far_w]
     scratch = [pltpu.VMEM((4, rows, chips // 2 * HEAD), BF16)]
     return vmem_call(body, "attention_mix", 2.5, meta, operands, [((rows, channels), kind)], scratch)[0]
 
@@ -570,46 +589,48 @@
     gain = norm_gain.reshape(1, -1)
     cosine, sine = rotation_tables(meta[6:7] + jnp.arange(rows, dtype=jnp.int32))
 
-    lower, out_held, picked, tables = gated_chunk(
-        meta, by_kind, halo, chunk, chunk, short_filter, medium_rows, skip, (out_weight, attn_out), None
+    *near_w, own_w = pick_weights(meta, attn_out, chips, channels)
+    near_w = [swap_ch(weight, mask) for mask, weight in zip((1, 2, 3), near_w)]
+    far_w = [swap_core(weight) for weight in near_w]
+
+    lower, out_held, tables = gated_chunk(
+        meta, by_kind, halo, chunk, chunk, short_filter, medium_rows, skip, out_weight, None
     )
     (upper,) = gated_chunk(meta, by_kind, halo, 0, chunk, short_filter, medium_rows, skip, None, tables)
     across_x, across_y = column_terms(meta, upper, lower, out_held, ((3, 0, 0, 0), (3, 1, 1, 0)))
     across_x, across_y = swap_ch(across_x, 1), swap_ch(across_y, 2)
     pieces = ((1, 0, 0, 0), (2, 1, 1, 0), (1, 1, 2, 0), (2, 0, 3, 0), (0, 0, 4, 0), (0, 1, 4, 1))
-    direct_x, direct_y, along_x, along_y, kept = column_terms(meta, upper, lower, out_held, pieces)
+    direct_x, direct_y, along_x, along_y, kept = column_terms(meta, upper, lower, out_held, pieces, near_w)
     direct_x, direct_y = swap_ch(direct_x, 1), swap_ch(direct_y, 2)
     along_x = (along_x.astype(F32) + across_y.astype(F32)).astype(BF16)
     along_y = (along_y.astype(F32) + across_x.astype(F32)).astype(BF16)
     late_x, late_y = swap_ch(along_x, 1), swap_ch(along_y, 2)
-    qkv_held, own_w = load(meta, attn_weight, attn_out, along_y, channels)
-
-    shares = jnp.stack([swap_ch(picked[index], index + 1) for index in range(3)])
-    others_w = lax.all_gather(shares, "ctx", axis=0)
-    quarters = vmem_call(
+    qkv_held = load(attn_weight, along_y)
+    parts = vmem_call(
         stream_kernel,
         "add_stream",
         1,
         meta,
-        [kept, direct_x, direct_y, late_x, late_y, residual_in, qkv_held, shares],
-        [((rows // 4, channels), BF16)] * 4,
+        [kept, direct_x, direct_y, late_x, late_y, residual_in],
+        [((chunk, channels), BF16)] * 2,
+        waits=[qkv_held, *far_w],
     )
 
     own, other, after = [], [], None
     width = attn_weight.shape[1]
     for start in starts:
-        top, bottom = quarters[start // (rows // 4) : start // (rows // 4) + 2]
+        part = parts[start // chunk]
         if after is not None:
-            (top, bottom), _ = lax.optimization_barrier(((top, bottom), after))
-        x_top, y_bottom, x_bottom, y_top = swap_ch(top, 1), swap_ch(bottom, 2), swap_ch(bottom, 1), swap_ch(top, 2)
-        diag_a, diag_b = swap_ch(x_top, 2), swap_ch(y_bottom, 1)
-        after = diag_a, diag_b
+            part, _ = lax.optimization_barrier((part, after))
+        by_x, by_y = swap_ch(part, 1), swap_ch(part, 2)
+        after = by_x[: chunk // 2], by_y[chunk // 2 :]
+        diag_a, diag_b = swap_ch(after[0], 2), swap_ch(after[1], 1)
         near, square = vmem_call(
             near_kernel,
             "qkv_near",
             3,
             meta,
-            [top, bottom, x_top, x_bottom, y_top, y_bottom, gain, qkv_held],
+            [part, by_x, by_y, gain, qkv_held],
             [((chunk, width), F32), ((chunk, LANES), F32)],
         )
         turn = slice(start, start + chunk)
@@ -621,7 +642,6 @@
             [diag_a, diag_b, near, square, gain, cosine[turn], sine[turn], qkv_held],
             [((3, chunk, HEAD), BF16)] * chips,
             [pltpu.VMEM((chunk, width), F32)],
-            waits=[others_w] if start == starts[-1] else [],
         )
         arrived = [outs[0]] + [rotate_chips(outs[d], d) for d in range(1, chips)]
         own.append(arrived)
@@ -630,20 +650,20 @@
     other = [swap_core(jnp.stack([piece[1:] for piece in arrived])) for arrived in own]
     own, other = own[1] + own[0], other[::-1]
 
-    laid, after, before, backs = None, [], quarters, []
+    laid, before, backs = None, parts, []
     groups = [(*range(2, chips, 2), 0), tuple(range(1, chips, 2))]
     for distances in groups:
         back = []
         for distance in distances:
+            after = backs if distance == chips - 1 else []
             piece, laid = attend(meta, own, other, laid, distance, after, chips)
             back.append(rotate_chips(piece, distance) if distance else piece)
-        after = [back[0]]
         backs.append(jnp.stack(back))
     for group, (distances, kind) in enumerate(zip(groups, [F32, BF16])):
         by_x, by_y = swap_ch(backs[group], 1), swap_ch(backs[group], 2)
         by_both = swap_ch(by_x, 2) if group == 0 else swap_ch(by_y, 1)
         heads = [backs[group], by_x, by_y, by_both]
-        before = [mix(meta, heads, distances, before, own_w, others_w, kind, chips)]
+        before = [mix(meta, heads, distances, before, own_w, near_w, far_w, kind, chips)]
     return before[0]
 
 

time: 251 us -> 192 us (0.76)
  starting transfers between devices: 90.1 us -> 49 us
  local copies, waits for them, and re-layouts: 17.8 us -> 2.54 us
  waiting for transfers between devices: 65.3 us -> 79 us
  between operations: 13.8 us -> 0.34 us
    ppermute x9, starting transfers between devices: 58.3 us -> 17.9 us  [rotate_chips(): lax.ppermute(value, 'ctx', [(i, (i + 2 * distance) % count) for i in rang...]
    ppermute x27 -> x23, waiting for transfers between devices: 40.9 us -> 61 us  [swap_ch(): return lax.ppermute(value, 'ch', [(i, i ^ mask) for i in range(count)])]
    unnamed x36 -> x6, local copies, waits for them, and re-layouts: 13.5 us -> 0.01 us
    ppermute x9, waiting for transfers between devices: 20.9 us -> 16.1 us  [rotate_chips(): lax.ppermute(value, 'ctx', [(i, (i + 2 * distance) % count) for i in rang...]
    ppermute x27 -> x23, starting transfers between devices: 29.4 us -> 26.6 us  [swap_ch(): return lax.ppermute(value, 'ch', [(i, i ^ mask) for i in range(count)])]
    another operation x8, local copies, waits for them, and re-layouts: 2.8 us -> 0.08 us  [shards(): jnp.stack([piece[1:] for piece in arrived])]
    pallas_call x1 -> x2, Pallas kernels: 5.44 us -> 6.86 us  [the longest x1 4.58 us: load(): pl.pallas_call(load_kernel, in_specs=[pl.BlockSpec(memory_space=pltpu.HBM...]
  transfers between devices with their start and end apart: 40 -> 38, of which waited for: 19 -> 19; matrix products, arithmetic and copies ran while one was open for 2% -> 1% of each run, Pallas kernels for 15% -> 27%
where the time goes in v6:
time: 192 us; the launch traced here: 191 us
  waiting for transfers between devices  79 us (41%)
  Pallas kernels  58.9 us (31%)
  starting transfers between devices  49 us (26%)
  local copies, waits for them, and re-layouts  2.54 us (1%)
    ppermute x23, waiting for transfers between devices, swap_ch(): return lax.ppermute(value, 'ch', [(i, i ^ mask) for i in range(count)])  61 us
    pallas_call x13, Pallas kernels, vmem_call(): pl.pallas_call(run, in_specs=[pl.BlockSpec(memory_space=pltpu.SMEM)] + [p...  35.4 us
    ppermute x23, starting transfers between devices, swap_ch(): return lax.ppermute(value, 'ch', [(i, i ^ mask) for i in range(count)])  26.6 us
    ppermute x9, starting transfers between devices, rotate_chips(): lax.ppermute(value, 'ctx', [(i, (i + 2 * distance) % count) for i in rang...  17.9 us
    pallas_call x2, Pallas kernels, gated_chunk(): pl.pallas_call(functools.partial(gated_kernel, first_row, loads), grid=(c...  16.7 us
    ppermute x9, waiting for transfers between devices, rotate_chips(): lax.ppermute(value, 'ctx', [(i, (i + 2 * distance) % count) for i in rang...  16.1 us
    pallas_call x1, Pallas kernels, load(): pl.pallas_call(load_kernel, in_specs=[pl.BlockSpec(memory_space=pltpu.HBM...  4.58 us
  transfers between devices with their start and end apart: 38, of which 19 were waited for; matrix products, arithmetic and copies ran while one was open for 1% of the time, Pallas kernels for 27%

profile of v6, /device:TPU:0, one launch (start us, length us, event | category | flops | bytes accessed | tf_op | source)
XLA Modules:
  0.0 191.5 jit_solution(17651438911586613240)
XLA Ops:
  2.3 3.3 %collective-permute-start = (bf16[3,144,1024]{2,1,0:T(8,128)(2,1)}, bf16[3,144,1024]{2,1,0:T(8,128)(2,1)}, u32[]{:S(2)}, u32[]{:S(2)}) collective-permute-start(bf16[3,144,1024]{2,1,0:T(8,128)(2,1)} %slice.68), channel_id=1, source_target_pairs={{0,4},{4,8},{8,12},{12,16},{16,20},{20,24},{24,28},{1,5},{5,9},{9,... | collective-permute-start | bytes 2654216 | tf_op jit(solution)/shard_map/ppermute | solution.py:577
  11.9 9.1 %hyena_filters.2 = (bf16[256,1024]{1,0:T(8,128)(2,1)S(1)}, bf16[1024,4096]{1,0:T(8,128)(2,1)S(1)}, bf16[8192,256]{1,0:T(8,128)(2,1)S(1)}) custom-call(s32[8]{0:T(128)S(1)} %stack.83.refs_0_.meta_ref, f32[3,7,64]{2,1,0:T(8,128)} %refs_1_.3, f32[64,128]{1,0:T(8,128)} %bitcast.40, f32[1,1024]{1,0:T(1,128)} %bitcast.45, bf16[3,512,1024]{2,1,0:T(8,128)(2,1)S(1)} %bitcast.33, ...), custom_call_target="tpu_custom_call" | custom-call | tf_op jit(solution)/shard_map/hyena_filters/pallas_call | solution.py:175
  21.0 7.6 %hyena_filters.3.refs_1_ = bf16[256,1024]{1,0:T(8,128)(2,1)S(1)} custom-call(s32[8]{0:T(128)S(1)} %stack.83.refs_0_.meta_ref, f32[3,7,64]{2,1,0:T(8,128)} %refs_1_.3, f32[64,128]{1,0:T(8,128)} %bitcast.41, f32[1,1024]{1,0:T(1,128)} %bitcast.46, bf16[3,144,1024]{2,1,0:T(8,128)(2,1)} %collective-permute-done.refs_4_, bf16[3,512,1024]{2,1,0:T(8,128)(2,1)S(1)} %bitcast.34, ...), custom_call_target="tpu_custom_call" | custom-call | tf_op jit(solution)/shard_map/hyena_filters/pallas_call | solution.py:175
  36.7 4.0 %hyena_terms.2 = (bf16[512,512]{1,0:T(8,128)(2,1)S(1)}, bf16[512,512]{1,0:T(8,128)(2,1)S(1)}, bf16[512,512]{1,0:T(8,128)(2,1)S(1)}, bf16[512,512]{1,0:T(8,128)(2,1)S(1)}, bf16[512,1024]{1,0:T(8,128)(2,1)S(1)}) custom-call(s32[8]{0:T(128)S(1)} %stack.83.refs_0_.meta_ref, bf16[256,1024]{1,0:T(8,128)(2,1)S(1)} %hyena_filters.3.refs_1_, ...), custom_call_target="tpu_custom_call" | custom-call | tf_op jit(solution)/shard_map/hyena_terms/pallas_call | solution.py:190
  40.7 6.6 %collective-permute-done.6 = bf16[512,512]{1,0:T(8,128)(2,1)S(1)} collective-permute-done((bf16[512,512]{1,0:T(8,128)(2,1)S(1)}, bf16[512,512]{1,0:T(8,128)(2,1)S(1)}, u32[]{:S(2)}, u32[]{:S(2)}) %collective-permute-start.6) | collective-permute-done | bytes 524320 | tf_op jit(solution)/shard_map/ppermute | solution.py:29
  51.8 4.6 %load_weight.1.refs_7_.refs_5_.refs_8_ = bf16[4096,1536]{1,0:T(8,128)(2,1)S(1)} custom-call(bf16[4096,1536]{1,0:T(8,128)(2,1)} %source.1, bf16[512,512]{1,0:T(8,128)(2,1)S(1)} %add_convert_fusion._), custom_call_target="tpu_custom_call" | custom-call | tf_op jit(solution)/shard_map/load_weight/pallas_call | solution.py:226
  56.4 5.7 %collective-permute-done.4.refs_2_ = bf16[512,512]{1,0:T(8,128)(2,1)S(1)} collective-permute-done((bf16[512,512]{1,0:T(8,128)(2,1)S(1)}, bf16[512,512]{1,0:T(8,128)(2,1)S(1)}, u32[]{:S(2)}, u32[]{:S(2)}) %collective-permute-start.4) | collective-permute-done | bytes 524320 | tf_op jit(solution)/shard_map/ppermute | solution.py:29
  63.6 8.8 %collective-permute-done.7.refs_4_ = bf16[512,512]{1,0:T(8,128)(2,1)S(1)} collective-permute-done((bf16[512,512]{1,0:T(8,128)(2,1)S(1)}, bf16[512,512]{1,0:T(8,128)(2,1)S(1)}, u32[]{:S(2)}, u32[]{:S(2)}) %collective-permute-start.7) | collective-permute-done | bytes 524320 | tf_op jit(solution)/shard_map/ppermute | solution.py:29
  77.8 9.6 %collective-permute-done.13.refs_2_ = bf16[256,1024]{1,0:T(8,128)(2,1)S(1)} collective-permute-done((bf16[256,1024]{1,0:T(8,128)(2,1)S(1)}, bf16[256,1024]{1,0:T(8,128)(2,1)S(1)}, u32[]{:S(2)}, u32[]{:S(2)}) %collective-permute-start.13) | collective-permute-done | bytes 524320 | tf_op jit(solution)/shard_map/ppermute | solution.py:29
  92.3 3.2 %qkv_near.2 = (f32[256,1536]{1,0:T(8,128)S(1)}, f32[256,128]{1,0:T(8,128)S(1)}) custom-call(s32[8]{0:T(128)S(1)} %stack.83.refs_0_.meta_ref, bf16[256,1024]{1,0:T(8,128)(2,1)S(1)} %get-tuple-element.58.refs_1_.refs_6_, bf16[256,1024]{1,0:T(8,128)(2,1)S(1)} %collective-permute-done.13.refs_2_, bf16[256,1024]{1,0:T(8,128)(2,1)S(1)} %collective-permute-done.15.refs_3_, ...), custom_call_target="tpu_custom_call" | custom-call | flops 3300000000 | bytes 10800000 | tf_op jit(solution)/shard_map/qkv_near/pallas_call | solution.py:190
  95.5 10.5 %collective-permute-done.14.refs_1_ = bf16[128,1024]{1,0:T(8,128)(2,1)S(1)} collective-permute-done((bf16[128,1024]{1,0:T(8,128)(2,1)S(1)}, bf16[128,1024]{1,0:T(8,128)(2,1)S(1)}, u32[]{:S(2)}, u32[]{:S(2)}) %collective-permute-start.14) | collective-permute-done | bytes 262176 | tf_op jit(solution)/shard_map/ppermute | solution.py:29
  110.3 2.8 %collective-permute-start.19 = (bf16[3,256,128]{2,1,0:T(8,128)(2,1)S(1)}, bf16[3,256,128]{2,1,0:T(8,128)(2,1)S(1)}, u32[]{:S(2)}, u32[]{:S(2)}) collective-permute-start(bf16[3,256,128]{2,1,0:T(8,128)(2,1)S(1)} %get-tuple-element.64), channel_id=1, source_target_pairs={{0,24},{4,28},{8,0},{12,4},{16,8},{20,12},{24,16},{28,20},{1,25},{... | collective-permute-start | bytes 589832 | tf_op jit(solution)/shard_map/ppermute | solution.py:39
  115.8 3.2 %qkv_near.3 = (f32[256,1536]{1,0:T(8,128)S(1)}, f32[256,128]{1,0:T(8,128)S(1)}) custom-call(s32[8]{0:T(128)S(1)} %stack.83.refs_0_.meta_ref, bf16[256,1024]{1,0:T(8,128)(2,1)S(1)} %get-tuple-element.66.refs_1_.refs_5_, bf16[256,1024]{1,0:T(8,128)(2,1)S(1)} %collective-permute-done.20.refs_2_, bf16[256,1024]{1,0:T(8,128)(2,1)S(1)} %collective-permute-done.22.refs_3_, ...), custom_call_target="tpu_custom_call" | custom-call | flops 3300000000 | bytes 10800000 | tf_op jit(solution)/shard_map/qkv_near/pallas_call | solution.py:190
  123.9 2.8 %collective-permute-start.26 = (bf16[3,256,128]{2,1,0:T(8,128)(2,1)S(1)}, bf16[3,256,128]{2,1,0:T(8,128)(2,1)S(1)}, u32[]{:S(2)}, u32[]{:S(2)}) collective-permute-start(bf16[3,256,128]{2,1,0:T(8,128)(2,1)S(1)} %get-tuple-element.72), channel_id=1, source_target_pairs={{0,24},{4,28},{8,0},{12,4},{16,8},{20,12},{24,16},{28,20},{1,25},{... | collective-permute-start | bytes 589832 | tf_op jit(solution)/shard_map/ppermute | solution.py:39
  126.7 4.0 %collective-permute-done.24.refs_2_.refs_1_ = bf16[3,256,128]{2,1,0:T(8,128)(2,1)S(1)} collective-permute-done((bf16[3,256,128]{2,1,0:T(8,128)(2,1)S(1)}, bf16[3,256,128]{2,1,0:T(8,128)(2,1)S(1)}, u32[]{:S(2)}, u32[]{:S(2)}) %collective-permute-start.24) | collective-permute-done | bytes 196640 | tf_op jit(solution)/shard_map/ppermute | solution.py:39
  130.7 8.4 %collective-permute-done.25.refs_3_ = bf16[3,256,128]{2,1,0:T(8,128)(2,1)S(1)} collective-permute-done((bf16[3,256,128]{2,1,0:T(8,128)(2,1)S(1)}, bf16[3,256,128]{2,1,0:T(8,128)(2,1)S(1)}, u32[]{:S(2)}, u32[]{:S(2)}) %collective-permute-start.25) | collective-permute-done | bytes 196640 | tf_op jit(solution)/shard_map/ppermute | solution.py:39
  141.9 3.9 %attention.4 = (bf16[512,128]{1,0:T(8,128)(2,1)S(1)}, bf16[2,4,512,128]{3,2,1,0:T(8,128)(2,1)S(1)}, bf16[2,4,128,512]{3,2,1,0:T(8,128)(2,1)S(1)}) custom-call(s32[8]{0:T(128)S(1)} %stack.83.refs_0_.meta_ref, bf16[3,256,128]{2,1,0:T(8,128)(2,1)S(1)} %get-tuple-element.75.refs_1_, bf16[3,256,128]{2,1,0:T(8,128)(2,1)S(1)} %collective-permute-done.24.refs_2_.refs_1_, ...), custom_call_target="tpu_custom_call" | custom-call | flops 3300000000 | bytes 10800000 | tf_op jit(solution)/shard_map/attention/pallas_call | solution.py:190
  151.4 6.3 %collective-permute-start.29 = (bf16[512,128]{1,0:T(8,128)(2,1)S(1)}, bf16[512,128]{1,0:T(8,128)(2,1)S(1)}, u32[]{:S(2)}, u32[]{:S(2)}) collective-permute-start(bf16[512,128]{1,0:T(8,128)(2,1)S(1)} %attention.5), channel_id=1, source_target_pairs={{0,8},{4,12},{8,16},{12,20},{16,24},{20,28},{24,0},{28,4},{1,9},{5... | collective-permute-start | bytes 393224 | tf_op jit(solution)/shard_map/ppermute | solution.py:39
  158.5 4.7 %attention.7 = bf16[512,128]{1,0:T(8,128)(2,1)S(1)} custom-call(s32[8]{0:T(128)S(1)} %stack.83.refs_0_.meta_ref, bf16[3,256,128]{2,1,0:T(8,128)(2,1)S(1)} %collective-permute-done.24.refs_2_.refs_1_, bf16[3,256,128]{2,1,0:T(8,128)(2,1)S(1)} %collective-permute-done.17.refs_6_.refs_2_, bf16[2,4,512,128]{3,2,1,0:T(8,128)(2,1)S(1)} %get-tuple-element.81.refs_3_, ...), custom_call_target="tpu_custom_call" | custom-call | flops 3300000000 | bytes 10800000 | tf_op jit(solution)/shard_map/attention/pallas_call | solution.py:190
  164.6 3.7 %collective-permute-done.31 = bf16[512,128]{1,0:T(8,128)(2,1)S(1)} collective-permute-done((bf16[512,128]{1,0:T(8,128)(2,1)S(1)}, bf16[512,128]{1,0:T(8,128)(2,1)S(1)}, u32[]{:S(2)}, u32[]{:S(2)}) %collective-permute-start.31) | collective-permute-done | bytes 131104 | tf_op jit(solution)/shard_map/ppermute | solution.py:39
  172.2 5.4 %collective-permute-done.33.refs_3_ = bf16[2,512,128]{2,1,0:T(8,128)(2,1)S(1)} collective-permute-done((bf16[2,512,128]{2,1,0:T(8,128)(2,1)S(1)}, bf16[2,512,128]{2,1,0:T(8,128)(2,1)S(1)}, u32[]{:S(2)}, u32[]{:S(2)}) %collective-permute-start.33) | collective-permute-done | bytes 262176 | tf_op jit(solution)/shard_map/ppermute | solution.py:29
  178.9 4.3 %collective-permute-done.36.refs_3_ = bf16[2,512,128]{2,1,0:T(8,128)(2,1)S(1)} collective-permute-done((bf16[2,512,128]{2,1,0:T(8,128)(2,1)S(1)}, bf16[2,512,128]{2,1,0:T(8,128)(2,1)S(1)}, u32[]{:S(2)}, u32[]{:S(2)}) %collective-permute-start.36) | collective-permute-done | bytes 262176 | tf_op jit(solution)/shard_map/ppermute | solution.py:29
  183.2 3.0 %collective-permute-done.37.refs_4_ = bf16[2,512,128]{2,1,0:T(8,128)(2,1)S(1)} collective-permute-done((bf16[2,512,128]{2,1,0:T(8,128)(2,1)S(1)}, bf16[2,512,128]{2,1,0:T(8,128)(2,1)S(1)}, u32[]{:S(2)}, u32[]{:S(2)}) %collective-permute-start.37) | collective-permute-done | bytes 262176 | tf_op jit(solution)/shard_map/ppermute | solution.py:29
  188.5 3.0 %attention_mix.3 = bf16[512,1024]{1,0:T(8,128)(2,1)} custom-call(s32[8]{0:T(128)S(1)} %stack.83.refs_0_.meta_ref, bf16[2,512,128]{2,1,0:T(8,128)(2,1)S(1)} %pad_maximum_fusion.3.refs_1_, bf16[2,512,128]{2,1,0:T(8,128)(2,1)S(1)} %collective-permute-done.32.refs_2_, bf16[2,512,128]{2,1,0:T(8,128)(2,1)S(1)} %collective-permute-done.33.refs_3_, ...), custom_call_target="tpu_custom_call" | custom-call | flops 2750000128 | bytes 9000000 | tf_op jit(solution)/shard_map/attention_mix/pallas_call | solution.py:190
  (99 shorter events, 62.7 us)
Async XLA Ops:
  2.3 18.7 %collective-permute-start = (bf16[3,144,1024]{2,1,0:T(8,128)(2,1)}, bf16[3,144,1024]{2,1,0:T(8,128)(2,1)}, u32[]{:S(2)}, u32[]{:S(2)}) collective-permute-start(bf16[3,144,1024]{2,1,0:T(8,128)(2,1)} %slice.68), channel_id=1, source_target_pairs={{0,4},{4,8},{8,12},{12,16},{16,20},{20,24},{24,28},{1,5},{5,9},{9,... | collective-permute-start | bytes 2654216 | tf_op jit(solution)/shard_map/ppermute | solution.py:577
  8.0 26.0 %collective-permute-start.1 = (bf16[256,1024]{1,0:T(8,128)(2,1)S(1)}, bf16[256,1024]{1,0:T(8,128)(2,1)S(1)}, u32[]{:S(2)}, u32[]{:S(2)}) collective-permute-start(bf16[256,1024]{1,0:T(8,128)(2,1)S(1)} %get-tuple-element.48), channel_id=1, source_target_pairs={{0,1},{1,0},{2,3},{3,2},{4,5},{5,4},{6,7},{7,6},{8,9},{9,8},{10,11... | collective-permute-start | bytes 1572872 | tf_op jit(solution)/shard_map/ppermute | solution.py:29
  10.3 25.8 %collective-permute-start.2 = (bf16[256,1024]{1,0:T(8,128)(2,1)S(1)}, bf16[256,1024]{1,0:T(8,128)(2,1)S(1)}, u32[]{:S(2)}, u32[]{:S(2)}) collective-permute-start(bf16[256,1024]{1,0:T(8,128)(2,1)S(1)} %get-tuple-element.49), channel_id=1, source_target_pairs={{0,2},{1,3},{2,0},{3,1},{4,6},{5,7},{6,4},{7,5},{8,10},{9,11},{10,... | collective-permute-start | bytes 1572872 | tf_op jit(solution)/shard_map/ppermute | solution.py:29
  11.9 24.3 %collective-permute-start.3 = (bf16[256,1024]{1,0:T(8,128)(2,1)S(1)}, bf16[256,1024]{1,0:T(8,128)(2,1)S(1)}, u32[]{:S(2)}, u32[]{:S(2)}) collective-permute-start(bf16[256,1024]{1,0:T(8,128)(2,1)S(1)} %get-tuple-element.50), channel_id=1, source_target_pairs={{0,3},{1,2},{2,1},{3,0},{4,7},{5,6},{6,5},{7,4},{8,11},{9,10},{10,... | collective-permute-start | bytes 1572872 | tf_op jit(solution)/shard_map/ppermute | solution.py:29
  30.4 16.9 %collective-permute-start.6 = (bf16[512,512]{1,0:T(8,128)(2,1)S(1)}, bf16[512,512]{1,0:T(8,128)(2,1)S(1)}, u32[]{:S(2)}, u32[]{:S(2)}) collective-permute-start(bf16[512,512]{1,0:T(8,128)(2,1)S(1)} %get-tuple-element.55), channel_id=1, source_target_pairs={{0,2},{1,3},{2,0},{3,1},{4,6},{5,7},{6,4},{7,5},{8,10},{9,11},{10,... | collective-permute-start | bytes 1572872 | tf_op jit(solution)/shard_map/ppermute | solution.py:29
  32.5 16.2 %collective-permute-start.8 = (bf16[512,512]{1,0:T(8,128)(2,1)S(1)}, bf16[512,512]{1,0:T(8,128)(2,1)S(1)}, u32[]{:S(2)}, u32[]{:S(2)}) collective-permute-start(bf16[512,512]{1,0:T(8,128)(2,1)S(1)} %get-tuple-element.57), channel_id=1, source_target_pairs={{0,1},{1,0},{2,3},{3,2},{4,5},{5,4},{6,7},{7,6},{8,9},{9,8},{10,11... | collective-permute-start | bytes 1572872 | tf_op jit(solution)/shard_map/ppermute | solution.py:29
  34.0 15.8 %collective-permute-start.10 = (bf16[256,1024]{1,0:T(8,128)(2,1)S(1)}, bf16[256,1024]{1,0:T(8,128)(2,1)S(1)}, u32[]{:S(2)}, u32[]{:S(2)}) collective-permute-start(bf16[256,1024]{1,0:T(8,128)(2,1)S(1)} %collective-permute-done.1.refs_4_.refs_8_.refs_7_), channel_id=1, source_target_pairs={{0,4},{4,0},{8,12},{12,8},{16,20},{20,16},{24,28},{28,24},{1,5},{5... | collective-permute-start | bytes 1572872 | tf_op jit(solution)/shard_map/ppermute | solution.py:34
  36.2 15.1 %collective-permute-start.11 = (bf16[256,1024]{1,0:T(8,128)(2,1)S(1)}, bf16[256,1024]{1,0:T(8,128)(2,1)S(1)}, u32[]{:S(2)}, u32[]{:S(2)}) collective-permute-start(bf16[256,1024]{1,0:T(8,128)(2,1)S(1)} %collective-permute-done.2.refs_5_.refs_9_.refs_8_), channel_id=1, source_target_pairs={{0,4},{4,0},{8,12},{12,8},{16,20},{20,16},{24,28},{28,24},{1,5},{5... | collective-permute-start | bytes 1572872 | tf_op jit(solution)/shard_map/ppermute | solution.py:34
  36.2 20.2 %collective-permute-start.12 = (bf16[256,1024]{1,0:T(8,128)(2,1)S(1)}, bf16[256,1024]{1,0:T(8,128)(2,1)S(1)}, u32[]{:S(2)}, u32[]{:S(2)}) collective-permute-start(bf16[256,1024]{1,0:T(8,128)(2,1)S(1)} %collective-permute-done.3.refs_6_.refs_10_.refs_9_), channel_id=1, source_target_pairs={{0,4},{4,0},{8,12},{12,8},{16,20},{20,16},{24,28},{28,24},{1,5},{5... | collective-permute-start | bytes 1572872 | tf_op jit(solution)/shard_map/ppermute | solution.py:34
  47.3 14.8 %collective-permute-start.4 = (bf16[512,512]{1,0:T(8,128)(2,1)S(1)}, bf16[512,512]{1,0:T(8,128)(2,1)S(1)}, u32[]{:S(2)}, u32[]{:S(2)}) collective-permute-start(bf16[512,512]{1,0:T(8,128)(2,1)S(1)} %get-tuple-element.52), channel_id=1, source_target_pairs={{0,1},{1,0},{2,3},{3,2},{4,5},{5,4},{6,7},{7,6},{8,9},{9,8},{10,11... | collective-permute-start | bytes 1572872 | tf_op jit(solution)/shard_map/ppermute | solution.py:29
  48.7 14.9 %collective-permute-start.5 = (bf16[512,512]{1,0:T(8,128)(2,1)S(1)}, bf16[512,512]{1,0:T(8,128)(2,1)S(1)}, u32[]{:S(2)}, u32[]{:S(2)}) collective-permute-start(bf16[512,512]{1,0:T(8,128)(2,1)S(1)} %get-tuple-element.53), channel_id=1, source_target_pairs={{0,2},{1,3},{2,0},{3,1},{4,6},{5,7},{6,4},{7,5},{8,10},{9,11},{10,... | collective-permute-start | bytes 1572872 | tf_op jit(solution)/shard_map/ppermute | solution.py:29
  49.7 22.7 %collective-permute-start.7 = (bf16[512,512]{1,0:T(8,128)(2,1)S(1)}, bf16[512,512]{1,0:T(8,128)(2,1)S(1)}, u32[]{:S(2)}, u32[]{:S(2)}) collective-permute-start(bf16[512,512]{1,0:T(8,128)(2,1)S(1)} %add_convert_fusion.1), channel_id=1, source_target_pairs={{0,1},{1,0},{2,3},{3,2},{4,5},{5,4},{6,7},{7,6},{8,9},{9,8},{10,11... | collective-permute-start | bytes 1572872 | tf_op jit(solution)/shard_map/ppermute | solution.py:29
  51.3 22.3 %collective-permute-start.9 = (bf16[512,512]{1,0:T(8,128)(2,1)S(1)}, bf16[512,512]{1,0:T(8,128)(2,1)S(1)}, u32[]{:S(2)}, u32[]{:S(2)}) collective-permute-start(bf16[512,512]{1,0:T(8,128)(2,1)S(1)} %add_convert_fusion._), channel_id=1, source_target_pairs={{0,2},{1,3},{2,0},{3,1},{4,6},{5,7},{6,4},{7,5},{8,10},{9,11},{10,... | collective-permute-start | bytes 1572872 | tf_op jit(solution)/shard_map/ppermute | solution.py:29
  87.9 25.3 %collective-permute-start.20 = (bf16[256,1024]{1,0:T(8,128)(2,1)S(1)}, bf16[256,1024]{1,0:T(8,128)(2,1)S(1)}, u32[]{:S(2)}, u32[]{:S(2)}) collective-permute-start(bf16[256,1024]{1,0:T(8,128)(2,1)S(1)} %get-tuple-element.66.refs_1_.refs_5_), channel_id=1, source_target_pairs={{0,1},{1,0},{2,3},{3,2},{4,5},{5,4},{6,7},{7,6},{8,9},{9,8},{10,11... | collective-permute-start | bytes 1572872 | tf_op jit(solution)/shard_map/ppermute | solution.py:29
  89.2 25.1 %collective-permute-start.22 = (bf16[256,1024]{1,0:T(8,128)(2,1)S(1)}, bf16[256,1024]{1,0:T(8,128)(2,1)S(1)}, u32[]{:S(2)}, u32[]{:S(2)}) collective-permute-start(bf16[256,1024]{1,0:T(8,128)(2,1)S(1)} %get-tuple-element.66.refs_1_.refs_5_), channel_id=1, source_target_pairs={{0,2},{1,3},{2,0},{3,1},{4,6},{5,7},{6,4},{7,5},{8,10},{9,11},{10,... | collective-permute-start | bytes 1572872 | tf_op jit(solution)/shard_map/ppermute | solution.py:29
  90.1 15.9 %collective-permute-start.14 = (bf16[128,1024]{1,0:T(8,128)(2,1)S(1)}, bf16[128,1024]{1,0:T(8,128)(2,1)S(1)}, u32[]{:S(2)}, u32[]{:S(2)}) collective-permute-start(bf16[128,1024]{1,0:T(8,128)(2,1)S(1)} %slice.69), channel_id=1, source_target_pairs={{0,2},{1,3},{2,0},{3,1},{4,6},{5,7},{6,4},{7,5},{8,10},{9,11},{10,... | collective-permute-start | bytes 786440 | tf_op jit(solution)/shard_map/ppermute | solution.py:29
  91.5 14.5 %collective-permute-start.16 = (bf16[128,1024]{1,0:T(8,128)(2,1)S(1)}, bf16[128,1024]{1,0:T(8,128)(2,1)S(1)}, u32[]{:S(2)}, u32[]{:S(2)}) collective-permute-start(bf16[128,1024]{1,0:T(8,128)(2,1)S(1)} %slice.70), channel_id=1, source_target_pairs={{0,1},{1,0},{2,3},{3,2},{4,5},{5,4},{6,7},{7,6},{8,9},{9,8},{10,11... | collective-permute-start | bytes 786440 | tf_op jit(solution)/shard_map/ppermute | solution.py:29
  108.1 15.8 %collective-permute-start.17 = (bf16[3,256,128]{2,1,0:T(8,128)(2,1)S(1)}, bf16[3,256,128]{2,1,0:T(8,128)(2,1)S(1)}, u32[]{:S(2)}, u32[]{:S(2)}) collective-permute-start(bf16[3,256,128]{2,1,0:T(8,128)(2,1)S(1)} %get-tuple-element.62), channel_id=1, source_target_pairs={{0,8},{4,12},{8,16},{12,20},{16,24},{20,28},{24,0},{28,4},{1,9},{5... | collective-permute-start | bytes 589832 | tf_op jit(solution)/shard_map/ppermute | solution.py:39
  109.3 17.4 %collective-permute-start.18 = (bf16[3,256,128]{2,1,0:T(8,128)(2,1)S(1)}, bf16[3,256,128]{2,1,0:T(8,128)(2,1)S(1)}, u32[]{:S(2)}, u32[]{:S(2)}) collective-permute-start(bf16[3,256,128]{2,1,0:T(8,128)(2,1)S(1)} %get-tuple-element.63), channel_id=1, source_target_pairs={{0,16},{4,20},{8,24},{12,28},{16,0},{20,4},{24,8},{28,12},{1,17},{... | collective-permute-start | bytes 589832 | tf_op jit(solution)/shard_map/ppermute | solution.py:39
  110.3 16.3 %collective-permute-start.19 = (bf16[3,256,128]{2,1,0:T(8,128)(2,1)S(1)}, bf16[3,256,128]{2,1,0:T(8,128)(2,1)S(1)}, u32[]{:S(2)}, u32[]{:S(2)}) collective-permute-start(bf16[3,256,128]{2,1,0:T(8,128)(2,1)S(1)} %get-tuple-element.64), channel_id=1, source_target_pairs={{0,24},{4,28},{8,0},{12,4},{16,8},{20,12},{24,16},{28,20},{1,25},{... | collective-permute-start | bytes 589832 | tf_op jit(solution)/shard_map/ppermute | solution.py:39
  122.9 16.2 %collective-permute-start.25 = (bf16[3,256,128]{2,1,0:T(8,128)(2,1)S(1)}, bf16[3,256,128]{2,1,0:T(8,128)(2,1)S(1)}, u32[]{:S(2)}, u32[]{:S(2)}) collective-permute-start(bf16[3,256,128]{2,1,0:T(8,128)(2,1)S(1)} %get-tuple-element.71), channel_id=1, source_target_pairs={{0,16},{4,20},{8,24},{12,28},{16,0},{20,4},{24,8},{28,12},{1,17},{... | collective-permute-start | bytes 589832 | tf_op jit(solution)/shard_map/ppermute | solution.py:39
  123.9 15.2 %collective-permute-start.26 = (bf16[3,256,128]{2,1,0:T(8,128)(2,1)S(1)}, bf16[3,256,128]{2,1,0:T(8,128)(2,1)S(1)}, u32[]{:S(2)}, u32[]{:S(2)}) collective-permute-start(bf16[3,256,128]{2,1,0:T(8,128)(2,1)S(1)} %get-tuple-element.72), channel_id=1, source_target_pairs={{0,24},{4,28},{8,0},{12,4},{16,8},{20,12},{24,16},{28,20},{1,25},{... | collective-permute-start | bytes 589832 | tf_op jit(solution)/shard_map/ppermute | solution.py:39
  170.4 15.8 %collective-permute-start.37 = (bf16[2,512,128]{2,1,0:T(8,128)(2,1)S(1)}, bf16[2,512,128]{2,1,0:T(8,128)(2,1)S(1)}, u32[]{:S(2)}, u32[]{:S(2)}) collective-permute-start(bf16[2,512,128]{2,1,0:T(8,128)(2,1)S(1)} %collective-permute-done.35.refs_2_), channel_id=1, source_target_pairs={{0,2},{1,3},{2,0},{3,1},{4,6},{5,7},{6,4},{7,5},{8,10},{9,11},{10,... | collective-permute-start | bytes 786440 | tf_op jit(solution)/shard_map/ppermute | solution.py:29
  171.3 17.1 %collective-permute-start.32 = (bf16[2,512,128]{2,1,0:T(8,128)(2,1)S(1)}, bf16[2,512,128]{2,1,0:T(8,128)(2,1)S(1)}, u32[]{:S(2)}, u32[]{:S(2)}) collective-permute-start(bf16[2,512,128]{2,1,0:T(8,128)(2,1)S(1)} %pad_maximum_fusion.3.refs_1_), channel_id=1, source_target_pairs={{0,1},{1,0},{2,3},{3,2},{4,5},{5,4},{6,7},{7,6},{8,9},{9,8},{10,11... | collective-permute-start | bytes 786440 | tf_op jit(solution)/shard_map/ppermute | solution.py:29
  (17 other events, 181.8 us)

commit v7 on v6

--- a/solution.py
+++ b/solution.py
@@ -34,12 +34,17 @@
     return lax.ppermute(value, "ctx", [(i, i ^ 1) for i in range(count)])
 
 
+def shift_rows(value):
+    count = lax.axis_size("ctx")
+    return lax.ppermute(value, "ctx", [(i, i + 1) for i in range(count - 1)])
+
+
 def rotate_chips(value, distance):
     count = lax.axis_size("ctx")
     return lax.ppermute(value, "ctx", [(i, (i + 2 * distance) % count) for i in range(count)])
 
 
-def filter_tile(first_row, tile, short_ref, medium_ref, skip_ref, halo_ref, rows_ref, wide, product, table, make_table, store):
+def filter_tile(first_row, tile, short_ref, medium_ref, skip_ref, halo_ref, rows_ref, wide, product, table, store):
     taps, groups_all = short_ref.shape[1:]
     groups, length = medium_ref.shape
     span = wide.shape[1]
@@ -61,15 +66,14 @@
         for kind in range(3)
     ]
 
-    if make_table:
-        tap_row = lax.broadcasted_iota(jnp.int32, (length, 2 * length), 0)
-        place = lax.broadcasted_iota(jnp.int32, (length, 2 * length), 1)
-        turned = jnp.where(tap_row + place == length, 1.0, 0.0).astype(BF16)
-        base = jnp.dot(medium_ref[...].astype(BF16), turned, preferred_element_type=F32)
-        for group in range(groups):
-            spread = jnp.broadcast_to(base[group : group + 1, :], (length, 2 * length))
-            rolled = pltpu.roll(spread, 0, 1, stride=1, stride_axis=0)
-            table[group * length : (group + 1) * length, :] = rolled.astype(BF16)
+    tap_row = lax.broadcasted_iota(jnp.int32, (length, 2 * length), 0)
+    place = lax.broadcasted_iota(jnp.int32, (length, 2 * length), 1)
+    turned = jnp.where(tap_row + place == length, 1.0, 0.0).astype(BF16)
+    base = jnp.dot(medium_ref[...].astype(BF16), turned, preferred_element_type=F32)
+    for group in range(groups):
+        spread = jnp.broadcast_to(base[group : group + 1, :], (length, 2 * length))
+        rolled = pltpu.roll(spread, 0, 1, stride=1, stride_axis=0)
+        table[group * length : (group + 1) * length, :] = rolled.astype(BF16)
 
     def featured(kind, start):
         total = weights[kind][0:1, :] * wide[kind, start : start + length, :]
@@ -109,7 +113,7 @@
     halo_ref, rest = (rest[0], rest[1:]) if first_row == 0 else (None, rest)
     rows_ref, rest = rest[0], rest[1:]
     if loads:
-        weight, out_ref, held, table, wide, product, sems = rest
+        weight, out_ref, held, wide, product, table, sems = rest
         parts = sems.shape[0]
         height = weight.shape[0] // parts
 
@@ -118,16 +122,13 @@
             return pltpu.make_async_copy(weight.at[span, :], held.at[span, :], sems.at[part])
 
         copy_of(pl.program_id(0)).start()
-    elif first_row == 0:
-        table, out_ref, wide, product = rest
     else:
-        out_ref, table, wide, product = rest
+        out_ref, wide, product, table = rest
 
     def store(row, value):
         out_ref[row : row + value.shape[0], :] = value
 
-    make_table = first_row > 0
-    filter_tile(first_row, pl.program_id(0), *head, halo_ref, rows_ref, wide, product, table, make_table, store)
+    filter_tile(first_row, pl.program_id(0), *head, halo_ref, rows_ref, wide, product, table, store)
     if loads:
 
         @pl.when(pl.program_id(0) == pl.num_programs(0) - 1)
@@ -136,13 +137,12 @@
                 copy_of(part).wait()
 
 
-def gated_chunk(meta, features, halo, first_row, count, short_filter, medium_rows, skip, weight, tables):
+def gated_chunk(meta, features, halo, first_row, count, short_filter, medium_rows, skip, weight=None):
     kinds, rows, channels = features.shape
     length = medium_rows.shape[1]
     groups = LANES // GROUP_SIZE
     loads = weight is not None
     in_hbm = lambda x: pltpu.with_memory_space_constraint(x, pltpu.HBM)
-    table_spec = pl.BlockSpec((groups * length, 2 * length), lambda i: (i, 0))
     in_specs = [
         pl.BlockSpec(memory_space=pltpu.SMEM),
         pl.BlockSpec(short_filter.shape, lambda i: (0, 0, 0)),
@@ -155,23 +155,21 @@
     scratch = [
         pltpu.VMEM((kinds, length + LEAD + count, LANES), F32),
         pltpu.VMEM((length + count, LANES), BF16),
+        pltpu.VMEM((groups * length, 2 * length), BF16),
     ]
     if first_row == 0:
         in_specs.append(pl.BlockSpec((kinds, length + LEAD, LANES), lambda i: (0, 0, i)))
         in_specs.append(pl.BlockSpec((kinds, count, LANES), lambda i: (0, 0, i)))
-        in_specs.append(table_spec)
-        operands += [halo, features, tables]
+        operands += [halo, features]
     else:
         in_specs.append(pl.BlockSpec((kinds, rows, LANES), lambda i: (0, 0, i)))
         operands.append(features)
-        if loads:
-            in_specs.append(pl.BlockSpec(memory_space=pltpu.HBM))
-            operands.append(in_hbm(weight))
-            out_specs.append(pl.BlockSpec(memory_space=pltpu.VMEM))
-            out_shape.append(pltpu.VMEM(weight.shape, weight.dtype))
-            scratch.append(pltpu.SemaphoreType.DMA((channels // LANES,)))
-        out_specs.append(table_spec)
-        out_shape.append(jax.ShapeDtypeStruct((channels // GROUP_SIZE * length, 2 * length), BF16))
+    if loads:
+        in_specs.append(pl.BlockSpec(memory_space=pltpu.HBM))
+        operands.append(in_hbm(weight))
+        out_specs.append(pl.BlockSpec(memory_space=pltpu.VMEM))
+        out_shape.append(pltpu.VMEM(weight.shape, weight.dtype))
+        scratch.append(pltpu.SemaphoreType.DMA((channels // LANES,)))
     return pl.pallas_call(
         functools.partial(gated_kernel, first_row, loads),
         grid=(channels // LANES,),
@@ -216,22 +214,31 @@
     return vmem_call(body, "hyena_terms", None, meta, [upper, lower, weight], outs, waits=waits)
 
 
-def load_kernel(source, _, held, sem):
-    copy = pltpu.make_async_copy(source, held, sem)
-    copy.start()
-    copy.wait()
-
-
-def load(weight, after):
+def load_kernel(meta_ref, source, outer, _, held, own, sems):
+    channels = own.shape[1]
+    columns = pl.ds(pl.multiple_of(meta_ref[0] * channels, channels), channels)
+    copies = [
+        pltpu.make_async_copy(source, held, sems.at[0]),
+        pltpu.make_async_copy(outer.at[:, columns], own, sems.at[1]),
+    ]
+    for copy in copies:
+        copy.start()
+    for copy in copies:
+        copy.wait()
+
+
+def load(meta, weight, outer, after, channels):
+    in_hbm = lambda x: pltpu.with_memory_space_constraint(x, pltpu.HBM)
+    hbm, vmem = pl.BlockSpec(memory_space=pltpu.HBM), pl.BlockSpec(memory_space=pltpu.VMEM)
     return pl.pallas_call(
         load_kernel,
-        in_specs=[pl.BlockSpec(memory_space=pltpu.HBM), pl.BlockSpec(memory_space=pltpu.VMEM)],
-        out_specs=pl.BlockSpec(memory_space=pltpu.VMEM),
-        out_shape=pltpu.VMEM(weight.shape, weight.dtype),
-        scratch_shapes=[pltpu.SemaphoreType.DMA],
+        in_specs=[pl.BlockSpec(memory_space=pltpu.SMEM), hbm, hbm, vmem],
+        out_specs=[vmem, vmem],
+        out_shape=[pltpu.VMEM(weight.shape, weight.dtype), pltpu.VMEM((outer.shape[0], channels), outer.dtype)],
+        scratch_shapes=[pltpu.SemaphoreType.DMA((2,))],
         compiler_params=pltpu.CompilerParams(vmem_limit_bytes=4 * MIB),
-        name="load_weight",
-    )(pltpu.with_memory_space_constraint(weight, pltpu.HBM), after)
+        name="load_weights",
+    )(meta, in_hbm(weight), in_hbm(outer), after)
 
 
 def stream_kernel(_, kept, direct_x, direct_y, late_x, late_y, residual, *parts):
@@ -301,14 +308,16 @@
                 values[1, place, :, first : first + HEAD] = stacked[distance, 1, taken, :]
 
 
-def attention_kernel(chips, chunks, distance, leading, meta_ref, *refs):
+def attention_kernel(chips, chunks, distances, leading, meta_ref, *refs):
     if leading:
         pieces, other = refs[: chunks * chips], refs[chunks * chips : chunks * (chips + 1)]
-        out, keys, values = refs[chunks * (chips + 1) :]
+        *outs, keys, values = refs[chunks * (chips + 1) :]
         gather_keys(chips, meta_ref, pieces, other, keys, values)
-        source = pieces[(chips - distance) % chips :: chips]
+        sources = [pieces[(chips - distance) % chips :: chips] for distance in distances]
     else:
-        source, (keys, values), out = refs[:chunks], refs[chunks : chunks + 2], refs[-1]
+        taken = chunks * len(distances)
+        pieces, (keys, values), outs = refs[:taken], refs[taken : taken + 2], refs[taken + 2 :]
+        sources = [pieces[index * chunks : (index + 1) * chunks] for index in range(len(distances))]
     chip, core = meta_ref[4], meta_ref[5]
     count = keys.shape[2]
 
@@ -334,104 +343,113 @@
 
     key_row = lax.broadcasted_iota(jnp.int32, (count, count), 0)
     query_column = lax.broadcasted_iota(jnp.int32, (count, count), 1)
-    place = lax.rem(chip + distance, chips)
-    queries = jnp.concatenate([piece[0] for piece in source], axis=0)
-    mine = jnp.where(key_row <= query_column, scores_of(0, place, queries), -1e30)
-    others = jnp.where(core == 1, scores_of(1, place, queries), -1e30)
-    state = update((None, None, None), mine, others, place)
-
-    def earlier(index, state):
-        return update(state, scores_of(0, index, queries), scores_of(1, index, queries), index)
-
-    state = lax.fori_loop(0, place, earlier, state)
-    out[...] = (state[2] / state[1]).T.astype(BF16)
-
-
-def attend(meta, own, other, laid, distance, after, chips):
+    for distance, source, out in zip(distances, sources, outs):
+        place = lax.rem(chip + distance, chips)
+        queries = jnp.concatenate([piece[0] for piece in source], axis=0)
+        mine = jnp.where(key_row <= query_column, scores_of(0, place, queries), -1e30)
+        others = jnp.where(core == 1, scores_of(1, place, queries), -1e30)
+        state = update((None, None, None), mine, others, place)
+
+        def earlier(index, state):
+            return update(state, scores_of(0, index, queries), scores_of(1, index, queries), index)
+
+        state = lax.fori_loop(0, place, earlier, state)
+        out[...] = (state[2] / state[1]).T.astype(BF16)
+
+
+def attend(meta, own, other, laid, distances, chips):
     chunks, leading = len(other), laid is None
     count = own[0].shape[1] * chunks
-    outs = [((count, HEAD), BF16)]
+    outs = [((count, HEAD), BF16)] * len(distances)
     if leading:
         operands = own + other
-        outs += [((2, chips, count, HEAD), BF16), ((2, chips, HEAD, count), BF16)]
+        outs = outs + [((2, chips, count, HEAD), BF16), ((2, chips, HEAD, count), BF16)]
     else:
-        operands = [*own[(chips - distance) % chips :: chips], *laid, *after]
-    body = functools.partial(attention_kernel, chips, chunks, distance, leading)
-    out, *made = vmem_call(body, "attention", 3, meta, operands, outs)
-    return out, laid or made
-
-
-def pick_kernel(chips, meta_ref, weight, *refs):
-    *near, own, sems = refs
-    channels = own.shape[1]
-    columns = [pl.ds(pl.multiple_of(meta_ref[index] * channels, channels), channels) for index in range(4)]
-    copies = [pltpu.make_async_copy(weight.at[:, columns[0]], own, sems.at[0])]
+        operands = [piece for distance in distances for piece in own[(chips - distance) % chips :: chips]]
+        operands = [*operands, *laid]
+    body = functools.partial(attention_kernel, chips, chunks, distances, leading)
+    made = list(vmem_call(body, "attention", 6, meta, operands, outs))
+    return made[: len(distances)], laid or made[len(distances) :]
+
+
+def pick_kernel(chips, meta_ref, weight, features, *refs):
+    *near, edge, sems = refs
+    channels = near[0].shape[1]
+    kinds, count, _ = edge.shape
+    last = features.shape[1] - count
+    copies = []
+    for kind in range(kinds):
+        copies.append(
+            pltpu.make_async_copy(features.at[kind, last : last + count], edge.at[kind], sems.at[kind])
+        )
     for index, out in enumerate(near):
+        columns = pl.ds(pl.multiple_of(meta_ref[index + 1] * channels, channels), channels)
         for head in range(chips // 2):
             rows = pl.ds(pl.multiple_of((2 * head + meta_ref[5]) * HEAD, HEAD), HEAD)
             target = out.at[head * HEAD : (head + 1) * HEAD]
-            sem = sems.at[1 + index * (chips // 2) + head]
-            copies.append(pltpu.make_async_copy(weight.at[rows, columns[index + 1]], target, sem))
+            sem = sems.at[kinds + index * (chips // 2) + head]
+            copies.append(pltpu.make_async_copy(weight.at[rows, columns], target, sem))
     for copy in copies:
         copy.start()
     for copy in copies:
         copy.wait()
 
 
-def pick_weights(meta, weight, chips, channels):
-    rows = weight.shape[0]
-    near = jax.ShapeDtypeStruct((rows // 2, channels), BF16)
+def pick(meta, weight, features, count, chips):
+    kinds, _, channels = features.shape
+    near = jax.ShapeDtypeStruct((weight.shape[0] // 2, channels), BF16)
+    in_hbm = lambda x: pltpu.with_memory_space_constraint(x, pltpu.HBM)
+    hbm, vmem = pl.BlockSpec(memory_space=pltpu.HBM), pl.BlockSpec(memory_space=pltpu.VMEM)
     return pl.pallas_call(
         functools.partial(pick_kernel, chips),
-        in_specs=[
-            pl.BlockSpec(memory_space=pltpu.SMEM),
-            pl.BlockSpec(memory_space=pltpu.HBM),
-        ],
-        out_specs=[pl.BlockSpec(memory_space=pltpu.VMEM)] * 4,
-        out_shape=[near, near, near, jax.ShapeDtypeStruct((rows, channels), BF16)],
-        scratch_shapes=[pltpu.SemaphoreType.DMA((1 + 3 * (chips // 2),))],
+        in_specs=[pl.BlockSpec(memory_space=pltpu.SMEM), hbm, hbm],
+        out_specs=[vmem] * 4,
+        out_shape=[near, near, near, jax.ShapeDtypeStruct((kinds, count, channels), BF16)],
+        scratch_shapes=[pltpu.SemaphoreType.DMA((kinds + 3 * (chips // 2),))],
         compiler_params=pltpu.CompilerParams(vmem_limit_bytes=4 * MIB),
-        name="pick_weights",
-    )(meta, pltpu.with_memory_space_constraint(weight, pltpu.HBM))
-
-
-def mix_kernel(chips, distances, streams, meta_ref, *refs):
-    heads, refs = refs[:4], refs[4:]
+        name="pick",
+    )(meta, in_hbm(weight), in_hbm(features))
+
+
+def mix_kernel(chips, groups, items, streams, meta_ref, *refs):
+    heads, refs = refs[: len(items)], refs[len(items) :]
     before, (own_w, *others_w), (out, ordered) = refs[:streams], refs[streams:-2], refs[-2:]
     near_w, far_w = others_w[:3], others_w[3:]
     chip, core = meta_ref[4], meta_ref[5]
-    parity = lax.rem(chip + distances[0], 2)
-    for index, distance in enumerate(distances):
-        head = lax.rem(chip - distance + chips, chips)
-        column = pl.ds(pl.multiple_of(head // 2 * HEAD, HEAD), HEAD)
-        for source in range(4):
-            ordered[source, :, column] = heads[source][index]
-    mine = jnp.concatenate(
-        [own_w[pl.ds(pl.multiple_of((2 * j + parity) * HEAD, HEAD), HEAD), :] for j in range(chips // 2)], axis=0
-    )
-
-    def finish(weights):
-        total = jnp.dot(ordered[0], mine, preferred_element_type=F32)
-        for source in range(3):
-            total = total + jnp.dot(ordered[source + 1], weights[source][...], preferred_element_type=F32)
-        total = total + jnp.concatenate([part[...].astype(F32) for part in before], axis=0)
+    parities = [lax.rem(chip + distances[0], 2) for distances in groups]
+    for place, (group, _) in enumerate(items):
+        for index, distance in enumerate(groups[group]):
+            head = lax.rem(chip - distance + chips, chips)
+            column = pl.ds(pl.multiple_of(head // 2 * HEAD, HEAD), HEAD)
+            ordered[place, :, column] = heads[place][index]
+
+    def own_rows(parity):
+        rows = [pl.ds(pl.multiple_of((2 * j + parity) * HEAD, HEAD), HEAD) for j in range(chips // 2)]
+        return jnp.concatenate([own_w[span, :] for span in rows], axis=0)
+
+    def finish(by_group):
+        total = jnp.concatenate([part[...].astype(F32) for part in before], axis=0)
+        for place, (group, source) in enumerate(items):
+            weights = by_group[group][source - 1][...] if source else own_rows(parities[group])
+            total = total + jnp.dot(ordered[place], weights, preferred_element_type=F32)
         out[...] = total.astype(out.dtype)
 
-    @pl.when(core == parity)
+    @pl.when(core == parities[0])
     def _():
-        finish(near_w)
-
-    @pl.when(core != parity)
+        finish([near_w, far_w])
+
+    @pl.when(core != parities[0])
     def _():
-        finish(far_w)
-
-
-def mix(meta, heads, distances, before, own_w, near_w, far_w, kind, chips):
+        finish([far_w, near_w])
+
+
+def mix(meta, heads, groups, items, before, own_w, near_w, far_w, kind, chips):
     rows, channels = heads[0].shape[1], own_w.shape[1]
-    body = functools.partial(mix_kernel, chips, distances, len(before))
+    body = functools.partial(mix_kernel, chips, groups, items, len(before))
     operands = [*heads, *before, own_w, *near_w, *far_w]
-    scratch = [pltpu.VMEM((4, rows, chips // 2 * HEAD), BF16)]
-    return vmem_call(body, "attention_mix", 2.5, meta, operands, [((rows, channels), kind)], scratch)[0]
+    scratch = [pltpu.VMEM((len(items), rows, chips // 2 * HEAD), BF16)]
+    micros = 0.6 * len(items)
+    return vmem_call(body, "attention_mix", micros, meta, operands, [((rows, channels), kind)], scratch)[0]
 
 
 def rotate_rows(block, positions):
@@ -573,15 +591,14 @@
     meta = jnp.stack(scalars).astype(jnp.int32)
 
     by_kind = jnp.transpose(features, (1, 0, 2))
-    count = lax.axis_size("ctx")
-    halo = lax.ppermute(by_kind[:, rows - length - LEAD :], "ctx", [(i, i + 1) for i in range(count - 1)])
     medium_rows = medium_filter.T
     skip = skip_gain.reshape(1, channels)
 
     starts = [rows - chunk, 0]
     if lax.axis_size("ch") != 4 or attn_weight.shape[1] != 3 * HEAD * chips or chips % 2:
-        lower, tables = gated_chunk(meta, by_kind, halo, chunk, chunk, short_filter, medium_rows, skip, None, None)
-        (upper,) = gated_chunk(meta, by_kind, halo, 0, chunk, short_filter, medium_rows, skip, None, tables)
+        halo = shift_rows(by_kind[:, rows - length - LEAD :])
+        (lower,) = gated_chunk(meta, by_kind, halo, chunk, chunk, short_filter, medium_rows, skip)
+        (upper,) = gated_chunk(meta, by_kind, halo, 0, chunk, short_filter, medium_rows, skip)
         return after_gating(
             jnp.concatenate([upper, lower], axis=0), residual_in, out_weight, norm_gain, attn_weight, attn_out
         )
@@ -589,14 +606,13 @@
     gain = norm_gain.reshape(1, -1)
     cosine, sine = rotation_tables(meta[6:7] + jnp.arange(rows, dtype=jnp.int32))
 
-    *near_w, own_w = pick_weights(meta, attn_out, chips, channels)
+    *near_w, edge = pick(meta, attn_out, by_kind, length + LEAD, chips)
+    halo = shift_rows(edge)
     near_w = [swap_ch(weight, mask) for mask, weight in zip((1, 2, 3), near_w)]
     far_w = [swap_core(weight) for weight in near_w]
 
-    lower, out_held, tables = gated_chunk(
-        meta, by_kind, halo, chunk, chunk, short_filter, medium_rows, skip, out_weight, None
-    )
-    (upper,) = gated_chunk(meta, by_kind, halo, 0, chunk, short_filter, medium_rows, skip, None, tables)
+    lower, out_held = gated_chunk(meta, by_kind, halo, chunk, chunk, short_filter, medium_rows, skip, out_weight)
+    (upper,) = gated_chunk(meta, by_kind, halo, 0, chunk, short_filter, medium_rows, skip)
     across_x, across_y = column_terms(meta, upper, lower, out_held, ((3, 0, 0, 0), (3, 1, 1, 0)))
     across_x, across_y = swap_ch(across_x, 1), swap_ch(across_y, 2)
     pieces = ((1, 0, 0, 0), (2, 1, 1, 0), (1, 1, 2, 0), (2, 0, 3, 0), (0, 0, 4, 0), (0, 1, 4, 1))
@@ -605,7 +621,7 @@
     along_x = (along_x.astype(F32) + across_y.astype(F32)).astype(BF16)
     along_y = (along_y.astype(F32) + across_x.astype(F32)).astype(BF16)
     late_x, late_y = swap_ch(along_x, 1), swap_ch(along_y, 2)
-    qkv_held = load(attn_weight, along_y)
+    qkv_held, own_w = load(meta, attn_weight, attn_out, along_y, channels)
     parts = vmem_call(
         stream_kernel,
         "add_stream",
@@ -623,8 +639,7 @@
         if after is not None:
             part, _ = lax.optimization_barrier((part, after))
         by_x, by_y = swap_ch(part, 1), swap_ch(part, 2)
-        after = by_x[: chunk // 2], by_y[chunk // 2 :]
-        diag_a, diag_b = swap_ch(after[0], 2), swap_ch(after[1], 1)
+        diag_a, diag_b = swap_ch(by_x[: chunk // 2], 2), swap_ch(by_y[chunk // 2 :], 1)
         near, square = vmem_call(
             near_kernel,
             "qkv_near",
@@ -633,6 +648,7 @@
             [part, by_x, by_y, gain, qkv_held],
             [((chunk, width), F32), ((chunk, LANES), F32)],
         )
+        after = diag_a, diag_b
         turn = slice(start, start + chunk)
         outs = vmem_call(
             functools.partial(far_kernel, chips),
@@ -650,21 +666,22 @@
     other = [swap_core(jnp.stack([piece[1:] for piece in arrived])) for arrived in own]
     own, other = own[1] + own[0], other[::-1]
 
-    laid, before, backs = None, parts, []
     groups = [(*range(2, chips, 2), 0), tuple(range(1, chips, 2))]
-    for distances in groups:
-        back = []
-        for distance in distances:
-            after = backs if distance == chips - 1 else []
-            piece, laid = attend(meta, own, other, laid, distance, after, chips)
-            back.append(rotate_chips(piece, distance) if distance else piece)
-        backs.append(jnp.stack(back))
-    for group, (distances, kind) in enumerate(zip(groups, [F32, BF16])):
-        by_x, by_y = swap_ch(backs[group], 1), swap_ch(backs[group], 2)
+    given, laid = attend(meta, own, other, None, groups[0], chips)
+    first = [rotate_chips(piece, d) if d else piece for d, piece in zip(groups[0], given)]
+    given, _ = attend(meta, own, other, laid, groups[1], chips)
+    first, given = lax.optimization_barrier((first, given))
+    second = [rotate_chips(piece, d) for d, piece in zip(groups[1], given)]
+    heads, places = [], []
+    for group, back in enumerate([first, second]):
+        back = jnp.stack(back)
+        by_x, by_y = swap_ch(back, 1), swap_ch(back, 2)
         by_both = swap_ch(by_x, 2) if group == 0 else swap_ch(by_y, 1)
-        heads = [backs[group], by_x, by_y, by_both]
-        before = [mix(meta, heads, distances, before, own_w, near_w, far_w, kind, chips)]
-    return before[0]
+        heads += [back, by_x, by_y, by_both]
+        places += [(group, source) for source in range(4)]
+    weights = own_w, near_w, far_w
+    early = mix(meta, heads[:-1], groups, places[:-1], parts, *weights, F32, chips)
+    return mix(meta, heads[-1:], groups, places[-1:], [early], *weights, BF16, chips)
 
 
 def solution(mesh):

time: 192 us -> 183 us (0.953)
  waiting for transfers between devices: 79 us -> 72.9 us
  local copies, waits for them, and re-layouts: 2.54 us -> 0.25 us
    ppermute x23, waiting for transfers between devices: 61 us -> 53.2 us  [swap_ch(): return lax.ppermute(value, 'ch', [(i, i ^ mask) for i in range(count)])]
    slice x5 -> x4, local copies, waits for them, and re-layouts: 2.36 us -> 0.07 us  [the longest x2 0.04 us: shards(): by_x[:chunk // 2]]
    pallas_call x13 -> x11, Pallas kernels: 35.4 us -> 34 us  [vmem_call(): pl.pallas_call(run, in_specs=[pl.BlockSpec(memory_space=pltpu.SMEM)] + [p...]
  transfers between devices with their start and end apart: 38 -> 38, of which waited for: 19 -> 20; matrix products, arithmetic and copies ran while one was open for 1% -> 1% of each run, Pallas kernels for 27% -> 26%
where the time goes in v7:
time: 183 us
  waiting for transfers between devices  72.9 us (40%)
  Pallas kernels  58.2 us (32%)
  starting transfers between devices  49.7 us (27%)
    ppermute x23, waiting for transfers between devices, swap_ch(): return lax.ppermute(value, 'ch', [(i, i ^ mask) for i in range(count)])  53.2 us
    pallas_call x11, Pallas kernels, vmem_call(): pl.pallas_call(run, in_specs=[pl.BlockSpec(memory_space=pltpu.SMEM)] + [p...  34 us
    ppermute x23, starting transfers between devices, swap_ch(): return lax.ppermute(value, 'ch', [(i, i ^ mask) for i in range(count)])  27.6 us
    ppermute x9, waiting for transfers between devices, rotate_chips(): lax.ppermute(value, 'ctx', [(i, (i + 2 * distance) % count) for i in rang...  17.7 us
    ppermute x9, starting transfers between devices, rotate_chips(): lax.ppermute(value, 'ctx', [(i, (i + 2 * distance) % count) for i in rang...  16.7 us
    pallas_call x2, Pallas kernels, gated_chunk(): pl.pallas_call(functools.partial(gated_kernel, first_row, loads), grid=(c...  16.3 us
    pallas_call x1, Pallas kernels, load(): pl.pallas_call(load_kernel, in_specs=[pl.BlockSpec(memory_space=pltpu.SME...  5.36 us
  transfers between devices with their start and end apart: 38, of which 20 were waited for; matrix products, arithmetic and copies ran while one was open for 1% of the time, Pallas kernels for 26%

profile of v7, /device:TPU:0, one launch (start us, length us, event | category | flops | bytes accessed | tf_op | source)
XLA Modules:
  0.0 183.0 jit_solution(15116584303911418859)
XLA Ops:
  9.0 8.9 %hyena_filters.3 = (bf16[256,1024]{1,0:T(8,128)(2,1)S(1)}, bf16[1024,4096]{1,0:T(8,128)(2,1)S(1)}) custom-call(s32[8]{0:T(128)S(1)} %stack.83.meta_ref.refs_0_, f32[3,7,64]{2,1,0:T(8,128)} %refs_1_.3, f32[64,128]{1,0:T(8,128)} %bitcast.40, f32[1,1024]{1,0:T(1,128)} %bitcast.45, bf16[3,512,1024]{2,1,0:T(8,128)(2,1)S(1)} %bitcast.33, bf16[1024,4096]{1,0:T(8,128)(2,1)} %refs_5_.1), custom_call_target="tpu_custom_call" | custom-call | tf_op jit(solution)/shard_map/hyena_filters/pallas_call | solution.py:173
  17.9 7.4 %hyena_filters.2.refs_1_ = bf16[256,1024]{1,0:T(8,128)(2,1)S(1)} custom-call(s32[8]{0:T(128)S(1)} %stack.83.meta_ref.refs_0_, f32[3,7,64]{2,1,0:T(8,128)} %refs_1_.3, f32[64,128]{1,0:T(8,128)} %bitcast.41, f32[1,1024]{1,0:T(1,128)} %bitcast.46, bf16[3,144,1024]{2,1,0:T(8,128)(2,1)S(1)} %collective-permute-done.refs_4_, bf16[3,512,1024]{2,1,0:T(8,128)(2,1)S(1)} %bitcast.34), custom_call_target="tpu_custom_call" | custom-call | tf_op jit(solution)/shard_map/hyena_filters/pallas_call | solution.py:173
  34.0 4.0 %hyena_terms.2 = (bf16[512,512]{1,0:T(8,128)(2,1)S(1)}, bf16[512,512]{1,0:T(8,128)(2,1)S(1)}, bf16[512,512]{1,0:T(8,128)(2,1)S(1)}, bf16[512,512]{1,0:T(8,128)(2,1)S(1)}, bf16[512,1024]{1,0:T(8,128)(2,1)S(1)}) custom-call(s32[8]{0:T(128)S(1)} %stack.83.meta_ref.refs_0_, bf16[256,1024]{1,0:T(8,128)(2,1)S(1)} %hyena_filters.2.refs_1_, ...), custom_call_target="tpu_custom_call" | custom-call | tf_op jit(solution)/shard_map/hyena_terms/pallas_call | solution.py:188
  38.0 6.4 %collective-permute-done.6 = bf16[512,512]{1,0:T(8,128)(2,1)S(1)} collective-permute-done((bf16[512,512]{1,0:T(8,128)(2,1)S(1)}, bf16[512,512]{1,0:T(8,128)(2,1)S(1)}, u32[]{:S(2)}, u32[]{:S(2)}) %collective-permute-start.6) | collective-permute-done | bytes 524320 | tf_op jit(solution)/shard_map/ppermute | solution.py:29
  48.8 5.4 %load_weights.1 = (bf16[4096,1536]{1,0:T(8,128)(2,1)S(1)}, bf16[512,1024]{1,0:T(8,128)(2,1)S(1)}) custom-call(s32[8]{0:T(128)S(1)} %stack.83.meta_ref.refs_0_, bf16[4096,1536]{1,0:T(8,128)(2,1)} %source.1, bf16[512,4096]{1,0:T(8,128)(2,1)} %outer.1, bf16[512,512]{1,0:T(8,128)(2,1)S(1)} %add_convert_fusion._), custom_call_target="tpu_custom_call" | custom-call | tf_op jit(solution)/shard_map/load_weights/pallas_call | solution.py:233
  54.2 4.9 %collective-permute-done.4.refs_2_ = bf16[512,512]{1,0:T(8,128)(2,1)S(1)} collective-permute-done((bf16[512,512]{1,0:T(8,128)(2,1)S(1)}, bf16[512,512]{1,0:T(8,128)(2,1)S(1)}, u32[]{:S(2)}, u32[]{:S(2)}) %collective-permute-start.4) | collective-permute-done | bytes 524320 | tf_op jit(solution)/shard_map/ppermute | solution.py:29
  60.7 8.9 %collective-permute-done.7.refs_4_ = bf16[512,512]{1,0:T(8,128)(2,1)S(1)} collective-permute-done((bf16[512,512]{1,0:T(8,128)(2,1)S(1)}, bf16[512,512]{1,0:T(8,128)(2,1)S(1)}, u32[]{:S(2)}, u32[]{:S(2)}) %collective-permute-start.7) | collective-permute-done | bytes 524320 | tf_op jit(solution)/shard_map/ppermute | solution.py:29
  74.2 10.5 %collective-permute-done.13.refs_2_ = bf16[256,1024]{1,0:T(8,128)(2,1)S(1)} collective-permute-done((bf16[256,1024]{1,0:T(8,128)(2,1)S(1)}, bf16[256,1024]{1,0:T(8,128)(2,1)S(1)}, u32[]{:S(2)}, u32[]{:S(2)}) %collective-permute-start.13) | collective-permute-done | bytes 524320 | tf_op jit(solution)/shard_map/ppermute | solution.py:29
  94.6 3.2 %qkv_near.2 = (f32[256,1536]{1,0:T(8,128)S(1)}, f32[256,128]{1,0:T(8,128)S(1)}) custom-call(s32[8]{0:T(128)S(1)} %stack.83.meta_ref.refs_0_, bf16[256,1024]{1,0:T(8,128)(2,1)S(1)} %get-tuple-element.67.refs_1_.refs_9_, bf16[256,1024]{1,0:T(8,128)(2,1)S(1)} %collective-permute-done.13.refs_2_, bf16[256,1024]{1,0:T(8,128)(2,1)S(1)} %collective-permute-done.15.refs_3_, ...), custom_call_target="tpu_custom_call" | custom-call | flops 3300000000 | bytes 10800000 | tf_op jit(solution)/shard_map/qkv_near/pallas_call | solution.py:188
  102.8 2.8 %collective-permute-start.19 = (bf16[3,256,128]{2,1,0:T(8,128)(2,1)S(1)}, bf16[3,256,128]{2,1,0:T(8,128)(2,1)S(1)}, u32[]{:S(2)}, u32[]{:S(2)}) collective-permute-start(bf16[3,256,128]{2,1,0:T(8,128)(2,1)S(1)} %get-tuple-element.73), channel_id=1, source_target_pairs={{0,24},{4,28},{8,0},{12,4},{16,8},{20,12},{24,16},{28,20},{1,25},{... | collective-permute-start | bytes 589832 | tf_op jit(solution)/shard_map/ppermute | solution.py:44
  107.9 3.2 %qkv_near.3 = (f32[256,1536]{1,0:T(8,128)S(1)}, f32[256,128]{1,0:T(8,128)S(1)}) custom-call(s32[8]{0:T(128)S(1)} %stack.83.meta_ref.refs_0_, bf16[256,1024]{1,0:T(8,128)(2,1)S(1)} %get-tuple-element.75.refs_1_.refs_8_, bf16[256,1024]{1,0:T(8,128)(2,1)S(1)} %collective-permute-done.20.refs_2_, bf16[256,1024]{1,0:T(8,128)(2,1)S(1)} %collective-permute-done.22.refs_3_, ...), custom_call_target="tpu_custom_call" | custom-call | flops 3300000000 | bytes 10800000 | tf_op jit(solution)/shard_map/qkv_near/pallas_call | solution.py:188
  117.4 2.8 %collective-permute-start.26 = (bf16[3,256,128]{2,1,0:T(8,128)(2,1)S(1)}, bf16[3,256,128]{2,1,0:T(8,128)(2,1)S(1)}, u32[]{:S(2)}, u32[]{:S(2)}) collective-permute-start(bf16[3,256,128]{2,1,0:T(8,128)(2,1)S(1)} %get-tuple-element.81), channel_id=1, source_target_pairs={{0,24},{4,28},{8,0},{12,4},{16,8},{20,12},{24,16},{28,20},{1,25},{... | collective-permute-start | bytes 589832 | tf_op jit(solution)/shard_map/ppermute | solution.py:44
  120.2 3.2 %collective-permute-done.24.refs_2_.refs_3_ = bf16[3,256,128]{2,1,0:T(8,128)(2,1)S(1)} collective-permute-done((bf16[3,256,128]{2,1,0:T(8,128)(2,1)S(1)}, bf16[3,256,128]{2,1,0:T(8,128)(2,1)S(1)}, u32[]{:S(2)}, u32[]{:S(2)}) %collective-permute-start.24) | collective-permute-done | bytes 196640 | tf_op jit(solution)/shard_map/ppermute | solution.py:44
  123.5 7.7 %collective-permute-done.25.refs_3_ = bf16[3,256,128]{2,1,0:T(8,128)(2,1)S(1)} collective-permute-done((bf16[3,256,128]{2,1,0:T(8,128)(2,1)S(1)}, bf16[3,256,128]{2,1,0:T(8,128)(2,1)S(1)}, u32[]{:S(2)}, u32[]{:S(2)}) %collective-permute-start.25) | collective-permute-done | bytes 196640 | tf_op jit(solution)/shard_map/ppermute | solution.py:44
  134.0 4.8 %attention.2 = (bf16[512,128]{1,0:T(8,128)(2,1)S(1)}, bf16[512,128]{1,0:T(8,128)(2,1)S(1)}, bf16[2,4,512,128]{3,2,1,0:T(8,128)(2,1)S(1)}, bf16[2,4,128,512]{3,2,1,0:T(8,128)(2,1)S(1)}) custom-call(s32[8]{0:T(128)S(1)} %stack.83.meta_ref.refs_0_, bf16[3,256,128]{2,1,0:T(8,128)(2,1)S(1)} %get-tuple-element.82.refs_1_, ...), custom_call_target="tpu_custom_call" | custom-call | flops 6600000000 | bytes 21600000 | tf_op jit(solution)/shard_map/attention/pallas_call | solution.py:188
  138.9 2.8 %collective-permute-start.29 = (bf16[512,128]{1,0:T(8,128)(2,1)S(1)}, bf16[512,128]{1,0:T(8,128)(2,1)S(1)}, u32[]{:S(2)}, u32[]{:S(2)}) collective-permute-start(bf16[512,128]{1,0:T(8,128)(2,1)S(1)} %get-tuple-element.90), channel_id=1, source_target_pairs={{0,16},{4,20},{8,24},{12,28},{16,0},{20,4},{24,8},{28,12},{1,17},{... | collective-permute-start | bytes 393224 | tf_op jit(solution)/shard_map/ppermute | solution.py:44
  141.7 6.7 %attention.3 = (bf16[512,128]{1,0:T(8,128)(2,1)S(1)}, bf16[512,128]{1,0:T(8,128)(2,1)S(1)}) custom-call(s32[8]{0:T(128)S(1)} %stack.83.meta_ref.refs_0_, bf16[3,256,128]{2,1,0:T(8,128)(2,1)S(1)} %collective-permute-done.26.refs_4_.refs_1_, bf16[3,256,128]{2,1,0:T(8,128)(2,1)S(1)} %collective-permute-done.19.refs_8_.refs_2_, ...), custom_call_target="tpu_custom_call" | custom-call | flops 6600000000 | bytes 21600000 | tf_op jit(solution)/shard_map/attention/pallas_call | solution.py:188
  149.9 3.6 %collective-permute-start.31 = (bf16[512,128]{1,0:T(8,128)(2,1)S(1)}, bf16[512,128]{1,0:T(8,128)(2,1)S(1)}, u32[]{:S(2)}, u32[]{:S(2)}) collective-permute-start(bf16[512,128]{1,0:T(8,128)(2,1)S(1)} %get-tuple-element.97), channel_id=1, source_target_pairs={{0,24},{4,28},{8,0},{12,4},{16,8},{20,12},{24,16},{28,20},{1,25},{... | collective-permute-start | bytes 393224 | tf_op jit(solution)/shard_map/ppermute | solution.py:44
  153.5 3.7 %collective-permute-done.31 = bf16[512,128]{1,0:T(8,128)(2,1)S(1)} collective-permute-done((bf16[512,128]{1,0:T(8,128)(2,1)S(1)}, bf16[512,128]{1,0:T(8,128)(2,1)S(1)}, u32[]{:S(2)}, u32[]{:S(2)}) %collective-permute-start.31) | collective-permute-done | bytes 131104 | tf_op jit(solution)/shard_map/ppermute | solution.py:44
  157.2 3.1 %collective-permute-done.30 = bf16[512,128]{1,0:T(8,128)(2,1)S(1)} collective-permute-done((bf16[512,128]{1,0:T(8,128)(2,1)S(1)}, bf16[512,128]{1,0:T(8,128)(2,1)S(1)}, u32[]{:S(2)}, u32[]{:S(2)}) %collective-permute-start.30) | collective-permute-done | bytes 131104 | tf_op jit(solution)/shard_map/ppermute | solution.py:44
  164.8 4.8 %collective-permute-done.32.refs_7_ = bf16[2,512,128]{2,1,0:T(8,128)(2,1)S(1)} collective-permute-done((bf16[2,512,128]{2,1,0:T(8,128)(2,1)S(1)}, bf16[2,512,128]{2,1,0:T(8,128)(2,1)S(1)}, u32[]{:S(2)}, u32[]{:S(2)}) %collective-permute-start.32) | collective-permute-done | bytes 262176 | tf_op jit(solution)/shard_map/ppermute | solution.py:29
  170.5 4.5 %collective-permute-done.35.refs_3_ = bf16[2,512,128]{2,1,0:T(8,128)(2,1)S(1)} collective-permute-done((bf16[2,512,128]{2,1,0:T(8,128)(2,1)S(1)}, bf16[2,512,128]{2,1,0:T(8,128)(2,1)S(1)}, u32[]{:S(2)}, u32[]{:S(2)}) %collective-permute-start.35) | collective-permute-done | bytes 262176 | tf_op jit(solution)/shard_map/ppermute | solution.py:29
  175.0 2.8 %collective-permute-done.36.refs_4_ = bf16[2,512,128]{2,1,0:T(8,128)(2,1)S(1)} collective-permute-done((bf16[2,512,128]{2,1,0:T(8,128)(2,1)S(1)}, bf16[2,512,128]{2,1,0:T(8,128)(2,1)S(1)}, u32[]{:S(2)}, u32[]{:S(2)}) %collective-permute-start.36) | collective-permute-done | bytes 262176 | tf_op jit(solution)/shard_map/ppermute | solution.py:29
  177.9 3.2 %attention_mix.2.refs_2_ = f32[512,1024]{1,0:T(8,128)S(1)} custom-call(s32[8]{0:T(128)S(1)} %stack.83.meta_ref.refs_0_, bf16[2,512,128]{2,1,0:T(8,128)(2,1)S(1)} %pad_maximum_fusion.3.refs_1_, bf16[2,512,128]{2,1,0:T(8,128)(2,1)S(1)} %collective-permute-done.34.refs_2_, bf16[2,512,128]{2,1,0:T(8,128)(2,1)S(1)} %collective-permute-done.35.refs_3_, ...), custom_call_target="tpu_custom_call" | custom-call | flops 4620000256 | bytes 15120000 | tf_op jit(solution)/shard_map/attention_mix/pallas_call | solution.py:188
  (96 shorter events, 63.4 us)
Async XLA Ops:
  2.6 15.3 %collective-permute-start = (bf16[3,144,1024]{2,1,0:T(8,128)(2,1)S(1)}, bf16[3,144,1024]{2,1,0:T(8,128)(2,1)S(1)}, u32[]{:S(2)}, u32[]{:S(2)}) collective-permute-start(bf16[3,144,1024]{2,1,0:T(8,128)(2,1)S(1)} %get-tuple-element.53), channel_id=1, source_target_pairs={{0,4},{4,8},{8,12},{12,16},{16,20},{20,24},{24,28},{1,5},{5,9},{9,... | collective-permute-start | bytes 2654216 | tf_op jit(solution)/shard_map/ppermute | solution.py:39
  5.1 25.6 %collective-permute-start.1 = (bf16[256,1024]{1,0:T(8,128)(2,1)S(1)}, bf16[256,1024]{1,0:T(8,128)(2,1)S(1)}, u32[]{:S(2)}, u32[]{:S(2)}) collective-permute-start(bf16[256,1024]{1,0:T(8,128)(2,1)S(1)} %get-tuple-element.56), channel_id=1, source_target_pairs={{0,1},{1,0},{2,3},{3,2},{4,5},{5,4},{6,7},{7,6},{8,9},{9,8},{10,11... | collective-permute-start | bytes 1572872 | tf_op jit(solution)/shard_map/ppermute | solution.py:29
  7.4 24.6 %collective-permute-start.2 = (bf16[256,1024]{1,0:T(8,128)(2,1)S(1)}, bf16[256,1024]{1,0:T(8,128)(2,1)S(1)}, u32[]{:S(2)}, u32[]{:S(2)}) collective-permute-start(bf16[256,1024]{1,0:T(8,128)(2,1)S(1)} %get-tuple-element.57), channel_id=1, source_target_pairs={{0,2},{1,3},{2,0},{3,1},{4,6},{5,7},{6,4},{7,5},{8,10},{9,11},{10,... | collective-permute-start | bytes 1572872 | tf_op jit(solution)/shard_map/ppermute | solution.py:29
  9.0 25.0 %collective-permute-start.3 = (bf16[256,1024]{1,0:T(8,128)(2,1)S(1)}, bf16[256,1024]{1,0:T(8,128)(2,1)S(1)}, u32[]{:S(2)}, u32[]{:S(2)}) collective-permute-start(bf16[256,1024]{1,0:T(8,128)(2,1)S(1)} %get-tuple-element.58), channel_id=1, source_target_pairs={{0,3},{1,2},{2,1},{3,0},{4,7},{5,6},{6,5},{7,4},{8,11},{9,10},{10,... | collective-permute-start | bytes 1572872 | tf_op jit(solution)/shard_map/ppermute | solution.py:29
  27.1 17.2 %collective-permute-start.6 = (bf16[512,512]{1,0:T(8,128)(2,1)S(1)}, bf16[512,512]{1,0:T(8,128)(2,1)S(1)}, u32[]{:S(2)}, u32[]{:S(2)}) collective-permute-start(bf16[512,512]{1,0:T(8,128)(2,1)S(1)} %get-tuple-element.63), channel_id=1, source_target_pairs={{0,2},{1,3},{2,0},{3,1},{4,6},{5,7},{6,4},{7,5},{8,10},{9,11},{10,... | collective-permute-start | bytes 1572872 | tf_op jit(solution)/shard_map/ppermute | solution.py:29
  29.2 16.6 %collective-permute-start.8 = (bf16[512,512]{1,0:T(8,128)(2,1)S(1)}, bf16[512,512]{1,0:T(8,128)(2,1)S(1)}, u32[]{:S(2)}, u32[]{:S(2)}) collective-permute-start(bf16[512,512]{1,0:T(8,128)(2,1)S(1)} %get-tuple-element.65), channel_id=1, source_target_pairs={{0,1},{1,0},{2,3},{3,2},{4,5},{5,4},{6,7},{7,6},{8,9},{9,8},{10,11... | collective-permute-start | bytes 1572872 | tf_op jit(solution)/shard_map/ppermute | solution.py:29
  30.7 16.0 %collective-permute-start.10 = (bf16[256,1024]{1,0:T(8,128)(2,1)S(1)}, bf16[256,1024]{1,0:T(8,128)(2,1)S(1)}, u32[]{:S(2)}, u32[]{:S(2)}) collective-permute-start(bf16[256,1024]{1,0:T(8,128)(2,1)S(1)} %collective-permute-done.1.refs_4_.refs_11_), channel_id=1, source_target_pairs={{0,4},{4,0},{8,12},{12,8},{16,20},{20,16},{24,28},{28,24},{1,5},{5... | collective-permute-start | bytes 1572872 | tf_op jit(solution)/shard_map/ppermute | solution.py:34
  32.0 16.2 %collective-permute-start.11 = (bf16[256,1024]{1,0:T(8,128)(2,1)S(1)}, bf16[256,1024]{1,0:T(8,128)(2,1)S(1)}, u32[]{:S(2)}, u32[]{:S(2)}) collective-permute-start(bf16[256,1024]{1,0:T(8,128)(2,1)S(1)} %collective-permute-done.2.refs_5_.refs_12_), channel_id=1, source_target_pairs={{0,4},{4,0},{8,12},{12,8},{16,20},{20,16},{24,28},{28,24},{1,5},{5... | collective-permute-start | bytes 1572872 | tf_op jit(solution)/shard_map/ppermute | solution.py:34
  34.0 20.3 %collective-permute-start.12 = (bf16[256,1024]{1,0:T(8,128)(2,1)S(1)}, bf16[256,1024]{1,0:T(8,128)(2,1)S(1)}, u32[]{:S(2)}, u32[]{:S(2)}) collective-permute-start(bf16[256,1024]{1,0:T(8,128)(2,1)S(1)} %collective-permute-done.3.refs_6_.refs_13_), channel_id=1, source_target_pairs={{0,4},{4,0},{8,12},{12,8},{16,20},{20,16},{24,28},{28,24},{1,5},{5... | collective-permute-start | bytes 1572872 | tf_op jit(solution)/shard_map/ppermute | solution.py:34
  44.3 14.8 %collective-permute-start.4 = (bf16[512,512]{1,0:T(8,128)(2,1)S(1)}, bf16[512,512]{1,0:T(8,128)(2,1)S(1)}, u32[]{:S(2)}, u32[]{:S(2)}) collective-permute-start(bf16[512,512]{1,0:T(8,128)(2,1)S(1)} %get-tuple-element.60), channel_id=1, source_target_pairs={{0,1},{1,0},{2,3},{3,2},{4,5},{5,4},{6,7},{7,6},{8,9},{9,8},{10,11... | collective-permute-start | bytes 1572872 | tf_op jit(solution)/shard_map/ppermute | solution.py:29
  45.8 14.9 %collective-permute-start.5 = (bf16[512,512]{1,0:T(8,128)(2,1)S(1)}, bf16[512,512]{1,0:T(8,128)(2,1)S(1)}, u32[]{:S(2)}, u32[]{:S(2)}) collective-permute-start(bf16[512,512]{1,0:T(8,128)(2,1)S(1)} %get-tuple-element.61), channel_id=1, source_target_pairs={{0,2},{1,3},{2,0},{3,1},{4,6},{5,7},{6,4},{7,5},{8,10},{9,11},{10,... | collective-permute-start | bytes 1572872 | tf_op jit(solution)/shard_map/ppermute | solution.py:29
  46.7 22.9 %collective-permute-start.7 = (bf16[512,512]{1,0:T(8,128)(2,1)S(1)}, bf16[512,512]{1,0:T(8,128)(2,1)S(1)}, u32[]{:S(2)}, u32[]{:S(2)}) collective-permute-start(bf16[512,512]{1,0:T(8,128)(2,1)S(1)} %add_convert_fusion.1), channel_id=1, source_target_pairs={{0,1},{1,0},{2,3},{3,2},{4,5},{5,4},{6,7},{7,6},{8,9},{9,8},{10,11... | collective-permute-start | bytes 1572872 | tf_op jit(solution)/shard_map/ppermute | solution.py:29
  48.2 22.6 %collective-permute-start.9 = (bf16[512,512]{1,0:T(8,128)(2,1)S(1)}, bf16[512,512]{1,0:T(8,128)(2,1)S(1)}, u32[]{:S(2)}, u32[]{:S(2)}) collective-permute-start(bf16[512,512]{1,0:T(8,128)(2,1)S(1)} %add_convert_fusion._), channel_id=1, source_target_pairs={{0,2},{1,3},{2,0},{3,1},{4,6},{5,7},{6,4},{7,5},{8,10},{9,11},{10,... | collective-permute-start | bytes 1572872 | tf_op jit(solution)/shard_map/ppermute | solution.py:29
  72.7 13.1 %collective-permute-start.15 = (bf16[256,1024]{1,0:T(8,128)(2,1)S(1)}, bf16[256,1024]{1,0:T(8,128)(2,1)S(1)}, u32[]{:S(2)}, u32[]{:S(2)}) collective-permute-start(bf16[256,1024]{1,0:T(8,128)(2,1)S(1)} %get-tuple-element.67.refs_1_.refs_9_), channel_id=1, source_target_pairs={{0,2},{1,3},{2,0},{3,1},{4,6},{5,7},{6,4},{7,5},{8,10},{9,11},{10,... | collective-permute-start | bytes 1572872 | tf_op jit(solution)/shard_map/ppermute | solution.py:29
  92.5 13.1 %collective-permute-start.20 = (bf16[256,1024]{1,0:T(8,128)(2,1)S(1)}, bf16[256,1024]{1,0:T(8,128)(2,1)S(1)}, u32[]{:S(2)}, u32[]{:S(2)}) collective-permute-start(bf16[256,1024]{1,0:T(8,128)(2,1)S(1)} %get-tuple-element.75.refs_1_.refs_8_), channel_id=1, source_target_pairs={{0,1},{1,0},{2,3},{3,2},{4,5},{5,4},{6,7},{7,6},{8,9},{9,8},{10,11... | collective-permute-start | bytes 1572872 | tf_op jit(solution)/shard_map/ppermute | solution.py:29
  94.0 13.3 %collective-permute-start.22 = (bf16[256,1024]{1,0:T(8,128)(2,1)S(1)}, bf16[256,1024]{1,0:T(8,128)(2,1)S(1)}, u32[]{:S(2)}, u32[]{:S(2)}) collective-permute-start(bf16[256,1024]{1,0:T(8,128)(2,1)S(1)} %get-tuple-element.75.refs_1_.refs_8_), channel_id=1, source_target_pairs={{0,2},{1,3},{2,0},{3,1},{4,6},{5,7},{6,4},{7,5},{8,10},{9,11},{10,... | collective-permute-start | bytes 1572872 | tf_op jit(solution)/shard_map/ppermute | solution.py:29
  99.9 17.5 %collective-permute-start.17 = (bf16[3,256,128]{2,1,0:T(8,128)(2,1)S(1)}, bf16[3,256,128]{2,1,0:T(8,128)(2,1)S(1)}, u32[]{:S(2)}, u32[]{:S(2)}) collective-permute-start(bf16[3,256,128]{2,1,0:T(8,128)(2,1)S(1)} %get-tuple-element.71), channel_id=1, source_target_pairs={{0,8},{4,12},{8,16},{12,20},{16,24},{20,28},{24,0},{28,4},{1,9},{5... | collective-permute-start | bytes 589832 | tf_op jit(solution)/shard_map/ppermute | solution.py:44
  101.7 18.5 %collective-permute-start.18 = (bf16[3,256,128]{2,1,0:T(8,128)(2,1)S(1)}, bf16[3,256,128]{2,1,0:T(8,128)(2,1)S(1)}, u32[]{:S(2)}, u32[]{:S(2)}) collective-permute-start(bf16[3,256,128]{2,1,0:T(8,128)(2,1)S(1)} %get-tuple-element.72), channel_id=1, source_target_pairs={{0,16},{4,20},{8,24},{12,28},{16,0},{20,4},{24,8},{28,12},{1,17},{... | collective-permute-start | bytes 589832 | tf_op jit(solution)/shard_map/ppermute | solution.py:44
  102.8 17.4 %collective-permute-start.19 = (bf16[3,256,128]{2,1,0:T(8,128)(2,1)S(1)}, bf16[3,256,128]{2,1,0:T(8,128)(2,1)S(1)}, u32[]{:S(2)}, u32[]{:S(2)}) collective-permute-start(bf16[3,256,128]{2,1,0:T(8,128)(2,1)S(1)} %get-tuple-element.73), channel_id=1, source_target_pairs={{0,24},{4,28},{8,0},{12,4},{16,8},{20,12},{24,16},{28,20},{1,25},{... | collective-permute-start | bytes 589832 | tf_op jit(solution)/shard_map/ppermute | solution.py:44
  116.3 14.9 %collective-permute-start.25 = (bf16[3,256,128]{2,1,0:T(8,128)(2,1)S(1)}, bf16[3,256,128]{2,1,0:T(8,128)(2,1)S(1)}, u32[]{:S(2)}, u32[]{:S(2)}) collective-permute-start(bf16[3,256,128]{2,1,0:T(8,128)(2,1)S(1)} %get-tuple-element.80), channel_id=1, source_target_pairs={{0,16},{4,20},{8,24},{12,28},{16,0},{20,4},{24,8},{28,12},{1,17},{... | collective-permute-start | bytes 589832 | tf_op jit(solution)/shard_map/ppermute | solution.py:44
  117.4 13.8 %collective-permute-start.26 = (bf16[3,256,128]{2,1,0:T(8,128)(2,1)S(1)}, bf16[3,256,128]{2,1,0:T(8,128)(2,1)S(1)}, u32[]{:S(2)}, u32[]{:S(2)}) collective-permute-start(bf16[3,256,128]{2,1,0:T(8,128)(2,1)S(1)} %get-tuple-element.81), channel_id=1, source_target_pairs={{0,24},{4,28},{8,0},{12,4},{16,8},{20,12},{24,16},{28,20},{1,25},{... | collective-permute-start | bytes 589832 | tf_op jit(solution)/shard_map/ppermute | solution.py:44
  148.4 14.9 %collective-permute-start.34 = (bf16[2,512,128]{2,1,0:T(8,128)(2,1)S(1)}, bf16[2,512,128]{2,1,0:T(8,128)(2,1)S(1)}, u32[]{:S(2)}, u32[]{:S(2)}) collective-permute-start(bf16[2,512,128]{2,1,0:T(8,128)(2,1)S(1)} %pad_maximum_fusion.3.refs_1_), channel_id=1, source_target_pairs={{0,1},{1,0},{2,3},{3,2},{4,5},{5,4},{6,7},{7,6},{8,9},{9,8},{10,11... | collective-permute-start | bytes 786440 | tf_op jit(solution)/shard_map/ppermute | solution.py:29
  161.3 13.8 %collective-permute-start.35 = (bf16[2,512,128]{2,1,0:T(8,128)(2,1)S(1)}, bf16[2,512,128]{2,1,0:T(8,128)(2,1)S(1)}, u32[]{:S(2)}, u32[]{:S(2)}) collective-permute-start(bf16[2,512,128]{2,1,0:T(8,128)(2,1)S(1)} %pad_maximum_fusion.3.refs_1_), channel_id=1, source_target_pairs={{0,2},{1,3},{2,0},{3,1},{4,6},{5,7},{6,4},{7,5},{8,10},{9,11},{10,... | collective-permute-start | bytes 786440 | tf_op jit(solution)/shard_map/ppermute | solution.py:29
  163.3 14.6 %collective-permute-start.36 = (bf16[2,512,128]{2,1,0:T(8,128)(2,1)S(1)}, bf16[2,512,128]{2,1,0:T(8,128)(2,1)S(1)}, u32[]{:S(2)}, u32[]{:S(2)}) collective-permute-start(bf16[2,512,128]{2,1,0:T(8,128)(2,1)S(1)} %collective-permute-done.34.refs_2_), channel_id=1, source_target_pairs={{0,2},{1,3},{2,0},{3,1},{4,6},{5,7},{6,4},{7,5},{8,10},{9,11},{10,... | collective-permute-start | bytes 786440 | tf_op jit(solution)/shard_map/ppermute | solution.py:29
  (17 other events, 164.9 us)

commit v8 on v7

--- a/solution.py
+++ b/solution.py
@@ -29,9 +29,9 @@
     return lax.ppermute(value, "ch", [(i, i ^ mask) for i in range(count)])
 
 
-def swap_core(value):
+def swap_ctx(value, mask):
     count = lax.axis_size("ctx")
-    return lax.ppermute(value, "ctx", [(i, i ^ 1) for i in range(count)])
+    return lax.ppermute(value, "ctx", [(i, i ^ mask) for i in range(count)])
 
 
 def shift_rows(value):
@@ -46,7 +46,10 @@
 
 def filter_tile(first_row, tile, short_ref, medium_ref, skip_ref, halo_ref, rows_ref, wide, product, table, store):
     taps, groups_all = short_ref.shape[1:]
-    groups, length = medium_ref.shape
+    length = medium_ref.shape[1]
+    groups = LANES // GROUP_SIZE
+    medium = medium_ref[pl.ds(pl.multiple_of(tile * groups, groups), groups), :]
+    gain = skip_ref[:, pl.ds(pl.multiple_of(tile * LANES, LANES), LANES)]
     span = wide.shape[1]
     halo_rows = length + LEAD
     count = span - halo_rows
@@ -69,7 +72,7 @@
     tap_row = lax.broadcasted_iota(jnp.int32, (length, 2 * length), 0)
     place = lax.broadcasted_iota(jnp.int32, (length, 2 * length), 1)
     turned = jnp.where(tap_row + place == length, 1.0, 0.0).astype(BF16)
-    base = jnp.dot(medium_ref[...].astype(BF16), turned, preferred_element_type=F32)
+    base = jnp.dot(medium.astype(BF16), turned, preferred_element_type=F32)
     for group in range(groups):
         spread = jnp.broadcast_to(base[group : group + 1, :], (length, 2 * length))
         rolled = pltpu.roll(spread, 0, 1, stride=1, stride_axis=0)
@@ -103,7 +106,7 @@
             mixed = jnp.where(group_of == group, spread[group * length : (group + 1) * length], mixed)
         for part in range(2):
             row = begin + part * length
-            direct = skip_ref[...] * product[row + length : row + 2 * length, :].astype(F32)
+            direct = gain * product[row + length : row + 2 * length, :].astype(F32)
             gate = featured(0, halo_rows + row)
             store(row, (gate * (mixed[:, part * LANES : (part + 1) * LANES] + direct)).astype(BF16))
 
@@ -146,8 +149,8 @@
     in_specs = [
         pl.BlockSpec(memory_space=pltpu.SMEM),
         pl.BlockSpec(short_filter.shape, lambda i: (0, 0, 0)),
-        pl.BlockSpec((groups, length), lambda i: (i, 0)),
-        pl.BlockSpec((1, LANES), lambda i: (0, i)),
+        pl.BlockSpec(medium_rows.shape, lambda i: (0, 0)),
+        pl.BlockSpec(skip.shape, lambda i: (0, 0)),
     ]
     operands = [meta, in_hbm(short_filter), in_hbm(medium_rows), in_hbm(skip)]
     out_specs = [pl.BlockSpec((count, LANES), lambda i: (0, i))]
@@ -372,7 +375,7 @@
     return made[: len(distances)], laid or made[len(distances) :]
 
 
-def pick_kernel(chips, meta_ref, weight, features, *refs):
+def pick_kernel(meta_ref, weight, features, *refs):
     *near, edge, sems = refs
     channels = near[0].shape[1]
     kinds, count, _ = edge.shape
@@ -382,30 +385,27 @@
         copies.append(
             pltpu.make_async_copy(features.at[kind, last : last + count], edge.at[kind], sems.at[kind])
         )
+    rows = pl.ds(pl.multiple_of((2 * lax.rem(meta_ref[4], 2) + meta_ref[5]) * HEAD, HEAD), HEAD)
     for index, out in enumerate(near):
         columns = pl.ds(pl.multiple_of(meta_ref[index + 1] * channels, channels), channels)
-        for head in range(chips // 2):
-            rows = pl.ds(pl.multiple_of((2 * head + meta_ref[5]) * HEAD, HEAD), HEAD)
-            target = out.at[head * HEAD : (head + 1) * HEAD]
-            sem = sems.at[kinds + index * (chips // 2) + head]
-            copies.append(pltpu.make_async_copy(weight.at[rows, columns], target, sem))
+        copies.append(pltpu.make_async_copy(weight.at[rows, columns], out, sems.at[kinds + index]))
     for copy in copies:
         copy.start()
     for copy in copies:
         copy.wait()
 
 
-def pick(meta, weight, features, count, chips):
+def pick(meta, weight, features, count):
     kinds, _, channels = features.shape
-    near = jax.ShapeDtypeStruct((weight.shape[0] // 2, channels), BF16)
+    near = jax.ShapeDtypeStruct((HEAD, channels), BF16)
     in_hbm = lambda x: pltpu.with_memory_space_constraint(x, pltpu.HBM)
     hbm, vmem = pl.BlockSpec(memory_space=pltpu.HBM), pl.BlockSpec(memory_space=pltpu.VMEM)
     return pl.pallas_call(
-        functools.partial(pick_kernel, chips),
+        pick_kernel,
         in_specs=[pl.BlockSpec(memory_space=pltpu.SMEM), hbm, hbm],
         out_specs=[vmem] * 4,
         out_shape=[near, near, near, jax.ShapeDtypeStruct((kinds, count, channels), BF16)],
-        scratch_shapes=[pltpu.SemaphoreType.DMA((kinds + 3 * (chips // 2),))],
+        scratch_shapes=[pltpu.SemaphoreType.DMA((kinds + 3,))],
         compiler_params=pltpu.CompilerParams(vmem_limit_bytes=4 * MIB),
         name="pick",
     )(meta, in_hbm(weight), in_hbm(features))
@@ -413,9 +413,9 @@
 
 def mix_kernel(chips, groups, items, streams, meta_ref, *refs):
     heads, refs = refs[: len(items)], refs[len(items) :]
-    before, (own_w, *others_w), (out, ordered) = refs[:streams], refs[streams:-2], refs[-2:]
-    near_w, far_w = others_w[:3], others_w[3:]
+    before, (own_w, near_w, far_w, out, ordered) = refs[:streams], refs[streams:]
     chip, core = meta_ref[4], meta_ref[5]
+    swapped = lax.rem(chip, 2)
     parities = [lax.rem(chip + distances[0], 2) for distances in groups]
     for place, (group, _) in enumerate(items):
         for index, distance in enumerate(groups[group]):
@@ -430,7 +430,11 @@
     def finish(by_group):
         total = jnp.concatenate([part[...].astype(F32) for part in before], axis=0)
         for place, (group, source) in enumerate(items):
-            weights = by_group[group][source - 1][...] if source else own_rows(parities[group])
+            if source:
+                held = by_group[group]
+                weights = jnp.concatenate([held[swapped, source - 1], held[1 - swapped, source - 1]], axis=0)
+            else:
+                weights = own_rows(parities[group])
             total = total + jnp.dot(ordered[place], weights, preferred_element_type=F32)
         out[...] = total.astype(out.dtype)
 
@@ -446,7 +450,7 @@
 def mix(meta, heads, groups, items, before, own_w, near_w, far_w, kind, chips):
     rows, channels = heads[0].shape[1], own_w.shape[1]
     body = functools.partial(mix_kernel, chips, groups, items, len(before))
-    operands = [*heads, *before, own_w, *near_w, *far_w]
+    operands = [*heads, *before, own_w, near_w, far_w]
     scratch = [pltpu.VMEM((len(items), rows, chips // 2 * HEAD), BF16)]
     micros = 0.6 * len(items)
     return vmem_call(body, "attention_mix", micros, meta, operands, [((rows, channels), kind)], scratch)[0]
@@ -595,7 +599,7 @@
     skip = skip_gain.reshape(1, channels)
 
     starts = [rows - chunk, 0]
-    if lax.axis_size("ch") != 4 or attn_weight.shape[1] != 3 * HEAD * chips or chips % 2:
+    if lax.axis_size("ch") != 4 or attn_weight.shape[1] != 3 * HEAD * chips or chips != 4:
         halo = shift_rows(by_kind[:, rows - length - LEAD :])
         (lower,) = gated_chunk(meta, by_kind, halo, chunk, chunk, short_filter, medium_rows, skip)
         (upper,) = gated_chunk(meta, by_kind, halo, 0, chunk, short_filter, medium_rows, skip)
@@ -606,21 +610,26 @@
     gain = norm_gain.reshape(1, -1)
     cosine, sine = rotation_tables(meta[6:7] + jnp.arange(rows, dtype=jnp.int32))
 
-    *near_w, edge = pick(meta, attn_out, by_kind, length + LEAD, chips)
+    *near_w, edge = pick(meta, attn_out, by_kind, length + LEAD)
     halo = shift_rows(edge)
-    near_w = [swap_ch(weight, mask) for mask, weight in zip((1, 2, 3), near_w)]
-    far_w = [swap_core(weight) for weight in near_w]
+    picked = [swap_ch(weight, mask) for mask, weight in zip((1, 2, 3), near_w)]
 
     lower, out_held = gated_chunk(meta, by_kind, halo, chunk, chunk, short_filter, medium_rows, skip, out_weight)
     (upper,) = gated_chunk(meta, by_kind, halo, 0, chunk, short_filter, medium_rows, skip)
+    picked, _ = lax.optimization_barrier((picked, upper))
+    picked = jnp.stack(picked)
+    swapped = swap_ctx(picked, 2)
     across_x, across_y = column_terms(meta, upper, lower, out_held, ((3, 0, 0, 0), (3, 1, 1, 0)))
     across_x, across_y = swap_ch(across_x, 1), swap_ch(across_y, 2)
     pieces = ((1, 0, 0, 0), (2, 1, 1, 0), (1, 1, 2, 0), (2, 0, 3, 0), (0, 0, 4, 0), (0, 1, 4, 1))
-    direct_x, direct_y, along_x, along_y, kept = column_terms(meta, upper, lower, out_held, pieces, near_w)
+    direct_x, direct_y, along_x, along_y, kept = column_terms(meta, upper, lower, out_held, pieces, [picked])
     direct_x, direct_y = swap_ch(direct_x, 1), swap_ch(direct_y, 2)
     along_x = (along_x.astype(F32) + across_y.astype(F32)).astype(BF16)
     along_y = (along_y.astype(F32) + across_x.astype(F32)).astype(BF16)
     late_x, late_y = swap_ch(along_x, 1), swap_ch(along_y, 2)
+    swapped, _ = lax.optimization_barrier((swapped, along_y))
+    near_w = jnp.stack([picked, swapped])
+    far_w = swap_ctx(near_w, 1)
     qkv_held, own_w = load(meta, attn_weight, attn_out, along_y, channels)
     parts = vmem_call(
         stream_kernel,
@@ -629,7 +638,7 @@
         meta,
         [kept, direct_x, direct_y, late_x, late_y, residual_in],
         [((chunk, channels), BF16)] * 2,
-        waits=[qkv_held, *far_w],
+        waits=[qkv_held, far_w],
     )
 
     own, other, after = [], [], None
@@ -648,7 +657,7 @@
             [part, by_x, by_y, gain, qkv_held],
             [((chunk, width), F32), ((chunk, LANES), F32)],
         )
-        after = diag_a, diag_b
+        after = diag_a, diag_b, square
         turn = slice(start, start + chunk)
         outs = vmem_call(
             functools.partial(far_kernel, chips),
@@ -663,7 +672,7 @@
         own.append(arrived)
 
     own, _ = lax.optimization_barrier((own, outs))
-    other = [swap_core(jnp.stack([piece[1:] for piece in arrived])) for arrived in own]
+    other = [swap_ctx(jnp.stack([piece[1:] for piece in arrived]), 1) for arrived in own]
     own, other = own[1] + own[0], other[::-1]
 
     groups = [(*range(2, chips, 2), 0), tuple(range(1, chips, 2))]
@@ -672,13 +681,14 @@
     given, _ = attend(meta, own, other, laid, groups[1], chips)
     first, given = lax.optimization_barrier((first, given))
     second = [rotate_chips(piece, d) for d, piece in zip(groups[1], given)]
-    heads, places = [], []
-    for group, back in enumerate([first, second]):
-        back = jnp.stack(back)
-        by_x, by_y = swap_ch(back, 1), swap_ch(back, 2)
-        by_both = swap_ch(by_x, 2) if group == 0 else swap_ch(by_y, 1)
-        heads += [back, by_x, by_y, by_both]
-        places += [(group, source) for source in range(4)]
+    back = jnp.stack(first)
+    by_x, by_y = swap_ch(back, 1), swap_ch(back, 2)
+    second, by_x, by_y = lax.optimization_barrier((second, by_x, by_y))
+    heads = [back, by_x, by_y, swap_ch(by_x, 2)]
+    back = jnp.stack(second)
+    by_x, by_y = swap_ch(back, 1), swap_ch(back, 2)
+    heads += [back, by_x, by_y, swap_ch(by_y, 1)]
+    places = [(group, source) for group in range(2) for source in range(4)]
     weights = own_w, near_w, far_w
     early = mix(meta, heads[:-1], groups, places[:-1], parts, *weights, F32, chips)
     return mix(meta, heads[-1:], groups, places[-1:], [early], *weights, BF16, chips)

time: 183 us -> 194 us (1.060)
  waiting for transfers between devices: 72.9 us -> 85 us
    ppermute x5 -> x4, waiting for transfers between devices: 1.95 us -> 9.73 us  [swap_ctx(): return lax.ppermute(value, 'ctx', [(i, i ^ mask) for i in range(count)])]
    ppermute x23, waiting for transfers between devices: 53.2 us -> 60.4 us  [swap_ch(): return lax.ppermute(value, 'ch', [(i, i ^ mask) for i in range(count)])]
    ppermute x23, starting transfers between devices: 27.6 us -> 24.4 us  [swap_ch(): return lax.ppermute(value, 'ch', [(i, i ^ mask) for i in range(count)])]
    ppermute x9, waiting for transfers between devices: 17.7 us -> 14.9 us  [rotate_chips(): lax.ppermute(value, 'ctx', [(i, (i + 2 * distance) % count) for i in rang...]
    ppermute x9, starting transfers between devices: 16.7 us -> 18.7 us  [rotate_chips(): lax.ppermute(value, 'ctx', [(i, (i + 2 * distance) % count) for i in rang...]
  transfers between devices with their start and end apart: 38 -> 37, of which waited for: 20 -> 21; matrix products, arithmetic and copies ran while one was open for 1% -> 1% of each run, Pallas kernels for 26% -> 24%
where the time goes in v8:
time: 194 us
  waiting for transfers between devices  85 us (44%)
  Pallas kernels  58.2 us (30%)
  starting transfers between devices  47.9 us (25%)
  other arithmetic  1.94 us (1%)
    ppermute x23, waiting for transfers between devices, swap_ch(): return lax.ppermute(value, 'ch', [(i, i ^ mask) for i in range(count)])  60.4 us
    pallas_call x11, Pallas kernels, vmem_call(): pl.pallas_call(run, in_specs=[pl.BlockSpec(memory_space=pltpu.SMEM)] + [p...  34 us
    ppermute x23, starting transfers between devices, swap_ch(): return lax.ppermute(value, 'ch', [(i, i ^ mask) for i in range(count)])  24.4 us
    ppermute x9, starting transfers between devices, rotate_chips(): lax.ppermute(value, 'ctx', [(i, (i + 2 * distance) % count) for i in rang...  18.7 us
    pallas_call x2, Pallas kernels, gated_chunk(): pl.pallas_call(functools.partial(gated_kernel, first_row, loads), grid=(c...  16.5 us
    ppermute x9, waiting for transfers between devices, rotate_chips(): lax.ppermute(value, 'ctx', [(i, (i + 2 * distance) % count) for i in rang...  14.9 us
    ppermute x4, waiting for transfers between devices, swap_ctx(): return lax.ppermute(value, 'ctx', [(i, i ^ mask) for i in range(count)])  9.73 us
    pallas_call x1, Pallas kernels, load(): pl.pallas_call(load_kernel, in_specs=[pl.BlockSpec(memory_space=pltpu.SME...  5.36 us
  transfers between devices with their start and end apart: 37, of which 21 were waited for; matrix products, arithmetic and copies ran while one was open for 1% of the time, Pallas kernels for 24%

profile of v8, /device:TPU:0, one launch (start us, length us, event | category | flops | bytes accessed | tf_op | source)
XLA Modules:
  0.0 193.6 jit_solution(8306332975017185576)
XLA Ops:
  8.7 9.0 %hyena_filters.3 = (bf16[256,1024]{1,0:T(8,128)(2,1)S(1)}, bf16[1024,4096]{1,0:T(8,128)(2,1)S(1)}) custom-call(s32[8]{0:T(128)S(1)} %stack.104.meta_ref.refs_0_, f32[3,7,64]{2,1,0:T(8,128)} %refs_1_.3, f32[64,128]{1,0:T(8,128)} %bitcast.50, f32[1,1024]{1,0:T(1,128)} %bitcast.55, bf16[3,512,1024]{2,1,0:T(8,128)(2,1)S(1)} %bitcast.39, bf16[1024,4096]{1,0:T(8,128)(2,1)} %refs_5_.1), custom_call_target="tpu_custom_call" | custom-call | tf_op jit(solution)/shard_map/hyena_filters/pallas_call | solution.py:176
  17.7 7.5 %hyena_filters.2.refs_1_ = bf16[256,1024]{1,0:T(8,128)(2,1)S(1)} custom-call(s32[8]{0:T(128)S(1)} %stack.104.meta_ref.refs_0_, f32[3,7,64]{2,1,0:T(8,128)} %refs_1_.3, f32[64,128]{1,0:T(8,128)} %bitcast.51, f32[1,1024]{1,0:T(1,128)} %bitcast.56, bf16[3,144,1024]{2,1,0:T(8,128)(2,1)S(1)} %collective-permute-done.refs_4_, bf16[3,512,1024]{2,1,0:T(8,128)(2,1)S(1)} %bitcast.40), custom_call_target="tpu_custom_call" | custom-call | tf_op jit(solution)/shard_map/hyena_filters/pallas_call | solution.py:176
  31.0 4.0 %hyena_terms.2 = (bf16[512,512]{1,0:T(8,128)(2,1)S(1)}, bf16[512,512]{1,0:T(8,128)(2,1)S(1)}, bf16[512,512]{1,0:T(8,128)(2,1)S(1)}, bf16[512,512]{1,0:T(8,128)(2,1)S(1)}, bf16[512,1024]{1,0:T(8,128)(2,1)S(1)}) custom-call(s32[8]{0:T(128)S(1)} %stack.104.meta_ref.refs_0_, bf16[256,1024]{1,0:T(8,128)(2,1)S(1)} %hyena_filters.2.refs_1_, ...), custom_call_target="tpu_custom_call" | custom-call | tf_op jit(solution)/shard_map/hyena_terms/pallas_call | solution.py:191
  35.0 6.6 %collective-permute-done.8 = bf16[512,512]{1,0:T(8,128)(2,1)S(1)} collective-permute-done((bf16[512,512]{1,0:T(8,128)(2,1)S(1)}, bf16[512,512]{1,0:T(8,128)(2,1)S(1)}, u32[]{:S(2)}, u32[]{:S(2)}) %collective-permute-start.8) | collective-permute-done | bytes 524320 | tf_op jit(solution)/shard_map/ppermute | solution.py:29
  41.7 7.7 %collective-permute-done.10 = bf16[3,128,1024]{2,1,0:T(8,128)(2,1)S(1)} collective-permute-done((bf16[3,128,1024]{2,1,0:T(8,128)(2,1)S(1)}, bf16[3,128,1024]{2,1,0:T(8,128)(2,1)S(1)}, u32[]{:S(2)}, u32[]{:S(2)}) %collective-permute-start.10) | collective-permute-done | bytes 786464 | tf_op jit(solution)/shard_map/ppermute | solution.py:34
  52.3 12.2 %collective-permute-done.6 = bf16[512,512]{1,0:T(8,128)(2,1)S(1)} collective-permute-done((bf16[512,512]{1,0:T(8,128)(2,1)S(1)}, bf16[512,512]{1,0:T(8,128)(2,1)S(1)}, u32[]{:S(2)}, u32[]{:S(2)}) %collective-permute-start.6) | collective-permute-done | bytes 524320 | tf_op jit(solution)/shard_map/ppermute | solution.py:29
  66.7 5.4 %load_weights.1 = (bf16[4096,1536]{1,0:T(8,128)(2,1)S(1)}, bf16[512,1024]{1,0:T(8,128)(2,1)S(1)}) custom-call(s32[8]{0:T(128)S(1)} %stack.104.meta_ref.refs_0_, bf16[4096,1536]{1,0:T(8,128)(2,1)} %source.1, bf16[512,4096]{1,0:T(8,128)(2,1)} %outer.1, bf16[512,512]{1,0:T(8,128)(2,1)S(1)} %add_convert_fusion._), custom_call_target="tpu_custom_call" | custom-call | tf_op jit(solution)/shard_map/load_weights/pallas_call | solution.py:236
  72.1 3.6 %collective-permute-done.5.refs_3_ = bf16[512,512]{1,0:T(8,128)(2,1)S(1)} collective-permute-done((bf16[512,512]{1,0:T(8,128)(2,1)S(1)}, bf16[512,512]{1,0:T(8,128)(2,1)S(1)}, u32[]{:S(2)}, u32[]{:S(2)}) %collective-permute-start.5) | collective-permute-done | bytes 524320 | tf_op jit(solution)/shard_map/ppermute | solution.py:29
  77.7 8.8 %collective-permute-done.9.refs_5_ = bf16[512,512]{1,0:T(8,128)(2,1)S(1)} collective-permute-done((bf16[512,512]{1,0:T(8,128)(2,1)S(1)}, bf16[512,512]{1,0:T(8,128)(2,1)S(1)}, u32[]{:S(2)}, u32[]{:S(2)}) %collective-permute-start.9) | collective-permute-done | bytes 524320 | tf_op jit(solution)/shard_map/ppermute | solution.py:29
  89.7 11.4 %collective-permute-done.14.refs_3_ = bf16[256,1024]{1,0:T(8,128)(2,1)S(1)} collective-permute-done((bf16[256,1024]{1,0:T(8,128)(2,1)S(1)}, bf16[256,1024]{1,0:T(8,128)(2,1)S(1)}, u32[]{:S(2)}, u32[]{:S(2)}) %collective-permute-start.14) | collective-permute-done | bytes 524320 | tf_op jit(solution)/shard_map/ppermute | solution.py:29
  103.3 3.2 %qkv_near.2 = (f32[256,1536]{1,0:T(8,128)S(1)}, f32[256,128]{1,0:T(8,128)S(1)}) custom-call(s32[8]{0:T(128)S(1)} %stack.104.meta_ref.refs_0_, bf16[256,1024]{1,0:T(8,128)(2,1)S(1)} %get-tuple-element.79.refs_1_.refs_9_, bf16[256,1024]{1,0:T(8,128)(2,1)S(1)} %collective-permute-done.12.refs_2_, bf16[256,1024]{1,0:T(8,128)(2,1)S(1)} %collective-permute-done.14.refs_3_, ...), custom_call_target="tpu_custom_call" | custom-call | flops 3300000000 | bytes 10800000 | tf_op jit(solution)/shard_map/qkv_near/pallas_call | solution.py:191
  117.7 2.6 %collective-permute-start.18 = (bf16[3,256,128]{2,1,0:T(8,128)(2,1)S(1)}, bf16[3,256,128]{2,1,0:T(8,128)(2,1)S(1)}, u32[]{:S(2)}, u32[]{:S(2)}) collective-permute-start(bf16[3,256,128]{2,1,0:T(8,128)(2,1)S(1)} %get-tuple-element.85), channel_id=1, source_target_pairs={{0,24},{4,28},{8,0},{12,4},{16,8},{20,12},{24,16},{28,20},{1,25},{... | collective-permute-start | bytes 589832 | tf_op jit(solution)/shard_map/ppermute | solution.py:44
  123.7 3.2 %qkv_near.3 = (f32[256,1536]{1,0:T(8,128)S(1)}, f32[256,128]{1,0:T(8,128)S(1)}) custom-call(s32[8]{0:T(128)S(1)} %stack.104.meta_ref.refs_0_, bf16[256,1024]{1,0:T(8,128)(2,1)S(1)} %get-tuple-element.87.refs_1_.refs_8_, bf16[256,1024]{1,0:T(8,128)(2,1)S(1)} %collective-permute-done.19.refs_2_, bf16[256,1024]{1,0:T(8,128)(2,1)S(1)} %collective-permute-done.21.refs_3_, ...), custom_call_target="tpu_custom_call" | custom-call | flops 3300000000 | bytes 10800000 | tf_op jit(solution)/shard_map/qkv_near/pallas_call | solution.py:191
  133.9 2.6 %collective-permute-start.25 = (bf16[3,256,128]{2,1,0:T(8,128)(2,1)S(1)}, bf16[3,256,128]{2,1,0:T(8,128)(2,1)S(1)}, u32[]{:S(2)}, u32[]{:S(2)}) collective-permute-start(bf16[3,256,128]{2,1,0:T(8,128)(2,1)S(1)} %get-tuple-element.93), channel_id=1, source_target_pairs={{0,24},{4,28},{8,0},{12,4},{16,8},{20,12},{24,16},{28,20},{1,25},{... | collective-permute-start | bytes 589832 | tf_op jit(solution)/shard_map/ppermute | solution.py:44
  136.5 2.7 %collective-permute-done.23.refs_2_.refs_3_ = bf16[3,256,128]{2,1,0:T(8,128)(2,1)S(1)} collective-permute-done((bf16[3,256,128]{2,1,0:T(8,128)(2,1)S(1)}, bf16[3,256,128]{2,1,0:T(8,128)(2,1)S(1)}, u32[]{:S(2)}, u32[]{:S(2)}) %collective-permute-start.23) | collective-permute-done | bytes 196640 | tf_op jit(solution)/shard_map/ppermute | solution.py:44
  139.2 6.6 %collective-permute-done.24.refs_3_ = bf16[3,256,128]{2,1,0:T(8,128)(2,1)S(1)} collective-permute-done((bf16[3,256,128]{2,1,0:T(8,128)(2,1)S(1)}, bf16[3,256,128]{2,1,0:T(8,128)(2,1)S(1)}, u32[]{:S(2)}, u32[]{:S(2)}) %collective-permute-start.24) | collective-permute-done | bytes 196640 | tf_op jit(solution)/shard_map/ppermute | solution.py:44
  148.8 4.8 %attention.2 = (bf16[512,128]{1,0:T(8,128)(2,1)S(1)}, bf16[512,128]{1,0:T(8,128)(2,1)S(1)}, bf16[2,4,512,128]{3,2,1,0:T(8,128)(2,1)S(1)}, bf16[2,4,128,512]{3,2,1,0:T(8,128)(2,1)S(1)}) custom-call(s32[8]{0:T(128)S(1)} %stack.104.meta_ref.refs_0_, bf16[3,256,128]{2,1,0:T(8,128)(2,1)S(1)} %get-tuple-element.94.refs_1_, ...), custom_call_target="tpu_custom_call" | custom-call | flops 6600000000 | bytes 21600000 | tf_op jit(solution)/shard_map/attention/pallas_call | solution.py:191
  153.7 3.7 %collective-permute-start.28 = (bf16[512,128]{1,0:T(8,128)(2,1)S(1)}, bf16[512,128]{1,0:T(8,128)(2,1)S(1)}, u32[]{:S(2)}, u32[]{:S(2)}) collective-permute-start(bf16[512,128]{1,0:T(8,128)(2,1)S(1)} %get-tuple-element.102), channel_id=1, source_target_pairs={{0,16},{4,20},{8,24},{12,28},{16,0},{20,4},{24,8},{28,12},{1,17},{... | collective-permute-start | bytes 393224 | tf_op jit(solution)/shard_map/ppermute | solution.py:44
  157.4 6.7 %attention.3 = (bf16[512,128]{1,0:T(8,128)(2,1)S(1)}, bf16[512,128]{1,0:T(8,128)(2,1)S(1)}) custom-call(s32[8]{0:T(128)S(1)} %stack.104.meta_ref.refs_0_, bf16[3,256,128]{2,1,0:T(8,128)(2,1)S(1)} %collective-permute-done.25.refs_4_.refs_1_, bf16[3,256,128]{2,1,0:T(8,128)(2,1)S(1)} %collective-permute-done.18.refs_8_.refs_2_, ...), custom_call_target="tpu_custom_call" | custom-call | flops 6600000000 | bytes 21600000 | tf_op jit(solution)/shard_map/attention/pallas_call | solution.py:191
  165.8 2.8 %collective-permute-start.29 = (bf16[512,128]{1,0:T(8,128)(2,1)S(1)}, bf16[512,128]{1,0:T(8,128)(2,1)S(1)}, u32[]{:S(2)}, u32[]{:S(2)}) collective-permute-start(bf16[512,128]{1,0:T(8,128)(2,1)S(1)} %get-tuple-element.108), channel_id=1, source_target_pairs={{0,8},{4,12},{8,16},{12,20},{16,24},{20,28},{24,0},{28,4},{1,9},{5... | collective-permute-start | bytes 393224 | tf_op jit(solution)/shard_map/ppermute | solution.py:44
  169.7 4.1 %collective-permute-done.29 = bf16[512,128]{1,0:T(8,128)(2,1)S(1)} collective-permute-done((bf16[512,128]{1,0:T(8,128)(2,1)S(1)}, bf16[512,128]{1,0:T(8,128)(2,1)S(1)}, u32[]{:S(2)}, u32[]{:S(2)}) %collective-permute-start.29) | collective-permute-done | bytes 131104 | tf_op jit(solution)/shard_map/ppermute | solution.py:44
  178.2 6.3 %collective-permute-done.33.refs_7_ = bf16[2,512,128]{2,1,0:T(8,128)(2,1)S(1)} collective-permute-done((bf16[2,512,128]{2,1,0:T(8,128)(2,1)S(1)}, bf16[2,512,128]{2,1,0:T(8,128)(2,1)S(1)}, u32[]{:S(2)}, u32[]{:S(2)}) %collective-permute-start.33) | collective-permute-done | bytes 262176 | tf_op jit(solution)/shard_map/ppermute | solution.py:29
  185.5 3.0 %collective-permute-done.35.refs_4_ = bf16[2,512,128]{2,1,0:T(8,128)(2,1)S(1)} collective-permute-done((bf16[2,512,128]{2,1,0:T(8,128)(2,1)S(1)}, bf16[2,512,128]{2,1,0:T(8,128)(2,1)S(1)}, u32[]{:S(2)}, u32[]{:S(2)}) %collective-permute-start.35) | collective-permute-done | bytes 262176 | tf_op jit(solution)/shard_map/ppermute | solution.py:29
  188.4 3.2 %attention_mix.2.refs_2_ = f32[512,1024]{1,0:T(8,128)S(1)} custom-call(s32[8]{0:T(128)S(1)} %stack.104.meta_ref.refs_0_, bf16[2,512,128]{2,1,0:T(8,128)(2,1)S(1)} %pad_maximum_fusion.4.refs_1_, bf16[2,512,128]{2,1,0:T(8,128)(2,1)S(1)} %collective-permute-done.31.refs_2_, bf16[2,512,128]{2,1,0:T(8,128)(2,1)S(1)} %collective-permute-done.32.refs_3_, ...), custom_call_target="tpu_custom_call" | custom-call | flops 4620000256 | bytes 15120000 | tf_op jit(solution)/shard_map/attention_mix/pallas_call | solution.py:191
  (96 shorter events, 61.5 us)
Async XLA Ops:
  2.3 15.4 %collective-permute-start = (bf16[3,144,1024]{2,1,0:T(8,128)(2,1)S(1)}, bf16[3,144,1024]{2,1,0:T(8,128)(2,1)S(1)}, u32[]{:S(2)}, u32[]{:S(2)}) collective-permute-start(bf16[3,144,1024]{2,1,0:T(8,128)(2,1)S(1)} %get-tuple-element.61), channel_id=1, source_target_pairs={{0,4},{4,8},{8,12},{12,16},{16,20},{20,24},{24,28},{1,5},{5,9},{9,... | collective-permute-start | bytes 2654216 | tf_op jit(solution)/shard_map/ppermute | solution.py:39
  4.7 20.5 %collective-permute-start.1 = (bf16[128,1024]{1,0:T(8,128)(2,1)S(1)}, bf16[128,1024]{1,0:T(8,128)(2,1)S(1)}, u32[]{:S(2)}, u32[]{:S(2)}) collective-permute-start(bf16[128,1024]{1,0:T(8,128)(2,1)S(1)} %get-tuple-element.64), channel_id=1, source_target_pairs={{0,1},{1,0},{2,3},{3,2},{4,5},{5,4},{6,7},{7,6},{8,9},{9,8},{10,11... | collective-permute-start | bytes 786440 | tf_op jit(solution)/shard_map/ppermute | solution.py:29
  7.1 18.1 %collective-permute-start.2 = (bf16[128,1024]{1,0:T(8,128)(2,1)S(1)}, bf16[128,1024]{1,0:T(8,128)(2,1)S(1)}, u32[]{:S(2)}, u32[]{:S(2)}) collective-permute-start(bf16[128,1024]{1,0:T(8,128)(2,1)S(1)} %get-tuple-element.65), channel_id=1, source_target_pairs={{0,2},{1,3},{2,0},{3,1},{4,6},{5,7},{6,4},{7,5},{8,10},{9,11},{10,... | collective-permute-start | bytes 786440 | tf_op jit(solution)/shard_map/ppermute | solution.py:29
  8.7 16.6 %collective-permute-start.3 = (bf16[128,1024]{1,0:T(8,128)(2,1)S(1)}, bf16[128,1024]{1,0:T(8,128)(2,1)S(1)}, u32[]{:S(2)}, u32[]{:S(2)}) collective-permute-start(bf16[128,1024]{1,0:T(8,128)(2,1)S(1)} %get-tuple-element.66), channel_id=1, source_target_pairs={{0,3},{1,2},{2,1},{3,0},{4,7},{5,6},{6,5},{7,4},{8,11},{9,10},{10,... | collective-permute-start | bytes 786440 | tf_op jit(solution)/shard_map/ppermute | solution.py:29
  27.1 14.5 %collective-permute-start.8 = (bf16[512,512]{1,0:T(8,128)(2,1)S(1)}, bf16[512,512]{1,0:T(8,128)(2,1)S(1)}, u32[]{:S(2)}, u32[]{:S(2)}) collective-permute-start(bf16[512,512]{1,0:T(8,128)(2,1)S(1)} %get-tuple-element.76), channel_id=1, source_target_pairs={{0,1},{1,0},{2,3},{3,2},{4,5},{5,4},{6,7},{7,6},{8,9},{9,8},{10,11... | collective-permute-start | bytes 1572872 | tf_op jit(solution)/shard_map/ppermute | solution.py:29
  29.2 20.2 %collective-permute-start.10 = (bf16[3,128,1024]{2,1,0:T(8,128)(2,1)S(1)}, bf16[3,128,1024]{2,1,0:T(8,128)(2,1)S(1)}, u32[]{:S(2)}, u32[]{:S(2)}) collective-permute-start(bf16[3,128,1024]{2,1,0:T(8,128)(2,1)S(1)} %get-tuple-element.118.refs_4_), channel_id=1, source_target_pairs={{0,8},{4,12},{8,0},{12,4},{16,24},{20,28},{24,16},{28,20},{1,9},{5... | collective-permute-start | bytes 2359304 | tf_op jit(solution)/shard_map/ppermute | solution.py:34
  49.6 36.9 %collective-permute-start.11 = (bf16[2,3,128,1024]{3,2,1,0:T(8,128)(2,1)S(1)}, bf16[2,3,128,1024]{3,2,1,0:T(8,128)(2,1)S(1)}, u32[]{:S(2)}, u32[]{:S(2)}) collective-permute-start(bf16[2,3,128,1024]{3,2,1,0:T(8,128)(2,1)S(1)} %pad_maximum_fusion.refs_11_.refs_4_), channel_id=1, source_target_pairs={{0,4},{4,0},{8,12},{12,8},{16,20},{20,16},{24,28},{28,24},{1,5},{5... | collective-permute-start | bytes 4718600 | tf_op jit(solution)/shard_map/ppermute | solution.py:34
  49.7 14.8 %collective-permute-start.6 = (bf16[512,512]{1,0:T(8,128)(2,1)S(1)}, bf16[512,512]{1,0:T(8,128)(2,1)S(1)}, u32[]{:S(2)}, u32[]{:S(2)}) collective-permute-start(bf16[512,512]{1,0:T(8,128)(2,1)S(1)} %get-tuple-element.74), channel_id=1, source_target_pairs={{0,2},{1,3},{2,0},{3,1},{4,6},{5,7},{6,4},{7,5},{8,10},{9,11},{10,... | collective-permute-start | bytes 1572872 | tf_op jit(solution)/shard_map/ppermute | solution.py:29
  51.2 20.9 %collective-permute-start.4 = (bf16[512,512]{1,0:T(8,128)(2,1)S(1)}, bf16[512,512]{1,0:T(8,128)(2,1)S(1)}, u32[]{:S(2)}, u32[]{:S(2)}) collective-permute-start(bf16[512,512]{1,0:T(8,128)(2,1)S(1)} %get-tuple-element.71), channel_id=1, source_target_pairs={{0,1},{1,0},{2,3},{3,2},{4,5},{5,4},{6,7},{7,6},{8,9},{9,8},{10,11... | collective-permute-start | bytes 1572872 | tf_op jit(solution)/shard_map/ppermute | solution.py:29
  51.8 23.9 %collective-permute-start.5 = (bf16[512,512]{1,0:T(8,128)(2,1)S(1)}, bf16[512,512]{1,0:T(8,128)(2,1)S(1)}, u32[]{:S(2)}, u32[]{:S(2)}) collective-permute-start(bf16[512,512]{1,0:T(8,128)(2,1)S(1)} %get-tuple-element.72), channel_id=1, source_target_pairs={{0,2},{1,3},{2,0},{3,1},{4,6},{5,7},{6,4},{7,5},{8,10},{9,11},{10,... | collective-permute-start | bytes 1572872 | tf_op jit(solution)/shard_map/ppermute | solution.py:29
  64.6 13.1 %collective-permute-start.7 = (bf16[512,512]{1,0:T(8,128)(2,1)S(1)}, bf16[512,512]{1,0:T(8,128)(2,1)S(1)}, u32[]{:S(2)}, u32[]{:S(2)}) collective-permute-start(bf16[512,512]{1,0:T(8,128)(2,1)S(1)} %add_convert_fusion.1), channel_id=1, source_target_pairs={{0,1},{1,0},{2,3},{3,2},{4,5},{5,4},{6,7},{7,6},{8,9},{9,8},{10,11... | collective-permute-start | bytes 1572872 | tf_op jit(solution)/shard_map/ppermute | solution.py:29
  65.2 21.3 %collective-permute-start.9 = (bf16[512,512]{1,0:T(8,128)(2,1)S(1)}, bf16[512,512]{1,0:T(8,128)(2,1)S(1)}, u32[]{:S(2)}, u32[]{:S(2)}) collective-permute-start(bf16[512,512]{1,0:T(8,128)(2,1)S(1)} %add_convert_fusion._), channel_id=1, source_target_pairs={{0,2},{1,3},{2,0},{3,1},{4,6},{5,7},{6,4},{7,5},{8,10},{9,11},{10,... | collective-permute-start | bytes 1572872 | tf_op jit(solution)/shard_map/ppermute | solution.py:29
  87.5 13.6 %collective-permute-start.14 = (bf16[256,1024]{1,0:T(8,128)(2,1)S(1)}, bf16[256,1024]{1,0:T(8,128)(2,1)S(1)}, u32[]{:S(2)}, u32[]{:S(2)}) collective-permute-start(bf16[256,1024]{1,0:T(8,128)(2,1)S(1)} %get-tuple-element.79.refs_1_.refs_9_), channel_id=1, source_target_pairs={{0,2},{1,3},{2,0},{3,1},{4,6},{5,7},{6,4},{7,5},{8,10},{9,11},{10,... | collective-permute-start | bytes 1572872 | tf_op jit(solution)/shard_map/ppermute | solution.py:29
  89.1 13.2 %collective-permute-start.12 = (bf16[256,1024]{1,0:T(8,128)(2,1)S(1)}, bf16[256,1024]{1,0:T(8,128)(2,1)S(1)}, u32[]{:S(2)}, u32[]{:S(2)}) collective-permute-start(bf16[256,1024]{1,0:T(8,128)(2,1)S(1)} %get-tuple-element.79.refs_1_.refs_9_), channel_id=1, source_target_pairs={{0,1},{1,0},{2,3},{3,2},{4,5},{5,4},{6,7},{7,6},{8,9},{9,8},{10,11... | collective-permute-start | bytes 1572872 | tf_op jit(solution)/shard_map/ppermute | solution.py:29
  109.1 11.4 %collective-permute-start.21 = (bf16[256,1024]{1,0:T(8,128)(2,1)S(1)}, bf16[256,1024]{1,0:T(8,128)(2,1)S(1)}, u32[]{:S(2)}, u32[]{:S(2)}) collective-permute-start(bf16[256,1024]{1,0:T(8,128)(2,1)S(1)} %get-tuple-element.87.refs_1_.refs_8_), channel_id=1, source_target_pairs={{0,2},{1,3},{2,0},{3,1},{4,6},{5,7},{6,4},{7,5},{8,10},{9,11},{10,... | collective-permute-start | bytes 1572872 | tf_op jit(solution)/shard_map/ppermute | solution.py:29
  110.0 12.4 %collective-permute-start.19 = (bf16[256,1024]{1,0:T(8,128)(2,1)S(1)}, bf16[256,1024]{1,0:T(8,128)(2,1)S(1)}, u32[]{:S(2)}, u32[]{:S(2)}) collective-permute-start(bf16[256,1024]{1,0:T(8,128)(2,1)S(1)} %get-tuple-element.87.refs_1_.refs_8_), channel_id=1, source_target_pairs={{0,1},{1,0},{2,3},{3,2},{4,5},{5,4},{6,7},{7,6},{8,9},{9,8},{10,11... | collective-permute-start | bytes 1572872 | tf_op jit(solution)/shard_map/ppermute | solution.py:29
  114.8 19.1 %collective-permute-start.16 = (bf16[3,256,128]{2,1,0:T(8,128)(2,1)S(1)}, bf16[3,256,128]{2,1,0:T(8,128)(2,1)S(1)}, u32[]{:S(2)}, u32[]{:S(2)}) collective-permute-start(bf16[3,256,128]{2,1,0:T(8,128)(2,1)S(1)} %get-tuple-element.83), channel_id=1, source_target_pairs={{0,8},{4,12},{8,16},{12,20},{16,24},{20,28},{24,0},{28,4},{1,9},{5... | collective-permute-start | bytes 589832 | tf_op jit(solution)/shard_map/ppermute | solution.py:44
  116.4 20.1 %collective-permute-start.17 = (bf16[3,256,128]{2,1,0:T(8,128)(2,1)S(1)}, bf16[3,256,128]{2,1,0:T(8,128)(2,1)S(1)}, u32[]{:S(2)}, u32[]{:S(2)}) collective-permute-start(bf16[3,256,128]{2,1,0:T(8,128)(2,1)S(1)} %get-tuple-element.84), channel_id=1, source_target_pairs={{0,16},{4,20},{8,24},{12,28},{16,0},{20,4},{24,8},{28,12},{1,17},{... | collective-permute-start | bytes 589832 | tf_op jit(solution)/shard_map/ppermute | solution.py:44
  117.7 18.8 %collective-permute-start.18 = (bf16[3,256,128]{2,1,0:T(8,128)(2,1)S(1)}, bf16[3,256,128]{2,1,0:T(8,128)(2,1)S(1)}, u32[]{:S(2)}, u32[]{:S(2)}) collective-permute-start(bf16[3,256,128]{2,1,0:T(8,128)(2,1)S(1)} %get-tuple-element.85), channel_id=1, source_target_pairs={{0,24},{4,28},{8,0},{12,4},{16,8},{20,12},{24,16},{28,20},{1,25},{... | collective-permute-start | bytes 589832 | tf_op jit(solution)/shard_map/ppermute | solution.py:44
  132.6 13.3 %collective-permute-start.24 = (bf16[3,256,128]{2,1,0:T(8,128)(2,1)S(1)}, bf16[3,256,128]{2,1,0:T(8,128)(2,1)S(1)}, u32[]{:S(2)}, u32[]{:S(2)}) collective-permute-start(bf16[3,256,128]{2,1,0:T(8,128)(2,1)S(1)} %get-tuple-element.92), channel_id=1, source_target_pairs={{0,16},{4,20},{8,24},{12,28},{16,0},{20,4},{24,8},{28,12},{1,17},{... | collective-permute-start | bytes 589832 | tf_op jit(solution)/shard_map/ppermute | solution.py:44
  133.9 12.0 %collective-permute-start.25 = (bf16[3,256,128]{2,1,0:T(8,128)(2,1)S(1)}, bf16[3,256,128]{2,1,0:T(8,128)(2,1)S(1)}, u32[]{:S(2)}, u32[]{:S(2)}) collective-permute-start(bf16[3,256,128]{2,1,0:T(8,128)(2,1)S(1)} %get-tuple-element.93), channel_id=1, source_target_pairs={{0,24},{4,28},{8,0},{12,4},{16,8},{20,12},{24,16},{28,20},{1,25},{... | collective-permute-start | bytes 589832 | tf_op jit(solution)/shard_map/ppermute | solution.py:44
  164.2 11.0 %collective-permute-start.32 = (bf16[2,512,128]{2,1,0:T(8,128)(2,1)S(1)}, bf16[2,512,128]{2,1,0:T(8,128)(2,1)S(1)}, u32[]{:S(2)}, u32[]{:S(2)}) collective-permute-start(bf16[2,512,128]{2,1,0:T(8,128)(2,1)S(1)} %pad_maximum_fusion.4.refs_1_), channel_id=1, source_target_pairs={{0,2},{1,3},{2,0},{3,1},{4,6},{5,7},{6,4},{7,5},{8,10},{9,11},{10,... | collective-permute-start | bytes 786440 | tf_op jit(solution)/shard_map/ppermute | solution.py:29
  164.7 10.5 %collective-permute-start.31 = (bf16[2,512,128]{2,1,0:T(8,128)(2,1)S(1)}, bf16[2,512,128]{2,1,0:T(8,128)(2,1)S(1)}, u32[]{:S(2)}, u32[]{:S(2)}) collective-permute-start(bf16[2,512,128]{2,1,0:T(8,128)(2,1)S(1)} %pad_maximum_fusion.4.refs_1_), channel_id=1, source_target_pairs={{0,1},{1,0},{2,3},{3,2},{4,5},{5,4},{6,7},{7,6},{8,9},{9,8},{10,11... | collective-permute-start | bytes 786440 | tf_op jit(solution)/shard_map/ppermute | solution.py:29
  177.7 10.7 %collective-permute-start.35 = (bf16[2,512,128]{2,1,0:T(8,128)(2,1)S(1)}, bf16[2,512,128]{2,1,0:T(8,128)(2,1)S(1)}, u32[]{:S(2)}, u32[]{:S(2)}) collective-permute-start(bf16[2,512,128]{2,1,0:T(8,128)(2,1)S(1)} %collective-permute-done.31.refs_2_), channel_id=1, source_target_pairs={{0,2},{1,3},{2,0},{3,1},{4,6},{5,7},{6,4},{7,5},{8,10},{9,11},{10,... | collective-permute-start | bytes 786440 | tf_op jit(solution)/shard_map/ppermute | solution.py:29
  (16 other events, 137.3 us)

commit v9 on v8

--- a/solution.py
+++ b/solution.py
@@ -116,15 +116,9 @@
     halo_ref, rest = (rest[0], rest[1:]) if first_row == 0 else (None, rest)
     rows_ref, rest = rest[0], rest[1:]
     if loads:
-        weight, out_ref, held, wide, product, table, sems = rest
-        parts = sems.shape[0]
-        height = weight.shape[0] // parts
-
-        def copy_of(part):
-            span = pl.ds(pl.multiple_of(part * height, height), height)
-            return pltpu.make_async_copy(weight.at[span, :], held.at[span, :], sems.at[part])
-
-        copy_of(pl.program_id(0)).start()
+        weight, out_ref, held, wide, product, table, sem = rest
+        copy = pltpu.make_async_copy(weight, held, sem)
+        pl.when(pl.program_id(0) == 0)(copy.start)
     else:
         out_ref, wide, product, table = rest
 
@@ -133,11 +127,7 @@
 
     filter_tile(first_row, pl.program_id(0), *head, halo_ref, rows_ref, wide, product, table, store)
     if loads:
-
-        @pl.when(pl.program_id(0) == pl.num_programs(0) - 1)
-        def _():
-            for part in range(parts):
-                copy_of(part).wait()
+        pl.when(pl.program_id(0) == pl.num_programs(0) - 1)(copy.wait)
 
 
 def gated_chunk(meta, features, halo, first_row, count, short_filter, medium_rows, skip, weight=None):
@@ -172,7 +162,7 @@
         operands.append(in_hbm(weight))
         out_specs.append(pl.BlockSpec(memory_space=pltpu.VMEM))
         out_shape.append(pltpu.VMEM(weight.shape, weight.dtype))
-        scratch.append(pltpu.SemaphoreType.DMA((channels // LANES,)))
+        scratch.append(pltpu.SemaphoreType.DMA)
     return pl.pallas_call(
         functools.partial(gated_kernel, first_row, loads),
         grid=(channels // LANES,),
@@ -217,7 +207,7 @@
     return vmem_call(body, "hyena_terms", None, meta, [upper, lower, weight], outs, waits=waits)
 
 
-def load_kernel(meta_ref, source, outer, _, held, own, sems):
+def load_kernel(meta_ref, source, outer, along, swapped, held, own, sems):
     channels = own.shape[1]
     columns = pl.ds(pl.multiple_of(meta_ref[0] * channels, channels), channels)
     copies = [
@@ -235,13 +225,13 @@
     hbm, vmem = pl.BlockSpec(memory_space=pltpu.HBM), pl.BlockSpec(memory_space=pltpu.VMEM)
     return pl.pallas_call(
         load_kernel,
-        in_specs=[pl.BlockSpec(memory_space=pltpu.SMEM), hbm, hbm, vmem],
+        in_specs=[pl.BlockSpec(memory_space=pltpu.SMEM), hbm, hbm, vmem, vmem],
         out_specs=[vmem, vmem],
         out_shape=[pltpu.VMEM(weight.shape, weight.dtype), pltpu.VMEM((outer.shape[0], channels), outer.dtype)],
         scratch_shapes=[pltpu.SemaphoreType.DMA((2,))],
         compiler_params=pltpu.CompilerParams(vmem_limit_bytes=4 * MIB),
         name="load_weights",
-    )(meta, in_hbm(weight), in_hbm(outer), after)
+    )(meta, in_hbm(weight), in_hbm(outer), *after)
 
 
 def stream_kernel(_, kept, direct_x, direct_y, late_x, late_y, residual, *parts):
@@ -360,7 +350,7 @@
         out[...] = (state[2] / state[1]).T.astype(BF16)
 
 
-def attend(meta, own, other, laid, distances, chips):
+def attend(meta, own, other, laid, distances, waits, chips):
     chunks, leading = len(other), laid is None
     count = own[0].shape[1] * chunks
     outs = [((count, HEAD), BF16)] * len(distances)
@@ -371,7 +361,7 @@
         operands = [piece for distance in distances for piece in own[(chips - distance) % chips :: chips]]
         operands = [*operands, *laid]
     body = functools.partial(attention_kernel, chips, chunks, distances, leading)
-    made = list(vmem_call(body, "attention", 6, meta, operands, outs))
+    made = list(vmem_call(body, "attention", 6, meta, operands, outs, waits=waits))
     return made[: len(distances)], laid or made[len(distances) :]
 
 
@@ -616,10 +606,9 @@
 
     lower, out_held = gated_chunk(meta, by_kind, halo, chunk, chunk, short_filter, medium_rows, skip, out_weight)
     (upper,) = gated_chunk(meta, by_kind, halo, 0, chunk, short_filter, medium_rows, skip)
-    picked, _ = lax.optimization_barrier((picked, upper))
+    across_x, across_y = column_terms(meta, upper, lower, out_held, ((3, 0, 0, 0), (3, 1, 1, 0)), picked)
     picked = jnp.stack(picked)
     swapped = swap_ctx(picked, 2)
-    across_x, across_y = column_terms(meta, upper, lower, out_held, ((3, 0, 0, 0), (3, 1, 1, 0)))
     across_x, across_y = swap_ch(across_x, 1), swap_ch(across_y, 2)
     pieces = ((1, 0, 0, 0), (2, 1, 1, 0), (1, 1, 2, 0), (2, 0, 3, 0), (0, 0, 4, 0), (0, 1, 4, 1))
     direct_x, direct_y, along_x, along_y, kept = column_terms(meta, upper, lower, out_held, pieces, [picked])
@@ -627,10 +616,7 @@
     along_x = (along_x.astype(F32) + across_y.astype(F32)).astype(BF16)
     along_y = (along_y.astype(F32) + across_x.astype(F32)).astype(BF16)
     late_x, late_y = swap_ch(along_x, 1), swap_ch(along_y, 2)
-    swapped, _ = lax.optimization_barrier((swapped, along_y))
-    near_w = jnp.stack([picked, swapped])
-    far_w = swap_ctx(near_w, 1)
-    qkv_held, own_w = load(meta, attn_weight, attn_out, along_y, channels)
+    qkv_held, own_w = load(meta, attn_weight, attn_out, (along_y, swapped), channels)
     parts = vmem_call(
         stream_kernel,
         "add_stream",
@@ -638,7 +624,7 @@
         meta,
         [kept, direct_x, direct_y, late_x, late_y, residual_in],
         [((chunk, channels), BF16)] * 2,
-        waits=[qkv_held, far_w],
+        waits=[qkv_held],
     )
 
     own, other, after = [], [], None
@@ -671,14 +657,17 @@
         arrived = [outs[0]] + [rotate_chips(outs[d], d) for d in range(1, chips)]
         own.append(arrived)
 
+    swapped, _ = lax.optimization_barrier((swapped, outs))
+    near_w = jnp.stack([picked, swapped])
+    far_w = swap_ctx(near_w, 1)
     own, _ = lax.optimization_barrier((own, outs))
     other = [swap_ctx(jnp.stack([piece[1:] for piece in arrived]), 1) for arrived in own]
     own, other = own[1] + own[0], other[::-1]
 
     groups = [(*range(2, chips, 2), 0), tuple(range(1, chips, 2))]
-    given, laid = attend(meta, own, other, None, groups[0], chips)
+    given, laid = attend(meta, own, other, None, groups[0], [far_w], chips)
     first = [rotate_chips(piece, d) if d else piece for d, piece in zip(groups[0], given)]
-    given, _ = attend(meta, own, other, laid, groups[1], chips)
+    given, _ = attend(meta, own, other, laid, groups[1], [], chips)
     first, given = lax.optimization_barrier((first, given))
     second = [rotate_chips(piece, d) for d, piece in zip(groups[1], given)]
     back = jnp.stack(first)

time: 194 us -> 172 us (0.89)
  waiting for transfers between devices: 85 us -> 63.1 us
    ppermute x23, waiting for transfers between devices: 60.4 us -> 40.2 us  [swap_ch(): return lax.ppermute(value, 'ch', [(i, i ^ mask) for i in range(count)])]
    ppermute x4, waiting for transfers between devices: 9.73 us -> 6.78 us  [swap_ctx(): return lax.ppermute(value, 'ctx', [(i, i ^ mask) for i in range(count)])]
    ppermute x23, starting transfers between devices: 24.4 us -> 26.9 us  [swap_ch(): return lax.ppermute(value, 'ch', [(i, i ^ mask) for i in range(count)])]
    ppermute x9, starting transfers between devices: 18.7 us -> 16.6 us  [rotate_chips(): lax.ppermute(value, 'ctx', [(i, (i + 2 * distance) % count) for i in rang...]
  transfers between devices with their start and end apart: 37 -> 37, of which waited for: 21 -> 17; matrix products, arithmetic and copies ran while one was open for 1% -> 1% of each run, Pallas kernels for 24% -> 26%
where the time goes in v9:
time: 172 us
  waiting for transfers between devices  63.1 us (37%)
  Pallas kernels  56.7 us (33%)
  starting transfers between devices  49.5 us (29%)
  other arithmetic  1.94 us (1%)
    ppermute x23, waiting for transfers between devices, swap_ch(): return lax.ppermute(value, 'ch', [(i, i ^ mask) for i in range(count)])  40.2 us
    pallas_call x11, Pallas kernels, vmem_call(): pl.pallas_call(run, in_specs=[pl.BlockSpec(memory_space=pltpu.SMEM)] + [p...  33.8 us
    ppermute x23, starting transfers between devices, swap_ch(): return lax.ppermute(value, 'ch', [(i, i ^ mask) for i in range(count)])  26.9 us
    ppermute x9, starting transfers between devices, rotate_chips(): lax.ppermute(value, 'ctx', [(i, (i + 2 * distance) % count) for i in rang...  16.6 us
    ppermute x9, waiting for transfers between devices, rotate_chips(): lax.ppermute(value, 'ctx', [(i, (i + 2 * distance) % count) for i in rang...  16.1 us
    pallas_call x2, Pallas kernels, gated_chunk(): pl.pallas_call(functools.partial(gated_kernel, first_row, loads), grid=(c...  15.3 us
    ppermute x4, waiting for transfers between devices, swap_ctx(): return lax.ppermute(value, 'ctx', [(i, i ^ mask) for i in range(count)])  6.78 us
    pallas_call x1, Pallas kernels, load(): pl.pallas_call(load_kernel, in_specs=[pl.BlockSpec(memory_space=pltpu.SME...  5.36 us
  transfers between devices with their start and end apart: 37, of which 17 were waited for; matrix products, arithmetic and copies ran while one was open for 1% of the time, Pallas kernels for 26%

profile of v9, /device:TPU:0, one launch (start us, length us, event | category | flops | bytes accessed | tf_op | source)
XLA Modules:
  0.0 171.8 jit_solution(3677260712689803083)
XLA Ops:
  2.3 2.4 %collective-permute-start = (bf16[3,144,1024]{2,1,0:T(8,128)(2,1)S(1)}, bf16[3,144,1024]{2,1,0:T(8,128)(2,1)S(1)}, u32[]{:S(2)}, u32[]{:S(2)}) collective-permute-start(bf16[3,144,1024]{2,1,0:T(8,128)(2,1)S(1)} %get-tuple-element.58), channel_id=1, source_target_pairs={{0,4},{4,8},{8,12},{12,16},{16,20},{20,24},{24,28},{1,5},{5,9},{9,... | collective-permute-start | bytes 2654216 | tf_op jit(solution)/shard_map/ppermute | solution.py:39
  8.7 7.7 %hyena_filters.3 = (bf16[256,1024]{1,0:T(8,128)(2,1)S(1)}, bf16[1024,4096]{1,0:T(8,128)(2,1)S(1)}) custom-call(s32[8]{0:T(128)S(1)} %stack.104.meta_ref.refs_0_, f32[3,7,64]{2,1,0:T(8,128)} %refs_1_.3, f32[64,128]{1,0:T(8,128)} %bitcast.50, f32[1,1024]{1,0:T(1,128)} %bitcast.55, bf16[3,512,1024]{2,1,0:T(8,128)(2,1)S(1)} %bitcast.39, bf16[1024,4096]{1,0:T(8,128)(2,1)} %refs_5_.1), custom_call_target="tpu_custom_call" | custom-call | tf_op jit(solution)/shard_map/hyena_filters/pallas_call | solution.py:166
  16.4 7.5 %hyena_filters.2.refs_1_ = bf16[256,1024]{1,0:T(8,128)(2,1)S(1)} custom-call(s32[8]{0:T(128)S(1)} %stack.104.meta_ref.refs_0_, f32[3,7,64]{2,1,0:T(8,128)} %refs_1_.3, f32[64,128]{1,0:T(8,128)} %bitcast.51, f32[1,1024]{1,0:T(1,128)} %bitcast.56, bf16[3,144,1024]{2,1,0:T(8,128)(2,1)S(1)} %collective-permute-done.refs_4_, bf16[3,512,1024]{2,1,0:T(8,128)(2,1)S(1)} %bitcast.40), custom_call_target="tpu_custom_call" | custom-call | tf_op jit(solution)/shard_map/hyena_filters/pallas_call | solution.py:166
  29.5 2.9 %collective-permute-start.10 = (bf16[3,128,1024]{2,1,0:T(8,128)(2,1)S(1)}, bf16[3,128,1024]{2,1,0:T(8,128)(2,1)S(1)}, u32[]{:S(2)}, u32[]{:S(2)}) collective-permute-start(bf16[3,128,1024]{2,1,0:T(8,128)(2,1)S(1)} %get-tuple-element.112.refs_4_), channel_id=1, source_target_pairs={{0,8},{4,12},{8,0},{12,4},{16,24},{20,28},{24,16},{28,20},{1,9},{5... | collective-permute-start | bytes 2359304 | tf_op jit(solution)/shard_map/ppermute | solution.py:34
  32.4 4.0 %hyena_terms.2 = (bf16[512,512]{1,0:T(8,128)(2,1)S(1)}, bf16[512,512]{1,0:T(8,128)(2,1)S(1)}, bf16[512,512]{1,0:T(8,128)(2,1)S(1)}, bf16[512,512]{1,0:T(8,128)(2,1)S(1)}, bf16[512,1024]{1,0:T(8,128)(2,1)S(1)}) custom-call(s32[8]{0:T(128)S(1)} %stack.104.meta_ref.refs_0_, bf16[256,1024]{1,0:T(8,128)(2,1)S(1)} %hyena_filters.2.refs_1_, ...), custom_call_target="tpu_custom_call" | custom-call | tf_op jit(solution)/shard_map/hyena_terms/pallas_call | solution.py:181
  37.5 2.9 %collective-permute-done.6 = bf16[512,512]{1,0:T(8,128)(2,1)S(1)} collective-permute-done((bf16[512,512]{1,0:T(8,128)(2,1)S(1)}, bf16[512,512]{1,0:T(8,128)(2,1)S(1)}, u32[]{:S(2)}, u32[]{:S(2)}) %collective-permute-start.6) | collective-permute-done | bytes 524320 | tf_op jit(solution)/shard_map/ppermute | solution.py:29
  40.5 2.4 %collective-permute-start.7 = (bf16[512,512]{1,0:T(8,128)(2,1)S(1)}, bf16[512,512]{1,0:T(8,128)(2,1)S(1)}, u32[]{:S(2)}, u32[]{:S(2)}) collective-permute-start(bf16[512,512]{1,0:T(8,128)(2,1)S(1)} %add_convert_fusion.1), channel_id=1, source_target_pairs={{0,1},{1,0},{2,3},{3,2},{4,5},{5,4},{6,7},{7,6},{8,9},{9,8},{10,11... | collective-permute-start | bytes 1572872 | tf_op jit(solution)/shard_map/ppermute | solution.py:29
  44.6 4.8 %collective-permute-done.10.swapped = bf16[3,128,1024]{2,1,0:T(8,128)(2,1)S(1)} collective-permute-done((bf16[3,128,1024]{2,1,0:T(8,128)(2,1)S(1)}, bf16[3,128,1024]{2,1,0:T(8,128)(2,1)S(1)}, u32[]{:S(2)}, u32[]{:S(2)}) %collective-permute-start.10) | collective-permute-done | bytes 786464 | tf_op jit(solution)/shard_map/ppermute | solution.py:34
  49.4 5.4 %load_weights.1 = (bf16[4096,1536]{1,0:T(8,128)(2,1)S(1)}, bf16[512,1024]{1,0:T(8,128)(2,1)S(1)}) custom-call(s32[8]{0:T(128)S(1)} %stack.104.meta_ref.refs_0_, bf16[4096,1536]{1,0:T(8,128)(2,1)} %source.1, bf16[512,4096]{1,0:T(8,128)(2,1)} %outer.1, bf16[512,512]{1,0:T(8,128)(2,1)S(1)} %add_convert_fusion.along, ...), custom_call_target="tpu_custom_call" | custom-call | tf_op jit(solution)/shard_map/load_weights/pallas_call | solution.py:226
  54.8 10.1 %collective-permute-done.7.refs_4_ = bf16[512,512]{1,0:T(8,128)(2,1)S(1)} collective-permute-done((bf16[512,512]{1,0:T(8,128)(2,1)S(1)}, bf16[512,512]{1,0:T(8,128)(2,1)S(1)}, u32[]{:S(2)}, u32[]{:S(2)}) %collective-permute-start.7) | collective-permute-done | bytes 524320 | tf_op jit(solution)/shard_map/ppermute | solution.py:29
  68.0 11.7 %collective-permute-done.13.refs_3_ = bf16[256,1024]{1,0:T(8,128)(2,1)S(1)} collective-permute-done((bf16[256,1024]{1,0:T(8,128)(2,1)S(1)}, bf16[256,1024]{1,0:T(8,128)(2,1)S(1)}, u32[]{:S(2)}, u32[]{:S(2)}) %collective-permute-start.13) | collective-permute-done | bytes 524320 | tf_op jit(solution)/shard_map/ppermute | solution.py:29
  81.9 3.2 %qkv_near.2 = (f32[256,1536]{1,0:T(8,128)S(1)}, f32[256,128]{1,0:T(8,128)S(1)}) custom-call(s32[8]{0:T(128)S(1)} %stack.104.meta_ref.refs_0_, bf16[256,1024]{1,0:T(8,128)(2,1)S(1)} %get-tuple-element.72.refs_1_.refs_9_, bf16[256,1024]{1,0:T(8,128)(2,1)S(1)} %collective-permute-done.11.refs_2_, bf16[256,1024]{1,0:T(8,128)(2,1)S(1)} %collective-permute-done.13.refs_3_, ...), custom_call_target="tpu_custom_call" | custom-call | flops 3300000000 | bytes 10800000 | tf_op jit(solution)/shard_map/qkv_near/pallas_call | solution.py:181
  103.1 3.2 %qkv_near.3 = (f32[256,1536]{1,0:T(8,128)S(1)}, f32[256,128]{1,0:T(8,128)S(1)}) custom-call(s32[8]{0:T(128)S(1)} %stack.104.meta_ref.refs_0_, bf16[256,1024]{1,0:T(8,128)(2,1)S(1)} %get-tuple-element.80.refs_1_.refs_8_, bf16[256,1024]{1,0:T(8,128)(2,1)S(1)} %collective-permute-done.18.refs_2_, bf16[256,1024]{1,0:T(8,128)(2,1)S(1)} %collective-permute-done.20.refs_3_, ...), custom_call_target="tpu_custom_call" | custom-call | flops 3300000000 | bytes 10800000 | tf_op jit(solution)/shard_map/qkv_near/pallas_call | solution.py:181
  109.7 2.6 %collective-permute-start.23 = (bf16[3,256,128]{2,1,0:T(8,128)(2,1)S(1)}, bf16[3,256,128]{2,1,0:T(8,128)(2,1)S(1)}, u32[]{:S(2)}, u32[]{:S(2)}) collective-permute-start(bf16[3,256,128]{2,1,0:T(8,128)(2,1)S(1)} %get-tuple-element.85), channel_id=1, source_target_pairs={{0,16},{4,20},{8,24},{12,28},{16,0},{20,4},{24,8},{28,12},{1,17},{... | collective-permute-start | bytes 589832 | tf_op jit(solution)/shard_map/ppermute | solution.py:44
  113.8 4.4 %collective-permute-done.22.refs_2_.refs_3_ = bf16[3,256,128]{2,1,0:T(8,128)(2,1)S(1)} collective-permute-done((bf16[3,256,128]{2,1,0:T(8,128)(2,1)S(1)}, bf16[3,256,128]{2,1,0:T(8,128)(2,1)S(1)}, u32[]{:S(2)}, u32[]{:S(2)}) %collective-permute-start.22) | collective-permute-done | bytes 196640 | tf_op jit(solution)/shard_map/ppermute | solution.py:44
  118.3 6.2 %collective-permute-done.23.refs_3_ = bf16[3,256,128]{2,1,0:T(8,128)(2,1)S(1)} collective-permute-done((bf16[3,256,128]{2,1,0:T(8,128)(2,1)S(1)}, bf16[3,256,128]{2,1,0:T(8,128)(2,1)S(1)}, u32[]{:S(2)}, u32[]{:S(2)}) %collective-permute-start.23) | collective-permute-done | bytes 196640 | tf_op jit(solution)/shard_map/ppermute | solution.py:44
  127.3 4.8 %attention.2 = (bf16[512,128]{1,0:T(8,128)(2,1)S(1)}, bf16[512,128]{1,0:T(8,128)(2,1)S(1)}, bf16[2,4,512,128]{3,2,1,0:T(8,128)(2,1)S(1)}, bf16[2,4,128,512]{3,2,1,0:T(8,128)(2,1)S(1)}) custom-call(s32[8]{0:T(128)S(1)} %stack.104.meta_ref.refs_0_, bf16[3,256,128]{2,1,0:T(8,128)(2,1)S(1)} %get-tuple-element.87.refs_1_, ...), custom_call_target="tpu_custom_call" | custom-call | flops 6600000000 | bytes 21600000 | tf_op jit(solution)/shard_map/attention/pallas_call | solution.py:181
  132.2 2.8 %collective-permute-start.28 = (bf16[512,128]{1,0:T(8,128)(2,1)S(1)}, bf16[512,128]{1,0:T(8,128)(2,1)S(1)}, u32[]{:S(2)}, u32[]{:S(2)}) collective-permute-start(bf16[512,128]{1,0:T(8,128)(2,1)S(1)} %get-tuple-element.96), channel_id=1, source_target_pairs={{0,16},{4,20},{8,24},{12,28},{16,0},{20,4},{24,8},{28,12},{1,17},{... | collective-permute-start | bytes 393224 | tf_op jit(solution)/shard_map/ppermute | solution.py:44
  135.0 6.7 %attention.3 = (bf16[512,128]{1,0:T(8,128)(2,1)S(1)}, bf16[512,128]{1,0:T(8,128)(2,1)S(1)}) custom-call(s32[8]{0:T(128)S(1)} %stack.104.meta_ref.refs_0_, bf16[3,256,128]{2,1,0:T(8,128)(2,1)S(1)} %collective-permute-done.24.refs_4_.refs_1_, bf16[3,256,128]{2,1,0:T(8,128)(2,1)S(1)} %collective-permute-done.17.refs_8_.refs_2_, ...), custom_call_target="tpu_custom_call" | custom-call | flops 6600000000 | bytes 21600000 | tf_op jit(solution)/shard_map/attention/pallas_call | solution.py:181
  144.3 2.8 %collective-permute-start.29 = (bf16[512,128]{1,0:T(8,128)(2,1)S(1)}, bf16[512,128]{1,0:T(8,128)(2,1)S(1)}, u32[]{:S(2)}, u32[]{:S(2)}) collective-permute-start(bf16[512,128]{1,0:T(8,128)(2,1)S(1)} %get-tuple-element.102), channel_id=1, source_target_pairs={{0,8},{4,12},{8,16},{12,20},{16,24},{20,28},{24,0},{28,4},{1,9},{5... | collective-permute-start | bytes 393224 | tf_op jit(solution)/shard_map/ppermute | solution.py:44
  148.1 4.1 %collective-permute-done.29 = bf16[512,128]{1,0:T(8,128)(2,1)S(1)} collective-permute-done((bf16[512,128]{1,0:T(8,128)(2,1)S(1)}, bf16[512,128]{1,0:T(8,128)(2,1)S(1)}, u32[]{:S(2)}, u32[]{:S(2)}) %collective-permute-start.29) | collective-permute-done | bytes 131104 | tf_op jit(solution)/shard_map/ppermute | solution.py:44
  156.4 6.6 %collective-permute-done.33.refs_7_ = bf16[2,512,128]{2,1,0:T(8,128)(2,1)S(1)} collective-permute-done((bf16[2,512,128]{2,1,0:T(8,128)(2,1)S(1)}, bf16[2,512,128]{2,1,0:T(8,128)(2,1)S(1)}, u32[]{:S(2)}, u32[]{:S(2)}) %collective-permute-start.33) | collective-permute-done | bytes 262176 | tf_op jit(solution)/shard_map/ppermute | solution.py:29
  163.6 3.2 %collective-permute-done.35.refs_4_ = bf16[2,512,128]{2,1,0:T(8,128)(2,1)S(1)} collective-permute-done((bf16[2,512,128]{2,1,0:T(8,128)(2,1)S(1)}, bf16[2,512,128]{2,1,0:T(8,128)(2,1)S(1)}, u32[]{:S(2)}, u32[]{:S(2)}) %collective-permute-start.35) | collective-permute-done | bytes 262176 | tf_op jit(solution)/shard_map/ppermute | solution.py:29
  166.8 2.9 %attention_mix.2.refs_2_ = f32[512,1024]{1,0:T(8,128)S(1)} custom-call(s32[8]{0:T(128)S(1)} %stack.104.meta_ref.refs_0_, bf16[2,512,128]{2,1,0:T(8,128)(2,1)S(1)} %pad_maximum_fusion.4.refs_1_, bf16[2,512,128]{2,1,0:T(8,128)(2,1)S(1)} %collective-permute-done.31.refs_2_, bf16[2,512,128]{2,1,0:T(8,128)(2,1)S(1)} %collective-permute-done.32.refs_3_, ...), custom_call_target="tpu_custom_call" | custom-call | flops 4620000256 | bytes 15120000 | tf_op jit(solution)/shard_map/attention_mix/pallas_call | solution.py:181
  (96 shorter events, 56.0 us)
Async XLA Ops:
  2.3 14.1 %collective-permute-start = (bf16[3,144,1024]{2,1,0:T(8,128)(2,1)S(1)}, bf16[3,144,1024]{2,1,0:T(8,128)(2,1)S(1)}, u32[]{:S(2)}, u32[]{:S(2)}) collective-permute-start(bf16[3,144,1024]{2,1,0:T(8,128)(2,1)S(1)} %get-tuple-element.58), channel_id=1, source_target_pairs={{0,4},{4,8},{8,12},{12,16},{16,20},{20,24},{24,28},{1,5},{5,9},{9,... | collective-permute-start | bytes 2654216 | tf_op jit(solution)/shard_map/ppermute | solution.py:39
  4.7 19.2 %collective-permute-start.1 = (bf16[128,1024]{1,0:T(8,128)(2,1)S(1)}, bf16[128,1024]{1,0:T(8,128)(2,1)S(1)}, u32[]{:S(2)}, u32[]{:S(2)}) collective-permute-start(bf16[128,1024]{1,0:T(8,128)(2,1)S(1)} %get-tuple-element.61), channel_id=1, source_target_pairs={{0,1},{1,0},{2,3},{3,2},{4,5},{5,4},{6,7},{7,6},{8,9},{9,8},{10,11... | collective-permute-start | bytes 786440 | tf_op jit(solution)/shard_map/ppermute | solution.py:29
  7.1 16.9 %collective-permute-start.2 = (bf16[128,1024]{1,0:T(8,128)(2,1)S(1)}, bf16[128,1024]{1,0:T(8,128)(2,1)S(1)}, u32[]{:S(2)}, u32[]{:S(2)}) collective-permute-start(bf16[128,1024]{1,0:T(8,128)(2,1)S(1)} %get-tuple-element.62), channel_id=1, source_target_pairs={{0,2},{1,3},{2,0},{3,1},{4,6},{5,7},{6,4},{7,5},{8,10},{9,11},{10,... | collective-permute-start | bytes 786440 | tf_op jit(solution)/shard_map/ppermute | solution.py:29
  8.7 15.4 %collective-permute-start.3 = (bf16[128,1024]{1,0:T(8,128)(2,1)S(1)}, bf16[128,1024]{1,0:T(8,128)(2,1)S(1)}, u32[]{:S(2)}, u32[]{:S(2)}) collective-permute-start(bf16[128,1024]{1,0:T(8,128)(2,1)S(1)} %get-tuple-element.63), channel_id=1, source_target_pairs={{0,3},{1,2},{2,1},{3,0},{4,7},{5,6},{6,5},{7,4},{8,11},{9,10},{10,... | collective-permute-start | bytes 786440 | tf_op jit(solution)/shard_map/ppermute | solution.py:29
  25.8 14.5 %collective-permute-start.6 = (bf16[512,512]{1,0:T(8,128)(2,1)S(1)}, bf16[512,512]{1,0:T(8,128)(2,1)S(1)}, u32[]{:S(2)}, u32[]{:S(2)}) collective-permute-start(bf16[512,512]{1,0:T(8,128)(2,1)S(1)} %get-tuple-element.68), channel_id=1, source_target_pairs={{0,2},{1,3},{2,0},{3,1},{4,6},{5,7},{6,4},{7,5},{8,10},{9,11},{10,... | collective-permute-start | bytes 1572872 | tf_op jit(solution)/shard_map/ppermute | solution.py:29
  27.9 15.0 %collective-permute-start.8 = (bf16[512,512]{1,0:T(8,128)(2,1)S(1)}, bf16[512,512]{1,0:T(8,128)(2,1)S(1)}, u32[]{:S(2)}, u32[]{:S(2)}) collective-permute-start(bf16[512,512]{1,0:T(8,128)(2,1)S(1)} %get-tuple-element.70), channel_id=1, source_target_pairs={{0,1},{1,0},{2,3},{3,2},{4,5},{5,4},{6,7},{7,6},{8,9},{9,8},{10,11... | collective-permute-start | bytes 1572872 | tf_op jit(solution)/shard_map/ppermute | solution.py:29
  29.5 19.9 %collective-permute-start.10 = (bf16[3,128,1024]{2,1,0:T(8,128)(2,1)S(1)}, bf16[3,128,1024]{2,1,0:T(8,128)(2,1)S(1)}, u32[]{:S(2)}, u32[]{:S(2)}) collective-permute-start(bf16[3,128,1024]{2,1,0:T(8,128)(2,1)S(1)} %get-tuple-element.112.refs_4_), channel_id=1, source_target_pairs={{0,8},{4,12},{8,0},{12,4},{16,24},{20,28},{24,16},{28,20},{1,9},{5... | collective-permute-start | bytes 2359304 | tf_op jit(solution)/shard_map/ppermute | solution.py:34
  36.4 18.5 %collective-permute-start.4 = (bf16[512,512]{1,0:T(8,128)(2,1)S(1)}, bf16[512,512]{1,0:T(8,128)(2,1)S(1)}, u32[]{:S(2)}, u32[]{:S(2)}) collective-permute-start(bf16[512,512]{1,0:T(8,128)(2,1)S(1)} %get-tuple-element.65), channel_id=1, source_target_pairs={{0,1},{1,0},{2,3},{3,2},{4,5},{5,4},{6,7},{7,6},{8,9},{9,8},{10,11... | collective-permute-start | bytes 1572872 | tf_op jit(solution)/shard_map/ppermute | solution.py:29
  37.0 17.9 %collective-permute-start.5 = (bf16[512,512]{1,0:T(8,128)(2,1)S(1)}, bf16[512,512]{1,0:T(8,128)(2,1)S(1)}, u32[]{:S(2)}, u32[]{:S(2)}) collective-permute-start(bf16[512,512]{1,0:T(8,128)(2,1)S(1)} %get-tuple-element.66), channel_id=1, source_target_pairs={{0,2},{1,3},{2,0},{3,1},{4,6},{5,7},{6,4},{7,5},{8,10},{9,11},{10,... | collective-permute-start | bytes 1572872 | tf_op jit(solution)/shard_map/ppermute | solution.py:29
  40.5 24.4 %collective-permute-start.7 = (bf16[512,512]{1,0:T(8,128)(2,1)S(1)}, bf16[512,512]{1,0:T(8,128)(2,1)S(1)}, u32[]{:S(2)}, u32[]{:S(2)}) collective-permute-start(bf16[512,512]{1,0:T(8,128)(2,1)S(1)} %add_convert_fusion.1), channel_id=1, source_target_pairs={{0,1},{1,0},{2,3},{3,2},{4,5},{5,4},{6,7},{7,6},{8,9},{9,8},{10,11... | collective-permute-start | bytes 1572872 | tf_op jit(solution)/shard_map/ppermute | solution.py:29
  43.0 21.9 %collective-permute-start.9 = (bf16[512,512]{1,0:T(8,128)(2,1)S(1)}, bf16[512,512]{1,0:T(8,128)(2,1)S(1)}, u32[]{:S(2)}, u32[]{:S(2)}) collective-permute-start(bf16[512,512]{1,0:T(8,128)(2,1)S(1)} %add_convert_fusion.along), channel_id=1, source_target_pairs={{0,2},{1,3},{2,0},{3,1},{4,6},{5,7},{6,4},{7,5},{8,10},{9,11},{10,... | collective-permute-start | bytes 1572872 | tf_op jit(solution)/shard_map/ppermute | solution.py:29
  65.9 13.7 %collective-permute-start.13 = (bf16[256,1024]{1,0:T(8,128)(2,1)S(1)}, bf16[256,1024]{1,0:T(8,128)(2,1)S(1)}, u32[]{:S(2)}, u32[]{:S(2)}) collective-permute-start(bf16[256,1024]{1,0:T(8,128)(2,1)S(1)} %get-tuple-element.72.refs_1_.refs_9_), channel_id=1, source_target_pairs={{0,2},{1,3},{2,0},{3,1},{4,6},{5,7},{6,4},{7,5},{8,10},{9,11},{10,... | collective-permute-start | bytes 1572872 | tf_op jit(solution)/shard_map/ppermute | solution.py:29
  66.3 15.0 %collective-permute-start.11 = (bf16[256,1024]{1,0:T(8,128)(2,1)S(1)}, bf16[256,1024]{1,0:T(8,128)(2,1)S(1)}, u32[]{:S(2)}, u32[]{:S(2)}) collective-permute-start(bf16[256,1024]{1,0:T(8,128)(2,1)S(1)} %get-tuple-element.72.refs_1_.refs_9_), channel_id=1, source_target_pairs={{0,1},{1,0},{2,3},{3,2},{4,5},{5,4},{6,7},{7,6},{8,9},{9,8},{10,11... | collective-permute-start | bytes 1572872 | tf_op jit(solution)/shard_map/ppermute | solution.py:29
  88.2 11.7 %collective-permute-start.20 = (bf16[256,1024]{1,0:T(8,128)(2,1)S(1)}, bf16[256,1024]{1,0:T(8,128)(2,1)S(1)}, u32[]{:S(2)}, u32[]{:S(2)}) collective-permute-start(bf16[256,1024]{1,0:T(8,128)(2,1)S(1)} %get-tuple-element.80.refs_1_.refs_8_), channel_id=1, source_target_pairs={{0,2},{1,3},{2,0},{3,1},{4,6},{5,7},{6,4},{7,5},{8,10},{9,11},{10,... | collective-permute-start | bytes 1572872 | tf_op jit(solution)/shard_map/ppermute | solution.py:29
  88.8 12.1 %collective-permute-start.18 = (bf16[256,1024]{1,0:T(8,128)(2,1)S(1)}, bf16[256,1024]{1,0:T(8,128)(2,1)S(1)}, u32[]{:S(2)}, u32[]{:S(2)}) collective-permute-start(bf16[256,1024]{1,0:T(8,128)(2,1)S(1)} %get-tuple-element.80.refs_1_.refs_8_), channel_id=1, source_target_pairs={{0,1},{1,0},{2,3},{3,2},{4,5},{5,4},{6,7},{7,6},{8,9},{9,8},{10,11... | collective-permute-start | bytes 1572872 | tf_op jit(solution)/shard_map/ppermute | solution.py:29
  93.1 19.3 %collective-permute-start.15 = (bf16[3,256,128]{2,1,0:T(8,128)(2,1)S(1)}, bf16[3,256,128]{2,1,0:T(8,128)(2,1)S(1)}, u32[]{:S(2)}, u32[]{:S(2)}) collective-permute-start(bf16[3,256,128]{2,1,0:T(8,128)(2,1)S(1)} %get-tuple-element.76), channel_id=1, source_target_pairs={{0,8},{4,12},{8,16},{12,20},{16,24},{20,28},{24,0},{28,4},{1,9},{5... | collective-permute-start | bytes 589832 | tf_op jit(solution)/shard_map/ppermute | solution.py:44
  95.0 18.8 %collective-permute-start.16 = (bf16[3,256,128]{2,1,0:T(8,128)(2,1)S(1)}, bf16[3,256,128]{2,1,0:T(8,128)(2,1)S(1)}, u32[]{:S(2)}, u32[]{:S(2)}) collective-permute-start(bf16[3,256,128]{2,1,0:T(8,128)(2,1)S(1)} %get-tuple-element.77), channel_id=1, source_target_pairs={{0,16},{4,20},{8,24},{12,28},{16,0},{20,4},{24,8},{28,12},{1,17},{... | collective-permute-start | bytes 589832 | tf_op jit(solution)/shard_map/ppermute | solution.py:44
  96.7 17.2 %collective-permute-start.17 = (bf16[3,256,128]{2,1,0:T(8,128)(2,1)S(1)}, bf16[3,256,128]{2,1,0:T(8,128)(2,1)S(1)}, u32[]{:S(2)}, u32[]{:S(2)}) collective-permute-start(bf16[3,256,128]{2,1,0:T(8,128)(2,1)S(1)} %get-tuple-element.78), channel_id=1, source_target_pairs={{0,24},{4,28},{8,0},{12,4},{16,8},{20,12},{24,16},{28,20},{1,25},{... | collective-permute-start | bytes 589832 | tf_op jit(solution)/shard_map/ppermute | solution.py:44
  109.7 14.7 %collective-permute-start.23 = (bf16[3,256,128]{2,1,0:T(8,128)(2,1)S(1)}, bf16[3,256,128]{2,1,0:T(8,128)(2,1)S(1)}, u32[]{:S(2)}, u32[]{:S(2)}) collective-permute-start(bf16[3,256,128]{2,1,0:T(8,128)(2,1)S(1)} %get-tuple-element.85), channel_id=1, source_target_pairs={{0,16},{4,20},{8,24},{12,28},{16,0},{20,4},{24,8},{28,12},{1,17},{... | collective-permute-start | bytes 589832 | tf_op jit(solution)/shard_map/ppermute | solution.py:44
  112.4 12.0 %collective-permute-start.24 = (bf16[3,256,128]{2,1,0:T(8,128)(2,1)S(1)}, bf16[3,256,128]{2,1,0:T(8,128)(2,1)S(1)}, u32[]{:S(2)}, u32[]{:S(2)}) collective-permute-start(bf16[3,256,128]{2,1,0:T(8,128)(2,1)S(1)} %get-tuple-element.86), channel_id=1, source_target_pairs={{0,24},{4,28},{8,0},{12,4},{16,8},{20,12},{24,16},{28,20},{1,25},{... | collective-permute-start | bytes 589832 | tf_op jit(solution)/shard_map/ppermute | solution.py:44
  113.8 13.6 %collective-permute-start.27 = (bf16[2,3,128,1024]{3,2,1,0:T(8,128)(2,1)S(1)}, bf16[2,3,128,1024]{3,2,1,0:T(8,128)(2,1)S(1)}, u32[]{:S(2)}, u32[]{:S(2)}) collective-permute-start(bf16[2,3,128,1024]{3,2,1,0:T(8,128)(2,1)S(1)} %pad_maximum_fusion.refs_11_.refs_4_), channel_id=1, source_target_pairs={{0,4},{4,0},{8,12},{12,8},{16,20},{20,16},{24,28},{28,24},{1,5},{5... | collective-permute-start | bytes 4718600 | tf_op jit(solution)/shard_map/ppermute | solution.py:34
  141.8 11.9 %collective-permute-start.32 = (bf16[2,512,128]{2,1,0:T(8,128)(2,1)S(1)}, bf16[2,512,128]{2,1,0:T(8,128)(2,1)S(1)}, u32[]{:S(2)}, u32[]{:S(2)}) collective-permute-start(bf16[2,512,128]{2,1,0:T(8,128)(2,1)S(1)} %pad_maximum_fusion.4.refs_1_), channel_id=1, source_target_pairs={{0,2},{1,3},{2,0},{3,1},{4,6},{5,7},{6,4},{7,5},{8,10},{9,11},{10,... | collective-permute-start | bytes 786440 | tf_op jit(solution)/shard_map/ppermute | solution.py:29
  142.9 10.7 %collective-permute-start.31 = (bf16[2,512,128]{2,1,0:T(8,128)(2,1)S(1)}, bf16[2,512,128]{2,1,0:T(8,128)(2,1)S(1)}, u32[]{:S(2)}, u32[]{:S(2)}) collective-permute-start(bf16[2,512,128]{2,1,0:T(8,128)(2,1)S(1)} %pad_maximum_fusion.4.refs_1_), channel_id=1, source_target_pairs={{0,1},{1,0},{2,3},{3,2},{4,5},{5,4},{6,7},{7,6},{8,9},{9,8},{10,11... | collective-permute-start | bytes 786440 | tf_op jit(solution)/shard_map/ppermute | solution.py:29
  155.3 11.5 %collective-permute-start.35 = (bf16[2,512,128]{2,1,0:T(8,128)(2,1)S(1)}, bf16[2,512,128]{2,1,0:T(8,128)(2,1)S(1)}, u32[]{:S(2)}, u32[]{:S(2)}) collective-permute-start(bf16[2,512,128]{2,1,0:T(8,128)(2,1)S(1)} %collective-permute-done.31.refs_2_), channel_id=1, source_target_pairs={{0,2},{1,3},{2,0},{3,1},{4,6},{5,7},{6,4},{7,5},{8,10},{9,11},{10,... | collective-permute-start | bytes 786440 | tf_op jit(solution)/shard_map/ppermute | solution.py:29
  (16 other events, 137.3 us)

commit v10 on v9

--- a/solution.py
+++ b/solution.py
@@ -10,6 +10,7 @@
 HEAD = 128
 GROUP_SIZE = 16
 LANES = 128
+TILES = 2
 LEAD = 16
 norm_eps = 1e-05
 SCORE_SCALE = 1.4426950408889634 / HEAD**0.5
@@ -44,7 +45,7 @@
     return lax.ppermute(value, "ctx", [(i, (i + 2 * distance) % count) for i in range(count)])
 
 
-def filter_tile(first_row, tile, short_ref, medium_ref, skip_ref, halo_ref, rows_ref, wide, product, table, store):
+def filter_tile(first_row, tile, lanes, short_ref, medium_ref, skip_ref, halo_ref, rows_ref, wide, product, table, store):
     taps, groups_all = short_ref.shape[1:]
     length = medium_ref.shape[1]
     groups = LANES // GROUP_SIZE
@@ -56,10 +57,10 @@
 
     for kind in range(3):
         if first_row == 0:
-            wide[kind, :halo_rows] = halo_ref[kind].astype(F32)
-            wide[kind, halo_rows:] = rows_ref[kind].astype(F32)
+            wide[kind, :halo_rows] = halo_ref[kind, :, lanes].astype(F32)
+            wide[kind, halo_rows:] = rows_ref[kind, :, lanes].astype(F32)
         else:
-            wide[kind] = rows_ref[kind, first_row - halo_rows : first_row + count].astype(F32)
+            wide[kind] = rows_ref[kind, first_row - halo_rows : first_row + count, lanes].astype(F32)
 
     group_row = lax.broadcasted_iota(jnp.int32, (groups_all, LANES), 0)
     group_col = lax.broadcasted_iota(jnp.int32, (groups_all, LANES), 1) // GROUP_SIZE + tile * groups
@@ -122,10 +123,15 @@
     else:
         out_ref, wide, product, table = rest
 
-    def store(row, value):
-        out_ref[row : row + value.shape[0], :] = value
-
-    filter_tile(first_row, pl.program_id(0), *head, halo_ref, rows_ref, wide, product, table, store)
+    for part in range(TILES):
+        lanes = slice(part * LANES, (part + 1) * LANES)
+
+        def store(row, value):
+            out_ref[row : row + value.shape[0], lanes] = value
+
+        scratch = wide.at[part], product.at[part], table.at[part]
+        tile = pl.program_id(0) * TILES + part
+        filter_tile(first_row, tile, lanes, *head, halo_ref, rows_ref, *scratch, store)
     if loads:
         pl.when(pl.program_id(0) == pl.num_programs(0) - 1)(copy.wait)
 
@@ -134,6 +140,7 @@
     kinds, rows, channels = features.shape
     length = medium_rows.shape[1]
     groups = LANES // GROUP_SIZE
+    step = TILES * LANES
     loads = weight is not None
     in_hbm = lambda x: pltpu.with_memory_space_constraint(x, pltpu.HBM)
     in_specs = [
@@ -143,19 +150,19 @@
         pl.BlockSpec(skip.shape, lambda i: (0, 0)),
     ]
     operands = [meta, in_hbm(short_filter), in_hbm(medium_rows), in_hbm(skip)]
-    out_specs = [pl.BlockSpec((count, LANES), lambda i: (0, i))]
+    out_specs = [pl.BlockSpec((count, step), lambda i: (0, i))]
     out_shape = [jax.ShapeDtypeStruct((count, channels), BF16)]
     scratch = [
-        pltpu.VMEM((kinds, length + LEAD + count, LANES), F32),
-        pltpu.VMEM((length + count, LANES), BF16),
-        pltpu.VMEM((groups * length, 2 * length), BF16),
+        pltpu.VMEM((TILES, kinds, length + LEAD + count, LANES), F32),
+        pltpu.VMEM((TILES, length + count, LANES), BF16),
+        pltpu.VMEM((TILES, groups * length, 2 * length), BF16),
     ]
     if first_row == 0:
-        in_specs.append(pl.BlockSpec((kinds, length + LEAD, LANES), lambda i: (0, 0, i)))
-        in_specs.append(pl.BlockSpec((kinds, count, LANES), lambda i: (0, 0, i)))
+        in_specs.append(pl.BlockSpec((kinds, length + LEAD, step), lambda i: (0, 0, i)))
+        in_specs.append(pl.BlockSpec((kinds, count, step), lambda i: (0, 0, i)))
         operands += [halo, features]
     else:
-        in_specs.append(pl.BlockSpec((kinds, rows, LANES), lambda i: (0, 0, i)))
+        in_specs.append(pl.BlockSpec((kinds, rows, step), lambda i: (0, 0, i)))
         operands.append(features)
     if loads:
         in_specs.append(pl.BlockSpec(memory_space=pltpu.HBM))
@@ -165,7 +172,7 @@
         scratch.append(pltpu.SemaphoreType.DMA)
     return pl.pallas_call(
         functools.partial(gated_kernel, first_row, loads),
-        grid=(channels // LANES,),
+        grid=(channels // step,),
         in_specs=in_specs,
         out_specs=out_specs,
         out_shape=out_shape,
@@ -437,7 +444,7 @@
         finish([far_w, near_w])
 
 
-def mix(meta, heads, groups, items, before, own_w, near_w, far_w, kind, chips):
+def mix(meta, heads, *, groups, items, before, own_w, near_w, far_w, kind, chips):
     rows, channels = heads[0].shape[1], own_w.shape[1]
     body = functools.partial(mix_kernel, chips, groups, items, len(before))
     operands = [*heads, *before, own_w, near_w, far_w]
@@ -624,7 +631,7 @@
         meta,
         [kept, direct_x, direct_y, late_x, late_y, residual_in],
         [((chunk, channels), BF16)] * 2,
-        waits=[qkv_held],
+        waits=[qkv_held, cosine, sine],
     )
 
     own, other, after = [], [], None
@@ -672,15 +679,14 @@
     second = [rotate_chips(piece, d) for d, piece in zip(groups[1], given)]
     back = jnp.stack(first)
     by_x, by_y = swap_ch(back, 1), swap_ch(back, 2)
-    second, by_x, by_y = lax.optimization_barrier((second, by_x, by_y))
-    heads = [back, by_x, by_y, swap_ch(by_x, 2)]
+    add = functools.partial(mix, meta, groups=groups, own_w=own_w, near_w=near_w, far_w=far_w, chips=chips)
+    total = add([back, by_x, by_y], items=((0, 0), (0, 1), (0, 2)), before=parts, kind=F32)
+    second, by_x, total = lax.optimization_barrier((second, by_x, total))
+    across = swap_ch(by_x, 2)
     back = jnp.stack(second)
     by_x, by_y = swap_ch(back, 1), swap_ch(back, 2)
-    heads += [back, by_x, by_y, swap_ch(by_y, 1)]
-    places = [(group, source) for group in range(2) for source in range(4)]
-    weights = own_w, near_w, far_w
-    early = mix(meta, heads[:-1], groups, places[:-1], parts, *weights, F32, chips)
-    return mix(meta, heads[-1:], groups, places[-1:], [early], *weights, BF16, chips)
+    total = add([across, back, by_y], items=((0, 3), (1, 0), (1, 2)), before=[total], kind=F32)
+    return add([by_x, swap_ch(by_y, 1)], items=((1, 1), (1, 3)), before=[total], kind=BF16)
 
 
 def solution(mesh):

time: 172 us -> 170 us (0.988)
  waiting for transfers between devices: 63.1 us -> 59.3 us
  starting transfers between devices: 49.5 us -> 52.9 us
  Pallas kernels: 56.7 us -> 54.5 us
    ppermute x9, waiting for transfers between devices: 16.1 us -> 9.69 us  [rotate_chips(): lax.ppermute(value, 'ctx', [(i, (i + 2 * distance) % count) for i in rang...]
    pallas_call x2, Pallas kernels: 15.3 us -> 12.2 us  [gated_chunk(): pl.pallas_call(functools.partial(gated_kernel, first_row, loads), grid=(c...]
    ppermute x9, starting transfers between devices: 16.6 us -> 18.8 us  [rotate_chips(): lax.ppermute(value, 'ctx', [(i, (i + 2 * distance) % count) for i in rang...]
    ppermute x23, waiting for transfers between devices: 40.2 us -> 41.9 us  [swap_ch(): return lax.ppermute(value, 'ch', [(i, i ^ mask) for i in range(count)])]
    pallas_call x11 -> x12, Pallas kernels: 33.8 us -> 34.8 us  [vmem_call(): pl.pallas_call(run, in_specs=[pl.BlockSpec(memory_space=pltpu.SMEM)] + [p...]
  transfers between devices with their start and end apart: 37 -> 37, of which waited for: 17 -> 20; matrix products, arithmetic and copies ran while one was open for 1% -> 1% of each run, Pallas kernels for 26% -> 25%
where the time goes in v10:
time: 170 us
  waiting for transfers between devices  59.3 us (35%)
  Pallas kernels  54.5 us (32%)
  starting transfers between devices  52.9 us (31%)
  other arithmetic  2.15 us (1%)
    ppermute x23, waiting for transfers between devices, swap_ch(): return lax.ppermute(value, 'ch', [(i, i ^ mask) for i in range(count)])  41.9 us
    pallas_call x12, Pallas kernels, vmem_call(): pl.pallas_call(run, in_specs=[pl.BlockSpec(memory_space=pltpu.SMEM)] + [p...  34.8 us
    ppermute x23, starting transfers between devices, swap_ch(): return lax.ppermute(value, 'ch', [(i, i ^ mask) for i in range(count)])  26.6 us
    ppermute x9, starting transfers between devices, rotate_chips(): lax.ppermute(value, 'ctx', [(i, (i + 2 * distance) % count) for i in rang...  18.8 us
    pallas_call x2, Pallas kernels, gated_chunk(): pl.pallas_call(functools.partial(gated_kernel, first_row, loads), grid=(c...  12.2 us
    ppermute x9, waiting for transfers between devices, rotate_chips(): lax.ppermute(value, 'ctx', [(i, (i + 2 * distance) % count) for i in rang...  9.69 us
    ppermute x4, waiting for transfers between devices, swap_ctx(): return lax.ppermute(value, 'ctx', [(i, i ^ mask) for i in range(count)])  7.69 us
    pallas_call x1, Pallas kernels, load(): pl.pallas_call(load_kernel, in_specs=[pl.BlockSpec(memory_space=pltpu.SME...  5.36 us
  transfers between devices with their start and end apart: 37, of which 20 were waited for; matrix products, arithmetic and copies ran while one was open for 1% of the time, Pallas kernels for 25%

profile of v10, /device:TPU:0, one launch (start us, length us, event | category | flops | bytes accessed | tf_op | source)
XLA Modules:
  0.0 169.6 jit_solution(10856171508043500892)
XLA Ops:
  2.3 2.4 %collective-permute-start = (bf16[3,144,1024]{2,1,0:T(8,128)(2,1)S(1)}, bf16[3,144,1024]{2,1,0:T(8,128)(2,1)S(1)}, u32[]{:S(2)}, u32[]{:S(2)}) collective-permute-start(bf16[3,144,1024]{2,1,0:T(8,128)(2,1)S(1)} %get-tuple-element.58), channel_id=1, source_target_pairs={{0,4},{4,8},{8,12},{12,16},{16,20},{20,24},{24,28},{1,5},{5,9},{9,... | collective-permute-start | bytes 2654216 | tf_op jit(solution)/shard_map/ppermute | solution.py:40
  4.7 2.4 %collective-permute-start.1 = (bf16[128,1024]{1,0:T(8,128)(2,1)S(1)}, bf16[128,1024]{1,0:T(8,128)(2,1)S(1)}, u32[]{:S(2)}, u32[]{:S(2)}) collective-permute-start(bf16[128,1024]{1,0:T(8,128)(2,1)S(1)} %get-tuple-element.61), channel_id=1, source_target_pairs={{0,1},{1,0},{2,3},{3,2},{4,5},{5,4},{6,7},{7,6},{8,9},{9,8},{10,11... | collective-permute-start | bytes 786440 | tf_op jit(solution)/shard_map/ppermute | solution.py:30
  8.7 6.1 %hyena_filters.3 = (bf16[256,1024]{1,0:T(8,128)(2,1)S(1)}, bf16[1024,4096]{1,0:T(8,128)(2,1)S(1)}) custom-call(s32[8]{0:T(128)S(1)} %stack.104.meta_ref.refs_0_, f32[3,7,64]{2,1,0:T(8,128)} %refs_1_.3, f32[64,128]{1,0:T(8,128)} %bitcast.50, f32[1,1024]{1,0:T(1,128)} %bitcast.55, bf16[3,512,1024]{2,1,0:T(8,128)(2,1)S(1)} %bitcast.39, bf16[1024,4096]{1,0:T(8,128)(2,1)} %refs_5_.1), custom_call_target="tpu_custom_call" | custom-call | tf_op jit(solution)/shard_map/hyena_filters/pallas_call | solution.py:173
  14.8 6.1 %hyena_filters.2.refs_1_ = bf16[256,1024]{1,0:T(8,128)(2,1)S(1)} custom-call(s32[8]{0:T(128)S(1)} %stack.104.meta_ref.refs_0_, f32[3,7,64]{2,1,0:T(8,128)} %refs_1_.3, f32[64,128]{1,0:T(8,128)} %bitcast.51, f32[1,1024]{1,0:T(1,128)} %bitcast.56, bf16[3,144,1024]{2,1,0:T(8,128)(2,1)S(1)} %collective-permute-done.refs_4_, bf16[3,512,1024]{2,1,0:T(8,128)(2,1)S(1)} %bitcast.40), custom_call_target="tpu_custom_call" | custom-call | tf_op jit(solution)/shard_map/hyena_filters/pallas_call | solution.py:173
  26.4 4.5 %collective-permute-start.10 = (bf16[3,128,1024]{2,1,0:T(8,128)(2,1)S(1)}, bf16[3,128,1024]{2,1,0:T(8,128)(2,1)S(1)}, u32[]{:S(2)}, u32[]{:S(2)}) collective-permute-start(bf16[3,128,1024]{2,1,0:T(8,128)(2,1)S(1)} %get-tuple-element.112.refs_4_), channel_id=1, source_target_pairs={{0,8},{4,12},{8,0},{12,4},{16,24},{20,28},{24,16},{28,20},{1,9},{5... | collective-permute-start | bytes 2359304 | tf_op jit(solution)/shard_map/ppermute | solution.py:35
  30.9 4.0 %hyena_terms.2 = (bf16[512,512]{1,0:T(8,128)(2,1)S(1)}, bf16[512,512]{1,0:T(8,128)(2,1)S(1)}, bf16[512,512]{1,0:T(8,128)(2,1)S(1)}, bf16[512,512]{1,0:T(8,128)(2,1)S(1)}, bf16[512,1024]{1,0:T(8,128)(2,1)S(1)}) custom-call(s32[8]{0:T(128)S(1)} %stack.104.meta_ref.refs_0_, bf16[256,1024]{1,0:T(8,128)(2,1)S(1)} %hyena_filters.2.refs_1_, ...), custom_call_target="tpu_custom_call" | custom-call | tf_op jit(solution)/shard_map/hyena_terms/pallas_call | solution.py:188
  41.6 5.8 %collective-permute-done.10.swapped = bf16[3,128,1024]{2,1,0:T(8,128)(2,1)S(1)} collective-permute-done((bf16[3,128,1024]{2,1,0:T(8,128)(2,1)S(1)}, bf16[3,128,1024]{2,1,0:T(8,128)(2,1)S(1)}, u32[]{:S(2)}, u32[]{:S(2)}) %collective-permute-start.10) | collective-permute-done | bytes 786464 | tf_op jit(solution)/shard_map/ppermute | solution.py:35
  47.4 5.4 %load_weights.1 = (bf16[4096,1536]{1,0:T(8,128)(2,1)S(1)}, bf16[512,1024]{1,0:T(8,128)(2,1)S(1)}) custom-call(s32[8]{0:T(128)S(1)} %stack.104.meta_ref.refs_0_, bf16[4096,1536]{1,0:T(8,128)(2,1)} %source.1, bf16[512,4096]{1,0:T(8,128)(2,1)} %outer.1, bf16[512,512]{1,0:T(8,128)(2,1)S(1)} %add_convert_fusion.along, ...), custom_call_target="tpu_custom_call" | custom-call | tf_op jit(solution)/shard_map/load_weights/pallas_call | solution.py:233
  52.8 8.6 %collective-permute-done.7.refs_4_ = bf16[512,512]{1,0:T(8,128)(2,1)S(1)} collective-permute-done((bf16[512,512]{1,0:T(8,128)(2,1)S(1)}, bf16[512,512]{1,0:T(8,128)(2,1)S(1)}, u32[]{:S(2)}, u32[]{:S(2)}) %collective-permute-start.7) | collective-permute-done | bytes 524320 | tf_op jit(solution)/shard_map/ppermute | solution.py:30
  64.7 12.2 %collective-permute-done.13.refs_3_ = bf16[256,1024]{1,0:T(8,128)(2,1)S(1)} collective-permute-done((bf16[256,1024]{1,0:T(8,128)(2,1)S(1)}, bf16[256,1024]{1,0:T(8,128)(2,1)S(1)}, u32[]{:S(2)}, u32[]{:S(2)}) %collective-permute-start.13) | collective-permute-done | bytes 524320 | tf_op jit(solution)/shard_map/ppermute | solution.py:30
  79.0 3.2 %qkv_near.2 = (f32[256,1536]{1,0:T(8,128)S(1)}, f32[256,128]{1,0:T(8,128)S(1)}) custom-call(s32[8]{0:T(128)S(1)} %stack.104.meta_ref.refs_0_, bf16[256,1024]{1,0:T(8,128)(2,1)S(1)} %get-tuple-element.72.refs_1_.refs_5_, bf16[256,1024]{1,0:T(8,128)(2,1)S(1)} %collective-permute-done.11.refs_2_, bf16[256,1024]{1,0:T(8,128)(2,1)S(1)} %collective-permute-done.13.refs_3_, ...), custom_call_target="tpu_custom_call" | custom-call | flops 3300000000 | bytes 10800000 | tf_op jit(solution)/shard_map/qkv_near/pallas_call | solution.py:188
  82.2 2.7 %collective-permute-done.14.refs_2_ = bf16[128,1024]{1,0:T(8,128)(2,1)S(1)} collective-permute-done((bf16[128,1024]{1,0:T(8,128)(2,1)S(1)}, bf16[128,1024]{1,0:T(8,128)(2,1)S(1)}, u32[]{:S(2)}, u32[]{:S(2)}) %collective-permute-start.14) | collective-permute-done | bytes 262176 | tf_op jit(solution)/shard_map/ppermute | solution.py:30
  90.1 2.6 %collective-permute-start.15 = (bf16[3,256,128]{2,1,0:T(8,128)(2,1)S(1)}, bf16[3,256,128]{2,1,0:T(8,128)(2,1)S(1)}, u32[]{:S(2)}, u32[]{:S(2)}) collective-permute-start(bf16[3,256,128]{2,1,0:T(8,128)(2,1)S(1)} %get-tuple-element.76), channel_id=1, source_target_pairs={{0,8},{4,12},{8,16},{12,20},{16,24},{20,28},{24,0},{28,4},{1,9},{5... | collective-permute-start | bytes 589832 | tf_op jit(solution)/shard_map/ppermute | solution.py:45
  93.8 2.8 %collective-permute-start.17 = (bf16[3,256,128]{2,1,0:T(8,128)(2,1)S(1)}, bf16[3,256,128]{2,1,0:T(8,128)(2,1)S(1)}, u32[]{:S(2)}, u32[]{:S(2)}) collective-permute-start(bf16[3,256,128]{2,1,0:T(8,128)(2,1)S(1)} %get-tuple-element.78), channel_id=1, source_target_pairs={{0,24},{4,28},{8,0},{12,4},{16,8},{20,12},{24,16},{28,20},{1,25},{... | collective-permute-start | bytes 589832 | tf_op jit(solution)/shard_map/ppermute | solution.py:45
  101.6 3.2 %qkv_near.3 = (f32[256,1536]{1,0:T(8,128)S(1)}, f32[256,128]{1,0:T(8,128)S(1)}) custom-call(s32[8]{0:T(128)S(1)} %stack.104.meta_ref.refs_0_, bf16[256,1024]{1,0:T(8,128)(2,1)S(1)} %get-tuple-element.80.refs_1_.refs_4_, bf16[256,1024]{1,0:T(8,128)(2,1)S(1)} %collective-permute-done.18.refs_2_, bf16[256,1024]{1,0:T(8,128)(2,1)S(1)} %collective-permute-done.20.refs_3_, ...), custom_call_target="tpu_custom_call" | custom-call | flops 3300000000 | bytes 10800000 | tf_op jit(solution)/shard_map/qkv_near/pallas_call | solution.py:188
  110.5 2.8 %collective-permute-start.24 = (bf16[3,256,128]{2,1,0:T(8,128)(2,1)S(1)}, bf16[3,256,128]{2,1,0:T(8,128)(2,1)S(1)}, u32[]{:S(2)}, u32[]{:S(2)}) collective-permute-start(bf16[3,256,128]{2,1,0:T(8,128)(2,1)S(1)} %get-tuple-element.86), channel_id=1, source_target_pairs={{0,24},{4,28},{8,0},{12,4},{16,8},{20,12},{24,16},{28,20},{1,25},{... | collective-permute-start | bytes 589832 | tf_op jit(solution)/shard_map/ppermute | solution.py:45
  113.6 3.8 %collective-permute-done.22.refs_2_.refs_3_ = bf16[3,256,128]{2,1,0:T(8,128)(2,1)S(1)} collective-permute-done((bf16[3,256,128]{2,1,0:T(8,128)(2,1)S(1)}, bf16[3,256,128]{2,1,0:T(8,128)(2,1)S(1)}, u32[]{:S(2)}, u32[]{:S(2)}) %collective-permute-start.22) | collective-permute-done | bytes 196640 | tf_op jit(solution)/shard_map/ppermute | solution.py:45
  117.4 4.8 %collective-permute-done.23.refs_3_ = bf16[3,256,128]{2,1,0:T(8,128)(2,1)S(1)} collective-permute-done((bf16[3,256,128]{2,1,0:T(8,128)(2,1)S(1)}, bf16[3,256,128]{2,1,0:T(8,128)(2,1)S(1)}, u32[]{:S(2)}, u32[]{:S(2)}) %collective-permute-start.23) | collective-permute-done | bytes 196640 | tf_op jit(solution)/shard_map/ppermute | solution.py:45
  125.1 4.8 %attention.2 = (bf16[512,128]{1,0:T(8,128)(2,1)S(1)}, bf16[512,128]{1,0:T(8,128)(2,1)S(1)}, bf16[2,4,512,128]{3,2,1,0:T(8,128)(2,1)S(1)}, bf16[2,4,128,512]{3,2,1,0:T(8,128)(2,1)S(1)}) custom-call(s32[8]{0:T(128)S(1)} %stack.104.meta_ref.refs_0_, bf16[3,256,128]{2,1,0:T(8,128)(2,1)S(1)} %get-tuple-element.87.refs_1_, ...), custom_call_target="tpu_custom_call" | custom-call | flops 6600000000 | bytes 21600000 | tf_op jit(solution)/shard_map/attention/pallas_call | solution.py:188
  129.9 3.0 %collective-permute-start.28 = (bf16[512,128]{1,0:T(8,128)(2,1)S(1)}, bf16[512,128]{1,0:T(8,128)(2,1)S(1)}, u32[]{:S(2)}, u32[]{:S(2)}) collective-permute-start(bf16[512,128]{1,0:T(8,128)(2,1)S(1)} %get-tuple-element.96), channel_id=1, source_target_pairs={{0,16},{4,20},{8,24},{12,28},{16,0},{20,4},{24,8},{28,12},{1,17},{... | collective-permute-start | bytes 393224 | tf_op jit(solution)/shard_map/ppermute | solution.py:45
  132.9 6.7 %attention.3 = (bf16[512,128]{1,0:T(8,128)(2,1)S(1)}, bf16[512,128]{1,0:T(8,128)(2,1)S(1)}) custom-call(s32[8]{0:T(128)S(1)} %stack.104.meta_ref.refs_0_, bf16[3,256,128]{2,1,0:T(8,128)(2,1)S(1)} %collective-permute-done.24.refs_4_.refs_1_, bf16[3,256,128]{2,1,0:T(8,128)(2,1)S(1)} %collective-permute-done.17.refs_8_.refs_2_, ...), custom_call_target="tpu_custom_call" | custom-call | flops 6600000000 | bytes 21600000 | tf_op jit(solution)/shard_map/attention/pallas_call | solution.py:188
  142.2 2.8 %collective-permute-start.29 = (bf16[512,128]{1,0:T(8,128)(2,1)S(1)}, bf16[512,128]{1,0:T(8,128)(2,1)S(1)}, u32[]{:S(2)}, u32[]{:S(2)}) collective-permute-start(bf16[512,128]{1,0:T(8,128)(2,1)S(1)} %get-tuple-element.102), channel_id=1, source_target_pairs={{0,8},{4,12},{8,16},{12,20},{16,24},{20,28},{24,0},{28,4},{1,9},{5... | collective-permute-start | bytes 393224 | tf_op jit(solution)/shard_map/ppermute | solution.py:45
  154.2 6.7 %collective-permute-done.34.refs_3_ = bf16[2,512,128]{2,1,0:T(8,128)(2,1)S(1)} collective-permute-done((bf16[2,512,128]{2,1,0:T(8,128)(2,1)S(1)}, bf16[2,512,128]{2,1,0:T(8,128)(2,1)S(1)}, u32[]{:S(2)}, u32[]{:S(2)}) %collective-permute-start.34) | collective-permute-done | bytes 262176 | tf_op jit(solution)/shard_map/ppermute | solution.py:30
  161.4 3.3 %collective-permute-done.36.refs_1_ = bf16[2,512,128]{2,1,0:T(8,128)(2,1)S(1)} collective-permute-done((bf16[2,512,128]{2,1,0:T(8,128)(2,1)S(1)}, bf16[2,512,128]{2,1,0:T(8,128)(2,1)S(1)}, u32[]{:S(2)}, u32[]{:S(2)}) %collective-permute-start.36) | collective-permute-done | bytes 262176 | tf_op jit(solution)/shard_map/ppermute | solution.py:30
  (98 shorter events, 58.4 us)
Async XLA Ops:
  2.3 12.5 %collective-permute-start = (bf16[3,144,1024]{2,1,0:T(8,128)(2,1)S(1)}, bf16[3,144,1024]{2,1,0:T(8,128)(2,1)S(1)}, u32[]{:S(2)}, u32[]{:S(2)}) collective-permute-start(bf16[3,144,1024]{2,1,0:T(8,128)(2,1)S(1)} %get-tuple-element.58), channel_id=1, source_target_pairs={{0,4},{4,8},{8,12},{12,16},{16,20},{20,24},{24,28},{1,5},{5,9},{9,... | collective-permute-start | bytes 2654216 | tf_op jit(solution)/shard_map/ppermute | solution.py:40
  4.7 16.1 %collective-permute-start.1 = (bf16[128,1024]{1,0:T(8,128)(2,1)S(1)}, bf16[128,1024]{1,0:T(8,128)(2,1)S(1)}, u32[]{:S(2)}, u32[]{:S(2)}) collective-permute-start(bf16[128,1024]{1,0:T(8,128)(2,1)S(1)} %get-tuple-element.61), channel_id=1, source_target_pairs={{0,1},{1,0},{2,3},{3,2},{4,5},{5,4},{6,7},{7,6},{8,9},{9,8},{10,11... | collective-permute-start | bytes 786440 | tf_op jit(solution)/shard_map/ppermute | solution.py:30
  7.1 13.8 %collective-permute-start.2 = (bf16[128,1024]{1,0:T(8,128)(2,1)S(1)}, bf16[128,1024]{1,0:T(8,128)(2,1)S(1)}, u32[]{:S(2)}, u32[]{:S(2)}) collective-permute-start(bf16[128,1024]{1,0:T(8,128)(2,1)S(1)} %get-tuple-element.62), channel_id=1, source_target_pairs={{0,2},{1,3},{2,0},{3,1},{4,6},{5,7},{6,4},{7,5},{8,10},{9,11},{10,... | collective-permute-start | bytes 786440 | tf_op jit(solution)/shard_map/ppermute | solution.py:30
  8.7 12.3 %collective-permute-start.3 = (bf16[128,1024]{1,0:T(8,128)(2,1)S(1)}, bf16[128,1024]{1,0:T(8,128)(2,1)S(1)}, u32[]{:S(2)}, u32[]{:S(2)}) collective-permute-start(bf16[128,1024]{1,0:T(8,128)(2,1)S(1)} %get-tuple-element.63), channel_id=1, source_target_pairs={{0,3},{1,2},{2,1},{3,0},{4,7},{5,6},{6,5},{7,4},{8,11},{9,10},{10,... | collective-permute-start | bytes 786440 | tf_op jit(solution)/shard_map/ppermute | solution.py:30
  22.7 13.4 %collective-permute-start.6 = (bf16[512,512]{1,0:T(8,128)(2,1)S(1)}, bf16[512,512]{1,0:T(8,128)(2,1)S(1)}, u32[]{:S(2)}, u32[]{:S(2)}) collective-permute-start(bf16[512,512]{1,0:T(8,128)(2,1)S(1)} %get-tuple-element.68), channel_id=1, source_target_pairs={{0,2},{1,3},{2,0},{3,1},{4,6},{5,7},{6,4},{7,5},{8,10},{9,11},{10,... | collective-permute-start | bytes 1572872 | tf_op jit(solution)/shard_map/ppermute | solution.py:30
  24.8 14.1 %collective-permute-start.8 = (bf16[512,512]{1,0:T(8,128)(2,1)S(1)}, bf16[512,512]{1,0:T(8,128)(2,1)S(1)}, u32[]{:S(2)}, u32[]{:S(2)}) collective-permute-start(bf16[512,512]{1,0:T(8,128)(2,1)S(1)} %get-tuple-element.70), channel_id=1, source_target_pairs={{0,1},{1,0},{2,3},{3,2},{4,5},{5,4},{6,7},{7,6},{8,9},{9,8},{10,11... | collective-permute-start | bytes 1572872 | tf_op jit(solution)/shard_map/ppermute | solution.py:30
  26.4 21.0 %collective-permute-start.10 = (bf16[3,128,1024]{2,1,0:T(8,128)(2,1)S(1)}, bf16[3,128,1024]{2,1,0:T(8,128)(2,1)S(1)}, u32[]{:S(2)}, u32[]{:S(2)}) collective-permute-start(bf16[3,128,1024]{2,1,0:T(8,128)(2,1)S(1)} %get-tuple-element.112.refs_4_), channel_id=1, source_target_pairs={{0,8},{4,12},{8,0},{12,4},{16,24},{20,28},{24,16},{28,20},{1,9},{5... | collective-permute-start | bytes 2359304 | tf_op jit(solution)/shard_map/ppermute | solution.py:35
  34.9 17.9 %collective-permute-start.4 = (bf16[512,512]{1,0:T(8,128)(2,1)S(1)}, bf16[512,512]{1,0:T(8,128)(2,1)S(1)}, u32[]{:S(2)}, u32[]{:S(2)}) collective-permute-start(bf16[512,512]{1,0:T(8,128)(2,1)S(1)} %get-tuple-element.65), channel_id=1, source_target_pairs={{0,1},{1,0},{2,3},{3,2},{4,5},{5,4},{6,7},{7,6},{8,9},{9,8},{10,11... | collective-permute-start | bytes 1572872 | tf_op jit(solution)/shard_map/ppermute | solution.py:30
  35.5 17.3 %collective-permute-start.5 = (bf16[512,512]{1,0:T(8,128)(2,1)S(1)}, bf16[512,512]{1,0:T(8,128)(2,1)S(1)}, u32[]{:S(2)}, u32[]{:S(2)}) collective-permute-start(bf16[512,512]{1,0:T(8,128)(2,1)S(1)} %get-tuple-element.66), channel_id=1, source_target_pairs={{0,2},{1,3},{2,0},{3,1},{4,6},{5,7},{6,4},{7,5},{8,10},{9,11},{10,... | collective-permute-start | bytes 1572872 | tf_op jit(solution)/shard_map/ppermute | solution.py:30
  36.3 25.1 %collective-permute-start.7 = (bf16[512,512]{1,0:T(8,128)(2,1)S(1)}, bf16[512,512]{1,0:T(8,128)(2,1)S(1)}, u32[]{:S(2)}, u32[]{:S(2)}) collective-permute-start(bf16[512,512]{1,0:T(8,128)(2,1)S(1)} %add_convert_fusion.1), channel_id=1, source_target_pairs={{0,1},{1,0},{2,3},{3,2},{4,5},{5,4},{6,7},{7,6},{8,9},{9,8},{10,11... | collective-permute-start | bytes 1572872 | tf_op jit(solution)/shard_map/ppermute | solution.py:30
  39.1 22.3 %collective-permute-start.9 = (bf16[512,512]{1,0:T(8,128)(2,1)S(1)}, bf16[512,512]{1,0:T(8,128)(2,1)S(1)}, u32[]{:S(2)}, u32[]{:S(2)}) collective-permute-start(bf16[512,512]{1,0:T(8,128)(2,1)S(1)} %add_convert_fusion.along), channel_id=1, source_target_pairs={{0,2},{1,3},{2,0},{3,1},{4,6},{5,7},{6,4},{7,5},{8,10},{9,11},{10,... | collective-permute-start | bytes 1572872 | tf_op jit(solution)/shard_map/ppermute | solution.py:30
  62.5 14.4 %collective-permute-start.13 = (bf16[256,1024]{1,0:T(8,128)(2,1)S(1)}, bf16[256,1024]{1,0:T(8,128)(2,1)S(1)}, u32[]{:S(2)}, u32[]{:S(2)}) collective-permute-start(bf16[256,1024]{1,0:T(8,128)(2,1)S(1)} %get-tuple-element.72.refs_1_.refs_5_), channel_id=1, source_target_pairs={{0,2},{1,3},{2,0},{3,1},{4,6},{5,7},{6,4},{7,5},{8,10},{9,11},{10,... | collective-permute-start | bytes 1572872 | tf_op jit(solution)/shard_map/ppermute | solution.py:30
  63.2 15.2 %collective-permute-start.11 = (bf16[256,1024]{1,0:T(8,128)(2,1)S(1)}, bf16[256,1024]{1,0:T(8,128)(2,1)S(1)}, u32[]{:S(2)}, u32[]{:S(2)}) collective-permute-start(bf16[256,1024]{1,0:T(8,128)(2,1)S(1)} %get-tuple-element.72.refs_1_.refs_5_), channel_id=1, source_target_pairs={{0,1},{1,0},{2,3},{3,2},{4,5},{5,4},{6,7},{7,6},{8,9},{9,8},{10,11... | collective-permute-start | bytes 1572872 | tf_op jit(solution)/shard_map/ppermute | solution.py:30
  86.2 12.5 %collective-permute-start.20 = (bf16[256,1024]{1,0:T(8,128)(2,1)S(1)}, bf16[256,1024]{1,0:T(8,128)(2,1)S(1)}, u32[]{:S(2)}, u32[]{:S(2)}) collective-permute-start(bf16[256,1024]{1,0:T(8,128)(2,1)S(1)} %get-tuple-element.80.refs_1_.refs_4_), channel_id=1, source_target_pairs={{0,2},{1,3},{2,0},{3,1},{4,6},{5,7},{6,4},{7,5},{8,10},{9,11},{10,... | collective-permute-start | bytes 1572872 | tf_op jit(solution)/shard_map/ppermute | solution.py:30
  86.5 12.8 %collective-permute-start.18 = (bf16[256,1024]{1,0:T(8,128)(2,1)S(1)}, bf16[256,1024]{1,0:T(8,128)(2,1)S(1)}, u32[]{:S(2)}, u32[]{:S(2)}) collective-permute-start(bf16[256,1024]{1,0:T(8,128)(2,1)S(1)} %get-tuple-element.80.refs_1_.refs_4_), channel_id=1, source_target_pairs={{0,1},{1,0},{2,3},{3,2},{4,5},{5,4},{6,7},{7,6},{8,9},{9,8},{10,11... | collective-permute-start | bytes 1572872 | tf_op jit(solution)/shard_map/ppermute | solution.py:30
  90.1 20.4 %collective-permute-start.15 = (bf16[3,256,128]{2,1,0:T(8,128)(2,1)S(1)}, bf16[3,256,128]{2,1,0:T(8,128)(2,1)S(1)}, u32[]{:S(2)}, u32[]{:S(2)}) collective-permute-start(bf16[3,256,128]{2,1,0:T(8,128)(2,1)S(1)} %get-tuple-element.76), channel_id=1, source_target_pairs={{0,8},{4,12},{8,16},{12,20},{16,24},{20,28},{24,0},{28,4},{1,9},{5... | collective-permute-start | bytes 589832 | tf_op jit(solution)/shard_map/ppermute | solution.py:45
  92.7 20.8 %collective-permute-start.16 = (bf16[3,256,128]{2,1,0:T(8,128)(2,1)S(1)}, bf16[3,256,128]{2,1,0:T(8,128)(2,1)S(1)}, u32[]{:S(2)}, u32[]{:S(2)}) collective-permute-start(bf16[3,256,128]{2,1,0:T(8,128)(2,1)S(1)} %get-tuple-element.77), channel_id=1, source_target_pairs={{0,16},{4,20},{8,24},{12,28},{16,0},{20,4},{24,8},{28,12},{1,17},{... | collective-permute-start | bytes 589832 | tf_op jit(solution)/shard_map/ppermute | solution.py:45
  93.8 19.8 %collective-permute-start.17 = (bf16[3,256,128]{2,1,0:T(8,128)(2,1)S(1)}, bf16[3,256,128]{2,1,0:T(8,128)(2,1)S(1)}, u32[]{:S(2)}, u32[]{:S(2)}) collective-permute-start(bf16[3,256,128]{2,1,0:T(8,128)(2,1)S(1)} %get-tuple-element.78), channel_id=1, source_target_pairs={{0,24},{4,28},{8,0},{12,4},{16,8},{20,12},{24,16},{28,20},{1,25},{... | collective-permute-start | bytes 589832 | tf_op jit(solution)/shard_map/ppermute | solution.py:45
  109.4 12.8 %collective-permute-start.23 = (bf16[3,256,128]{2,1,0:T(8,128)(2,1)S(1)}, bf16[3,256,128]{2,1,0:T(8,128)(2,1)S(1)}, u32[]{:S(2)}, u32[]{:S(2)}) collective-permute-start(bf16[3,256,128]{2,1,0:T(8,128)(2,1)S(1)} %get-tuple-element.85), channel_id=1, source_target_pairs={{0,16},{4,20},{8,24},{12,28},{16,0},{20,4},{24,8},{28,12},{1,17},{... | collective-permute-start | bytes 589832 | tf_op jit(solution)/shard_map/ppermute | solution.py:45
  110.5 11.7 %collective-permute-start.24 = (bf16[3,256,128]{2,1,0:T(8,128)(2,1)S(1)}, bf16[3,256,128]{2,1,0:T(8,128)(2,1)S(1)}, u32[]{:S(2)}, u32[]{:S(2)}) collective-permute-start(bf16[3,256,128]{2,1,0:T(8,128)(2,1)S(1)} %get-tuple-element.86), channel_id=1, source_target_pairs={{0,24},{4,28},{8,0},{12,4},{16,8},{20,12},{24,16},{28,20},{1,25},{... | collective-permute-start | bytes 589832 | tf_op jit(solution)/shard_map/ppermute | solution.py:45
  113.5 11.5 %collective-permute-start.27 = (bf16[2,3,128,1024]{3,2,1,0:T(8,128)(2,1)S(1)}, bf16[2,3,128,1024]{3,2,1,0:T(8,128)(2,1)S(1)}, u32[]{:S(2)}, u32[]{:S(2)}) collective-permute-start(bf16[2,3,128,1024]{3,2,1,0:T(8,128)(2,1)S(1)} %pad_maximum_fusion.refs_7_.refs_6_.refs_5_), channel_id=1, source_target_pairs={{0,4},{4,0},{8,12},{12,8},{16,20},{20,16},{24,28},{28,24},{1,5},{5... | collective-permute-start | bytes 4718600 | tf_op jit(solution)/shard_map/ppermute | solution.py:35
  129.9 9.8 %collective-permute-start.28 = (bf16[512,128]{1,0:T(8,128)(2,1)S(1)}, bf16[512,128]{1,0:T(8,128)(2,1)S(1)}, u32[]{:S(2)}, u32[]{:S(2)}) collective-permute-start(bf16[512,128]{1,0:T(8,128)(2,1)S(1)} %get-tuple-element.96), channel_id=1, source_target_pairs={{0,16},{4,20},{8,24},{12,28},{16,0},{20,4},{24,8},{28,12},{1,17},{... | collective-permute-start | bytes 393224 | tf_op jit(solution)/shard_map/ppermute | solution.py:45
  152.1 12.7 %collective-permute-start.36 = (bf16[2,512,128]{2,1,0:T(8,128)(2,1)S(1)}, bf16[2,512,128]{2,1,0:T(8,128)(2,1)S(1)}, u32[]{:S(2)}, u32[]{:S(2)}) collective-permute-start(bf16[2,512,128]{2,1,0:T(8,128)(2,1)S(1)} %collective-permute-done.31.refs_2_), channel_id=1, source_target_pairs={{0,2},{1,3},{2,0},{3,1},{4,6},{5,7},{6,4},{7,5},{8,10},{9,11},{10,... | collective-permute-start | bytes 786440 | tf_op jit(solution)/shard_map/ppermute | solution.py:30
  153.7 12.8 %collective-permute-start.33 = (bf16[2,512,128]{2,1,0:T(8,128)(2,1)S(1)}, bf16[2,512,128]{2,1,0:T(8,128)(2,1)S(1)}, u32[]{:S(2)}, u32[]{:S(2)}) collective-permute-start(bf16[2,512,128]{2,1,0:T(8,128)(2,1)S(1)} %pad_maximum_fusion.5.refs_2_), channel_id=1, source_target_pairs={{0,1},{1,0},{2,3},{3,2},{4,5},{5,4},{6,7},{7,6},{8,9},{9,8},{10,11... | collective-permute-start | bytes 786440 | tf_op jit(solution)/shard_map/ppermute | solution.py:30
  (16 other events, 135.1 us)

commit v11 on v10

--- a/solution.py
+++ b/solution.py
@@ -10,7 +10,7 @@
 HEAD = 128
 GROUP_SIZE = 16
 LANES = 128
-TILES = 2
+TILES = 4
 LEAD = 16
 norm_eps = 1e-05
 SCORE_SCALE = 1.4426950408889634 / HEAD**0.5
@@ -308,16 +308,10 @@
                 values[1, place, :, first : first + HEAD] = stacked[distance, 1, taken, :]
 
 
-def attention_kernel(chips, chunks, distances, leading, meta_ref, *refs):
-    if leading:
-        pieces, other = refs[: chunks * chips], refs[chunks * chips : chunks * (chips + 1)]
-        *outs, keys, values = refs[chunks * (chips + 1) :]
-        gather_keys(chips, meta_ref, pieces, other, keys, values)
-        sources = [pieces[(chips - distance) % chips :: chips] for distance in distances]
-    else:
-        taken = chunks * len(distances)
-        pieces, (keys, values), outs = refs[:taken], refs[taken : taken + 2], refs[taken + 2 :]
-        sources = [pieces[index * chunks : (index + 1) * chunks] for index in range(len(distances))]
+def attention_kernel(chips, chunks, meta_ref, *refs):
+    pieces, other = refs[: chunks * chips], refs[chunks * chips : chunks * (chips + 1)]
+    *outs, keys, values = refs[chunks * (chips + 1) :]
+    gather_keys(chips, meta_ref, pieces, other, keys, values)
     chip, core = meta_ref[4], meta_ref[5]
     count = keys.shape[2]
 
@@ -343,7 +337,8 @@
 
     key_row = lax.broadcasted_iota(jnp.int32, (count, count), 0)
     query_column = lax.broadcasted_iota(jnp.int32, (count, count), 1)
-    for distance, source, out in zip(distances, sources, outs):
+    for distance, out in enumerate(outs):
+        source = pieces[(chips - distance) % chips :: chips]
         place = lax.rem(chip + distance, chips)
         queries = jnp.concatenate([piece[0] for piece in source], axis=0)
         mine = jnp.where(key_row <= query_column, scores_of(0, place, queries), -1e30)
@@ -357,19 +352,13 @@
         out[...] = (state[2] / state[1]).T.astype(BF16)
 
 
-def attend(meta, own, other, laid, distances, waits, chips):
-    chunks, leading = len(other), laid is None
+def attend(meta, own, other, waits, chips):
+    chunks = len(other)
     count = own[0].shape[1] * chunks
-    outs = [((count, HEAD), BF16)] * len(distances)
-    if leading:
-        operands = own + other
-        outs = outs + [((2, chips, count, HEAD), BF16), ((2, chips, HEAD, count), BF16)]
-    else:
-        operands = [piece for distance in distances for piece in own[(chips - distance) % chips :: chips]]
-        operands = [*operands, *laid]
-    body = functools.partial(attention_kernel, chips, chunks, distances, leading)
-    made = list(vmem_call(body, "attention", 6, meta, operands, outs, waits=waits))
-    return made[: len(distances)], laid or made[len(distances) :]
+    body = functools.partial(attention_kernel, chips, chunks)
+    outs = [((count, HEAD), BF16)] * chips
+    scratch = [pltpu.VMEM((2, chips, count, HEAD), BF16), pltpu.VMEM((2, chips, HEAD, count), BF16)]
+    return vmem_call(body, "attention", 12, meta, own + other, outs, scratch, waits)
 
 
 def pick_kernel(meta_ref, weight, features, *refs):
@@ -672,11 +661,9 @@
     own, other = own[1] + own[0], other[::-1]
 
     groups = [(*range(2, chips, 2), 0), tuple(range(1, chips, 2))]
-    given, laid = attend(meta, own, other, None, groups[0], [far_w], chips)
-    first = [rotate_chips(piece, d) if d else piece for d, piece in zip(groups[0], given)]
-    given, _ = attend(meta, own, other, laid, groups[1], [], chips)
-    first, given = lax.optimization_barrier((first, given))
-    second = [rotate_chips(piece, d) for d, piece in zip(groups[1], given)]
+    given = attend(meta, own, other, [far_w], chips)
+    first, second = [[rotate_chips(given[d], d) if d else given[d] for d in group] for group in groups]
+    first, second = lax.optimization_barrier((first, second[:1]))[0], second
     back = jnp.stack(first)
     by_x, by_y = swap_ch(back, 1), swap_ch(back, 2)
     add = functools.partial(mix, meta, groups=groups, own_w=own_w, near_w=near_w, far_w=far_w, chips=chips)

time: 170 us -> 179 us (1.053)
  waiting for transfers between devices: 59.3 us -> 67.2 us
    ppermute x9, waiting for transfers between devices: 9.69 us -> 17.3 us  [rotate_chips(): lax.ppermute(value, 'ctx', [(i, (i + 2 * distance) % count) for i in rang...]
    pallas_call x12 -> x11, Pallas kernels: 34.8 us -> 34.1 us  [vmem_call(): pl.pallas_call(run, in_specs=[pl.BlockSpec(memory_space=pltpu.SMEM)] + [p...]
  transfers between devices with their start and end apart: 37 -> 37, of which waited for: 20 -> 21; matrix products, arithmetic and copies ran while one was open for 1% -> 1% of each run, Pallas kernels for 25% -> 20%
where the time goes in v11:
time: 179 us; the launch traced here: 178 us
  waiting for transfers between devices  67.2 us (38%)
  starting transfers between devices  54.3 us (30%)
  Pallas kernels  53.9 us (30%)
  other arithmetic  2.15 us (1%)
    ppermute x23, waiting for transfers between devices, swap_ch(): return lax.ppermute(value, 'ch', [(i, i ^ mask) for i in range(count)])  42.7 us
    pallas_call x11, Pallas kernels, vmem_call(): pl.pallas_call(run, in_specs=[pl.BlockSpec(memory_space=pltpu.SMEM)] + [p...  34.1 us
    ppermute x23, starting transfers between devices, swap_ch(): return lax.ppermute(value, 'ch', [(i, i ^ mask) for i in range(count)])  27.9 us
    ppermute x9, starting transfers between devices, rotate_chips(): lax.ppermute(value, 'ctx', [(i, (i + 2 * distance) % count) for i in rang...  19.1 us
    ppermute x9, waiting for transfers between devices, rotate_chips(): lax.ppermute(value, 'ctx', [(i, (i + 2 * distance) % count) for i in rang...  17.3 us
    pallas_call x2, Pallas kernels, gated_chunk(): pl.pallas_call(functools.partial(gated_kernel, first_row, loads), grid=(c...  12.1 us
    ppermute x4, waiting for transfers between devices, swap_ctx(): return lax.ppermute(value, 'ctx', [(i, i ^ mask) for i in range(count)])  7.24 us
    pallas_call x1, Pallas kernels, load(): pl.pallas_call(load_kernel, in_specs=[pl.BlockSpec(memory_space=pltpu.SME...  5.36 us
  transfers between devices with their start and end apart: 37, of which 21 were waited for; matrix products, arithmetic and copies ran while one was open for 1% of the time, Pallas kernels for 20%

profile of v11, /device:TPU:0, one launch (start us, length us, event | category | flops | bytes accessed | tf_op | source)
XLA Modules:
  0.0 178.2 jit_solution(14677686723379639357)
XLA Ops:
  2.3 2.4 %collective-permute-start = (bf16[3,144,1024]{2,1,0:T(8,128)(2,1)S(1)}, bf16[3,144,1024]{2,1,0:T(8,128)(2,1)S(1)}, u32[]{:S(2)}, u32[]{:S(2)}) collective-permute-start(bf16[3,144,1024]{2,1,0:T(8,128)(2,1)S(1)} %get-tuple-element.54), channel_id=1, source_target_pairs={{0,4},{4,8},{8,12},{12,16},{16,20},{20,24},{24,28},{1,5},{5,9},{9,... | collective-permute-start | bytes 2654216 | tf_op jit(solution)/shard_map/ppermute | solution.py:40
  4.7 2.4 %collective-permute-start.1 = (bf16[128,1024]{1,0:T(8,128)(2,1)S(1)}, bf16[128,1024]{1,0:T(8,128)(2,1)S(1)}, u32[]{:S(2)}, u32[]{:S(2)}) collective-permute-start(bf16[128,1024]{1,0:T(8,128)(2,1)S(1)} %get-tuple-element.57), channel_id=1, source_target_pairs={{0,1},{1,0},{2,3},{3,2},{4,5},{5,4},{6,7},{7,6},{8,9},{9,8},{10,11... | collective-permute-start | bytes 786440 | tf_op jit(solution)/shard_map/ppermute | solution.py:30
  8.7 6.3 %hyena_filters.3 = (bf16[256,1024]{1,0:T(8,128)(2,1)S(1)}, bf16[1024,4096]{1,0:T(8,128)(2,1)S(1)}) custom-call(s32[8]{0:T(128)S(1)} %stack.104.meta_ref.refs_0_, f32[3,7,64]{2,1,0:T(8,128)} %refs_1_.3, f32[64,128]{1,0:T(8,128)} %bitcast.50, f32[1,1024]{1,0:T(1,128)} %bitcast.55, bf16[3,512,1024]{2,1,0:T(8,128)(2,1)S(1)} %bitcast.39, bf16[1024,4096]{1,0:T(8,128)(2,1)} %refs_5_.1), custom_call_target="tpu_custom_call" | custom-call | tf_op jit(solution)/shard_map/hyena_filters/pallas_call | solution.py:173
  15.0 5.8 %hyena_filters.2.refs_1_ = bf16[256,1024]{1,0:T(8,128)(2,1)S(1)} custom-call(s32[8]{0:T(128)S(1)} %stack.104.meta_ref.refs_0_, f32[3,7,64]{2,1,0:T(8,128)} %refs_1_.3, f32[64,128]{1,0:T(8,128)} %bitcast.51, f32[1,1024]{1,0:T(1,128)} %bitcast.56, bf16[3,144,1024]{2,1,0:T(8,128)(2,1)S(1)} %collective-permute-done.refs_4_, bf16[3,512,1024]{2,1,0:T(8,128)(2,1)S(1)} %bitcast.40), custom_call_target="tpu_custom_call" | custom-call | tf_op jit(solution)/shard_map/hyena_filters/pallas_call | solution.py:173
  26.3 4.3 %collective-permute-start.10 = (bf16[3,128,1024]{2,1,0:T(8,128)(2,1)S(1)}, bf16[3,128,1024]{2,1,0:T(8,128)(2,1)S(1)}, u32[]{:S(2)}, u32[]{:S(2)}) collective-permute-start(bf16[3,128,1024]{2,1,0:T(8,128)(2,1)S(1)} %get-tuple-element.104.refs_4_), channel_id=1, source_target_pairs={{0,8},{4,12},{8,0},{12,4},{16,24},{20,28},{24,16},{28,20},{1,9},{5... | collective-permute-start | bytes 2359304 | tf_op jit(solution)/shard_map/ppermute | solution.py:35
  30.6 4.0 %hyena_terms.2 = (bf16[512,512]{1,0:T(8,128)(2,1)S(1)}, bf16[512,512]{1,0:T(8,128)(2,1)S(1)}, bf16[512,512]{1,0:T(8,128)(2,1)S(1)}, bf16[512,512]{1,0:T(8,128)(2,1)S(1)}, bf16[512,1024]{1,0:T(8,128)(2,1)S(1)}) custom-call(s32[8]{0:T(128)S(1)} %stack.104.meta_ref.refs_0_, bf16[256,1024]{1,0:T(8,128)(2,1)S(1)} %hyena_filters.2.refs_1_, ...), custom_call_target="tpu_custom_call" | custom-call | tf_op jit(solution)/shard_map/hyena_terms/pallas_call | solution.py:188
  41.8 5.3 %collective-permute-done.10.swapped = bf16[3,128,1024]{2,1,0:T(8,128)(2,1)S(1)} collective-permute-done((bf16[3,128,1024]{2,1,0:T(8,128)(2,1)S(1)}, bf16[3,128,1024]{2,1,0:T(8,128)(2,1)S(1)}, u32[]{:S(2)}, u32[]{:S(2)}) %collective-permute-start.10) | collective-permute-done | bytes 786464 | tf_op jit(solution)/shard_map/ppermute | solution.py:35
  47.1 5.4 %load_weights.1 = (bf16[4096,1536]{1,0:T(8,128)(2,1)S(1)}, bf16[512,1024]{1,0:T(8,128)(2,1)S(1)}) custom-call(s32[8]{0:T(128)S(1)} %stack.104.meta_ref.refs_0_, bf16[4096,1536]{1,0:T(8,128)(2,1)} %source.1, bf16[512,4096]{1,0:T(8,128)(2,1)} %outer.1, bf16[512,512]{1,0:T(8,128)(2,1)S(1)} %add_convert_fusion.along, ...), custom_call_target="tpu_custom_call" | custom-call | tf_op jit(solution)/shard_map/load_weights/pallas_call | solution.py:233
  52.5 9.2 %collective-permute-done.7.refs_4_ = bf16[512,512]{1,0:T(8,128)(2,1)S(1)} collective-permute-done((bf16[512,512]{1,0:T(8,128)(2,1)S(1)}, bf16[512,512]{1,0:T(8,128)(2,1)S(1)}, u32[]{:S(2)}, u32[]{:S(2)}) %collective-permute-start.7) | collective-permute-done | bytes 524320 | tf_op jit(solution)/shard_map/ppermute | solution.py:30
  64.6 12.3 %collective-permute-done.13.refs_3_ = bf16[256,1024]{1,0:T(8,128)(2,1)S(1)} collective-permute-done((bf16[256,1024]{1,0:T(8,128)(2,1)S(1)}, bf16[256,1024]{1,0:T(8,128)(2,1)S(1)}, u32[]{:S(2)}, u32[]{:S(2)}) %collective-permute-start.13) | collective-permute-done | bytes 524320 | tf_op jit(solution)/shard_map/ppermute | solution.py:30
  79.0 3.2 %qkv_near.2 = (f32[256,1536]{1,0:T(8,128)S(1)}, f32[256,128]{1,0:T(8,128)S(1)}) custom-call(s32[8]{0:T(128)S(1)} %stack.104.meta_ref.refs_0_, bf16[256,1024]{1,0:T(8,128)(2,1)S(1)} %get-tuple-element.68.refs_1_.refs_5_, bf16[256,1024]{1,0:T(8,128)(2,1)S(1)} %collective-permute-done.11.refs_2_, bf16[256,1024]{1,0:T(8,128)(2,1)S(1)} %collective-permute-done.13.refs_3_, ...), custom_call_target="tpu_custom_call" | custom-call | flops 3300000000 | bytes 10800000 | tf_op jit(solution)/shard_map/qkv_near/pallas_call | solution.py:188
  82.2 2.4 %collective-permute-done.14.refs_2_ = bf16[128,1024]{1,0:T(8,128)(2,1)S(1)} collective-permute-done((bf16[128,1024]{1,0:T(8,128)(2,1)S(1)}, bf16[128,1024]{1,0:T(8,128)(2,1)S(1)}, u32[]{:S(2)}, u32[]{:S(2)}) %collective-permute-start.14) | collective-permute-done | bytes 262176 | tf_op jit(solution)/shard_map/ppermute | solution.py:30
  89.8 2.7 %collective-permute-start.15 = (bf16[3,256,128]{2,1,0:T(8,128)(2,1)S(1)}, bf16[3,256,128]{2,1,0:T(8,128)(2,1)S(1)}, u32[]{:S(2)}, u32[]{:S(2)}) collective-permute-start(bf16[3,256,128]{2,1,0:T(8,128)(2,1)S(1)} %get-tuple-element.72), channel_id=1, source_target_pairs={{0,8},{4,12},{8,16},{12,20},{16,24},{20,28},{24,0},{28,4},{1,9},{5... | collective-permute-start | bytes 589832 | tf_op jit(solution)/shard_map/ppermute | solution.py:45
  93.5 2.8 %collective-permute-start.17 = (bf16[3,256,128]{2,1,0:T(8,128)(2,1)S(1)}, bf16[3,256,128]{2,1,0:T(8,128)(2,1)S(1)}, u32[]{:S(2)}, u32[]{:S(2)}) collective-permute-start(bf16[3,256,128]{2,1,0:T(8,128)(2,1)S(1)} %get-tuple-element.74), channel_id=1, source_target_pairs={{0,24},{4,28},{8,0},{12,4},{16,8},{20,12},{24,16},{28,20},{1,25},{... | collective-permute-start | bytes 589832 | tf_op jit(solution)/shard_map/ppermute | solution.py:45
  101.0 3.2 %qkv_near.3 = (f32[256,1536]{1,0:T(8,128)S(1)}, f32[256,128]{1,0:T(8,128)S(1)}) custom-call(s32[8]{0:T(128)S(1)} %stack.104.meta_ref.refs_0_, bf16[256,1024]{1,0:T(8,128)(2,1)S(1)} %get-tuple-element.76.refs_1_.refs_4_, bf16[256,1024]{1,0:T(8,128)(2,1)S(1)} %collective-permute-done.18.refs_2_, bf16[256,1024]{1,0:T(8,128)(2,1)S(1)} %collective-permute-done.20.refs_3_, ...), custom_call_target="tpu_custom_call" | custom-call | flops 3300000000 | bytes 10800000 | tf_op jit(solution)/shard_map/qkv_near/pallas_call | solution.py:188
  110.2 2.8 %collective-permute-start.24 = (bf16[3,256,128]{2,1,0:T(8,128)(2,1)S(1)}, bf16[3,256,128]{2,1,0:T(8,128)(2,1)S(1)}, u32[]{:S(2)}, u32[]{:S(2)}) collective-permute-start(bf16[3,256,128]{2,1,0:T(8,128)(2,1)S(1)} %get-tuple-element.82), channel_id=1, source_target_pairs={{0,24},{4,28},{8,0},{12,4},{16,8},{20,12},{24,16},{28,20},{1,25},{... | collective-permute-start | bytes 589832 | tf_op jit(solution)/shard_map/ppermute | solution.py:45
  113.3 3.1 %collective-permute-done.22.refs_2_ = bf16[3,256,128]{2,1,0:T(8,128)(2,1)S(1)} collective-permute-done((bf16[3,256,128]{2,1,0:T(8,128)(2,1)S(1)}, bf16[3,256,128]{2,1,0:T(8,128)(2,1)S(1)}, u32[]{:S(2)}, u32[]{:S(2)}) %collective-permute-start.22) | collective-permute-done | bytes 196640 | tf_op jit(solution)/shard_map/ppermute | solution.py:45
  116.5 5.3 %collective-permute-done.23.refs_3_ = bf16[3,256,128]{2,1,0:T(8,128)(2,1)S(1)} collective-permute-done((bf16[3,256,128]{2,1,0:T(8,128)(2,1)S(1)}, bf16[3,256,128]{2,1,0:T(8,128)(2,1)S(1)}, u32[]{:S(2)}, u32[]{:S(2)}) %collective-permute-start.23) | collective-permute-done | bytes 196640 | tf_op jit(solution)/shard_map/ppermute | solution.py:45
  124.7 10.9 %attention.1 = (bf16[512,128]{1,0:T(8,128)(2,1)S(1)}, bf16[512,128]{1,0:T(8,128)(2,1)S(1)}, bf16[512,128]{1,0:T(8,128)(2,1)S(1)}, bf16[512,128]{1,0:T(8,128)(2,1)S(1)}) custom-call(s32[8]{0:T(128)S(1)} %stack.104.meta_ref.refs_0_, bf16[3,256,128]{2,1,0:T(8,128)(2,1)S(1)} %get-tuple-element.83.refs_1_, ...), custom_call_target="tpu_custom_call" | custom-call | flops 13200000000 | bytes 43200000 | tf_op jit(solution)/shard_map/attention/pallas_call | solution.py:188
  135.6 3.8 %collective-permute-start.28 = (bf16[512,128]{1,0:T(8,128)(2,1)S(1)}, bf16[512,128]{1,0:T(8,128)(2,1)S(1)}, u32[]{:S(2)}, u32[]{:S(2)}) collective-permute-start(bf16[512,128]{1,0:T(8,128)(2,1)S(1)} %get-tuple-element.92), channel_id=1, source_target_pairs={{0,8},{4,12},{8,16},{12,20},{16,24},{20,28},{24,0},{28,4},{1,9},{5... | collective-permute-start | bytes 393224 | tf_op jit(solution)/shard_map/ppermute | solution.py:45
  140.4 3.8 %collective-permute-done.28 = bf16[512,128]{1,0:T(8,128)(2,1)S(1)} collective-permute-done((bf16[512,128]{1,0:T(8,128)(2,1)S(1)}, bf16[512,128]{1,0:T(8,128)(2,1)S(1)}, u32[]{:S(2)}, u32[]{:S(2)}) %collective-permute-start.28) | collective-permute-done | bytes 131104 | tf_op jit(solution)/shard_map/ppermute | solution.py:45
  144.2 5.0 %collective-permute-done.30 = bf16[512,128]{1,0:T(8,128)(2,1)S(1)} collective-permute-done((bf16[512,128]{1,0:T(8,128)(2,1)S(1)}, bf16[512,128]{1,0:T(8,128)(2,1)S(1)}, u32[]{:S(2)}, u32[]{:S(2)}) %collective-permute-start.30) | collective-permute-done | bytes 131104 | tf_op jit(solution)/shard_map/ppermute | solution.py:45
  153.7 3.9 %collective-permute-done.32.refs_3_ = bf16[2,512,128]{2,1,0:T(8,128)(2,1)S(1)} collective-permute-done((bf16[2,512,128]{2,1,0:T(8,128)(2,1)S(1)}, bf16[2,512,128]{2,1,0:T(8,128)(2,1)S(1)}, u32[]{:S(2)}, u32[]{:S(2)}) %collective-permute-start.32) | collective-permute-done | bytes 262176 | tf_op jit(solution)/shard_map/ppermute | solution.py:30
  163.8 5.7 %collective-permute-done.34.refs_3_ = bf16[2,512,128]{2,1,0:T(8,128)(2,1)S(1)} collective-permute-done((bf16[2,512,128]{2,1,0:T(8,128)(2,1)S(1)}, bf16[2,512,128]{2,1,0:T(8,128)(2,1)S(1)}, u32[]{:S(2)}, u32[]{:S(2)}) %collective-permute-start.34) | collective-permute-done | bytes 262176 | tf_op jit(solution)/shard_map/ppermute | solution.py:30
  (97 shorter events, 61.7 us)
Async XLA Ops:
  2.3 12.7 %collective-permute-start = (bf16[3,144,1024]{2,1,0:T(8,128)(2,1)S(1)}, bf16[3,144,1024]{2,1,0:T(8,128)(2,1)S(1)}, u32[]{:S(2)}, u32[]{:S(2)}) collective-permute-start(bf16[3,144,1024]{2,1,0:T(8,128)(2,1)S(1)} %get-tuple-element.54), channel_id=1, source_target_pairs={{0,4},{4,8},{8,12},{12,16},{16,20},{20,24},{24,28},{1,5},{5,9},{9,... | collective-permute-start | bytes 2654216 | tf_op jit(solution)/shard_map/ppermute | solution.py:40
  4.7 16.1 %collective-permute-start.1 = (bf16[128,1024]{1,0:T(8,128)(2,1)S(1)}, bf16[128,1024]{1,0:T(8,128)(2,1)S(1)}, u32[]{:S(2)}, u32[]{:S(2)}) collective-permute-start(bf16[128,1024]{1,0:T(8,128)(2,1)S(1)} %get-tuple-element.57), channel_id=1, source_target_pairs={{0,1},{1,0},{2,3},{3,2},{4,5},{5,4},{6,7},{7,6},{8,9},{9,8},{10,11... | collective-permute-start | bytes 786440 | tf_op jit(solution)/shard_map/ppermute | solution.py:30
  7.1 13.7 %collective-permute-start.2 = (bf16[128,1024]{1,0:T(8,128)(2,1)S(1)}, bf16[128,1024]{1,0:T(8,128)(2,1)S(1)}, u32[]{:S(2)}, u32[]{:S(2)}) collective-permute-start(bf16[128,1024]{1,0:T(8,128)(2,1)S(1)} %get-tuple-element.58), channel_id=1, source_target_pairs={{0,2},{1,3},{2,0},{3,1},{4,6},{5,7},{6,4},{7,5},{8,10},{9,11},{10,... | collective-permute-start | bytes 786440 | tf_op jit(solution)/shard_map/ppermute | solution.py:30
  8.7 12.2 %collective-permute-start.3 = (bf16[128,1024]{1,0:T(8,128)(2,1)S(1)}, bf16[128,1024]{1,0:T(8,128)(2,1)S(1)}, u32[]{:S(2)}, u32[]{:S(2)}) collective-permute-start(bf16[128,1024]{1,0:T(8,128)(2,1)S(1)} %get-tuple-element.59), channel_id=1, source_target_pairs={{0,3},{1,2},{2,1},{3,0},{4,7},{5,6},{6,5},{7,4},{8,11},{9,10},{10,... | collective-permute-start | bytes 786440 | tf_op jit(solution)/shard_map/ppermute | solution.py:30
  22.7 13.8 %collective-permute-start.6 = (bf16[512,512]{1,0:T(8,128)(2,1)S(1)}, bf16[512,512]{1,0:T(8,128)(2,1)S(1)}, u32[]{:S(2)}, u32[]{:S(2)}) collective-permute-start(bf16[512,512]{1,0:T(8,128)(2,1)S(1)} %get-tuple-element.64), channel_id=1, source_target_pairs={{0,2},{1,3},{2,0},{3,1},{4,6},{5,7},{6,4},{7,5},{8,10},{9,11},{10,... | collective-permute-start | bytes 1572872 | tf_op jit(solution)/shard_map/ppermute | solution.py:30
  24.8 14.4 %collective-permute-start.8 = (bf16[512,512]{1,0:T(8,128)(2,1)S(1)}, bf16[512,512]{1,0:T(8,128)(2,1)S(1)}, u32[]{:S(2)}, u32[]{:S(2)}) collective-permute-start(bf16[512,512]{1,0:T(8,128)(2,1)S(1)} %get-tuple-element.66), channel_id=1, source_target_pairs={{0,1},{1,0},{2,3},{3,2},{4,5},{5,4},{6,7},{7,6},{8,9},{9,8},{10,11... | collective-permute-start | bytes 1572872 | tf_op jit(solution)/shard_map/ppermute | solution.py:30
  26.3 20.8 %collective-permute-start.10 = (bf16[3,128,1024]{2,1,0:T(8,128)(2,1)S(1)}, bf16[3,128,1024]{2,1,0:T(8,128)(2,1)S(1)}, u32[]{:S(2)}, u32[]{:S(2)}) collective-permute-start(bf16[3,128,1024]{2,1,0:T(8,128)(2,1)S(1)} %get-tuple-element.104.refs_4_), channel_id=1, source_target_pairs={{0,8},{4,12},{8,0},{12,4},{16,24},{20,28},{24,16},{28,20},{1,9},{5... | collective-permute-start | bytes 2359304 | tf_op jit(solution)/shard_map/ppermute | solution.py:35
  34.6 17.9 %collective-permute-start.4 = (bf16[512,512]{1,0:T(8,128)(2,1)S(1)}, bf16[512,512]{1,0:T(8,128)(2,1)S(1)}, u32[]{:S(2)}, u32[]{:S(2)}) collective-permute-start(bf16[512,512]{1,0:T(8,128)(2,1)S(1)} %get-tuple-element.61), channel_id=1, source_target_pairs={{0,1},{1,0},{2,3},{3,2},{4,5},{5,4},{6,7},{7,6},{8,9},{9,8},{10,11... | collective-permute-start | bytes 1572872 | tf_op jit(solution)/shard_map/ppermute | solution.py:30
  35.2 17.3 %collective-permute-start.5 = (bf16[512,512]{1,0:T(8,128)(2,1)S(1)}, bf16[512,512]{1,0:T(8,128)(2,1)S(1)}, u32[]{:S(2)}, u32[]{:S(2)}) collective-permute-start(bf16[512,512]{1,0:T(8,128)(2,1)S(1)} %get-tuple-element.62), channel_id=1, source_target_pairs={{0,2},{1,3},{2,0},{3,1},{4,6},{5,7},{6,4},{7,5},{8,10},{9,11},{10,... | collective-permute-start | bytes 1572872 | tf_op jit(solution)/shard_map/ppermute | solution.py:30
  36.6 25.1 %collective-permute-start.7 = (bf16[512,512]{1,0:T(8,128)(2,1)S(1)}, bf16[512,512]{1,0:T(8,128)(2,1)S(1)}, u32[]{:S(2)}, u32[]{:S(2)}) collective-permute-start(bf16[512,512]{1,0:T(8,128)(2,1)S(1)} %add_convert_fusion.1), channel_id=1, source_target_pairs={{0,1},{1,0},{2,3},{3,2},{4,5},{5,4},{6,7},{7,6},{8,9},{9,8},{10,11... | collective-permute-start | bytes 1572872 | tf_op jit(solution)/shard_map/ppermute | solution.py:30
  39.4 22.3 %collective-permute-start.9 = (bf16[512,512]{1,0:T(8,128)(2,1)S(1)}, bf16[512,512]{1,0:T(8,128)(2,1)S(1)}, u32[]{:S(2)}, u32[]{:S(2)}) collective-permute-start(bf16[512,512]{1,0:T(8,128)(2,1)S(1)} %add_convert_fusion.along), channel_id=1, source_target_pairs={{0,2},{1,3},{2,0},{3,1},{4,6},{5,7},{6,4},{7,5},{8,10},{9,11},{10,... | collective-permute-start | bytes 1572872 | tf_op jit(solution)/shard_map/ppermute | solution.py:30
  62.8 14.1 %collective-permute-start.13 = (bf16[256,1024]{1,0:T(8,128)(2,1)S(1)}, bf16[256,1024]{1,0:T(8,128)(2,1)S(1)}, u32[]{:S(2)}, u32[]{:S(2)}) collective-permute-start(bf16[256,1024]{1,0:T(8,128)(2,1)S(1)} %get-tuple-element.68.refs_1_.refs_5_), channel_id=1, source_target_pairs={{0,2},{1,3},{2,0},{3,1},{4,6},{5,7},{6,4},{7,5},{8,10},{9,11},{10,... | collective-permute-start | bytes 1572872 | tf_op jit(solution)/shard_map/ppermute | solution.py:30
  62.9 15.4 %collective-permute-start.11 = (bf16[256,1024]{1,0:T(8,128)(2,1)S(1)}, bf16[256,1024]{1,0:T(8,128)(2,1)S(1)}, u32[]{:S(2)}, u32[]{:S(2)}) collective-permute-start(bf16[256,1024]{1,0:T(8,128)(2,1)S(1)} %get-tuple-element.68.refs_1_.refs_5_), channel_id=1, source_target_pairs={{0,1},{1,0},{2,3},{3,2},{4,5},{5,4},{6,7},{7,6},{8,9},{9,8},{10,11... | collective-permute-start | bytes 1572872 | tf_op jit(solution)/shard_map/ppermute | solution.py:30
  85.9 12.2 %collective-permute-start.20 = (bf16[256,1024]{1,0:T(8,128)(2,1)S(1)}, bf16[256,1024]{1,0:T(8,128)(2,1)S(1)}, u32[]{:S(2)}, u32[]{:S(2)}) collective-permute-start(bf16[256,1024]{1,0:T(8,128)(2,1)S(1)} %get-tuple-element.76.refs_1_.refs_4_), channel_id=1, source_target_pairs={{0,2},{1,3},{2,0},{3,1},{4,6},{5,7},{6,4},{7,5},{8,10},{9,11},{10,... | collective-permute-start | bytes 1572872 | tf_op jit(solution)/shard_map/ppermute | solution.py:30
  86.4 12.2 %collective-permute-start.18 = (bf16[256,1024]{1,0:T(8,128)(2,1)S(1)}, bf16[256,1024]{1,0:T(8,128)(2,1)S(1)}, u32[]{:S(2)}, u32[]{:S(2)}) collective-permute-start(bf16[256,1024]{1,0:T(8,128)(2,1)S(1)} %get-tuple-element.76.refs_1_.refs_4_), channel_id=1, source_target_pairs={{0,1},{1,0},{2,3},{3,2},{4,5},{5,4},{6,7},{7,6},{8,9},{9,8},{10,11... | collective-permute-start | bytes 1572872 | tf_op jit(solution)/shard_map/ppermute | solution.py:30
  89.8 20.5 %collective-permute-start.15 = (bf16[3,256,128]{2,1,0:T(8,128)(2,1)S(1)}, bf16[3,256,128]{2,1,0:T(8,128)(2,1)S(1)}, u32[]{:S(2)}, u32[]{:S(2)}) collective-permute-start(bf16[3,256,128]{2,1,0:T(8,128)(2,1)S(1)} %get-tuple-element.72), channel_id=1, source_target_pairs={{0,8},{4,12},{8,16},{12,20},{16,24},{20,28},{24,0},{28,4},{1,9},{5... | collective-permute-start | bytes 589832 | tf_op jit(solution)/shard_map/ppermute | solution.py:45
  92.4 20.8 %collective-permute-start.16 = (bf16[3,256,128]{2,1,0:T(8,128)(2,1)S(1)}, bf16[3,256,128]{2,1,0:T(8,128)(2,1)S(1)}, u32[]{:S(2)}, u32[]{:S(2)}) collective-permute-start(bf16[3,256,128]{2,1,0:T(8,128)(2,1)S(1)} %get-tuple-element.73), channel_id=1, source_target_pairs={{0,16},{4,20},{8,24},{12,28},{16,0},{20,4},{24,8},{28,12},{1,17},{... | collective-permute-start | bytes 589832 | tf_op jit(solution)/shard_map/ppermute | solution.py:45
  93.5 19.8 %collective-permute-start.17 = (bf16[3,256,128]{2,1,0:T(8,128)(2,1)S(1)}, bf16[3,256,128]{2,1,0:T(8,128)(2,1)S(1)}, u32[]{:S(2)}, u32[]{:S(2)}) collective-permute-start(bf16[3,256,128]{2,1,0:T(8,128)(2,1)S(1)} %get-tuple-element.74), channel_id=1, source_target_pairs={{0,24},{4,28},{8,0},{12,4},{16,8},{20,12},{24,16},{28,20},{1,25},{... | collective-permute-start | bytes 589832 | tf_op jit(solution)/shard_map/ppermute | solution.py:45
  109.2 12.6 %collective-permute-start.23 = (bf16[3,256,128]{2,1,0:T(8,128)(2,1)S(1)}, bf16[3,256,128]{2,1,0:T(8,128)(2,1)S(1)}, u32[]{:S(2)}, u32[]{:S(2)}) collective-permute-start(bf16[3,256,128]{2,1,0:T(8,128)(2,1)S(1)} %get-tuple-element.81), channel_id=1, source_target_pairs={{0,16},{4,20},{8,24},{12,28},{16,0},{20,4},{24,8},{28,12},{1,17},{... | collective-permute-start | bytes 589832 | tf_op jit(solution)/shard_map/ppermute | solution.py:45
  110.2 11.6 %collective-permute-start.24 = (bf16[3,256,128]{2,1,0:T(8,128)(2,1)S(1)}, bf16[3,256,128]{2,1,0:T(8,128)(2,1)S(1)}, u32[]{:S(2)}, u32[]{:S(2)}) collective-permute-start(bf16[3,256,128]{2,1,0:T(8,128)(2,1)S(1)} %get-tuple-element.82), channel_id=1, source_target_pairs={{0,24},{4,28},{8,0},{12,4},{16,8},{20,12},{24,16},{28,20},{1,25},{... | collective-permute-start | bytes 589832 | tf_op jit(solution)/shard_map/ppermute | solution.py:45
  113.3 11.4 %collective-permute-start.27 = (bf16[2,3,128,1024]{3,2,1,0:T(8,128)(2,1)S(1)}, bf16[2,3,128,1024]{3,2,1,0:T(8,128)(2,1)S(1)}, u32[]{:S(2)}, u32[]{:S(2)}) collective-permute-start(bf16[2,3,128,1024]{3,2,1,0:T(8,128)(2,1)S(1)} %pad_maximum_fusion.refs_7_.refs_6_.refs_5_), channel_id=1, source_target_pairs={{0,4},{4,0},{8,12},{12,8},{16,20},{20,16},{24,28},{28,24},{1,5},{5... | collective-permute-start | bytes 4718600 | tf_op jit(solution)/shard_map/ppermute | solution.py:35
  139.4 9.9 %collective-permute-start.30 = (bf16[512,128]{1,0:T(8,128)(2,1)S(1)}, bf16[512,128]{1,0:T(8,128)(2,1)S(1)}, u32[]{:S(2)}, u32[]{:S(2)}) collective-permute-start(bf16[512,128]{1,0:T(8,128)(2,1)S(1)} %get-tuple-element.94), channel_id=1, source_target_pairs={{0,16},{4,20},{8,24},{12,28},{16,0},{20,4},{24,8},{28,12},{1,17},{... | collective-permute-start | bytes 393224 | tf_op jit(solution)/shard_map/ppermute | solution.py:45
  161.4 11.5 %collective-permute-start.36 = (bf16[2,512,128]{2,1,0:T(8,128)(2,1)S(1)}, bf16[2,512,128]{2,1,0:T(8,128)(2,1)S(1)}, u32[]{:S(2)}, u32[]{:S(2)}) collective-permute-start(bf16[2,512,128]{2,1,0:T(8,128)(2,1)S(1)} %collective-permute-done.31.refs_2_), channel_id=1, source_target_pairs={{0,2},{1,3},{2,0},{3,1},{4,6},{5,7},{6,4},{7,5},{8,10},{9,11},{10,... | collective-permute-start | bytes 786440 | tf_op jit(solution)/shard_map/ppermute | solution.py:30
  162.3 12.4 %collective-permute-start.33 = (bf16[2,512,128]{2,1,0:T(8,128)(2,1)S(1)}, bf16[2,512,128]{2,1,0:T(8,128)(2,1)S(1)}, u32[]{:S(2)}, u32[]{:S(2)}) collective-permute-start(bf16[2,512,128]{2,1,0:T(8,128)(2,1)S(1)} %pad_maximum_fusion.5.refs_2_), channel_id=1, source_target_pairs={{0,1},{1,0},{2,3},{3,2},{4,5},{5,4},{6,7},{7,6},{8,9},{9,8},{10,11... | collective-permute-start | bytes 786440 | tf_op jit(solution)/shard_map/ppermute | solution.py:30
  (16 other events, 136.5 us)

commit v12 on v10

--- a/solution.py
+++ b/solution.py
@@ -10,7 +10,7 @@
 HEAD = 128
 GROUP_SIZE = 16
 LANES = 128
-TILES = 2
+TILES = 4
 LEAD = 16
 norm_eps = 1e-05
 SCORE_SCALE = 1.4426950408889634 / HEAD**0.5
@@ -671,12 +671,12 @@
     other = [swap_ctx(jnp.stack([piece[1:] for piece in arrived]), 1) for arrived in own]
     own, other = own[1] + own[0], other[::-1]
 
-    groups = [(*range(2, chips, 2), 0), tuple(range(1, chips, 2))]
+    groups = [tuple(range(1, chips, 2)), (*range(2, chips, 2), 0)]
     given, laid = attend(meta, own, other, None, groups[0], [far_w], chips)
-    first = [rotate_chips(piece, d) if d else piece for d, piece in zip(groups[0], given)]
+    first = [rotate_chips(piece, d) for d, piece in zip(groups[0], given)]
     given, _ = attend(meta, own, other, laid, groups[1], [], chips)
     first, given = lax.optimization_barrier((first, given))
-    second = [rotate_chips(piece, d) for d, piece in zip(groups[1], given)]
+    second = [rotate_chips(piece, d) if d else piece for d, piece in zip(groups[1], given)]
     back = jnp.stack(first)
     by_x, by_y = swap_ch(back, 1), swap_ch(back, 2)
     add = functools.partial(mix, meta, groups=groups, own_w=own_w, near_w=near_w, far_w=far_w, chips=chips)

time: 170 us -> 171 us (level)
  transfers between devices with their start and end apart: 37 -> 37, of which waited for: 20 -> 21; matrix products, arithmetic and copies ran while one was open for 1% -> 1% of each run, Pallas kernels for 25% -> 24%
where the time goes in v12:
time: 171 us; the launch traced here: 170 us
  waiting for transfers between devices  60.4 us (35%)
  Pallas kernels  54.6 us (32%)
  starting transfers between devices  52.4 us (31%)
  other arithmetic  2.15 us (1%)
    ppermute x23, waiting for transfers between devices, swap_ch(): return lax.ppermute(value, 'ch', [(i, i ^ mask) for i in range(count)])  43 us
    pallas_call x12, Pallas kernels, vmem_call(): pl.pallas_call(run, in_specs=[pl.BlockSpec(memory_space=pltpu.SMEM)] + [p...  34.9 us
    ppermute x23, starting transfers between devices, swap_ch(): return lax.ppermute(value, 'ch', [(i, i ^ mask) for i in range(count)])  27.5 us
    ppermute x9, starting transfers between devices, rotate_chips(): lax.ppermute(value, 'ctx', [(i, (i + 2 * distance) % count) for i in rang...  17.5 us
    pallas_call x2, Pallas kernels, gated_chunk(): pl.pallas_call(functools.partial(gated_kernel, first_row, loads), grid=(c...  12.1 us
    ppermute x9, waiting for transfers between devices, rotate_chips(): lax.ppermute(value, 'ctx', [(i, (i + 2 * distance) % count) for i in rang...  10.2 us
    ppermute x4, waiting for transfers between devices, swap_ctx(): return lax.ppermute(value, 'ctx', [(i, i ^ mask) for i in range(count)])  7.24 us
    pallas_call x1, Pallas kernels, load(): pl.pallas_call(load_kernel, in_specs=[pl.BlockSpec(memory_space=pltpu.SME...  5.36 us
  transfers between devices with their start and end apart: 37, of which 21 were waited for; matrix products, arithmetic and copies ran while one was open for 1% of the time, Pallas kernels for 24%

profile of v12, /device:TPU:0, one launch (start us, length us, event | category | flops | bytes accessed | tf_op | source)
XLA Modules:
  0.0 170.2 jit_solution(18033622339435012181)
XLA Ops:
  2.3 2.4 %collective-permute-start = (bf16[3,144,1024]{2,1,0:T(8,128)(2,1)S(1)}, bf16[3,144,1024]{2,1,0:T(8,128)(2,1)S(1)}, u32[]{:S(2)}, u32[]{:S(2)}) collective-permute-start(bf16[3,144,1024]{2,1,0:T(8,128)(2,1)S(1)} %get-tuple-element.58), channel_id=1, source_target_pairs={{0,4},{4,8},{8,12},{12,16},{16,20},{20,24},{24,28},{1,5},{5,9},{9,... | collective-permute-start | bytes 2654216 | tf_op jit(solution)/shard_map/ppermute | solution.py:40
  4.7 2.4 %collective-permute-start.1 = (bf16[128,1024]{1,0:T(8,128)(2,1)S(1)}, bf16[128,1024]{1,0:T(8,128)(2,1)S(1)}, u32[]{:S(2)}, u32[]{:S(2)}) collective-permute-start(bf16[128,1024]{1,0:T(8,128)(2,1)S(1)} %get-tuple-element.61), channel_id=1, source_target_pairs={{0,1},{1,0},{2,3},{3,2},{4,5},{5,4},{6,7},{7,6},{8,9},{9,8},{10,11... | collective-permute-start | bytes 786440 | tf_op jit(solution)/shard_map/ppermute | solution.py:30
  8.7 6.3 %hyena_filters.3 = (bf16[256,1024]{1,0:T(8,128)(2,1)S(1)}, bf16[1024,4096]{1,0:T(8,128)(2,1)S(1)}) custom-call(s32[8]{0:T(128)S(1)} %stack.104.meta_ref.refs_0_, f32[3,7,64]{2,1,0:T(8,128)} %refs_1_.3, f32[64,128]{1,0:T(8,128)} %bitcast.50, f32[1,1024]{1,0:T(1,128)} %bitcast.55, bf16[3,512,1024]{2,1,0:T(8,128)(2,1)S(1)} %bitcast.39, bf16[1024,4096]{1,0:T(8,128)(2,1)} %refs_5_.1), custom_call_target="tpu_custom_call" | custom-call | tf_op jit(solution)/shard_map/hyena_filters/pallas_call | solution.py:173
  15.0 5.8 %hyena_filters.2.refs_1_ = bf16[256,1024]{1,0:T(8,128)(2,1)S(1)} custom-call(s32[8]{0:T(128)S(1)} %stack.104.meta_ref.refs_0_, f32[3,7,64]{2,1,0:T(8,128)} %refs_1_.3, f32[64,128]{1,0:T(8,128)} %bitcast.51, f32[1,1024]{1,0:T(1,128)} %bitcast.56, bf16[3,144,1024]{2,1,0:T(8,128)(2,1)S(1)} %collective-permute-done.refs_4_, bf16[3,512,1024]{2,1,0:T(8,128)(2,1)S(1)} %bitcast.40), custom_call_target="tpu_custom_call" | custom-call | tf_op jit(solution)/shard_map/hyena_filters/pallas_call | solution.py:173
  26.3 4.3 %collective-permute-start.10 = (bf16[3,128,1024]{2,1,0:T(8,128)(2,1)S(1)}, bf16[3,128,1024]{2,1,0:T(8,128)(2,1)S(1)}, u32[]{:S(2)}, u32[]{:S(2)}) collective-permute-start(bf16[3,128,1024]{2,1,0:T(8,128)(2,1)S(1)} %get-tuple-element.112.refs_4_), channel_id=1, source_target_pairs={{0,8},{4,12},{8,0},{12,4},{16,24},{20,28},{24,16},{28,20},{1,9},{5... | collective-permute-start | bytes 2359304 | tf_op jit(solution)/shard_map/ppermute | solution.py:35
  30.6 4.0 %hyena_terms.2 = (bf16[512,512]{1,0:T(8,128)(2,1)S(1)}, bf16[512,512]{1,0:T(8,128)(2,1)S(1)}, bf16[512,512]{1,0:T(8,128)(2,1)S(1)}, bf16[512,512]{1,0:T(8,128)(2,1)S(1)}, bf16[512,1024]{1,0:T(8,128)(2,1)S(1)}) custom-call(s32[8]{0:T(128)S(1)} %stack.104.meta_ref.refs_0_, bf16[256,1024]{1,0:T(8,128)(2,1)S(1)} %hyena_filters.2.refs_1_, ...), custom_call_target="tpu_custom_call" | custom-call | tf_op jit(solution)/shard_map/hyena_terms/pallas_call | solution.py:188
  41.8 5.3 %collective-permute-done.10.swapped = bf16[3,128,1024]{2,1,0:T(8,128)(2,1)S(1)} collective-permute-done((bf16[3,128,1024]{2,1,0:T(8,128)(2,1)S(1)}, bf16[3,128,1024]{2,1,0:T(8,128)(2,1)S(1)}, u32[]{:S(2)}, u32[]{:S(2)}) %collective-permute-start.10) | collective-permute-done | bytes 786464 | tf_op jit(solution)/shard_map/ppermute | solution.py:35
  47.1 5.4 %load_weights.1 = (bf16[4096,1536]{1,0:T(8,128)(2,1)S(1)}, bf16[512,1024]{1,0:T(8,128)(2,1)S(1)}) custom-call(s32[8]{0:T(128)S(1)} %stack.104.meta_ref.refs_0_, bf16[4096,1536]{1,0:T(8,128)(2,1)} %source.1, bf16[512,4096]{1,0:T(8,128)(2,1)} %outer.1, bf16[512,512]{1,0:T(8,128)(2,1)S(1)} %add_convert_fusion.along, ...), custom_call_target="tpu_custom_call" | custom-call | tf_op jit(solution)/shard_map/load_weights/pallas_call | solution.py:233
  52.5 9.2 %collective-permute-done.7.refs_4_ = bf16[512,512]{1,0:T(8,128)(2,1)S(1)} collective-permute-done((bf16[512,512]{1,0:T(8,128)(2,1)S(1)}, bf16[512,512]{1,0:T(8,128)(2,1)S(1)}, u32[]{:S(2)}, u32[]{:S(2)}) %collective-permute-start.7) | collective-permute-done | bytes 524320 | tf_op jit(solution)/shard_map/ppermute | solution.py:30
  64.6 12.3 %collective-permute-done.13.refs_3_ = bf16[256,1024]{1,0:T(8,128)(2,1)S(1)} collective-permute-done((bf16[256,1024]{1,0:T(8,128)(2,1)S(1)}, bf16[256,1024]{1,0:T(8,128)(2,1)S(1)}, u32[]{:S(2)}, u32[]{:S(2)}) %collective-permute-start.13) | collective-permute-done | bytes 524320 | tf_op jit(solution)/shard_map/ppermute | solution.py:30
  79.0 3.2 %qkv_near.2 = (f32[256,1536]{1,0:T(8,128)S(1)}, f32[256,128]{1,0:T(8,128)S(1)}) custom-call(s32[8]{0:T(128)S(1)} %stack.104.meta_ref.refs_0_, bf16[256,1024]{1,0:T(8,128)(2,1)S(1)} %get-tuple-element.72.refs_1_.refs_5_, bf16[256,1024]{1,0:T(8,128)(2,1)S(1)} %collective-permute-done.11.refs_2_, bf16[256,1024]{1,0:T(8,128)(2,1)S(1)} %collective-permute-done.13.refs_3_, ...), custom_call_target="tpu_custom_call" | custom-call | flops 3300000000 | bytes 10800000 | tf_op jit(solution)/shard_map/qkv_near/pallas_call | solution.py:188
  82.2 2.4 %collective-permute-done.14.refs_2_ = bf16[128,1024]{1,0:T(8,128)(2,1)S(1)} collective-permute-done((bf16[128,1024]{1,0:T(8,128)(2,1)S(1)}, bf16[128,1024]{1,0:T(8,128)(2,1)S(1)}, u32[]{:S(2)}, u32[]{:S(2)}) %collective-permute-start.14) | collective-permute-done | bytes 262176 | tf_op jit(solution)/shard_map/ppermute | solution.py:30
  89.8 2.7 %collective-permute-start.15 = (bf16[3,256,128]{2,1,0:T(8,128)(2,1)S(1)}, bf16[3,256,128]{2,1,0:T(8,128)(2,1)S(1)}, u32[]{:S(2)}, u32[]{:S(2)}) collective-permute-start(bf16[3,256,128]{2,1,0:T(8,128)(2,1)S(1)} %get-tuple-element.76), channel_id=1, source_target_pairs={{0,8},{4,12},{8,16},{12,20},{16,24},{20,28},{24,0},{28,4},{1,9},{5... | collective-permute-start | bytes 589832 | tf_op jit(solution)/shard_map/ppermute | solution.py:45
  93.5 2.8 %collective-permute-start.17 = (bf16[3,256,128]{2,1,0:T(8,128)(2,1)S(1)}, bf16[3,256,128]{2,1,0:T(8,128)(2,1)S(1)}, u32[]{:S(2)}, u32[]{:S(2)}) collective-permute-start(bf16[3,256,128]{2,1,0:T(8,128)(2,1)S(1)} %get-tuple-element.78), channel_id=1, source_target_pairs={{0,24},{4,28},{8,0},{12,4},{16,8},{20,12},{24,16},{28,20},{1,25},{... | collective-permute-start | bytes 589832 | tf_op jit(solution)/shard_map/ppermute | solution.py:45
  101.0 3.2 %qkv_near.3 = (f32[256,1536]{1,0:T(8,128)S(1)}, f32[256,128]{1,0:T(8,128)S(1)}) custom-call(s32[8]{0:T(128)S(1)} %stack.104.meta_ref.refs_0_, bf16[256,1024]{1,0:T(8,128)(2,1)S(1)} %get-tuple-element.80.refs_1_.refs_4_, bf16[256,1024]{1,0:T(8,128)(2,1)S(1)} %collective-permute-done.18.refs_2_, bf16[256,1024]{1,0:T(8,128)(2,1)S(1)} %collective-permute-done.20.refs_3_, ...), custom_call_target="tpu_custom_call" | custom-call | flops 3300000000 | bytes 10800000 | tf_op jit(solution)/shard_map/qkv_near/pallas_call | solution.py:188
  110.2 2.8 %collective-permute-start.24 = (bf16[3,256,128]{2,1,0:T(8,128)(2,1)S(1)}, bf16[3,256,128]{2,1,0:T(8,128)(2,1)S(1)}, u32[]{:S(2)}, u32[]{:S(2)}) collective-permute-start(bf16[3,256,128]{2,1,0:T(8,128)(2,1)S(1)} %get-tuple-element.86), channel_id=1, source_target_pairs={{0,24},{4,28},{8,0},{12,4},{16,8},{20,12},{24,16},{28,20},{1,25},{... | collective-permute-start | bytes 589832 | tf_op jit(solution)/shard_map/ppermute | solution.py:45
  113.3 3.1 %collective-permute-done.22.refs_2_ = bf16[3,256,128]{2,1,0:T(8,128)(2,1)S(1)} collective-permute-done((bf16[3,256,128]{2,1,0:T(8,128)(2,1)S(1)}, bf16[3,256,128]{2,1,0:T(8,128)(2,1)S(1)}, u32[]{:S(2)}, u32[]{:S(2)}) %collective-permute-start.22) | collective-permute-done | bytes 196640 | tf_op jit(solution)/shard_map/ppermute | solution.py:45
  116.5 5.3 %collective-permute-done.23.refs_3_.refs_1_ = bf16[3,256,128]{2,1,0:T(8,128)(2,1)S(1)} collective-permute-done((bf16[3,256,128]{2,1,0:T(8,128)(2,1)S(1)}, bf16[3,256,128]{2,1,0:T(8,128)(2,1)S(1)}, u32[]{:S(2)}, u32[]{:S(2)}) %collective-permute-start.23) | collective-permute-done | bytes 196640 | tf_op jit(solution)/shard_map/ppermute | solution.py:45
  124.7 7.0 %attention.2 = (bf16[512,128]{1,0:T(8,128)(2,1)S(1)}, bf16[512,128]{1,0:T(8,128)(2,1)S(1)}, bf16[2,4,512,128]{3,2,1,0:T(8,128)(2,1)S(1)}, bf16[2,4,128,512]{3,2,1,0:T(8,128)(2,1)S(1)}) custom-call(s32[8]{0:T(128)S(1)} %stack.104.meta_ref.refs_0_, bf16[3,256,128]{2,1,0:T(8,128)(2,1)S(1)} %get-tuple-element.87.refs_1_.refs_3_, ...), custom_call_target="tpu_custom_call" | custom-call | flops 6600000000 | bytes 21600000 | tf_op jit(solution)/shard_map/attention/pallas_call | solution.py:188
  135.5 4.7 %attention.3 = (bf16[512,128]{1,0:T(8,128)(2,1)S(1)}, bf16[512,128]{1,0:T(8,128)(2,1)S(1)}) custom-call(s32[8]{0:T(128)S(1)} %stack.104.meta_ref.refs_0_, bf16[3,256,128]{2,1,0:T(8,128)(2,1)S(1)} %collective-permute-done.23.refs_3_.refs_1_, bf16[3,256,128]{2,1,0:T(8,128)(2,1)S(1)} %collective-permute-done.16.refs_7_.refs_2_, ...), custom_call_target="tpu_custom_call" | custom-call | flops 6600000000 | bytes 21600000 | tf_op jit(solution)/shard_map/attention/pallas_call | solution.py:188
  145.4 4.1 %collective-permute-done.32.refs_3_ = bf16[2,512,128]{2,1,0:T(8,128)(2,1)S(1)} collective-permute-done((bf16[2,512,128]{2,1,0:T(8,128)(2,1)S(1)}, bf16[2,512,128]{2,1,0:T(8,128)(2,1)S(1)}, u32[]{:S(2)}, u32[]{:S(2)}) %collective-permute-start.32) | collective-permute-done | bytes 262176 | tf_op jit(solution)/shard_map/ppermute | solution.py:30
  155.6 5.9 %collective-permute-done.34.refs_3_ = bf16[2,512,128]{2,1,0:T(8,128)(2,1)S(1)} collective-permute-done((bf16[2,512,128]{2,1,0:T(8,128)(2,1)S(1)}, bf16[2,512,128]{2,1,0:T(8,128)(2,1)S(1)}, u32[]{:S(2)}, u32[]{:S(2)}) %collective-permute-start.34) | collective-permute-done | bytes 262176 | tf_op jit(solution)/shard_map/ppermute | solution.py:30
  162.9 2.4 %collective-permute-done.36.refs_1_ = bf16[2,512,128]{2,1,0:T(8,128)(2,1)S(1)} collective-permute-done((bf16[2,512,128]{2,1,0:T(8,128)(2,1)S(1)}, bf16[2,512,128]{2,1,0:T(8,128)(2,1)S(1)}, u32[]{:S(2)}, u32[]{:S(2)}) %collective-permute-start.36) | collective-permute-done | bytes 262176 | tf_op jit(solution)/shard_map/ppermute | solution.py:30
  167.9 2.3 %attention_mix.5 = bf16[512,1024]{1,0:T(8,128)(2,1)} custom-call(s32[8]{0:T(128)S(1)} %stack.104.meta_ref.refs_0_, bf16[2,512,128]{2,1,0:T(8,128)(2,1)S(1)} %collective-permute-done.33.refs_1_, bf16[2,512,128]{2,1,0:T(8,128)(2,1)S(1)} %collective-permute-done.35.refs_2_, f32[512,1024]{1,0:T(8,128)S(1)} %attention_mix.4.refs_3_, ...), custom_call_target="tpu_custom_call" | custom-call | flops 1320000000 | bytes 4320000 | tf_op jit(solution)/shard_map/attention_mix/pallas_call | solution.py:188
  (98 shorter events, 60.5 us)
Async XLA Ops:
  2.3 12.7 %collective-permute-start = (bf16[3,144,1024]{2,1,0:T(8,128)(2,1)S(1)}, bf16[3,144,1024]{2,1,0:T(8,128)(2,1)S(1)}, u32[]{:S(2)}, u32[]{:S(2)}) collective-permute-start(bf16[3,144,1024]{2,1,0:T(8,128)(2,1)S(1)} %get-tuple-element.58), channel_id=1, source_target_pairs={{0,4},{4,8},{8,12},{12,16},{16,20},{20,24},{24,28},{1,5},{5,9},{9,... | collective-permute-start | bytes 2654216 | tf_op jit(solution)/shard_map/ppermute | solution.py:40
  4.7 16.1 %collective-permute-start.1 = (bf16[128,1024]{1,0:T(8,128)(2,1)S(1)}, bf16[128,1024]{1,0:T(8,128)(2,1)S(1)}, u32[]{:S(2)}, u32[]{:S(2)}) collective-permute-start(bf16[128,1024]{1,0:T(8,128)(2,1)S(1)} %get-tuple-element.61), channel_id=1, source_target_pairs={{0,1},{1,0},{2,3},{3,2},{4,5},{5,4},{6,7},{7,6},{8,9},{9,8},{10,11... | collective-permute-start | bytes 786440 | tf_op jit(solution)/shard_map/ppermute | solution.py:30
  7.1 13.7 %collective-permute-start.2 = (bf16[128,1024]{1,0:T(8,128)(2,1)S(1)}, bf16[128,1024]{1,0:T(8,128)(2,1)S(1)}, u32[]{:S(2)}, u32[]{:S(2)}) collective-permute-start(bf16[128,1024]{1,0:T(8,128)(2,1)S(1)} %get-tuple-element.62), channel_id=1, source_target_pairs={{0,2},{1,3},{2,0},{3,1},{4,6},{5,7},{6,4},{7,5},{8,10},{9,11},{10,... | collective-permute-start | bytes 786440 | tf_op jit(solution)/shard_map/ppermute | solution.py:30
  8.7 12.2 %collective-permute-start.3 = (bf16[128,1024]{1,0:T(8,128)(2,1)S(1)}, bf16[128,1024]{1,0:T(8,128)(2,1)S(1)}, u32[]{:S(2)}, u32[]{:S(2)}) collective-permute-start(bf16[128,1024]{1,0:T(8,128)(2,1)S(1)} %get-tuple-element.63), channel_id=1, source_target_pairs={{0,3},{1,2},{2,1},{3,0},{4,7},{5,6},{6,5},{7,4},{8,11},{9,10},{10,... | collective-permute-start | bytes 786440 | tf_op jit(solution)/shard_map/ppermute | solution.py:30
  22.7 13.8 %collective-permute-start.6 = (bf16[512,512]{1,0:T(8,128)(2,1)S(1)}, bf16[512,512]{1,0:T(8,128)(2,1)S(1)}, u32[]{:S(2)}, u32[]{:S(2)}) collective-permute-start(bf16[512,512]{1,0:T(8,128)(2,1)S(1)} %get-tuple-element.68), channel_id=1, source_target_pairs={{0,2},{1,3},{2,0},{3,1},{4,6},{5,7},{6,4},{7,5},{8,10},{9,11},{10,... | collective-permute-start | bytes 1572872 | tf_op jit(solution)/shard_map/ppermute | solution.py:30
  24.8 14.4 %collective-permute-start.8 = (bf16[512,512]{1,0:T(8,128)(2,1)S(1)}, bf16[512,512]{1,0:T(8,128)(2,1)S(1)}, u32[]{:S(2)}, u32[]{:S(2)}) collective-permute-start(bf16[512,512]{1,0:T(8,128)(2,1)S(1)} %get-tuple-element.70), channel_id=1, source_target_pairs={{0,1},{1,0},{2,3},{3,2},{4,5},{5,4},{6,7},{7,6},{8,9},{9,8},{10,11... | collective-permute-start | bytes 1572872 | tf_op jit(solution)/shard_map/ppermute | solution.py:30
  26.3 20.8 %collective-permute-start.10 = (bf16[3,128,1024]{2,1,0:T(8,128)(2,1)S(1)}, bf16[3,128,1024]{2,1,0:T(8,128)(2,1)S(1)}, u32[]{:S(2)}, u32[]{:S(2)}) collective-permute-start(bf16[3,128,1024]{2,1,0:T(8,128)(2,1)S(1)} %get-tuple-element.112.refs_4_), channel_id=1, source_target_pairs={{0,8},{4,12},{8,0},{12,4},{16,24},{20,28},{24,16},{28,20},{1,9},{5... | collective-permute-start | bytes 2359304 | tf_op jit(solution)/shard_map/ppermute | solution.py:35
  34.6 17.9 %collective-permute-start.4 = (bf16[512,512]{1,0:T(8,128)(2,1)S(1)}, bf16[512,512]{1,0:T(8,128)(2,1)S(1)}, u32[]{:S(2)}, u32[]{:S(2)}) collective-permute-start(bf16[512,512]{1,0:T(8,128)(2,1)S(1)} %get-tuple-element.65), channel_id=1, source_target_pairs={{0,1},{1,0},{2,3},{3,2},{4,5},{5,4},{6,7},{7,6},{8,9},{9,8},{10,11... | collective-permute-start | bytes 1572872 | tf_op jit(solution)/shard_map/ppermute | solution.py:30
  35.2 17.3 %collective-permute-start.5 = (bf16[512,512]{1,0:T(8,128)(2,1)S(1)}, bf16[512,512]{1,0:T(8,128)(2,1)S(1)}, u32[]{:S(2)}, u32[]{:S(2)}) collective-permute-start(bf16[512,512]{1,0:T(8,128)(2,1)S(1)} %get-tuple-element.66), channel_id=1, source_target_pairs={{0,2},{1,3},{2,0},{3,1},{4,6},{5,7},{6,4},{7,5},{8,10},{9,11},{10,... | collective-permute-start | bytes 1572872 | tf_op jit(solution)/shard_map/ppermute | solution.py:30
  36.6 25.1 %collective-permute-start.7 = (bf16[512,512]{1,0:T(8,128)(2,1)S(1)}, bf16[512,512]{1,0:T(8,128)(2,1)S(1)}, u32[]{:S(2)}, u32[]{:S(2)}) collective-permute-start(bf16[512,512]{1,0:T(8,128)(2,1)S(1)} %add_convert_fusion.1), channel_id=1, source_target_pairs={{0,1},{1,0},{2,3},{3,2},{4,5},{5,4},{6,7},{7,6},{8,9},{9,8},{10,11... | collective-permute-start | bytes 1572872 | tf_op jit(solution)/shard_map/ppermute | solution.py:30
  39.4 22.3 %collective-permute-start.9 = (bf16[512,512]{1,0:T(8,128)(2,1)S(1)}, bf16[512,512]{1,0:T(8,128)(2,1)S(1)}, u32[]{:S(2)}, u32[]{:S(2)}) collective-permute-start(bf16[512,512]{1,0:T(8,128)(2,1)S(1)} %add_convert_fusion.along), channel_id=1, source_target_pairs={{0,2},{1,3},{2,0},{3,1},{4,6},{5,7},{6,4},{7,5},{8,10},{9,11},{10,... | collective-permute-start | bytes 1572872 | tf_op jit(solution)/shard_map/ppermute | solution.py:30
  62.8 14.1 %collective-permute-start.13 = (bf16[256,1024]{1,0:T(8,128)(2,1)S(1)}, bf16[256,1024]{1,0:T(8,128)(2,1)S(1)}, u32[]{:S(2)}, u32[]{:S(2)}) collective-permute-start(bf16[256,1024]{1,0:T(8,128)(2,1)S(1)} %get-tuple-element.72.refs_1_.refs_5_), channel_id=1, source_target_pairs={{0,2},{1,3},{2,0},{3,1},{4,6},{5,7},{6,4},{7,5},{8,10},{9,11},{10,... | collective-permute-start | bytes 1572872 | tf_op jit(solution)/shard_map/ppermute | solution.py:30
  62.9 15.4 %collective-permute-start.11 = (bf16[256,1024]{1,0:T(8,128)(2,1)S(1)}, bf16[256,1024]{1,0:T(8,128)(2,1)S(1)}, u32[]{:S(2)}, u32[]{:S(2)}) collective-permute-start(bf16[256,1024]{1,0:T(8,128)(2,1)S(1)} %get-tuple-element.72.refs_1_.refs_5_), channel_id=1, source_target_pairs={{0,1},{1,0},{2,3},{3,2},{4,5},{5,4},{6,7},{7,6},{8,9},{9,8},{10,11... | collective-permute-start | bytes 1572872 | tf_op jit(solution)/shard_map/ppermute | solution.py:30
  85.9 12.2 %collective-permute-start.20 = (bf16[256,1024]{1,0:T(8,128)(2,1)S(1)}, bf16[256,1024]{1,0:T(8,128)(2,1)S(1)}, u32[]{:S(2)}, u32[]{:S(2)}) collective-permute-start(bf16[256,1024]{1,0:T(8,128)(2,1)S(1)} %get-tuple-element.80.refs_1_.refs_4_), channel_id=1, source_target_pairs={{0,2},{1,3},{2,0},{3,1},{4,6},{5,7},{6,4},{7,5},{8,10},{9,11},{10,... | collective-permute-start | bytes 1572872 | tf_op jit(solution)/shard_map/ppermute | solution.py:30
  86.4 12.2 %collective-permute-start.18 = (bf16[256,1024]{1,0:T(8,128)(2,1)S(1)}, bf16[256,1024]{1,0:T(8,128)(2,1)S(1)}, u32[]{:S(2)}, u32[]{:S(2)}) collective-permute-start(bf16[256,1024]{1,0:T(8,128)(2,1)S(1)} %get-tuple-element.80.refs_1_.refs_4_), channel_id=1, source_target_pairs={{0,1},{1,0},{2,3},{3,2},{4,5},{5,4},{6,7},{7,6},{8,9},{9,8},{10,11... | collective-permute-start | bytes 1572872 | tf_op jit(solution)/shard_map/ppermute | solution.py:30
  89.8 20.5 %collective-permute-start.15 = (bf16[3,256,128]{2,1,0:T(8,128)(2,1)S(1)}, bf16[3,256,128]{2,1,0:T(8,128)(2,1)S(1)}, u32[]{:S(2)}, u32[]{:S(2)}) collective-permute-start(bf16[3,256,128]{2,1,0:T(8,128)(2,1)S(1)} %get-tuple-element.76), channel_id=1, source_target_pairs={{0,8},{4,12},{8,16},{12,20},{16,24},{20,28},{24,0},{28,4},{1,9},{5... | collective-permute-start | bytes 589832 | tf_op jit(solution)/shard_map/ppermute | solution.py:45
  92.4 20.8 %collective-permute-start.16 = (bf16[3,256,128]{2,1,0:T(8,128)(2,1)S(1)}, bf16[3,256,128]{2,1,0:T(8,128)(2,1)S(1)}, u32[]{:S(2)}, u32[]{:S(2)}) collective-permute-start(bf16[3,256,128]{2,1,0:T(8,128)(2,1)S(1)} %get-tuple-element.77), channel_id=1, source_target_pairs={{0,16},{4,20},{8,24},{12,28},{16,0},{20,4},{24,8},{28,12},{1,17},{... | collective-permute-start | bytes 589832 | tf_op jit(solution)/shard_map/ppermute | solution.py:45
  93.5 19.8 %collective-permute-start.17 = (bf16[3,256,128]{2,1,0:T(8,128)(2,1)S(1)}, bf16[3,256,128]{2,1,0:T(8,128)(2,1)S(1)}, u32[]{:S(2)}, u32[]{:S(2)}) collective-permute-start(bf16[3,256,128]{2,1,0:T(8,128)(2,1)S(1)} %get-tuple-element.78), channel_id=1, source_target_pairs={{0,24},{4,28},{8,0},{12,4},{16,8},{20,12},{24,16},{28,20},{1,25},{... | collective-permute-start | bytes 589832 | tf_op jit(solution)/shard_map/ppermute | solution.py:45
  109.2 12.6 %collective-permute-start.23 = (bf16[3,256,128]{2,1,0:T(8,128)(2,1)S(1)}, bf16[3,256,128]{2,1,0:T(8,128)(2,1)S(1)}, u32[]{:S(2)}, u32[]{:S(2)}) collective-permute-start(bf16[3,256,128]{2,1,0:T(8,128)(2,1)S(1)} %get-tuple-element.85), channel_id=1, source_target_pairs={{0,16},{4,20},{8,24},{12,28},{16,0},{20,4},{24,8},{28,12},{1,17},{... | collective-permute-start | bytes 589832 | tf_op jit(solution)/shard_map/ppermute | solution.py:45
  110.2 11.6 %collective-permute-start.24 = (bf16[3,256,128]{2,1,0:T(8,128)(2,1)S(1)}, bf16[3,256,128]{2,1,0:T(8,128)(2,1)S(1)}, u32[]{:S(2)}, u32[]{:S(2)}) collective-permute-start(bf16[3,256,128]{2,1,0:T(8,128)(2,1)S(1)} %get-tuple-element.86), channel_id=1, source_target_pairs={{0,24},{4,28},{8,0},{12,4},{16,8},{20,12},{24,16},{28,20},{1,25},{... | collective-permute-start | bytes 589832 | tf_op jit(solution)/shard_map/ppermute | solution.py:45
  113.3 11.4 %collective-permute-start.27 = (bf16[2,3,128,1024]{3,2,1,0:T(8,128)(2,1)S(1)}, bf16[2,3,128,1024]{3,2,1,0:T(8,128)(2,1)S(1)}, u32[]{:S(2)}, u32[]{:S(2)}) collective-permute-start(bf16[2,3,128,1024]{3,2,1,0:T(8,128)(2,1)S(1)} %pad_maximum_fusion.refs_7_.refs_6_.refs_5_), channel_id=1, source_target_pairs={{0,4},{4,0},{8,12},{12,8},{16,20},{20,16},{24,28},{28,24},{1,5},{5... | collective-permute-start | bytes 4718600 | tf_op jit(solution)/shard_map/ppermute | solution.py:35
  152.2 9.3 %collective-permute-start.34 = (bf16[2,512,128]{2,1,0:T(8,128)(2,1)S(1)}, bf16[2,512,128]{2,1,0:T(8,128)(2,1)S(1)}, u32[]{:S(2)}, u32[]{:S(2)}) collective-permute-start(bf16[2,512,128]{2,1,0:T(8,128)(2,1)S(1)} %pad_maximum_fusion.5.refs_2_), channel_id=1, source_target_pairs={{0,2},{1,3},{2,0},{3,1},{4,6},{5,7},{6,4},{7,5},{8,10},{9,11},{10,... | collective-permute-start | bytes 786440 | tf_op jit(solution)/shard_map/ppermute | solution.py:30
  153.2 12.1 %collective-permute-start.36 = (bf16[2,512,128]{2,1,0:T(8,128)(2,1)S(1)}, bf16[2,512,128]{2,1,0:T(8,128)(2,1)S(1)}, u32[]{:S(2)}, u32[]{:S(2)}) collective-permute-start(bf16[2,512,128]{2,1,0:T(8,128)(2,1)S(1)} %collective-permute-done.31.refs_2_), channel_id=1, source_target_pairs={{0,2},{1,3},{2,0},{3,1},{4,6},{5,7},{6,4},{7,5},{8,10},{9,11},{10,... | collective-permute-start | bytes 786440 | tf_op jit(solution)/shard_map/ppermute | solution.py:30
  154.3 12.7 %collective-permute-start.33 = (bf16[2,512,128]{2,1,0:T(8,128)(2,1)S(1)}, bf16[2,512,128]{2,1,0:T(8,128)(2,1)S(1)}, u32[]{:S(2)}, u32[]{:S(2)}) collective-permute-start(bf16[2,512,128]{2,1,0:T(8,128)(2,1)S(1)} %pad_maximum_fusion.5.refs_2_), channel_id=1, source_target_pairs={{0,1},{1,0},{2,3},{3,2},{4,5},{5,4},{6,7},{7,6},{8,9},{9,8},{10,11... | collective-permute-start | bytes 786440 | tf_op jit(solution)/shard_map/ppermute | solution.py:30
  (16 other events, 134.0 us)

commit v13 on v10

--- a/solution.py
+++ b/solution.py
@@ -10,7 +10,7 @@
 HEAD = 128
 GROUP_SIZE = 16
 LANES = 128
-TILES = 2
+TILES = 4
 LEAD = 16
 norm_eps = 1e-05
 SCORE_SCALE = 1.4426950408889634 / HEAD**0.5
@@ -685,8 +685,8 @@
     across = swap_ch(by_x, 2)
     back = jnp.stack(second)
     by_x, by_y = swap_ch(back, 1), swap_ch(back, 2)
-    total = add([across, back, by_y], items=((0, 3), (1, 0), (1, 2)), before=[total], kind=F32)
-    return add([by_x, swap_ch(by_y, 1)], items=((1, 1), (1, 3)), before=[total], kind=BF16)
+    total = add([across, back, by_x, by_y], items=((0, 3), (1, 0), (1, 1), (1, 2)), before=[total], kind=F32)
+    return add([swap_ch(by_y, 1)], items=((1, 3),), before=[total], kind=BF16)
 
 
 def solution(mesh):

time: 170 us -> 169 us (level)
  no operation moved by 1% of the time
where the time goes in v13:
time: 169 us
  waiting for transfers between devices  59.2 us (35%)
  Pallas kernels  54.5 us (32%)
  starting transfers between devices  52.1 us (31%)
  other arithmetic  2.15 us (1%)
    ppermute x23, waiting for transfers between devices, swap_ch(): return lax.ppermute(value, 'ch', [(i, i ^ mask) for i in range(count)])  42.4 us
    pallas_call x12, Pallas kernels, vmem_call(): pl.pallas_call(run, in_specs=[pl.BlockSpec(memory_space=pltpu.SMEM)] + [p...  34.8 us
    ppermute x23, starting transfers between devices, swap_ch(): return lax.ppermute(value, 'ch', [(i, i ^ mask) for i in range(count)])  25.8 us
    ppermute x9, starting transfers between devices, rotate_chips(): lax.ppermute(value, 'ctx', [(i, (i + 2 * distance) % count) for i in rang...  18.9 us
    pallas_call x2, Pallas kernels, gated_chunk(): pl.pallas_call(functools.partial(gated_kernel, first_row, loads), grid=(c...  12.1 us
    ppermute x9, waiting for transfers between devices, rotate_chips(): lax.ppermute(value, 'ctx', [(i, (i + 2 * distance) % count) for i in rang...  9.6 us
    ppermute x4, waiting for transfers between devices, swap_ctx(): return lax.ppermute(value, 'ctx', [(i, i ^ mask) for i in range(count)])  7.24 us
    pallas_call x1, Pallas kernels, load(): pl.pallas_call(load_kernel, in_specs=[pl.BlockSpec(memory_space=pltpu.SME...  5.36 us
  transfers between devices with their start and end apart: 37, of which 20 were waited for; matrix products, arithmetic and copies ran while one was open for 1% of the time, Pallas kernels for 25%

profile of v13, /device:TPU:0, one launch (start us, length us, event | category | flops | bytes accessed | tf_op | source)
XLA Modules:
  0.0 168.7 jit_solution(11356830362085509036)
XLA Ops:
  2.3 2.4 %collective-permute-start = (bf16[3,144,1024]{2,1,0:T(8,128)(2,1)S(1)}, bf16[3,144,1024]{2,1,0:T(8,128)(2,1)S(1)}, u32[]{:S(2)}, u32[]{:S(2)}) collective-permute-start(bf16[3,144,1024]{2,1,0:T(8,128)(2,1)S(1)} %get-tuple-element.58), channel_id=1, source_target_pairs={{0,4},{4,8},{8,12},{12,16},{16,20},{20,24},{24,28},{1,5},{5,9},{9,... | collective-permute-start | bytes 2654216 | tf_op jit(solution)/shard_map/ppermute | solution.py:40
  4.7 2.4 %collective-permute-start.1 = (bf16[128,1024]{1,0:T(8,128)(2,1)S(1)}, bf16[128,1024]{1,0:T(8,128)(2,1)S(1)}, u32[]{:S(2)}, u32[]{:S(2)}) collective-permute-start(bf16[128,1024]{1,0:T(8,128)(2,1)S(1)} %get-tuple-element.61), channel_id=1, source_target_pairs={{0,1},{1,0},{2,3},{3,2},{4,5},{5,4},{6,7},{7,6},{8,9},{9,8},{10,11... | collective-permute-start | bytes 786440 | tf_op jit(solution)/shard_map/ppermute | solution.py:30
  8.7 6.3 %hyena_filters.3 = (bf16[256,1024]{1,0:T(8,128)(2,1)S(1)}, bf16[1024,4096]{1,0:T(8,128)(2,1)S(1)}) custom-call(s32[8]{0:T(128)S(1)} %stack.104.meta_ref.refs_0_, f32[3,7,64]{2,1,0:T(8,128)} %refs_1_.3, f32[64,128]{1,0:T(8,128)} %bitcast.50, f32[1,1024]{1,0:T(1,128)} %bitcast.55, bf16[3,512,1024]{2,1,0:T(8,128)(2,1)S(1)} %bitcast.39, bf16[1024,4096]{1,0:T(8,128)(2,1)} %refs_5_.1), custom_call_target="tpu_custom_call" | custom-call | tf_op jit(solution)/shard_map/hyena_filters/pallas_call | solution.py:173
  15.0 5.8 %hyena_filters.2.refs_1_ = bf16[256,1024]{1,0:T(8,128)(2,1)S(1)} custom-call(s32[8]{0:T(128)S(1)} %stack.104.meta_ref.refs_0_, f32[3,7,64]{2,1,0:T(8,128)} %refs_1_.3, f32[64,128]{1,0:T(8,128)} %bitcast.51, f32[1,1024]{1,0:T(1,128)} %bitcast.56, bf16[3,144,1024]{2,1,0:T(8,128)(2,1)S(1)} %collective-permute-done.refs_4_, bf16[3,512,1024]{2,1,0:T(8,128)(2,1)S(1)} %bitcast.40), custom_call_target="tpu_custom_call" | custom-call | tf_op jit(solution)/shard_map/hyena_filters/pallas_call | solution.py:173
  26.3 4.3 %collective-permute-start.10 = (bf16[3,128,1024]{2,1,0:T(8,128)(2,1)S(1)}, bf16[3,128,1024]{2,1,0:T(8,128)(2,1)S(1)}, u32[]{:S(2)}, u32[]{:S(2)}) collective-permute-start(bf16[3,128,1024]{2,1,0:T(8,128)(2,1)S(1)} %get-tuple-element.112.refs_4_), channel_id=1, source_target_pairs={{0,8},{4,12},{8,0},{12,4},{16,24},{20,28},{24,16},{28,20},{1,9},{5... | collective-permute-start | bytes 2359304 | tf_op jit(solution)/shard_map/ppermute | solution.py:35
  30.6 4.0 %hyena_terms.2 = (bf16[512,512]{1,0:T(8,128)(2,1)S(1)}, bf16[512,512]{1,0:T(8,128)(2,1)S(1)}, bf16[512,512]{1,0:T(8,128)(2,1)S(1)}, bf16[512,512]{1,0:T(8,128)(2,1)S(1)}, bf16[512,1024]{1,0:T(8,128)(2,1)S(1)}) custom-call(s32[8]{0:T(128)S(1)} %stack.104.meta_ref.refs_0_, bf16[256,1024]{1,0:T(8,128)(2,1)S(1)} %hyena_filters.2.refs_1_, ...), custom_call_target="tpu_custom_call" | custom-call | tf_op jit(solution)/shard_map/hyena_terms/pallas_call | solution.py:188
  41.8 5.3 %collective-permute-done.10.swapped = bf16[3,128,1024]{2,1,0:T(8,128)(2,1)S(1)} collective-permute-done((bf16[3,128,1024]{2,1,0:T(8,128)(2,1)S(1)}, bf16[3,128,1024]{2,1,0:T(8,128)(2,1)S(1)}, u32[]{:S(2)}, u32[]{:S(2)}) %collective-permute-start.10) | collective-permute-done | bytes 786464 | tf_op jit(solution)/shard_map/ppermute | solution.py:35
  47.1 5.4 %load_weights.1 = (bf16[4096,1536]{1,0:T(8,128)(2,1)S(1)}, bf16[512,1024]{1,0:T(8,128)(2,1)S(1)}) custom-call(s32[8]{0:T(128)S(1)} %stack.104.meta_ref.refs_0_, bf16[4096,1536]{1,0:T(8,128)(2,1)} %source.1, bf16[512,4096]{1,0:T(8,128)(2,1)} %outer.1, bf16[512,512]{1,0:T(8,128)(2,1)S(1)} %add_convert_fusion.along, ...), custom_call_target="tpu_custom_call" | custom-call | tf_op jit(solution)/shard_map/load_weights/pallas_call | solution.py:233
  52.5 9.2 %collective-permute-done.7.refs_4_ = bf16[512,512]{1,0:T(8,128)(2,1)S(1)} collective-permute-done((bf16[512,512]{1,0:T(8,128)(2,1)S(1)}, bf16[512,512]{1,0:T(8,128)(2,1)S(1)}, u32[]{:S(2)}, u32[]{:S(2)}) %collective-permute-start.7) | collective-permute-done | bytes 524320 | tf_op jit(solution)/shard_map/ppermute | solution.py:30
  64.6 12.3 %collective-permute-done.13.refs_3_ = bf16[256,1024]{1,0:T(8,128)(2,1)S(1)} collective-permute-done((bf16[256,1024]{1,0:T(8,128)(2,1)S(1)}, bf16[256,1024]{1,0:T(8,128)(2,1)S(1)}, u32[]{:S(2)}, u32[]{:S(2)}) %collective-permute-start.13) | collective-permute-done | bytes 524320 | tf_op jit(solution)/shard_map/ppermute | solution.py:30
  79.0 3.2 %qkv_near.2 = (f32[256,1536]{1,0:T(8,128)S(1)}, f32[256,128]{1,0:T(8,128)S(1)}) custom-call(s32[8]{0:T(128)S(1)} %stack.104.meta_ref.refs_0_, bf16[256,1024]{1,0:T(8,128)(2,1)S(1)} %get-tuple-element.72.refs_1_.refs_5_, bf16[256,1024]{1,0:T(8,128)(2,1)S(1)} %collective-permute-done.11.refs_2_, bf16[256,1024]{1,0:T(8,128)(2,1)S(1)} %collective-permute-done.13.refs_3_, ...), custom_call_target="tpu_custom_call" | custom-call | flops 3300000000 | bytes 10800000 | tf_op jit(solution)/shard_map/qkv_near/pallas_call | solution.py:188
  82.2 2.4 %collective-permute-done.14.refs_2_ = bf16[128,1024]{1,0:T(8,128)(2,1)S(1)} collective-permute-done((bf16[128,1024]{1,0:T(8,128)(2,1)S(1)}, bf16[128,1024]{1,0:T(8,128)(2,1)S(1)}, u32[]{:S(2)}, u32[]{:S(2)}) %collective-permute-start.14) | collective-permute-done | bytes 262176 | tf_op jit(solution)/shard_map/ppermute | solution.py:30
  89.8 2.7 %collective-permute-start.15 = (bf16[3,256,128]{2,1,0:T(8,128)(2,1)S(1)}, bf16[3,256,128]{2,1,0:T(8,128)(2,1)S(1)}, u32[]{:S(2)}, u32[]{:S(2)}) collective-permute-start(bf16[3,256,128]{2,1,0:T(8,128)(2,1)S(1)} %get-tuple-element.76), channel_id=1, source_target_pairs={{0,8},{4,12},{8,16},{12,20},{16,24},{20,28},{24,0},{28,4},{1,9},{5... | collective-permute-start | bytes 589832 | tf_op jit(solution)/shard_map/ppermute | solution.py:45
  93.5 2.8 %collective-permute-start.17 = (bf16[3,256,128]{2,1,0:T(8,128)(2,1)S(1)}, bf16[3,256,128]{2,1,0:T(8,128)(2,1)S(1)}, u32[]{:S(2)}, u32[]{:S(2)}) collective-permute-start(bf16[3,256,128]{2,1,0:T(8,128)(2,1)S(1)} %get-tuple-element.78), channel_id=1, source_target_pairs={{0,24},{4,28},{8,0},{12,4},{16,8},{20,12},{24,16},{28,20},{1,25},{... | collective-permute-start | bytes 589832 | tf_op jit(solution)/shard_map/ppermute | solution.py:45
  101.0 3.2 %qkv_near.3 = (f32[256,1536]{1,0:T(8,128)S(1)}, f32[256,128]{1,0:T(8,128)S(1)}) custom-call(s32[8]{0:T(128)S(1)} %stack.104.meta_ref.refs_0_, bf16[256,1024]{1,0:T(8,128)(2,1)S(1)} %get-tuple-element.80.refs_1_.refs_4_, bf16[256,1024]{1,0:T(8,128)(2,1)S(1)} %collective-permute-done.18.refs_2_, bf16[256,1024]{1,0:T(8,128)(2,1)S(1)} %collective-permute-done.20.refs_3_, ...), custom_call_target="tpu_custom_call" | custom-call | flops 3300000000 | bytes 10800000 | tf_op jit(solution)/shard_map/qkv_near/pallas_call | solution.py:188
  110.2 2.8 %collective-permute-start.24 = (bf16[3,256,128]{2,1,0:T(8,128)(2,1)S(1)}, bf16[3,256,128]{2,1,0:T(8,128)(2,1)S(1)}, u32[]{:S(2)}, u32[]{:S(2)}) collective-permute-start(bf16[3,256,128]{2,1,0:T(8,128)(2,1)S(1)} %get-tuple-element.86), channel_id=1, source_target_pairs={{0,24},{4,28},{8,0},{12,4},{16,8},{20,12},{24,16},{28,20},{1,25},{... | collective-permute-start | bytes 589832 | tf_op jit(solution)/shard_map/ppermute | solution.py:45
  113.3 3.1 %collective-permute-done.22.refs_2_.refs_3_ = bf16[3,256,128]{2,1,0:T(8,128)(2,1)S(1)} collective-permute-done((bf16[3,256,128]{2,1,0:T(8,128)(2,1)S(1)}, bf16[3,256,128]{2,1,0:T(8,128)(2,1)S(1)}, u32[]{:S(2)}, u32[]{:S(2)}) %collective-permute-start.22) | collective-permute-done | bytes 196640 | tf_op jit(solution)/shard_map/ppermute | solution.py:45
  116.5 5.3 %collective-permute-done.23.refs_3_ = bf16[3,256,128]{2,1,0:T(8,128)(2,1)S(1)} collective-permute-done((bf16[3,256,128]{2,1,0:T(8,128)(2,1)S(1)}, bf16[3,256,128]{2,1,0:T(8,128)(2,1)S(1)}, u32[]{:S(2)}, u32[]{:S(2)}) %collective-permute-start.23) | collective-permute-done | bytes 196640 | tf_op jit(solution)/shard_map/ppermute | solution.py:45
  124.7 4.9 %attention.2 = (bf16[512,128]{1,0:T(8,128)(2,1)S(1)}, bf16[512,128]{1,0:T(8,128)(2,1)S(1)}, bf16[2,4,512,128]{3,2,1,0:T(8,128)(2,1)S(1)}, bf16[2,4,128,512]{3,2,1,0:T(8,128)(2,1)S(1)}) custom-call(s32[8]{0:T(128)S(1)} %stack.104.meta_ref.refs_0_, bf16[3,256,128]{2,1,0:T(8,128)(2,1)S(1)} %get-tuple-element.87.refs_1_, ...), custom_call_target="tpu_custom_call" | custom-call | flops 6600000000 | bytes 21600000 | tf_op jit(solution)/shard_map/attention/pallas_call | solution.py:188
  129.5 2.8 %collective-permute-start.28 = (bf16[512,128]{1,0:T(8,128)(2,1)S(1)}, bf16[512,128]{1,0:T(8,128)(2,1)S(1)}, u32[]{:S(2)}, u32[]{:S(2)}) collective-permute-start(bf16[512,128]{1,0:T(8,128)(2,1)S(1)} %get-tuple-element.96), channel_id=1, source_target_pairs={{0,16},{4,20},{8,24},{12,28},{16,0},{20,4},{24,8},{28,12},{1,17},{... | collective-permute-start | bytes 393224 | tf_op jit(solution)/shard_map/ppermute | solution.py:45
  132.4 6.7 %attention.3 = (bf16[512,128]{1,0:T(8,128)(2,1)S(1)}, bf16[512,128]{1,0:T(8,128)(2,1)S(1)}) custom-call(s32[8]{0:T(128)S(1)} %stack.104.meta_ref.refs_0_, bf16[3,256,128]{2,1,0:T(8,128)(2,1)S(1)} %collective-permute-done.24.refs_4_.refs_1_, bf16[3,256,128]{2,1,0:T(8,128)(2,1)S(1)} %collective-permute-done.17.refs_8_.refs_2_, ...), custom_call_target="tpu_custom_call" | custom-call | flops 6600000000 | bytes 21600000 | tf_op jit(solution)/shard_map/attention/pallas_call | solution.py:188
  141.6 2.8 %collective-permute-start.29 = (bf16[512,128]{1,0:T(8,128)(2,1)S(1)}, bf16[512,128]{1,0:T(8,128)(2,1)S(1)}, u32[]{:S(2)}, u32[]{:S(2)}) collective-permute-start(bf16[512,128]{1,0:T(8,128)(2,1)S(1)} %get-tuple-element.102), channel_id=1, source_target_pairs={{0,8},{4,12},{8,16},{12,20},{16,24},{20,28},{24,0},{28,4},{1,9},{5... | collective-permute-start | bytes 393224 | tf_op jit(solution)/shard_map/ppermute | solution.py:45
  153.6 6.7 %collective-permute-done.33.refs_4_ = bf16[2,512,128]{2,1,0:T(8,128)(2,1)S(1)} collective-permute-done((bf16[2,512,128]{2,1,0:T(8,128)(2,1)S(1)}, bf16[2,512,128]{2,1,0:T(8,128)(2,1)S(1)}, u32[]{:S(2)}, u32[]{:S(2)}) %collective-permute-start.33) | collective-permute-done | bytes 262176 | tf_op jit(solution)/shard_map/ppermute | solution.py:30
  160.8 3.4 %collective-permute-done.35.refs_1_ = bf16[2,512,128]{2,1,0:T(8,128)(2,1)S(1)} collective-permute-done((bf16[2,512,128]{2,1,0:T(8,128)(2,1)S(1)}, bf16[2,512,128]{2,1,0:T(8,128)(2,1)S(1)}, u32[]{:S(2)}, u32[]{:S(2)}) %collective-permute-start.35) | collective-permute-done | bytes 262176 | tf_op jit(solution)/shard_map/ppermute | solution.py:30
  (98 shorter events, 58.0 us)
Async XLA Ops:
  2.3 12.7 %collective-permute-start = (bf16[3,144,1024]{2,1,0:T(8,128)(2,1)S(1)}, bf16[3,144,1024]{2,1,0:T(8,128)(2,1)S(1)}, u32[]{:S(2)}, u32[]{:S(2)}) collective-permute-start(bf16[3,144,1024]{2,1,0:T(8,128)(2,1)S(1)} %get-tuple-element.58), channel_id=1, source_target_pairs={{0,4},{4,8},{8,12},{12,16},{16,20},{20,24},{24,28},{1,5},{5,9},{9,... | collective-permute-start | bytes 2654216 | tf_op jit(solution)/shard_map/ppermute | solution.py:40
  4.7 16.1 %collective-permute-start.1 = (bf16[128,1024]{1,0:T(8,128)(2,1)S(1)}, bf16[128,1024]{1,0:T(8,128)(2,1)S(1)}, u32[]{:S(2)}, u32[]{:S(2)}) collective-permute-start(bf16[128,1024]{1,0:T(8,128)(2,1)S(1)} %get-tuple-element.61), channel_id=1, source_target_pairs={{0,1},{1,0},{2,3},{3,2},{4,5},{5,4},{6,7},{7,6},{8,9},{9,8},{10,11... | collective-permute-start | bytes 786440 | tf_op jit(solution)/shard_map/ppermute | solution.py:30
  7.1 13.7 %collective-permute-start.2 = (bf16[128,1024]{1,0:T(8,128)(2,1)S(1)}, bf16[128,1024]{1,0:T(8,128)(2,1)S(1)}, u32[]{:S(2)}, u32[]{:S(2)}) collective-permute-start(bf16[128,1024]{1,0:T(8,128)(2,1)S(1)} %get-tuple-element.62), channel_id=1, source_target_pairs={{0,2},{1,3},{2,0},{3,1},{4,6},{5,7},{6,4},{7,5},{8,10},{9,11},{10,... | collective-permute-start | bytes 786440 | tf_op jit(solution)/shard_map/ppermute | solution.py:30
  8.7 12.2 %collective-permute-start.3 = (bf16[128,1024]{1,0:T(8,128)(2,1)S(1)}, bf16[128,1024]{1,0:T(8,128)(2,1)S(1)}, u32[]{:S(2)}, u32[]{:S(2)}) collective-permute-start(bf16[128,1024]{1,0:T(8,128)(2,1)S(1)} %get-tuple-element.63), channel_id=1, source_target_pairs={{0,3},{1,2},{2,1},{3,0},{4,7},{5,6},{6,5},{7,4},{8,11},{9,10},{10,... | collective-permute-start | bytes 786440 | tf_op jit(solution)/shard_map/ppermute | solution.py:30
  22.7 13.8 %collective-permute-start.6 = (bf16[512,512]{1,0:T(8,128)(2,1)S(1)}, bf16[512,512]{1,0:T(8,128)(2,1)S(1)}, u32[]{:S(2)}, u32[]{:S(2)}) collective-permute-start(bf16[512,512]{1,0:T(8,128)(2,1)S(1)} %get-tuple-element.68), channel_id=1, source_target_pairs={{0,2},{1,3},{2,0},{3,1},{4,6},{5,7},{6,4},{7,5},{8,10},{9,11},{10,... | collective-permute-start | bytes 1572872 | tf_op jit(solution)/shard_map/ppermute | solution.py:30
  24.8 14.4 %collective-permute-start.8 = (bf16[512,512]{1,0:T(8,128)(2,1)S(1)}, bf16[512,512]{1,0:T(8,128)(2,1)S(1)}, u32[]{:S(2)}, u32[]{:S(2)}) collective-permute-start(bf16[512,512]{1,0:T(8,128)(2,1)S(1)} %get-tuple-element.70), channel_id=1, source_target_pairs={{0,1},{1,0},{2,3},{3,2},{4,5},{5,4},{6,7},{7,6},{8,9},{9,8},{10,11... | collective-permute-start | bytes 1572872 | tf_op jit(solution)/shard_map/ppermute | solution.py:30
  26.3 20.8 %collective-permute-start.10 = (bf16[3,128,1024]{2,1,0:T(8,128)(2,1)S(1)}, bf16[3,128,1024]{2,1,0:T(8,128)(2,1)S(1)}, u32[]{:S(2)}, u32[]{:S(2)}) collective-permute-start(bf16[3,128,1024]{2,1,0:T(8,128)(2,1)S(1)} %get-tuple-element.112.refs_4_), channel_id=1, source_target_pairs={{0,8},{4,12},{8,0},{12,4},{16,24},{20,28},{24,16},{28,20},{1,9},{5... | collective-permute-start | bytes 2359304 | tf_op jit(solution)/shard_map/ppermute | solution.py:35
  34.6 17.9 %collective-permute-start.4 = (bf16[512,512]{1,0:T(8,128)(2,1)S(1)}, bf16[512,512]{1,0:T(8,128)(2,1)S(1)}, u32[]{:S(2)}, u32[]{:S(2)}) collective-permute-start(bf16[512,512]{1,0:T(8,128)(2,1)S(1)} %get-tuple-element.65), channel_id=1, source_target_pairs={{0,1},{1,0},{2,3},{3,2},{4,5},{5,4},{6,7},{7,6},{8,9},{9,8},{10,11... | collective-permute-start | bytes 1572872 | tf_op jit(solution)/shard_map/ppermute | solution.py:30
  35.2 17.3 %collective-permute-start.5 = (bf16[512,512]{1,0:T(8,128)(2,1)S(1)}, bf16[512,512]{1,0:T(8,128)(2,1)S(1)}, u32[]{:S(2)}, u32[]{:S(2)}) collective-permute-start(bf16[512,512]{1,0:T(8,128)(2,1)S(1)} %get-tuple-element.66), channel_id=1, source_target_pairs={{0,2},{1,3},{2,0},{3,1},{4,6},{5,7},{6,4},{7,5},{8,10},{9,11},{10,... | collective-permute-start | bytes 1572872 | tf_op jit(solution)/shard_map/ppermute | solution.py:30
  36.6 25.1 %collective-permute-start.7 = (bf16[512,512]{1,0:T(8,128)(2,1)S(1)}, bf16[512,512]{1,0:T(8,128)(2,1)S(1)}, u32[]{:S(2)}, u32[]{:S(2)}) collective-permute-start(bf16[512,512]{1,0:T(8,128)(2,1)S(1)} %add_convert_fusion.1), channel_id=1, source_target_pairs={{0,1},{1,0},{2,3},{3,2},{4,5},{5,4},{6,7},{7,6},{8,9},{9,8},{10,11... | collective-permute-start | bytes 1572872 | tf_op jit(solution)/shard_map/ppermute | solution.py:30
  39.4 22.3 %collective-permute-start.9 = (bf16[512,512]{1,0:T(8,128)(2,1)S(1)}, bf16[512,512]{1,0:T(8,128)(2,1)S(1)}, u32[]{:S(2)}, u32[]{:S(2)}) collective-permute-start(bf16[512,512]{1,0:T(8,128)(2,1)S(1)} %add_convert_fusion.along), channel_id=1, source_target_pairs={{0,2},{1,3},{2,0},{3,1},{4,6},{5,7},{6,4},{7,5},{8,10},{9,11},{10,... | collective-permute-start | bytes 1572872 | tf_op jit(solution)/shard_map/ppermute | solution.py:30
  62.8 14.1 %collective-permute-start.13 = (bf16[256,1024]{1,0:T(8,128)(2,1)S(1)}, bf16[256,1024]{1,0:T(8,128)(2,1)S(1)}, u32[]{:S(2)}, u32[]{:S(2)}) collective-permute-start(bf16[256,1024]{1,0:T(8,128)(2,1)S(1)} %get-tuple-element.72.refs_1_.refs_5_), channel_id=1, source_target_pairs={{0,2},{1,3},{2,0},{3,1},{4,6},{5,7},{6,4},{7,5},{8,10},{9,11},{10,... | collective-permute-start | bytes 1572872 | tf_op jit(solution)/shard_map/ppermute | solution.py:30
  62.9 15.4 %collective-permute-start.11 = (bf16[256,1024]{1,0:T(8,128)(2,1)S(1)}, bf16[256,1024]{1,0:T(8,128)(2,1)S(1)}, u32[]{:S(2)}, u32[]{:S(2)}) collective-permute-start(bf16[256,1024]{1,0:T(8,128)(2,1)S(1)} %get-tuple-element.72.refs_1_.refs_5_), channel_id=1, source_target_pairs={{0,1},{1,0},{2,3},{3,2},{4,5},{5,4},{6,7},{7,6},{8,9},{9,8},{10,11... | collective-permute-start | bytes 1572872 | tf_op jit(solution)/shard_map/ppermute | solution.py:30
  85.9 12.2 %collective-permute-start.20 = (bf16[256,1024]{1,0:T(8,128)(2,1)S(1)}, bf16[256,1024]{1,0:T(8,128)(2,1)S(1)}, u32[]{:S(2)}, u32[]{:S(2)}) collective-permute-start(bf16[256,1024]{1,0:T(8,128)(2,1)S(1)} %get-tuple-element.80.refs_1_.refs_4_), channel_id=1, source_target_pairs={{0,2},{1,3},{2,0},{3,1},{4,6},{5,7},{6,4},{7,5},{8,10},{9,11},{10,... | collective-permute-start | bytes 1572872 | tf_op jit(solution)/shard_map/ppermute | solution.py:30
  86.4 12.2 %collective-permute-start.18 = (bf16[256,1024]{1,0:T(8,128)(2,1)S(1)}, bf16[256,1024]{1,0:T(8,128)(2,1)S(1)}, u32[]{:S(2)}, u32[]{:S(2)}) collective-permute-start(bf16[256,1024]{1,0:T(8,128)(2,1)S(1)} %get-tuple-element.80.refs_1_.refs_4_), channel_id=1, source_target_pairs={{0,1},{1,0},{2,3},{3,2},{4,5},{5,4},{6,7},{7,6},{8,9},{9,8},{10,11... | collective-permute-start | bytes 1572872 | tf_op jit(solution)/shard_map/ppermute | solution.py:30
  89.8 20.5 %collective-permute-start.15 = (bf16[3,256,128]{2,1,0:T(8,128)(2,1)S(1)}, bf16[3,256,128]{2,1,0:T(8,128)(2,1)S(1)}, u32[]{:S(2)}, u32[]{:S(2)}) collective-permute-start(bf16[3,256,128]{2,1,0:T(8,128)(2,1)S(1)} %get-tuple-element.76), channel_id=1, source_target_pairs={{0,8},{4,12},{8,16},{12,20},{16,24},{20,28},{24,0},{28,4},{1,9},{5... | collective-permute-start | bytes 589832 | tf_op jit(solution)/shard_map/ppermute | solution.py:45
  92.4 20.8 %collective-permute-start.16 = (bf16[3,256,128]{2,1,0:T(8,128)(2,1)S(1)}, bf16[3,256,128]{2,1,0:T(8,128)(2,1)S(1)}, u32[]{:S(2)}, u32[]{:S(2)}) collective-permute-start(bf16[3,256,128]{2,1,0:T(8,128)(2,1)S(1)} %get-tuple-element.77), channel_id=1, source_target_pairs={{0,16},{4,20},{8,24},{12,28},{16,0},{20,4},{24,8},{28,12},{1,17},{... | collective-permute-start | bytes 589832 | tf_op jit(solution)/shard_map/ppermute | solution.py:45
  93.5 19.8 %collective-permute-start.17 = (bf16[3,256,128]{2,1,0:T(8,128)(2,1)S(1)}, bf16[3,256,128]{2,1,0:T(8,128)(2,1)S(1)}, u32[]{:S(2)}, u32[]{:S(2)}) collective-permute-start(bf16[3,256,128]{2,1,0:T(8,128)(2,1)S(1)} %get-tuple-element.78), channel_id=1, source_target_pairs={{0,24},{4,28},{8,0},{12,4},{16,8},{20,12},{24,16},{28,20},{1,25},{... | collective-permute-start | bytes 589832 | tf_op jit(solution)/shard_map/ppermute | solution.py:45
  109.2 12.6 %collective-permute-start.23 = (bf16[3,256,128]{2,1,0:T(8,128)(2,1)S(1)}, bf16[3,256,128]{2,1,0:T(8,128)(2,1)S(1)}, u32[]{:S(2)}, u32[]{:S(2)}) collective-permute-start(bf16[3,256,128]{2,1,0:T(8,128)(2,1)S(1)} %get-tuple-element.85), channel_id=1, source_target_pairs={{0,16},{4,20},{8,24},{12,28},{16,0},{20,4},{24,8},{28,12},{1,17},{... | collective-permute-start | bytes 589832 | tf_op jit(solution)/shard_map/ppermute | solution.py:45
  110.2 11.6 %collective-permute-start.24 = (bf16[3,256,128]{2,1,0:T(8,128)(2,1)S(1)}, bf16[3,256,128]{2,1,0:T(8,128)(2,1)S(1)}, u32[]{:S(2)}, u32[]{:S(2)}) collective-permute-start(bf16[3,256,128]{2,1,0:T(8,128)(2,1)S(1)} %get-tuple-element.86), channel_id=1, source_target_pairs={{0,24},{4,28},{8,0},{12,4},{16,8},{20,12},{24,16},{28,20},{1,25},{... | collective-permute-start | bytes 589832 | tf_op jit(solution)/shard_map/ppermute | solution.py:45
  113.3 11.4 %collective-permute-start.27 = (bf16[2,3,128,1024]{3,2,1,0:T(8,128)(2,1)S(1)}, bf16[2,3,128,1024]{3,2,1,0:T(8,128)(2,1)S(1)}, u32[]{:S(2)}, u32[]{:S(2)}) collective-permute-start(bf16[2,3,128,1024]{3,2,1,0:T(8,128)(2,1)S(1)} %pad_maximum_fusion.refs_7_.refs_4_), channel_id=1, source_target_pairs={{0,4},{4,0},{8,12},{12,8},{16,20},{20,16},{24,28},{28,24},{1,5},{5... | collective-permute-start | bytes 4718600 | tf_op jit(solution)/shard_map/ppermute | solution.py:35
  129.5 9.6 %collective-permute-start.28 = (bf16[512,128]{1,0:T(8,128)(2,1)S(1)}, bf16[512,128]{1,0:T(8,128)(2,1)S(1)}, u32[]{:S(2)}, u32[]{:S(2)}) collective-permute-start(bf16[512,128]{1,0:T(8,128)(2,1)S(1)} %get-tuple-element.96), channel_id=1, source_target_pairs={{0,16},{4,20},{8,24},{12,28},{16,0},{20,4},{24,8},{28,12},{1,17},{... | collective-permute-start | bytes 393224 | tf_op jit(solution)/shard_map/ppermute | solution.py:45
  151.0 9.3 %collective-permute-start.33 = (bf16[2,512,128]{2,1,0:T(8,128)(2,1)S(1)}, bf16[2,512,128]{2,1,0:T(8,128)(2,1)S(1)}, u32[]{:S(2)}, u32[]{:S(2)}) collective-permute-start(bf16[2,512,128]{2,1,0:T(8,128)(2,1)S(1)} %pad_maximum_fusion.5.refs_2_), channel_id=1, source_target_pairs={{0,2},{1,3},{2,0},{3,1},{4,6},{5,7},{6,4},{7,5},{8,10},{9,11},{10,... | collective-permute-start | bytes 786440 | tf_op jit(solution)/shard_map/ppermute | solution.py:30
  152.7 11.5 %collective-permute-start.35 = (bf16[2,512,128]{2,1,0:T(8,128)(2,1)S(1)}, bf16[2,512,128]{2,1,0:T(8,128)(2,1)S(1)}, u32[]{:S(2)}, u32[]{:S(2)}) collective-permute-start(bf16[2,512,128]{2,1,0:T(8,128)(2,1)S(1)} %collective-permute-done.31.refs_2_), channel_id=1, source_target_pairs={{0,2},{1,3},{2,0},{3,1},{4,6},{5,7},{6,4},{7,5},{8,10},{9,11},{10,... | collective-permute-start | bytes 786440 | tf_op jit(solution)/shard_map/ppermute | solution.py:30
  (16 other events, 133.8 us)
